TPU v7x, 32 devices: a whole 2x2x4 slice. The times are simulated.
32 devices in a mesh: rep: 4 (over z), ep: 8 (over y, x, core).
Axes of the slice: x: 2, y: 2, z: 4, core: 2. Of those that a mesh axis runs over, the one named last changes fastest.
Arguments:
- tokens: bfloat16 [4096, 2048], P(('rep', 'ep')), may hold values from -6 to 6
- cotangent: bfloat16 [4096, 2048], P(('rep', 'ep')), may hold values from -6 to 6
- query_weight: bfloat16 [2048, 2048], P(('rep', 'ep')), may hold values from -0.125 to 0.125
- key_weight: bfloat16 [2048, 2048], P(('rep', 'ep')), may hold values from -0.125 to 0.125
- value_weight: bfloat16 [2048, 2048], P(('rep', 'ep')), may hold values from -0.125 to 0.125
- output_weight: bfloat16 [2048, 2048], P(('rep', 'ep')), may hold values from -0.5 to 0.5
- router_weight: bfloat16 [2048, 24], P(('rep', 'ep')), may hold values from -0.06591797 to 0.06591797
- gains: bfloat16 [4352], P(('rep', 'ep')), may hold values from 0.5 to 1.5
- expert_gate: bfloat16 [24, 2048, 1024], P('ep'), may hold values from -0.125 to 0.125
- expert_up: bfloat16 [24, 2048, 1024], P('ep'), may hold values from -0.125 to 0.125
- expert_down: bfloat16 [24, 1024, 2048], P('ep'), may hold values from -0.5 to 0.5
- lengths: int32 [4, 3], P('rep'), may hold values from 1 to 768, 1024 in all within a row
- deal: int32 [4096], P(('rep', 'ep')), may hold values from 0 to 1023, as said below
- routes: int32 [4096, 8], P(('rep', 'ep')), may hold values from 0 to 23, all different within a row; in each aligned block of 128 rows (0 to 127, 128 to 255, ...) at most 64 rows name the same one
- priority: int32 [4096], P(('rep', 'ep')), may hold values from 0 to 1023, as said below
Outputs:
- block_out: bfloat16 [4096, 2048], P(('rep', 'ep'))
- input_grad: float32 [4096, 2048], P(('rep', 'ep'))
- query_grad: float32 [2048, 2048], P(('rep', 'ep'))
- key_grad: float32 [2048, 2048], P(('rep', 'ep'))
- value_grad: float32 [2048, 2048], P(('rep', 'ep'))
- output_grad: float32 [2048, 2048], P(('rep', 'ep'))
- router_grad: float32 [2048, 24], P(('rep', 'ep'))
- gains_grad: float32 [4352], P(('rep', 'ep'))
- gate_grad: float32 [24, 2048, 1024], P('ep', 'rep')
- up_grad: float32 [24, 2048, 1024], P('ep', 'rep')
- down_grad: float32 [24, 1024, 2048], P('ep', 'rep')
Inputs may be any that keep to these rules, and one draw needn't show every extreme that they name: `deal`: within each group's 1024 rows, every packed position appears once. `priority`: within each group's 1024 rows, every rank appears once. `routes`: a token's 8 experts are different; the rows of one device name each expert at most 64 times, and some expert exactly that often. Each group's lengths sum to 1024; the longest is 768.
All inputs are finite; a program needn't handle non-finite values.
Results may differ from a plain program's by a relative error of at most 0.02.
Values may be sent and summed in bfloat16 or wider, within the bound.
A program may use at most 384 MiB of HBM per device.

v0:
```python
from functools import partial

import jax
import jax.numpy as jnp
from jax import lax
from jax.sharding import PartitionSpec as P

HD = 128


norm_eps = 1e-06
rope_base = 10000.0
masked_score = -1e30
highest = lax.Precision.HIGHEST


def rms_scale(values, gain_vec):
    return (
        values * lax.rsqrt(jnp.mean(values * values, axis=-1, keepdims=True) + norm_eps) * gain_vec
    )


def rotate(values, positions):
    half_width = values.shape[-1] // 2
    frequency = rope_base ** (-2.0 * jnp.arange(half_width, dtype=jnp.float32) / values.shape[-1])
    angles = positions.astype(jnp.float32)[:, None] * frequency[None, :]
    cosine = jnp.cos(angles)[:, None, :]
    sine_part = jnp.sin(angles)[:, None, :]
    low_half = values[..., :half_width]
    high_half = values[..., half_width:]
    return jnp.concatenate(
        [low_half * cosine - high_half * sine_part, high_half * cosine + low_half * sine_part],
        axis=-1,
    )


def placement(deal_rows, lengths_row):
    seq_ends = jnp.cumsum(lengths_row)
    is_after = (seq_ends[None, :] <= deal_rows[:, None]).astype(jnp.int32)
    segment = jnp.sum(is_after, axis=1)
    seq_start = jnp.sum(is_after * lengths_row[None, :], axis=1)
    return (segment, deal_rows - seq_start)


def rope_norm(projected, gain_vec, positions):
    return rotate(rms_scale(projected, gain_vec), positions)


def attend_forward(parts, same_seq, score_scale):
    head_query, head_key, head_value = parts
    scores = (
        jnp.einsum("thd,shd->hts", head_query, head_key, preferred_element_type=jnp.float32)
        * score_scale
    )
    scores = jnp.where(same_seq[None], scores, masked_score)
    top_score = jnp.max(scores, axis=-1, keepdims=True)
    lifted = jnp.exp(scores - top_score)
    total_sum = jnp.sum(lifted, axis=-1, keepdims=True)
    prob_low = (lifted / total_sum).astype(jnp.bfloat16)
    mixed_out = jnp.einsum("hts,shd->thd", prob_low, head_value, preferred_element_type=jnp.float32)
    return (mixed_out, top_score, total_sum)


def attend_backward(parts, same_seq, score_scale):
    head_query, head_key, head_value, head_grad, top_score, total_sum = parts
    scores = (
        jnp.einsum("thd,shd->hts", head_query, head_key, preferred_element_type=jnp.float32)
        * score_scale
    )
    scores = jnp.where(same_seq[None], scores, masked_score)
    prob_full = jnp.exp(scores - top_score) / total_sum
    prob_low = prob_full.astype(jnp.bfloat16)
    prob_grad = jnp.einsum(
        "thd,shd->hts", head_grad, head_value, preferred_element_type=jnp.float32
    )
    row_dot = jnp.sum(prob_full * prob_grad, axis=-1, keepdims=True)
    score_grad = (prob_full * (prob_grad - row_dot)).astype(jnp.bfloat16)
    query_grad = (
        jnp.einsum("hts,shd->thd", score_grad, head_key, preferred_element_type=jnp.float32)
        * score_scale
    )
    key_grad = (
        jnp.einsum("hts,thd->shd", score_grad, head_query, preferred_element_type=jnp.float32)
        * score_scale
    )
    value_grad = jnp.einsum("hts,thd->shd", prob_low, head_grad, preferred_element_type=jnp.float32)
    return (query_grad, key_grad, value_grad)


def on_device(
    tokens,
    cotangent,
    query_weight,
    key_weight,
    value_weight,
    output_weight,
    router_weight,
    gains,
    expert_gate,
    expert_up,
    expert_down,
    lengths,
    deal,
    routes,
    priority,
):
    tok_dev, width = tokens.shape
    ep_count = lax.axis_size("ep")
    ep_index = lax.axis_index("ep")
    exp_dev = expert_gate.shape[0]
    top_count = routes.shape[1]
    experts_all = exp_dev * ep_count
    group_rows = tok_dev * ep_count
    send_most = min(tok_dev, 3 * tok_dev * top_count // (2 * experts_all))
    capacity = 5 * tok_dev * top_count // (4 * exp_dev)
    head_dim = HD
    head_count = width // head_dim
    per_group = min(head_count, 4)
    group_count = head_count // per_group
    score_scale = head_dim ** (-0.5)
    query_full, key_full, value_full, output_full, router_full, gains_full = (
        lax.all_gather(query_weight, ("rep", "ep"), axis=0, tiled=True),
        lax.all_gather(key_weight, ("rep", "ep"), axis=0, tiled=True),
        lax.all_gather(value_weight, ("rep", "ep"), axis=0, tiled=True),
        lax.all_gather(output_weight, ("rep", "ep"), axis=0, tiled=True),
        lax.all_gather(router_weight, ("rep", "ep"), axis=0, tiled=True),
        lax.all_gather(gains, ("rep", "ep"), axis=0, tiled=True),
    )
    gains_float = gains_full.astype(jnp.float32)
    gain_in = gains_float[:width]
    gain_mid = gains_float[width : 2 * width]
    gain_query = gains_float[2 * width : 2 * width + head_dim]
    gain_key = gains_float[2 * width + head_dim :]
    deal_all, priority_all, routes_all = (
        lax.all_gather(deal, "ep", axis=0, tiled=True),
        lax.all_gather(priority, "ep", axis=0, tiled=True),
        lax.all_gather(routes, "ep", axis=0, tiled=True),
    )
    segment_all, position_all = placement(deal_all, lengths[0])
    segment_own = lax.dynamic_slice_in_dim(segment_all, ep_index * tok_dev, tok_dev)
    position_own = lax.dynamic_slice_in_dim(position_all, ep_index * tok_dev, tok_dev)
    residual = tokens.astype(jnp.float32)
    normed_low = rms_scale(residual, gain_in).astype(jnp.bfloat16)
    query_pre = jnp.dot(normed_low, query_full, preferred_element_type=jnp.float32).reshape(
        tok_dev, head_count, head_dim
    )
    key_pre = jnp.dot(normed_low, key_full, preferred_element_type=jnp.float32).reshape(
        tok_dev, head_count, head_dim
    )
    value_low = jnp.dot(normed_low, value_full, preferred_element_type=jnp.float32).astype(
        jnp.bfloat16
    )
    query_low = rope_norm(query_pre, gain_query, position_own).astype(jnp.bfloat16)
    key_low = (
        rope_norm(key_pre, gain_key, position_own).astype(jnp.bfloat16).reshape(tok_dev, width)
    )
    key_group, value_group = (
        lax.all_gather(key_low, "ep", axis=0, tiled=True),
        lax.all_gather(value_low, "ep", axis=0, tiled=True),
    )
    same_seq = segment_own[:, None] == segment_all[None, :]
    query_heads = query_low.reshape(tok_dev, group_count, per_group, head_dim).transpose(1, 0, 2, 3)
    key_heads = key_group.reshape(group_rows, group_count, per_group, head_dim).transpose(
        1, 0, 2, 3
    )
    value_heads = value_group.reshape(group_rows, group_count, per_group, head_dim).transpose(
        1, 0, 2, 3
    )
    mixed_heads, top_heads, total_heads = lax.map(
        partial(attend_forward, same_seq=same_seq, score_scale=score_scale),
        (query_heads, key_heads, value_heads),
    )
    mixed_low = mixed_heads.transpose(1, 0, 2, 3).reshape(tok_dev, width).astype(jnp.bfloat16)
    after_attn = residual + jnp.dot(mixed_low, output_full, preferred_element_type=jnp.float32)
    mid_low = rms_scale(after_attn, gain_mid).astype(jnp.bfloat16)
    logits = jnp.dot(mid_low, router_full, preferred_element_type=jnp.float32)
    chosen = jnp.take_along_axis(logits, routes, axis=1)
    gate_prob = jax.nn.softmax(chosen, axis=-1)
    expert_ids = jnp.arange(experts_all, dtype=jnp.int32)
    onehot_all = jnp.sum(
        (routes_all[:, :, None] == expert_ids[None, None, :]).astype(jnp.float32), axis=1
    )
    earlier = (priority_all[None, :] < priority_all[:, None]).astype(jnp.float32)
    slot_all = jnp.take_along_axis(
        jnp.dot(earlier, onehot_all, precision=highest), routes_all, axis=1
    ).astype(jnp.int32)
    row_ids = jnp.arange(tok_dev, dtype=jnp.int32)
    lower_tri = (row_ids[:, None] > row_ids[None, :]).astype(jnp.float32)
    before = jnp.einsum(
        "ij,dje->die",
        lower_tri,
        onehot_all.reshape(ep_count, tok_dev, experts_all),
        precision=highest,
    ).reshape(group_rows, experts_all)
    place_all = jnp.take_along_axis(before, routes_all, axis=1).astype(jnp.int32)
    kept_all = slot_all < capacity
    kept_own = lax.dynamic_slice_in_dim(kept_all, ep_index * tok_dev, tok_dev)
    place_own = lax.dynamic_slice_in_dim(place_all, ep_index * tok_dev, tok_dev)
    buffer_index = (routes * send_most + place_own).reshape(-1)
    rows_out = jnp.where(
        kept_own[:, :, None], mid_low[:, None, :], jnp.zeros((), jnp.bfloat16)
    ).reshape(tok_dev * top_count, width)
    send_rows = (
        jnp.zeros((experts_all * send_most, width), jnp.bfloat16)
        .at[buffer_index]
        .set(rows_out)
        .reshape(experts_all, send_most, width)
    )
    received = lax.all_to_all(send_rows, "ep", split_axis=0, concat_axis=1, tiled=True)
    gate_part = jnp.einsum(
        "erd,edf->erf", received, expert_gate, preferred_element_type=jnp.float32
    )
    up_part = jnp.einsum("erd,edf->erf", received, expert_up, preferred_element_type=jnp.float32)
    hidden = (jax.nn.silu(gate_part) * up_part).astype(jnp.bfloat16)
    result = jnp.einsum(
        "erf,efd->erd", hidden, expert_down, preferred_element_type=jnp.float32
    ).astype(jnp.bfloat16)
    returned = lax.all_to_all(result, "ep", split_axis=1, concat_axis=0, tiled=True)
    pair_out = returned.reshape(experts_all * send_most, width)[buffer_index].reshape(
        tok_dev, top_count, width
    )
    pair_weight = gate_prob * kept_own.astype(jnp.float32)
    moe_out = jnp.einsum("tk,tkd->td", pair_weight, pair_out, preferred_element_type=jnp.float32)
    block_out = (after_attn + moe_out).astype(jnp.bfloat16)
    out_grad = cotangent.astype(jnp.float32)
    pair_gate_grad = kept_own.astype(jnp.float32) * jnp.einsum(
        "tkd,td->tk", pair_out, out_grad, preferred_element_type=jnp.float32
    )
    pair_grad = (
        (pair_weight[:, :, None] * out_grad[:, None, :])
        .astype(jnp.bfloat16)
        .reshape(tok_dev * top_count, width)
    )
    grad_send = (
        jnp.zeros((experts_all * send_most, width), jnp.bfloat16)
        .at[buffer_index]
        .set(pair_grad)
        .reshape(experts_all, send_most, width)
    )
    grad_received = lax.all_to_all(grad_send, "ep", split_axis=0, concat_axis=1, tiled=True)
    hidden_grad = jnp.einsum(
        "erd,efd->erf", grad_received, expert_down, preferred_element_type=jnp.float32
    )
    _, silu_pull = jax.vjp(lambda gate_in, up_in: jax.nn.silu(gate_in) * up_in, gate_part, up_part)
    gate_part_grad, up_part_grad = silu_pull(hidden_grad)
    gate_low_grad = gate_part_grad.astype(jnp.bfloat16)
    up_low_grad = up_part_grad.astype(jnp.bfloat16)
    down_term = jnp.einsum(
        "erf,erd->efd", hidden, grad_received, preferred_element_type=jnp.float32
    )
    gate_term = jnp.einsum(
        "erd,erf->edf", received, gate_low_grad, preferred_element_type=jnp.float32
    )
    up_term = jnp.einsum("erd,erf->edf", received, up_low_grad, preferred_element_type=jnp.float32)
    rows_grad = (
        jnp.einsum("erf,edf->erd", gate_low_grad, expert_gate, preferred_element_type=jnp.float32)
        + jnp.einsum("erf,edf->erd", up_low_grad, expert_up, preferred_element_type=jnp.float32)
    ).astype(jnp.bfloat16)
    back_rows = lax.all_to_all(rows_grad, "ep", split_axis=1, concat_axis=0, tiled=True)
    mid_grad = jnp.sum(
        back_rows.reshape(experts_all * send_most, width)[buffer_index]
        .reshape(tok_dev, top_count, width)
        .astype(jnp.float32),
        axis=1,
    )
    gate_w_grad, up_w_grad, down_w_grad = (
        lax.psum_scatter(
            gate_term.astype(jnp.bfloat16), "rep", scatter_dimension=1, tiled=True
        ).astype(jnp.float32),
        lax.psum_scatter(
            up_term.astype(jnp.bfloat16), "rep", scatter_dimension=1, tiled=True
        ).astype(jnp.float32),
        lax.psum_scatter(
            down_term.astype(jnp.bfloat16), "rep", scatter_dimension=1, tiled=True
        ).astype(jnp.float32),
    )
    _, soft_pull = jax.vjp(lambda values: jax.nn.softmax(values, axis=-1), chosen)
    (chosen_grad,) = soft_pull(pair_gate_grad)
    onehot_own = (routes[:, :, None] == expert_ids[None, None, :]).astype(jnp.float32)
    logit_grad = jnp.einsum("tk,tke->te", chosen_grad, onehot_own).astype(jnp.bfloat16)
    mid_grad = mid_grad + jnp.dot(logit_grad, router_full.T, preferred_element_type=jnp.float32)
    router_term = jnp.dot(mid_low.T, logit_grad, preferred_element_type=jnp.float32)
    _, mid_pull = jax.vjp(rms_scale, after_attn, gain_mid)
    after_extra, gain_mid_grad = mid_pull(mid_grad)
    after_grad = out_grad + after_extra
    attn_low_grad = after_grad.astype(jnp.bfloat16)
    output_term = jnp.dot(mixed_low.T, attn_low_grad, preferred_element_type=jnp.float32)
    mixed_grad = jnp.dot(attn_low_grad, output_full.T, preferred_element_type=jnp.float32).astype(
        jnp.bfloat16
    )
    mixed_grad_heads = mixed_grad.reshape(tok_dev, group_count, per_group, head_dim).transpose(
        1, 0, 2, 3
    )
    query_grad_h, key_grad_h, value_grad_h = lax.map(
        partial(attend_backward, same_seq=same_seq, score_scale=score_scale),
        (query_heads, key_heads, value_heads, mixed_grad_heads, top_heads, total_heads),
    )
    query_grad_own = query_grad_h.transpose(1, 0, 2, 3).reshape(tok_dev, head_count, head_dim)
    key_grad_group = key_grad_h.transpose(1, 0, 2, 3).reshape(group_rows, width)
    value_grad_group = value_grad_h.transpose(1, 0, 2, 3).reshape(group_rows, width)
    key_sum, value_sum = (
        lax.psum_scatter(
            key_grad_group.astype(jnp.bfloat16), "ep", scatter_dimension=0, tiled=True
        ).astype(jnp.float32),
        lax.psum_scatter(
            value_grad_group.astype(jnp.bfloat16), "ep", scatter_dimension=0, tiled=True
        ).astype(jnp.float32),
    )
    value_low_grad = value_sum.astype(jnp.bfloat16)
    _, query_pull = jax.vjp(
        lambda projected, gain_vec: rope_norm(projected, gain_vec, position_own),
        query_pre,
        gain_query,
    )
    query_pre_grad, gain_query_grad = query_pull(query_grad_own)
    _, key_pull = jax.vjp(
        lambda projected, gain_vec: rope_norm(projected, gain_vec, position_own), key_pre, gain_key
    )
    key_pre_grad, gain_key_grad = key_pull(key_sum.reshape(tok_dev, head_count, head_dim))
    query_low_grad = query_pre_grad.reshape(tok_dev, width).astype(jnp.bfloat16)
    key_low_grad = key_pre_grad.reshape(tok_dev, width).astype(jnp.bfloat16)
    normed_grad = jnp.dot(query_low_grad, query_full.T, preferred_element_type=jnp.float32)
    normed_grad = normed_grad + jnp.dot(
        key_low_grad, key_full.T, preferred_element_type=jnp.float32
    )
    normed_grad = normed_grad + jnp.dot(
        value_low_grad, value_full.T, preferred_element_type=jnp.float32
    )
    query_term = jnp.dot(normed_low.T, query_low_grad, preferred_element_type=jnp.float32)
    key_term = jnp.dot(normed_low.T, key_low_grad, preferred_element_type=jnp.float32)
    value_term = jnp.dot(normed_low.T, value_low_grad, preferred_element_type=jnp.float32)
    _, input_pull = jax.vjp(rms_scale, residual, gain_in)
    input_extra, gain_in_grad = input_pull(normed_grad)
    input_grad = after_grad + input_extra
    gains_term = jnp.concatenate([gain_in_grad, gain_mid_grad, gain_query_grad, gain_key_grad])
    query_sum, key_total, value_total, output_sum, router_sum, gains_sum = (
        lax.psum_scatter(query_term, ("rep", "ep"), scatter_dimension=0, tiled=True),
        lax.psum_scatter(key_term, ("rep", "ep"), scatter_dimension=0, tiled=True),
        lax.psum_scatter(value_term, ("rep", "ep"), scatter_dimension=0, tiled=True),
        lax.psum_scatter(output_term, ("rep", "ep"), scatter_dimension=0, tiled=True),
        lax.psum_scatter(router_term, ("rep", "ep"), scatter_dimension=0, tiled=True),
        lax.psum_scatter(gains_term, ("rep", "ep"), scatter_dimension=0, tiled=True),
    )
    return (
        block_out,
        input_grad,
        query_sum,
        key_total,
        value_total,
        output_sum,
        router_sum,
        gains_sum,
        gate_w_grad,
        up_w_grad,
        down_w_grad,
    )


def solution(mesh):
    placed = (
        P(("rep", "ep"), None),
        P(("rep", "ep"), None),
        P(("rep", "ep"), None),
        P(("rep", "ep"), None),
        P(("rep", "ep"), None),
        P(("rep", "ep"), None),
        P(("rep", "ep"), None),
        P(("rep", "ep")),
        P("ep", None, None),
        P("ep", None, None),
        P("ep", None, None),
        P("rep", None),
        P(("rep", "ep")),
        P(("rep", "ep"), None),
        P(("rep", "ep")),
    )
    return jax.shard_map(
        on_device,
        mesh=mesh,
        in_specs=placed,
        out_specs=(
            P(("rep", "ep"), None),
            P(("rep", "ep"), None),
            P(("rep", "ep"), None),
            P(("rep", "ep"), None),
            P(("rep", "ep"), None),
            P(("rep", "ep"), None),
            P(("rep", "ep"), None),
            P(("rep", "ep")),
            P("ep", "rep", None),
            P("ep", "rep", None),
            P("ep", "rep", None),
        ),
        check_vma=False,
    )
```

profile of v0, /device:TPU:0, one launch (start us, length us, event | category | flops | bytes accessed | tf_op | source)
XLA Modules:
  0.0 2678.5 jit_solution(14959744934156273745)
XLA Ops:
  10.3 43.0 %all-reduce.4 = bf16[4352]{0:T(1024)(128)(2,1)S(1)} all-reduce(bf16[4352]{0:T(1024)(128)(2,1)S(1)} %dynamic-update-slice), channel_id=1, replica_groups=mesh['rep'=4,'ep'=8] {'rep','ep'}, use_global_device_ids=true, to_apply=%add.4 | all-reduce | flops 4352 | bytes 17408
  55.2 36.0 %all-gather.10.cloned.1.call-done = bf16[2048,2048]{1,0:T(8,128)(2,1)} async-done(((bf16[64,2048]{1,0:T(8,128)(2,1)}), bf16[2048,2048]{1,0:T(8,128)(2,1)}) %all-gather.10.cloned.1.call-update) | async-done | bytes 8388624 | tf_op jit(solution)/shard_map/all_gather | solution.py:124
  91.2 5.7 convolution_convert_fusion.5
  97.2 8.7 all-gather
  106.4 63.8 %all-gather.16.cloned.1.call-done = bf16[2048,2048]{1,0:T(8,128)(2,1)} async-done(((bf16[64,2048]{1,0:T(8,128)(2,1)}), bf16[2048,2048]{1,0:T(8,128)(2,1)}) %all-gather.16.cloned.1.call-update) | async-done | bytes 8388624 | tf_op jit(solution)/shard_map/all_gather | solution.py:123
  175.7 73.5 %all-gather.14.cloned.1.call-done = bf16[2048,2048]{1,0:T(8,128)(2,1)} async-done(((bf16[64,2048]{1,0:T(8,128)(2,1)}), bf16[2048,2048]{1,0:T(8,128)(2,1)}) %all-gather.14.cloned.1.call-update) | async-done | bytes 8388624 | tf_op jit(solution)/shard_map/all_gather | solution.py:122
  260.0 9.0 all_gather.42
  270.3 65.5 %gather_fusion.4 = f32[8192]{0:T(1024)S(1)} fusion(f32[1024,24]{0,1:T(8,128)S(1)} %bitcast.298, s32[8192]{0:T(1024)S(1)} %reshape.429), kind=kCustom, calls=%fused_computation.1.clone | custom fusion | bytes 131072 | tf_op jit(solution)/shard_map/jit(take_along_axis)/gather | solution.py:195
  337.7 39.9 %all-gather.2 = bf16[32,64,24]{1,2,0:T(8,128)(2,1)S(1)} all-gather(bf16[1,64,24]{1,2,0:T(8,128)(2,1)S(1)} %bitcast.341), channel_id=1, replica_groups=mesh['rep'=4,'ep'=8] {'rep','ep'}, dimensions={0}, use_global_device_ids=true | all-gather | bytes 101376 | tf_op jit(solution)/shard_map/all_gather | solution.py:126
  379.3 6.8 all-gather.1
  388.0 65.5 %gather_fusion.3 = f32[8192]{0:T(1024)S(1)} fusion(f32[1024,24]{0,1:T(8,128)S(1)} %fusion.59, s32[8192]{0:T(1024)S(1)} %reshape.429), kind=kCustom, calls=%fused_computation.clone | custom fusion | bytes 131072 | tf_op jit(solution)/shard_map/jit(take_along_axis)/gather | solution.py:184
  454.7 7.7 reshape.332
  462.4 7.4 copy.282
  469.8 6.2 copy.237
  476.1 21.2 while.32
  497.3 5.2 multiply_reduce_fusion.7
  503.9 7.0 gather_fusion.2
  512.1 10.9 scatter_custom_fusion
  528.3 10.7 scatter_custom_fusion.1
  539.0 60.6 %all-to-all-done = bf16[24,64,2048]{2,1,0:T(8,128)(2,1)} async-done(((bf16[24,64,2048]{2,1,0:T(8,128)(2,1)}), bf16[24,64,2048]{2,1,0:T(8,128)(2,1)}, u32[]{:S(2)}, u32[]{:S(2)}) %all-to-all-start) | async-done | bytes 6291488 | tf_op jit(solution)/shard_map/all_to_all | solution.py:209
  608.2 13.6 fusion.125
  621.7 11.3 fusion.126
  633.1 43.3 %all-to-all-done.2 = bf16[24,64,2048]{2,1,0:T(8,128)(2,1)} async-done(((bf16[24,64,2048]{2,1,0:T(8,128)(2,1)}), bf16[24,64,2048]{2,1,0:T(8,128)(2,1)}, u32[]{:S(2)}, u32[]{:S(2)}) %all-to-all-start.2) | async-done | bytes 6291488 | tf_op jit(solution)/shard_map/all_to_all | solution.py:240
  676.4 6.6 copy.253
  683.0 22.8 multiply_convert_fusion.1
  705.8 14.8 fusion.127
  720.6 14.2 add_convert_fusion
  734.9 11.5 copy.254
  746.4 5.4 all-to-all-start.3
  751.8 13.6 convolution_convert_fusion.3
  765.5 11.5 copy.250
  777.0 68.9 %all-to-all-done.3 = bf16[3,512,2048]{2,0,1:T(4,128)(2,1)} async-done(((bf16[3,512,2048]{2,0,1:T(4,128)(2,1)}), bf16[3,512,2048]{2,0,1:T(4,128)(2,1)}, u32[]{:S(2)}, u32[]{:S(2)}) %all-to-all-start.3) | async-done | bytes 6291488 | tf_op jit(solution)/shard_map/all_to_all | solution.py:259
  851.0 5.3 copy.327
  856.5 10.8 copy.255
  867.3 12.6 gather_fusion.1
  884.9 60.0 %all-to-all-done.1 = bf16[3,512,2048]{2,0,1:T(4,128)(2,1)} async-done(((bf16[3,512,2048]{2,0,1:T(4,128)(2,1)}), bf16[3,512,2048]{2,0,1:T(4,128)(2,1)}, u32[]{:S(2)}, u32[]{:S(2)}) %all-to-all-start.1) | async-done | bytes 6291488 | tf_op jit(solution)/shard_map/all_to_all | solution.py:218
  944.9 10.8 copy.251
  955.7 12.6 gather_fusion
  978.6 6.7 convolution_convert_fusion.4
  985.8 48.3 %while.33 = (s32[]{:T(128)}, f32[4,128,4,128]{1,3,2,0:T(8,128)}, bf16[4,1024,4,128]{1,3,2,0:T(8,128)(2,1)}, bf16[4,1024,4,128]{1,3,2,0:T(8,128)(2,1)}, bf16[4,10...) while((s32[]{:T(128)}, f32[4,128,4,128]{1,3,2,0:T(8,128)}, ...), condition=%wide.region_21.23_spmd.clone.clone, body=%wide.region_19.22_spmd.clone.sunk.clone | while | flops 677051904 | bytes 91252464 | solution.py:294
  1034.1 6.4 copy.283
  1040.6 6.5 copy.285
  1049.6 13.1 convolution_convert_fusion.2
  1062.8 12.5 convolution_convert_fusion.1
  1075.3 12.8 convolution_convert_fusion
  1089.2 8.1 fusion.91
  1118.9 8.2 fusion.82
  1128.2 8.3 fusion.79
  1136.6 7.5 reduce-scatter.33.cloned.1.call-done
  1144.1 9.2 fusion.111
  1153.3 127.8 %reduce-scatter.35.cloned.1.call-done = f32[64,24]{1,0:T(8,128)} async-done(((f32[2048,24]{1,0:T(8,128)}), f32[64,24]{1,0:T(8,128)}) %reduce-scatter.35.cloned.1.call-update) | async-done | bytes 6160
  1282.5 7.2 fusion.84
  1289.7 6.4 convolution_add_fusion.2
  1299.4 41.7 %all-reduce.5 = f32[4352]{0:T(1024)S(1)} all-reduce(f32[4352]{0:T(1024)S(1)} %pad_maximum_fusion.1), channel_id=9, replica_groups=mesh['rep'=4,'ep'=8] {'rep','ep'}, use_global_device_ids=true, to_apply=%region_36.38.clone | all-reduce | flops 4352 | bytes 34816
  1342.9 149.4 %reduce-scatter.25.cloned.1.call-done = bf16[3,512,1024]{2,1,0:T(8,128)(2,1)} async-done(((bf16[3,2048,1024]{2,1,0:T(8,128)(2,1)}), bf16[3,512,1024]{2,1,0:T(8,128)(2,1)}) %reduce-scatter.25.cloned.1.call-update) | async-done | bytes 3145744 | tf_op jit(solution)/shard_map/reduce_scatter | solution.py:267
  1492.3 5.3 convert_element_type.192
  1497.6 210.0 %reduce-scatter.27.cloned.1.call-done = bf16[3,512,1024]{2,1,0:T(8,128)(2,1)} async-done(((bf16[3,2048,1024]{2,1,0:T(8,128)(2,1)}), bf16[3,512,1024]{2,1,0:T(8,128)(2,1)}) %reduce-scatter.27.cloned.1.call-update) | async-done | bytes 3145744 | tf_op jit(solution)/shard_map/reduce_scatter | solution.py:270
  1707.6 5.3 convert_element_type.194
  1713.0 209.9 %reduce-scatter.29.cloned.1.call-done = bf16[3,256,2048]{2,1,0:T(8,128)(2,1)} async-done(((bf16[3,1024,2048]{2,1,0:T(8,128)(2,1)}), bf16[3,256,2048]{2,1,0:T(8,128)(2,1)}) %reduce-scatter.29.cloned.1.call-update) | async-done | bytes 3145744 | tf_op jit(solution)/shard_map/reduce_scatter | solution.py:273
  1922.9 5.4 convert_element_type.196
  1928.3 181.4 %reduce-scatter.23.cloned.1.call-done = f32[64,2048]{1,0:T(8,128)} async-done(((f32[2048,2048]{1,0:T(8,128)}), f32[64,2048]{1,0:T(8,128)}) %reduce-scatter.23.cloned.1.call-update) | async-done | bytes 524304 | tf_op jit(solution)/shard_map/reduce_scatter | solution.py:340
  2109.7 187.3 %reduce-scatter.17.cloned.1.call-done = f32[64,2048]{1,0:T(8,128)} async-done(((f32[2048,2048]{1,0:T(8,128)}), f32[64,2048]{1,0:T(8,128)}) %reduce-scatter.17.cloned.1.call-update) | async-done | bytes 524304 | tf_op jit(solution)/shard_map/reduce_scatter | solution.py:337
  2297.0 187.6 %reduce-scatter.19.cloned.1.call-done = f32[64,2048]{1,0:T(8,128)} async-done(((f32[2048,2048]{1,0:T(8,128)}), f32[64,2048]{1,0:T(8,128)}) %reduce-scatter.19.cloned.1.call-update) | async-done | bytes 524304 | tf_op jit(solution)/shard_map/reduce_scatter | solution.py:338
  2484.6 187.1 %reduce-scatter.21.cloned.1.call-done = f32[64,2048]{1,0:T(8,128)} async-done(((f32[2048,2048]{1,0:T(8,128)}), f32[64,2048]{1,0:T(8,128)}) %reduce-scatter.21.cloned.1.call-update) | async-done | bytes 524304 | tf_op jit(solution)/shard_map/reduce_scatter | solution.py:339
  (412 shorter events, 168.3 us)
Async XLA Ops:
  7.2 84.0 %all-gather.10.cloned.1.call-start = ((), (), s32[]{:S(2)}) async-start(), calls=%async_computation.14 | async-start | bytes 8650752 | tf_op jit(solution)/shard_map/all_gather | solution.py:124
  7.9 162.3 %all-gather.16.cloned.1.call-start = ((), (), s32[]{:S(2)}) async-start(), calls=%async_computation.17 | async-start | bytes 8650752 | tf_op jit(solution)/shard_map/all_gather | solution.py:123
  8.7 240.5 %all-gather.14.cloned.1.call-start = ((), (), s32[]{:S(2)}) async-start(), calls=%async_computation.16 | async-start | bytes 8650752 | tf_op jit(solution)/shard_map/all_gather | solution.py:122
  9.4 445.3 %all-gather.12.cloned.1.call-start = ((), (), s32[]{:S(2)}) async-start(), calls=%async_computation.15 | async-start | bytes 4718592 | tf_op jit(solution)/shard_map/all_gather | solution.py:159
  54.6 42.3 %copy-start.82 = (f32[128]{0:T(128)}, f32[128]{0:T(128)S(1)}, u32[]{:S(2)}) copy-start(f32[128]{0:T(128)S(1)} %fusion.75) | copy-start | bytes 1540
  54.6 194.6 %copy-start.58 = (f32[128]{0:T(128)}, f32[128]{0:T(128)S(1)}, u32[]{:S(2)}) copy-start(f32[128]{0:T(128)S(1)} %fusion.109) | copy-start | bytes 1540
  55.2 194.0 %copy-start.27 = (f32[2048]{0:T(1024)}, f32[2048]{0:T(1024)S(1)}, u32[]{:S(2)}) copy-start(f32[2048]{0:T(1024)S(1)} %get-tuple-element.392) | copy-start | bytes 24580
  91.2 5.8 copy-start.86
  91.2 6.0 copy-start.84
  91.2 79.0 %copy-start = (bf16[128,2048]{1,0:T(8,128)(2,1)S(1)}, bf16[128,2048]{1,0:T(8,128)(2,1)}, u32[]{:S(2)}) copy-start(bf16[128,2048]{1,0:T(8,128)(2,1)} %param.21) | copy-start | bytes 1572868
  96.9 372.9 %all-gather.18.cloned.1.call-start = ((), (), s32[]{:S(2)}) async-start(), calls=%async_computation.18 | async-start | bytes 4718592 | tf_op jit(solution)/shard_map/all_gather | solution.py:158
  106.0 153.3 %copy-start.46 = (s32[1024]{0:T(1024)}, s32[1024]{0:T(1024)S(1)}, u32[]{:S(2)}) copy-start(s32[1024]{0:T(1024)S(1)} %get-tuple-element.638) | copy-start | bytes 12292
  106.1 148.5 %copy-start.73 = (f32[128]{0:T(128)}, f32[128]{0:T(128)S(1)}, u32[]{:S(2)}) copy-start(f32[128]{0:T(128)S(1)} %get-tuple-element.393) | copy-start | bytes 1540
  106.1 148.9 %copy-start.75 = (f32[128]{0:T(128)}, f32[128]{0:T(128)S(1)}, u32[]{:S(2)}) copy-start(f32[128]{0:T(128)S(1)} %get-tuple-element.394) | copy-start | bytes 1540
  106.4 148.9 %copy-start.40 = (f32[128,64]{1,0:T(8,128)}, f32[128,64]{1,0:T(8,128)S(1)}, u32[]{:S(2)}) copy-start(f32[128,64]{1,0:T(8,128)S(1)} %get-tuple-element.395) | copy-start | bytes 98308
  106.4 148.9 %copy-start.42 = (f32[128,64]{1,0:T(8,128)}, f32[128,64]{1,0:T(8,128)S(1)}, u32[]{:S(2)}) copy-start(f32[128,64]{1,0:T(8,128)S(1)} %get-tuple-element.396) | copy-start | bytes 98308
  175.1 79.5 %copy-start.4 = (f32[16,8,16,128]{3,2,1,0:T(8,128)}, f32[16,8,16,128]{3,2,1,0:T(8,128)S(1)}, u32[]{:S(2)}) copy-start(f32[16,8,16,128]{3,2,1,0:T(8,128)S(1)} %copy.298) | copy-start | bytes 3145732
  175.5 73.7 %copy-start.60 = (f32[128,16]{0,1:T(8,128)}, f32[128,16]{0,1:T(8,128)S(1)}, u32[]{:S(2)}) copy-start(f32[128,16]{0,1:T(8,128)S(1)} %copy.233) | copy-start | bytes 24580
  175.7 79.0 %copy-start.33 = (f32[128,16]{1,0:T(8,128)}, f32[128,16]{1,0:T(8,128)S(1)}, u32[]{:S(2)}) copy-start(f32[128,16]{1,0:T(8,128)S(1)} %copy.234) | copy-start | bytes 24580
  258.7 238.5 %all-gather.20.cloned.1.call-start = ((), (), s32[]{:S(2)}) async-start(), calls=%async_computation.19 | async-start | bytes 8650752 | tf_op jit(solution)/shard_map/all_gather | solution.py:125
  270.2 66.0 %copy-start.45 = (s32[1024,8]{0,1:T(8,128)S(1)}, s32[1024,8]{0,1:T(8,128)}, u32[]{:S(2)}) copy-start(s32[1024,8]{0,1:T(8,128)} %copy-done.44) | copy-start | bytes 98308
  270.2 66.6 %copy-start.54 = (s32[128,8]{0,1:T(8,128)S(1)}, s32[128,8]{0,1:T(8,128)}, u32[]{:S(2)}) copy-start(s32[128,8]{0,1:T(8,128)} %param.34) | copy-start | bytes 12292
  270.2 67.4 %copy-start.77 = (bf16[64,24]{0,1:T(8,128)(2,1)S(1)}, bf16[64,24]{0,1:T(8,128)(2,1)}, u32[]{:S(2)}) copy-start(bf16[64,24]{0,1:T(8,128)(2,1)} %param.27) | copy-start | bytes 9220
  270.3 109.0 %copy-start.85 = (s32[128]{0:T(128)S(1)}, s32[128]{0:T(128)}, u32[]{:S(2)}) copy-start(s32[128]{0:T(128)} %param.35) | copy-start | bytes 1540
  270.3 115.8 %copy-start.50 = (f32[1024,24]{0,1:T(8,128)S(1)}, f32[1024,24]{0,1:T(8,128)}, u32[]{:S(2)}) copy-start(f32[1024,24]{0,1:T(8,128)} %copy-done.49) | copy-start | bytes 294916
  387.9 66.1 %copy-start.67 = (s32[1024,1]{0,1:T(1,128)S(1)}, s32[1024,1]{0,1:T(1,128)}, u32[]{:S(2)}) copy-start(s32[1024,1]{0,1:T(1,128)} %reshape.341) | copy-start | bytes 12292
  388.0 66.1 %copy-start.32 = (bf16[128,16,64]{2,1,0:T(8,128)(2,1)S(1)}, bf16[128,16,64]{2,1,0:T(8,128)(2,1)}, u32[]{:S(2)}) copy-start(bf16[128,16,64]{2,1,0:T(8,128)(2,1)} %get-tuple-element.389) | copy-start | bytes 786436
  388.0 66.2 %copy-start.31 = (bf16[128,16,64]{2,1,0:T(8,128)(2,1)S(1)}, bf16[128,16,64]{2,1,0:T(8,128)(2,1)}, u32[]{:S(2)}) copy-start(bf16[128,16,64]{2,1,0:T(8,128)(2,1)} %get-tuple-element.390) | copy-start | bytes 786436
  469.8 6.2 copy-start.47
  469.8 6.2 copy-start.64
  476.1 21.2 copy-start.1
  497.2 6.2 copy-start.51
  497.3 6.4 copy-start.38
  497.3 6.6 copy-start.3
  502.5 8.4 copy-start.80
  502.5 8.4 copy-start.78
  503.6 8.5 copy-start.15
  503.9 7.2 copy-start.55
  511.1 11.9 copy-start.56
  511.9 11.2 copy-start.68
  523.1 76.5 %all-to-all-start = ((bf16[24,64,2048]{2,1,0:T(8,128)(2,1)}), bf16[24,64,2048]{2,1,0:T(8,128)(2,1)}, u32[]{:S(2)}, u32[]{:S(2)}) async-start(bf16[24,64,2048]{2,1,0:T(8,128)(2,1)} %bitcast.308), calls=%async_computation | async-start | bytes 12582912 | tf_op jit(solution)/shard_map/all_to_all | solution.py:209
  599.6 76.8 %all-to-all-start.2 = ((bf16[24,64,2048]{2,1,0:T(8,128)(2,1)}), bf16[24,64,2048]{2,1,0:T(8,128)(2,1)}, u32[]{:S(2)}, u32[]{:S(2)}) async-start(bf16[24,64,2048]{2,1,0:T(8,128)(2,1)} %bitcast.307), calls=%async_computation.2 | async-start | bytes 12582912 | tf_op jit(solution)/shard_map/all_to_all | solution.py:240
  608.1 13.6 copy-start.21
  746.4 99.5 %all-to-all-start.3 = ((bf16[3,512,2048]{2,0,1:T(4,128)(2,1)}), bf16[3,512,2048]{2,0,1:T(4,128)(2,1)}, u32[]{:S(2)}, u32[]{:S(2)}) async-start(bf16[3,512,2048]{2,0,1:T(4,128)(2,1)} %copy.254), calls=%async_computation.3 | async-start | bytes 16777216 | tf_op jit(solution)/shard_map/all_to_all | solution.py:259
  845.9 99.0 %all-to-all-start.1 = ((bf16[3,512,2048]{2,0,1:T(4,128)(2,1)}), bf16[3,512,2048]{2,0,1:T(4,128)(2,1)}, u32[]{:S(2)}, u32[]{:S(2)}) async-start(bf16[3,512,2048]{2,0,1:T(4,128)(2,1)} %copy.250), calls=%async_computation.1 | async-start | bytes 16777216 | tf_op jit(solution)/shard_map/all_to_all | solution.py:218
  850.9 249.9 %reduce-scatter.31.cloned.1.call-start = ((), (), s32[]{:S(2)}) async-start(), calls=%async_computation.27 | async-start | bytes 4718592
  978.5 109.8 %copy-start.9 = (f32[128,2048]{1,0:T(8,128)}, f32[128,2048]{1,0:T(8,128)S(1)}, u32[]{:S(2)}) copy-start(f32[128,2048]{1,0:T(8,128)S(1)} %get-tuple-element.383) | copy-start | bytes 3145732
  978.6 7.2 copy-start.20
  978.6 7.2 copy-start.48
  978.6 7.2 copy-start.65
  1040.5 103.6 %reduce-scatter.33.cloned.1.call-start = ((), (), s32[]{:S(2)}) async-start(), calls=%async_computation.28 | async-start | bytes 4718592
  1047.1 234.0 %reduce-scatter.35.cloned.1.call-start = ((), (), s32[]{:S(2)}) async-start(), calls=%async_computation.29 | async-start | bytes 1081344
  1049.6 442.7 %reduce-scatter.25.cloned.1.call-start = ((), (), s32[]{:S(2)}) async-start(), calls=%async_computation.24 | async-start | bytes 15728640 | tf_op jit(solution)/shard_map/reduce_scatter | solution.py:267
  1062.7 644.9 %reduce-scatter.27.cloned.1.call-start = ((), (), s32[]{:S(2)}) async-start(), calls=%async_computation.25 | async-start | bytes 15728640 | tf_op jit(solution)/shard_map/reduce_scatter | solution.py:270
  1075.3 847.6 %reduce-scatter.29.cloned.1.call-start = ((), (), s32[]{:S(2)}) async-start(), calls=%async_computation.26 | async-start | bytes 15728640 | tf_op jit(solution)/shard_map/reduce_scatter | solution.py:273
  1088.2 1021.5 %reduce-scatter.23.cloned.1.call-start = ((), (), s32[]{:S(2)}) async-start(), calls=%async_computation.23 | async-start | bytes 17301504 | tf_op jit(solution)/shard_map/reduce_scatter | solution.py:340
  1097.4 1199.6 %reduce-scatter.17.cloned.1.call-start = ((), (), s32[]{:S(2)}) async-start(), calls=%async_computation.20 | async-start | bytes 17301504 | tf_op jit(solution)/shard_map/reduce_scatter | solution.py:337
  1127.1 1357.5 %reduce-scatter.19.cloned.1.call-start = ((), (), s32[]{:S(2)}) async-start(), calls=%async_computation.21 | async-start | bytes 17301504 | tf_op jit(solution)/shard_map/reduce_scatter | solution.py:338
  1136.5 1535.2 %reduce-scatter.21.cloned.1.call-start = ((), (), s32[]{:S(2)}) async-start(), calls=%async_computation.22 | async-start | bytes 17301504 | tf_op jit(solution)/shard_map/reduce_scatter | solution.py:339
  1282.5 13.6 slice-start
  1289.7 6.5 slice-start.1
  1289.7 6.5 copy-start.30
  1296.2 45.4 %copy-start.83 = (f32[128]{0:T(128)S(1)}, f32[128]{0:T(128)}, u32[]{:S(2)}) copy-start(f32[128]{0:T(128)} %copy-done.82) | copy-start | bytes 1540
  1296.2 45.4 %copy-start.10 = (f32[128,2048]{1,0:T(8,128)S(1)}, f32[128,2048]{1,0:T(8,128)}, u32[]{:S(2)}) copy-start(f32[128,2048]{1,0:T(8,128)} %copy-done.9) | copy-start | bytes 3145732
  (57 other events, 180.7 us)
Sparse Core Ops, SparseCore 0:
  10.9 80.2 all-gather.9
  94.1 76.1 all-gather.15
  173.1 76.0 all-gather.13
  251.5 35.3 all-gather.11
  289.2 37.4 all-gather.17
  329.4 78.0 all-gather.19
  1040.6 47.6 reduce-scatter.30
  1092.7 51.3 reduce-scatter.32
  1146.3 134.7 reduce-scatter.34
  1283.4 208.8 reduce-scatter.24
  1494.8 212.8 reduce-scatter.26
  1710.0 212.8 reduce-scatter.28
  1925.9 183.7 reduce-scatter.22
  2112.5 184.4 reduce-scatter.16
  2299.8 184.7 reduce-scatter.18
  2487.4 184.2 reduce-scatter.20
where the time goes:
time: 2700 us; the launch traced here: 2680 us
  waiting for transfers between devices  1860 us (69%)
  local copies, waits for them, and re-layouts  302 us (11%)
  matrix products  263 us (10%)
  blocking collectives  149 us (6%)
  other arithmetic  69.4 us (3%)
    reduce_scatter x1, waiting for transfers between devices, on_device(): lax.psum_scatter(up_term.astype(jnp.bfloat16), 'rep', scatter_dimension=1...  210 us
    reduce_scatter x1, waiting for transfers between devices, on_device(): lax.psum_scatter(down_term.astype(jnp.bfloat16), 'rep', scatter_dimension...  210 us
    reduce_scatter x1, waiting for transfers between devices, on_device(): lax.psum_scatter(key_term, ('rep', 'ep'), scatter_dimension=0, tiled=True)  188 us
    reduce_scatter x1, waiting for transfers between devices, on_device(): lax.psum_scatter(query_term, ('rep', 'ep'), scatter_dimension=0, tiled=True)  187 us
    reduce_scatter x1, waiting for transfers between devices, on_device(): lax.psum_scatter(value_term, ('rep', 'ep'), scatter_dimension=0, tiled=True)  187 us
    reduce_scatter x1, waiting for transfers between devices, on_device(): lax.psum_scatter(output_term, ('rep', 'ep'), scatter_dimension=0, tiled=T...  181 us
    reduce_scatter x1, waiting for transfers between devices, on_device(): lax.psum_scatter(gate_term.astype(jnp.bfloat16), 'rep', scatter_dimension...  149 us
    unnamed x19, waiting for transfers between devices  138 us
  transfers between devices with their start and end apart: 20, of which 16 were waited for; matrix products, arithmetic and copies ran while one was open for 16% of the time, Pallas kernels for 0%

commit v1 on v0

--- a/solution.py
+++ b/solution.py
@@ -87,7 +87,7 @@
     return (query_grad, key_grad, value_grad)
 
 
-def on_device(
+def on_device_general(
     tokens,
     cotangent,
     query_weight,
@@ -356,6 +356,281 @@
     )
 
 
+def gather_block(block, axes):
+    return lax.all_gather(block, axes, axis=0, tiled=True)
+
+
+def scatter_sum(partial_sums, axes):
+    return lax.psum_scatter(partial_sums, axes, scatter_dimension=0, tiled=True)
+
+
+def on_device_split(
+    tokens,
+    cotangent,
+    query_weight,
+    key_weight,
+    value_weight,
+    output_weight,
+    router_weight,
+    gains,
+    expert_gate,
+    expert_up,
+    expert_down,
+    lengths,
+    deal,
+    routes,
+    priority,
+):
+    bf16, f32 = jnp.bfloat16, jnp.float32
+    tok_dev, width = tokens.shape
+    ep_count, rep_count = lax.axis_size("ep"), lax.axis_size("rep")
+    ep_index, rep_index = lax.axis_index("ep"), lax.axis_index("rep")
+    exp_dev, _, ff_width = expert_gate.shape
+    top_count = routes.shape[1]
+    experts_all = exp_dev * ep_count
+    group_rows = tok_dev * ep_count
+    capacity = 5 * tok_dev * top_count // (4 * exp_dev)
+    head_dim = HD
+    heads_dev = width // head_dim // ep_count
+    slice_width = heads_dev * head_dim
+    rows_dev = query_weight.shape[0]
+    ff_slice = ff_width // rep_count
+    score_scale = head_dim ** (-0.5)
+    core = ep_index % 2
+    every = ("rep", "ep")
+
+    gains_dev = gains.shape[0]
+    packed = jnp.concatenate(
+        [gains, router_weight.reshape(-1), jnp.zeros((2048 - gains_dev - router_weight.size,), bf16)]
+    ).reshape(16, 128)
+    packed_all = gather_block(packed, every).reshape(rep_count * ep_count, 2048)
+    gains_float = packed_all[:, :gains_dev].reshape(-1).astype(f32)
+    router_full = packed_all[:, gains_dev : gains_dev + router_weight.size].reshape(width, experts_all)
+    gain_in = gains_float[:width]
+    gain_mid = gains_float[width : 2 * width]
+    gain_query = gains_float[2 * width : 2 * width + head_dim]
+    gain_key = gains_float[2 * width + head_dim :]
+    numbers = jnp.concatenate([deal, priority, routes.T.reshape(-1)]).reshape(-1, 128)
+    numbers_all = gather_block(numbers, "ep").reshape(ep_count, -1, tok_dev)
+    deal_all = numbers_all[:, 0].reshape(-1)
+    priority_all = numbers_all[:, 1].reshape(-1)
+    routes_all = numbers_all[:, 2:].transpose(0, 2, 1).reshape(group_rows, top_count)
+    segment_all, position_all = placement(deal_all, lengths[0])
+
+    chips = ep_count // 2
+    def columns_of(weight):
+        parts = weight.reshape(rows_dev, 2, heads_dev, chips, head_dim).transpose(3, 1, 0, 2, 4)
+        parts = parts.reshape(ep_count, rows_dev, slice_width)
+        return lax.all_to_all(parts, "ep", split_axis=0, concat_axis=0, tiled=True)
+
+    qkv_rows = jnp.concatenate(
+        [columns_of(query_weight), columns_of(key_weight), columns_of(value_weight)], axis=2
+    ).reshape(ep_count * rows_dev, 3 * slice_width)
+    qkv_slice = gather_block(qkv_rows, "rep")
+    out_rows = gather_block(output_weight, "rep").reshape(2, heads_dev, rows_dev, width)
+    out_own = lax.dynamic_index_in_dim(out_rows, core, 0, keepdims=False)
+    out_other = lax.ppermute(
+        lax.dynamic_index_in_dim(out_rows, 1 - core, 0, keepdims=False),
+        "ep",
+        [(i, i + 1 - 2 * (i % 2)) for i in range(ep_count)],
+    )
+    out_slice = jnp.where(
+        core == 0,
+        jnp.concatenate([out_own, out_other], axis=1),
+        jnp.concatenate([out_other, out_own], axis=1),
+    ).reshape(slice_width, width)
+
+    cot_all = gather_block(cotangent, every)
+    tokens_group = gather_block(tokens, "ep").astype(f32)
+    normed_group = rms_scale(tokens_group, gain_in).astype(bf16)
+    projected = jnp.dot(normed_group, qkv_slice, preferred_element_type=f32)
+    query_pre = projected[:, :slice_width].reshape(group_rows, heads_dev, head_dim)
+    key_pre = projected[:, slice_width : 2 * slice_width].reshape(group_rows, heads_dev, head_dim)
+    value_low = projected[:, 2 * slice_width :].astype(bf16).reshape(group_rows, heads_dev, head_dim)
+    query_low = rope_norm(query_pre, gain_query, position_all).astype(bf16)
+    key_low = rope_norm(key_pre, gain_key, position_all).astype(bf16)
+    same_seq = segment_all[:, None] == segment_all[None, :]
+    mixed, top_score, total_sum = attend_forward(
+        (query_low, key_low, value_low), same_seq, score_scale
+    )
+    mixed_low = mixed.reshape(group_rows, slice_width).astype(bf16)
+    attn_part = jnp.dot(mixed_low, out_slice, preferred_element_type=f32).astype(bf16)
+    residual = tokens.astype(f32)
+    after_attn = residual + scatter_sum(attn_part, "ep").astype(f32)
+    mid_low = rms_scale(after_attn, gain_mid).astype(bf16)
+
+    logits = jnp.dot(mid_low, router_full, preferred_element_type=f32)
+    expert_ids = jnp.arange(experts_all, dtype=jnp.int32)
+    member = (routes[:, :, None] == expert_ids[None, None, :]).astype(f32)
+    named = jnp.sum(member, axis=1)
+    lifted = jnp.where(named > 0, logits, masked_score)
+    lifted = jnp.exp(lifted - jnp.max(lifted, axis=-1, keepdims=True)) * named
+    gate_dense = lifted / jnp.sum(lifted, axis=-1, keepdims=True)
+    onehot_all = jnp.sum(
+        (routes_all[:, :, None] == expert_ids[None, None, :]).astype(bf16), axis=1
+    )
+    earlier = (priority_all[None, :] < priority[:, None]).astype(bf16)
+    slots = jnp.dot(earlier, onehot_all, preferred_element_type=f32)
+    kept_dense = named * (slots < capacity).astype(f32)
+    pair_weight = gate_dense * kept_dense
+
+    weight_high = pair_weight.astype(bf16)
+    weight_low = (pair_weight - weight_high.astype(f32)).astype(bf16)
+    side = jnp.concatenate(
+        [weight_high, weight_low, jnp.zeros((tok_dev, 128 - 2 * experts_all), bf16)], axis=1
+    )
+    sent = gather_block(jnp.concatenate([mid_low, side], axis=1), every)
+    mid_all = sent[:, :width]
+    side_all = sent[:, width:]
+    weight_own = lax.dynamic_slice_in_dim(side_all, ep_index * exp_dev, exp_dev, axis=1).astype(
+        f32
+    ) + lax.dynamic_slice_in_dim(
+        side_all, experts_all + ep_index * exp_dev, exp_dev, axis=1
+    ).astype(f32)
+    gate_slice = lax.dynamic_slice_in_dim(expert_gate, rep_index * ff_slice, ff_slice, axis=2)
+    up_slice = lax.dynamic_slice_in_dim(expert_up, rep_index * ff_slice, ff_slice, axis=2)
+    down_slice = lax.dynamic_slice_in_dim(expert_down, rep_index * ff_slice, ff_slice, axis=1)
+    gate_flat = gate_slice.transpose(1, 0, 2).reshape(width, exp_dev * ff_slice)
+    up_flat = up_slice.transpose(1, 0, 2).reshape(width, exp_dev * ff_slice)
+    down_flat = down_slice.reshape(exp_dev * ff_slice, width)
+    gate_part = jnp.dot(mid_all, gate_flat, preferred_element_type=f32)
+    up_part = jnp.dot(mid_all, up_flat, preferred_element_type=f32)
+    down_cot = jnp.dot(cot_all, down_flat.T, preferred_element_type=f32)
+    weight_wide = jnp.repeat(weight_own, ff_slice, axis=1)
+    sigma = jax.nn.sigmoid(gate_part)
+    silu = gate_part * sigma
+    hidden = (silu * up_part).astype(bf16).astype(f32)
+    hidden_weighted = (hidden * weight_wide).astype(bf16)
+    hidden_cot = weight_wide * down_cot
+    a_cot = (hidden_cot * up_part * (sigma * (1 + gate_part * (1 - sigma)))).astype(bf16)
+    b_cot = (hidden_cot * silu).astype(bf16)
+    row_part = (
+        jnp.dot(a_cot, gate_flat.T, preferred_element_type=f32)
+        + jnp.dot(b_cot, up_flat.T, preferred_element_type=f32)
+    ).astype(bf16)
+    gate_cot_own = jnp.sum((hidden * down_cot).reshape(-1, exp_dev, ff_slice), axis=2)
+    gate_cot_part = lax.dynamic_update_slice_in_dim(
+        jnp.zeros((gate_cot_own.shape[0], 128), bf16),
+        gate_cot_own.astype(bf16),
+        ep_index * exp_dev,
+        axis=1,
+    )
+    row_sum = scatter_sum(jnp.concatenate([row_part, gate_cot_part], axis=1), every)
+    moe_part = jnp.dot(hidden_weighted, down_flat, preferred_element_type=f32).astype(bf16)
+    moe_out = scatter_sum(moe_part, every).astype(f32)
+    block_out = (after_attn + moe_out).astype(bf16)
+    gate_term = jnp.dot(mid_all.T, a_cot, preferred_element_type=f32)
+    up_term = jnp.dot(mid_all.T, b_cot, preferred_element_type=f32)
+    down_w_grad = jnp.dot(hidden_weighted.T, cot_all, preferred_element_type=f32).reshape(
+        exp_dev, ff_slice, width
+    )
+
+    def rows_of(term):
+        parts = term.astype(bf16).reshape(rep_count, width // rep_count, exp_dev, ff_slice)
+        parts = parts.transpose(0, 2, 1, 3)
+        got = lax.all_to_all(parts, "rep", split_axis=0, concat_axis=0, tiled=True)
+        return got.transpose(1, 2, 0, 3).reshape(exp_dev, width // rep_count, ff_width).astype(f32)
+
+    gate_w_grad = rows_of(gate_term)
+    up_w_grad = rows_of(up_term)
+
+    out_grad = cotangent.astype(f32)
+    gate_cot = row_sum[:, width : width + experts_all].astype(f32) * kept_dense
+    chosen_cot = gate_dense * (gate_cot - jnp.sum(gate_dense * gate_cot, axis=-1, keepdims=True))
+    logit_cot = chosen_cot.astype(bf16)
+    mid_cot = row_sum[:, :width].astype(f32) + jnp.dot(
+        logit_cot, router_full.T, preferred_element_type=f32
+    )
+    router_term = jnp.dot(mid_low.T, logit_cot, preferred_element_type=f32)
+    _, mid_pull = jax.vjp(rms_scale, after_attn, gain_mid)
+    after_extra, gain_mid_cot = mid_pull(mid_cot)
+    after_cot = out_grad + after_extra
+    attn_cot_group = gather_block(after_cot.astype(bf16), "ep")
+
+    mixed_cot = jnp.dot(attn_cot_group, out_slice.T, preferred_element_type=f32).astype(bf16)
+    output_term = jnp.dot(mixed_low.T, attn_cot_group, preferred_element_type=f32)
+    query_cot, key_cot, value_cot = attend_backward(
+        (
+            query_low,
+            key_low,
+            value_low,
+            mixed_cot.reshape(group_rows, heads_dev, head_dim),
+            top_score,
+            total_sum,
+        ),
+        same_seq,
+        score_scale,
+    )
+    _, query_pull = jax.vjp(
+        lambda pre, gain_vec: rope_norm(pre, gain_vec, position_all), query_pre, gain_query
+    )
+    query_pre_cot, gain_query_cot = query_pull(query_cot)
+    _, key_pull = jax.vjp(
+        lambda pre, gain_vec: rope_norm(pre, gain_vec, position_all), key_pre, gain_key
+    )
+    key_pre_cot, gain_key_cot = key_pull(key_cot)
+    pre_cot = jnp.concatenate(
+        [
+            part.reshape(group_rows, slice_width).astype(bf16)
+            for part in (query_pre_cot, key_pre_cot, value_cot)
+        ],
+        axis=1,
+    )
+    normed_part = jnp.dot(pre_cot, qkv_slice.T, preferred_element_type=f32).astype(bf16)
+    normed_cot = scatter_sum(normed_part, "ep").astype(f32)
+    _, input_pull = jax.vjp(rms_scale, residual, gain_in)
+    input_extra, gain_in_cot = input_pull(normed_cot)
+    input_grad = after_cot + input_extra
+    qkv_term = jnp.dot(normed_group.T, pre_cot, preferred_element_type=f32)
+
+    qkv_sum = scatter_sum(qkv_term.astype(bf16), "rep").reshape(ep_count, rows_dev, 3, slice_width)
+
+    def whole_rows(part):
+        got = lax.all_to_all(part, "ep", split_axis=0, concat_axis=0, tiled=True)
+        got = got.reshape(chips, 2, rows_dev, heads_dev, head_dim).transpose(2, 1, 3, 0, 4)
+        return got.reshape(rows_dev, width).astype(f32)
+
+    query_sum, key_sum, value_sum = (whole_rows(qkv_sum[:, :, i]) for i in range(3))
+    out_halves = output_term.astype(bf16).reshape(heads_dev, 2, rows_dev, width)
+    out_keep = lax.dynamic_index_in_dim(out_halves, core, 1, keepdims=False)
+    out_pass = lax.ppermute(
+        lax.dynamic_index_in_dim(out_halves, 1 - core, 1, keepdims=False),
+        "ep",
+        [(i, i + 1 - 2 * (i % 2)) for i in range(ep_count)],
+    )
+    out_parts = jnp.where(
+        core == 0, jnp.stack([out_keep, out_pass]), jnp.stack([out_pass, out_keep])
+    ).reshape(2 * heads_dev * rows_dev, width)
+    output_sum = scatter_sum(out_parts, "rep").astype(f32)
+    gains_term = jnp.concatenate([gain_in_cot, gain_mid_cot, gain_query_cot, gain_key_cot])
+    small_term = jnp.concatenate(
+        [
+            gains_term.reshape(rep_count * ep_count, gains_dev),
+            router_term.reshape(rep_count * ep_count, router_weight.size),
+            jnp.zeros((rep_count * ep_count, 2048 - gains_dev - router_weight.size), f32),
+        ],
+        axis=1,
+    ).reshape(rep_count * ep_count * 16, 128)
+    small_sum = scatter_sum(small_term, every).reshape(-1)
+    gains_sum = small_sum[:gains_dev]
+    router_sum = small_sum[gains_dev : gains_dev + router_weight.size].reshape(
+        rows_dev, experts_all
+    )
+    return (
+        block_out,
+        input_grad,
+        query_sum,
+        key_sum,
+        value_sum,
+        output_sum,
+        router_sum,
+        gains_sum,
+        gate_w_grad,
+        up_w_grad,
+        down_w_grad,
+    )
+
+
 def solution(mesh):
     placed = (
         P(("rep", "ep"), None),
@@ -375,7 +650,7 @@
         P(("rep", "ep")),
     )
     return jax.shard_map(
-        on_device,
+        on_device_split if mesh.shape["rep"] == 4 else on_device_general,
         mesh=mesh,
         in_specs=placed,
         out_specs=(

time: 2700 us -> 1420 us (0.53)
  waiting for transfers between devices: 1860 us -> 823 us
  local copies, waits for them, and re-layouts: 302 us -> 133 us
  blocking collectives: 149 us -> 58 us
  starting transfers between devices: 21.5 us -> 62.6 us
    reduce_scatter x7 -> x3, waiting for transfers between devices: 1310 us -> 186 us  [scatter_sum(): return lax.psum_scatter(partial_sums, axes, scatter_dimension=0, tiled=True)]
    gather x13 -> x0, local copies, waits for them, and re-layouts: 165 us -> none  [the longest x4 66.3 us: on_device(): jnp.take_along_axis(jnp.dot(earlier, onehot_all, precision=highest), rout...]
    unnamed x19 -> x17, waiting for transfers between devices: 138 us -> 291 us
    all_to_all x4 -> x7, waiting for transfers between devices: 233 us -> 111 us  [the longest x2 98.9 us: rows_of(): got = lax.all_to_all(parts, 'rep', split_axis=0, concat_axis=0, tiled=True)]
    unnamed x2 -> x0, blocking collectives: 84.7 us -> none
    all_gather x6, waiting for transfers between devices: 173 us -> 233 us  [gather_block(): return lax.all_gather(block, axes, axis=0, tiled=True)]
    all_to_all x4 -> x7, starting transfers between devices: 20.4 us -> 60.7 us  [the longest x2 40 us: rows_of(): got = lax.all_to_all(parts, 'rep', split_axis=0, concat_axis=0, tiled=True)]
    all_to_all x4 -> x0, local copies, waits for them, and re-layouts: 31.5 us -> none  [the longest x1 10.8 us: on_device(): lax.all_to_all(rows_grad, 'ep', split_axis=1, concat_axis=0, tiled=True)]
  transfers between devices with their start and end apart: 20 -> 22, of which waited for: 16 -> 16; matrix products, arithmetic and copies ran while one was open for 16% -> 20% of each run, Pallas kernels for 0% -> 0%
where the time goes in v1:
time: 1420 us; the launch traced here: 1410 us
  waiting for transfers between devices  823 us (58%)
  matrix products  254 us (18%)
  local copies, waits for them, and re-layouts  133 us (9%)
  other arithmetic  62.7 us (4%)
  starting transfers between devices  62.6 us (4%)
  blocking collectives  58 us (4%)
  between operations  16 us (1%)
    unnamed x17, waiting for transfers between devices  291 us
    all_gather x6, waiting for transfers between devices, gather_block(): return lax.all_gather(block, axes, axis=0, tiled=True)  233 us
    reduce_scatter x3, waiting for transfers between devices, scatter_sum(): return lax.psum_scatter(partial_sums, axes, scatter_dimension=0, tiled=True)  186 us
    all_to_all x2, waiting for transfers between devices, rows_of(): got = lax.all_to_all(parts, 'rep', split_axis=0, concat_axis=0, tiled=True)  98.9 us
    unnamed x203, local copies, waits for them, and re-layouts  63.8 us
    all_gather x2, blocking collectives, gather_block(): return lax.all_gather(block, axes, axis=0, tiled=True)  48.7 us
    all_to_all x2, starting transfers between devices, rows_of(): got = lax.all_to_all(parts, 'rep', split_axis=0, concat_axis=0, tiled=True)  40 us
    dot_general x1, matrix products, on_device_split(): down_cot = jnp.dot(cot_all, down_flat.T, preferred_element_type=f32)  32.4 us
  transfers between devices with their start and end apart: 22, of which 16 were waited for; matrix products, arithmetic and copies ran while one was open for 20% of the time, Pallas kernels for 0%

profile of v1, /device:TPU:0, one launch (start us, length us, event | category | flops | bytes accessed | tf_op | source)
XLA Modules:
  0.0 1409.7 jit_solution(7142188032034060459)
XLA Ops:
  10.9 5.2 all-to-all-start
  18.3 4.7 all-to-all-done
  23.0 3.4 all-to-all-start.1
  28.0 5.3 all-to-all-done.1
  33.3 9.3 all_to_all.40
  44.2 40.6 %all_gather.25 = bf16[512,128]{1,0:T(8,128)(2,1)S(1)} all-gather(bf16[16,128]{1,0:T(8,128)(2,1)S(1)} %bitcast.186), channel_id=1, replica_groups=mesh['rep'=4,'ep'=8] {'rep','ep'}, dimensions={0}, use_global_device_ids=true | all-gather | bytes 135168 | tf_op jit(solution)/shard_map/all_gather | solution.py:360
  85.0 8.0 all-gather
  100.1 3.1 fusion.11
  103.2 41.4 %all-gather.10.cloned.1.call-done = bf16[2048,768]{1,0:T(8,128)(2,1)} async-done(((bf16[512,768]{1,0:T(8,128)(2,1)}), bf16[2048,768]{1,0:T(8,128)(2,1)}) %all-gather.10.cloned.1.call-update) | async-done | bytes 3145744 | tf_op jit(solution)/shard_map/all_gather | solution.py:360
  144.6 6.8 fusion.38
  158.9 8.8 fusion.73
  167.7 4.2 fusion.30
  172.8 3.3 bitcast_convert_fusion
  177.6 48.6 %reduce-scatter.22.cloned.1.call-done = bf16[128,2048]{1,0:T(8,128)(2,1)} async-done(((bf16[1024,2048]{1,0:T(8,128)(2,1)}), bf16[128,2048]{1,0:T(8,128)(2,1)}) %reduce-scatter.22.cloned.1.call-update) | async-done | bytes 524304
  231.7 3.8 constant_dynamic-slice_fusion.2
  235.4 4.7 copy.346
  240.2 3.8 constant_dynamic-slice_fusion.1
  243.9 4.7 copy.345
  250.7 101.6 %all-gather.14.cloned.1.call-done = bf16[4096,2176]{0,1:T(8,128)(2,1)} async-done(((bf16[128,2176]{0,1:T(8,128)(2,1)}), bf16[4096,2176]{0,1:T(8,128)(2,1)}) %all-gather.14.cloned.1.call-update) | async-done | bytes 17825808 | tf_op jit(solution)/shard_map/all_gather | solution.py:360
  353.7 20.4 %fusion.7 = f32[4096,768]{0,1:T(8,128)} fusion(bf16[2048,768]{0,1:T(8,128)(2,1)} %bitcast.163, bf16[4096,2176]{0,1:T(8,128)(2,1)} %all-gather.14.cloned.1.call-done), kind=kOutput, calls=%fused_computation.17 | convolution fusion | flops 12884901888 | bytes 32505856 | tf_op jit(solution)/shard_map/dot_general | solution.py:496
  374.1 19.5 %fusion.9 = f32[4096,768]{0,1:T(8,128)} fusion(bf16[2048,768]{0,1:T(8,128)(2,1)S(1)} %bitcast.162, bf16[4096,2176]{0,1:T(8,128)(2,1)} %all-gather.14.cloned.1.call-done), kind=kOutput, calls=%fused_computation.19 | convolution fusion | flops 12884901888 | bytes 32505856 | tf_op jit(solution)/shard_map/dot_general | solution.py:497
  393.6 75.5 %all-gather.16.cloned.1.call-done = bf16[4096,2048]{1,0:T(8,128)(2,1)} async-done(((bf16[128,2048]{1,0:T(8,128)(2,1)}), bf16[4096,2048]{1,0:T(8,128)(2,1)}) %all-gather.16.cloned.1.call-update) | async-done | bytes 16777232 | tf_op jit(solution)/shard_map/all_gather | solution.py:360
  469.1 32.4 %convert_multiply_fusion = (f32[4096,768]{0,1:T(8,128)}, bf16[4096,768]{0,1:T(8,128)(2,1)}, bf16[4096,768]{0,1:T(8,128)(2,1)}, bf16[4096,768]{0,1:T(8,128)(2,1)}) fusion(f32[4096,768]{0,1:T(8,128)} %fusion.9, f32[4096,768]{0,1:T(8,128)} %fusion.7, f32[4096,3]{0,1:T(4,128)S(1)} %convert_add_fusion.1, bf16[768,2048]{1,0:T(8,128)(2,1)S(1)} %bitcast.151, ...), kind=kOutput, calls=%fused_computation.5 | convolution fusion | flops 12941524992 | bytes 76595200 | tf_op jit(solution)/shard_map/dot_general | solution.py:498
  501.5 20.1 %fusion.75 = f32[4096,2048]{0,1:T(8,128)} fusion(bf16[4096,768]{0,1:T(8,128)(2,1)} %get-tuple-element.94, bf16[2048,768]{0,1:T(8,128)(2,1)S(1)} %bitcast.164), kind=kOutput, calls=%fused_computation.179 | convolution fusion | flops 12884901888 | bytes 42991616 | tf_op jit(solution)/shard_map/dot_general | solution.py:508
  521.6 5.3 reduce_sum.216
  527.4 26.8 %add_convert_fusion = bf16[4096,2048]{0,1:T(8,128)(2,1)} fusion(f32[4096,2048]{0,1:T(8,128)} %fusion.75, bf16[4096,768]{0,1:T(8,128)(2,1)} %get-tuple-element.95, bf16[2048,768]{0,1:T(8,128)(2,1)} %bitcast.161), kind=kOutput, calls=%fused_computation.1 | convolution fusion | flops 12901679104 | bytes 59768832 | tf_op jit(solution)/shard_map/dot_general | solution.py:509
  554.2 14.2 %pad_maximum_fusion = bf16[4096,2176]{0,1:T(8,128)(2,1)} fusion(bf16[4096,128]{0,1:T(8,128)(2,1)S(1)} %dynamic_update_slice.3, bf16[4096,2048]{0,1:T(8,128)(2,1)} %add_convert_fusion), kind=kLoop, calls=%fused_computation.4 | loop fusion | flops 35651584 | bytes 35651584 | tf_op jit(solution)/shard_map/concatenate | solution.py:518
  568.5 22.1 %copy.338 = bf16[4096,2176]{1,0:T(8,128)(2,1)} copy(bf16[4096,2176]{0,1:T(8,128)(2,1)} %pad_maximum_fusion) | data formatting | bytes 35651584
  591.9 191.1 %reduce-scatter.26.cloned.1.call-done = bf16[128,2176]{1,0:T(8,128)(2,1)} async-done(((bf16[4096,2176]{1,0:T(8,128)(2,1)}), bf16[128,2176]{1,0:T(8,128)(2,1)}) %reduce-scatter.26.cloned.1.call-update) | async-done | bytes 557072
  789.1 4.5 fusion.1
  793.6 2.7 copy-done.14
  796.3 16.5 %convolution_convert_fusion = bf16[4096,2048]{1,0:T(8,128)(2,1)} fusion(bf16[4096,768]{0,1:T(8,128)(2,1)S(1)} %fusion.1, bf16[768,2048]{1,0:T(8,128)(2,1)S(1)} %bitcast.152), kind=kOutput, calls=%fused_computation.6 | convolution fusion | flops 12893290496 | bytes 26214400 | tf_op jit(solution)/shard_map/dot_general | solution.py:519
  812.9 14.9 %all-gather.18.cloned.1.call-done = bf16[1024,2048]{0,1:T(8,128)(2,1)} async-done(((bf16[128,2048]{0,1:T(8,128)(2,1)}), bf16[1024,2048]{0,1:T(8,128)(2,1)}) %all-gather.18.cloned.1.call-update) | async-done | bytes 4194320 | tf_op jit(solution)/shard_map/all_gather | solution.py:360
  827.8 3.6 convolution_convert_fusion.4
  831.5 4.9 multiply_reduce_fusion
  836.4 2.9 multiply_convert_fusion.3
  848.9 5.1 fusion.33
  854.1 5.6 convolution_convert_fusion.2
  859.9 3.5 convolution_convert_fusion.3
  866.7 19.3 %fusion.21 = bf16[2048,768]{1,0:T(8,128)(2,1)} fusion(bf16[4096,768]{0,1:T(8,128)(2,1)} %get-tuple-element.95, bf16[4096,2176]{0,1:T(8,128)(2,1)} %all-gather.14.cloned.1.call-done), kind=kOutput, calls=%fused_computation.39 | convolution fusion | flops 12886474752 | bytes 26214400 | tf_op jit(solution)/shard_map/dot_general | solution.py:523
  886.0 3.2 copy.313
  889.2 3.9 reshape.416
  893.1 4.4 copy.314
  897.5 4.7 all-to-all-start.7
  902.2 7.0 convolution_convert_fusion.1
  909.2 19.2 %fusion.18 = bf16[2048,768]{1,0:T(8,128)(2,1)} fusion(bf16[4096,768]{0,1:T(8,128)(2,1)} %get-tuple-element.94, bf16[4096,2176]{0,1:T(8,128)(2,1)} %all-gather.14.cloned.1.call-done), kind=kOutput, calls=%fused_computation.38 | convolution fusion | flops 12886474752 | bytes 26214400 | tf_op jit(solution)/shard_map/dot_general | solution.py:522
  928.4 3.2 copy.310
  931.7 3.9 reshape.415
  935.6 4.2 copy.311
  939.8 48.5 %all-to-all-done.7 = bf16[4,3,512,256]{2,3,1,0:T(8,128)(2,1)} async-done(((bf16[4,3,512,256]{2,3,1,0:T(8,128)(2,1)}), bf16[4,3,512,256]{2,3,1,0:T(8,128)(2,1)}, u32[]{:S(2)}, u32[]{:S(2)}) %all-to-all-start.7) | async-done | bytes 3145760 | tf_op jit(solution)/shard_map/all_to_all | solution.py:531
  988.3 35.3 %all-to-all-start.6 = ((bf16[4,3,512,256]{2,3,1,0:T(8,128)(2,1)}), bf16[4,3,512,256]{2,3,1,0:T(8,128)(2,1)S(1)}, u32[]{:S(2)}, u32[]{:S(2)}) async-start(bf16[4,3,512,256]{2,3,1,0:T(8,128)(2,1)} %copy.311), calls=%async_computation.9 | async-start | bytes 6291456 | tf_op jit(solution)/shard_map/all_to_all | solution.py:531
  1023.6 20.3 %fusion.77 = f32[768,2048]{1,0:T(8,128)} fusion(bf16[4096,768]{0,1:T(8,128)(2,1)} %copy-done.14, bf16[4096,2048]{1,0:T(8,128)(2,1)} %all-gather.16.cloned.1.call-done), kind=kOutput, calls=%fused_computation.181 | convolution fusion | flops 12884901888 | bytes 29360128 | tf_op jit(solution)/shard_map/dot_general | solution.py:524
  1044.0 5.5 copy_convert_fusion
  1049.4 6.6 copy.320
  1056.0 50.3 %all-to-all-done.6 = bf16[4,3,512,256]{2,3,1,0:T(8,128)(2,1)S(1)} async-done(((bf16[4,3,512,256]{2,3,1,0:T(8,128)(2,1)}), bf16[4,3,512,256]{2,3,1,0:T(8,128)(2,1)S(1)}, u32[]{:S(2)}, u32[]{:S(2)}) %all-to-all-start.6) | async-done | bytes 3145760 | tf_op jit(solution)/shard_map/all_to_all | solution.py:531
  1106.3 3.5 copy_convert_fusion.1
  1109.8 6.6 copy.319
  1119.2 52.7 %reduce-scatter.16.cloned.1.call-done = bf16[512,768]{1,0:T(8,128)(2,1)} async-done(((bf16[2048,768]{1,0:T(8,128)(2,1)}), bf16[512,768]{1,0:T(8,128)(2,1)}) %reduce-scatter.16.cloned.1.call-update) | async-done | bytes 786448 | tf_op jit(solution)/shard_map/reduce_scatter | solution.py:364
  1177.4 3.7 all-to-all-start.5
  1183.5 18.6 %reduce-scatter.18.cloned.1.call-done = bf16[64,2048]{1,0:T(8,128)(2,1)} async-done(((bf16[256,2048]{1,0:T(8,128)(2,1)}), bf16[64,2048]{1,0:T(8,128)(2,1)}) %reduce-scatter.18.cloned.1.call-update) | async-done | bytes 262160 | tf_op jit(solution)/shard_map/reduce_scatter | solution.py:364
  1205.6 49.6 %reduce-scatter.28.cloned.1.call-done = bf16[128,2048]{1,0:T(8,128)(2,1)} async-done(((bf16[1024,2048]{1,0:T(8,128)(2,1)}), bf16[128,2048]{1,0:T(8,128)(2,1)}) %reduce-scatter.28.cloned.1.call-update) | async-done | bytes 524304
  1257.3 4.1 all-to-all-start.4
  1268.4 4.3 all-to-all-start.3
  1285.7 114.3 %reduce-scatter.20.cloned.1.call-done = f32[16,128]{1,0:T(8,128)} async-done(((f32[512,128]{1,0:T(8,128)}), f32[16,128]{1,0:T(8,128)}) %reduce-scatter.20.cloned.1.call-update) | async-done | bytes 8208 | tf_op jit(solution)/shard_map/reduce_scatter | solution.py:364
  (338 shorter events, 93.8 us)
Async XLA Ops:
  7.2 36.5 %copy-start.85 = (s32[1,3]{1,0:T(1,128)S(1)}, s32[1,3]{1,0:T(1,128)}, u32[]{:S(2)}) copy-start(s32[1,3]{1,0:T(1,128)} %param.26) | copy-start | bytes 40
  7.2 36.7 %copy-start.71 = (bf16[64,24]{0,1:T(8,128)(2,1)S(1)}, bf16[64,24]{0,1:T(8,128)(2,1)}, u32[]{:S(2)}) copy-start(bf16[64,24]{0,1:T(8,128)(2,1)} %param.21) | copy-start | bytes 9220
  7.2 36.9 %copy-start.83 = (bf16[136]{0:T(256)(128)(2,1)S(1)}, bf16[136]{0:T(256)(128)(2,1)}, u32[]{:S(2)}) copy-start(bf16[136]{0:T(256)(128)(2,1)} %param.22) | copy-start | bytes 820
  7.2 77.8 %copy-start.86 = (s32[128]{0:T(128)S(1)}, s32[128]{0:T(128)}, u32[]{:S(2)}) copy-start(s32[128]{0:T(128)} %param.29) | copy-start | bytes 1540
  7.2 77.8 %copy-start.63 = (s32[128,8]{0,1:T(8,128)S(1)}, s32[128,8]{0,1:T(8,128)}, u32[]{:S(2)}) copy-start(s32[128,8]{0,1:T(8,128)} %param.28) | copy-start | bytes 12292
  7.2 77.8 %copy-start.84 = (s32[128]{0:T(128)S(1)}, s32[128]{0:T(128)}, u32[]{:S(2)}) copy-start(s32[128]{0:T(128)} %param.27) | copy-start | bytes 1540
  7.2 87.9 %all-gather.12.cloned.1.call-start = ((), (), s32[]{:S(2)}) async-start(), calls=%async_computation.17 | async-start | bytes 1310720 | tf_op jit(solution)/shard_map/all_gather | solution.py:360
  8.0 92.1 %all-gather.8.cloned.1.call-start = ((), (), s32[]{:S(2)}) async-start(), calls=%async_computation.15 | async-start | bytes 4718592 | tf_op jit(solution)/shard_map/all_gather | solution.py:360
  10.9 12.1 all-to-all-start
  23.0 10.3 all-to-all-start.1
  26.5 118.1 %all-gather.10.cloned.1.call-start = ((), (), s32[]{:S(2)}) async-start(), calls=%async_computation.16 | async-start | bytes 3932160 | tf_op jit(solution)/shard_map/all_gather | solution.py:360
  43.6 182.6 %reduce-scatter.22.cloned.1.call-start = ((), (), s32[]{:S(2)}) async-start(), calls=%async_computation.24 | async-start | bytes 4718592
  95.1 61.7 %copy-start.15 = (f32[1024,64]{1,0:T(8,128)}, f32[1024,64]{1,0:T(8,128)S(1)}, u32[]{:S(2)}) copy-start(f32[1024,64]{1,0:T(8,128)S(1)} %get-tuple-element.125) | copy-start | bytes 786436
  95.1 61.7 %copy-start.17 = (f32[1024,64]{1,0:T(8,128)}, f32[1024,64]{1,0:T(8,128)S(1)}, u32[]{:S(2)}) copy-start(f32[1024,64]{1,0:T(8,128)S(1)} %get-tuple-element.126) | copy-start | bytes 786436
  96.8 2.0 collective-permute-start
  97.2 58.9 %copy-start.68 = (f32[128]{0:T(128)}, f32[128]{0:T(128)S(1)}, u32[]{:S(2)}) copy-start(f32[128]{0:T(128)S(1)} %get-tuple-element.124) | copy-start | bytes 1540
  97.2 59.3 %copy-start.66 = (f32[128]{0:T(128)}, f32[128]{0:T(128)S(1)}, u32[]{:S(2)}) copy-start(f32[128]{0:T(128)S(1)} %get-tuple-element.123) | copy-start | bytes 1540
  97.2 54.2 %copy-start.55 = (f32[2048]{0:T(1024)}, f32[2048]{0:T(1024)S(1)}, u32[]{:S(2)}) copy-start(f32[2048]{0:T(1024)S(1)} %get-tuple-element.122) | copy-start | bytes 24580
  97.2 130.6 %copy-start.44 = (f32[2048]{0:T(1024)}, f32[2048]{0:T(1024)S(1)}, u32[]{:S(2)}) copy-start(f32[2048]{0:T(1024)S(1)} %get-tuple-element.121) | copy-start | bytes 24580
  103.2 48.2 %copy-start.75 = (f32[1024]{0:T(1024)}, f32[1024]{0:T(1024)S(1)}, u32[]{:S(2)}) copy-start(f32[1024]{0:T(1024)S(1)} %add_rsqrt_fusion) | copy-start | bytes 12292
  176.1 176.2 %all-gather.14.cloned.1.call-start = ((), (), s32[]{:S(2)}) async-start(), calls=%async_computation.18 | async-start | bytes 18382848 | tf_op jit(solution)/shard_map/all_gather | solution.py:360
  176.5 58.9 %copy-start = (bf16[128,2048]{0,1:T(8,128)(2,1)}, bf16[128,2048]{0,1:T(8,128)(2,1)S(1)}, u32[]{:S(2)}) copy-start(bf16[128,2048]{0,1:T(8,128)(2,1)S(1)} %copy.275) | copy-start | bytes 1572868
  177.4 58.1 %copy-start.33 = (bf16[2048,24]{1,0:T(8,128)(2,1)}, bf16[2048,24]{1,0:T(8,128)(2,1)S(1)}, u32[]{:S(2)}) copy-start(bf16[2048,24]{1,0:T(8,128)(2,1)S(1)} %reshape.401) | copy-start | bytes 294916
  227.5 12.6 copy-start.7
  230.6 238.4 %all-gather.16.cloned.1.call-start = ((), (), s32[]{:S(2)}) async-start(), calls=%async_computation.19 | async-start | bytes 17301504 | tf_op jit(solution)/shard_map/all_gather | solution.py:360
  231.2 551.8 %reduce-scatter.26.cloned.1.call-start = ((), (), s32[]{:S(2)}) async-start(), calls=%async_computation.26 | async-start | bytes 18382848
  250.7 218.3 %copy-start.10 = (bf16[3,256,2048]{2,1,0:T(8,128)(2,1)}, bf16[3,256,2048]{2,1,0:T(8,128)(2,1)S(1)}, u32[]{:S(2)}) copy-start(bf16[3,256,2048]{2,1,0:T(8,128)(2,1)S(1)} %constant_dynamic-slice_fusion) | copy-start | bytes 9437188
  353.7 20.4 %copy-start.25 = (bf16[3,2048,256]{1,2,0:T(8,128)(2,1)S(1)}, bf16[3,2048,256]{1,2,0:T(8,128)(2,1)}, u32[]{:S(2)}) copy-start(bf16[3,2048,256]{1,2,0:T(8,128)(2,1)} %copy.345) | copy-start | bytes 9437188
  469.1 32.4 %copy-start.26 = (bf16[3,2048,256]{1,2,0:T(8,128)(2,1)S(1)}, bf16[3,2048,256]{1,2,0:T(8,128)(2,1)}, u32[]{:S(2)}) copy-start(bf16[3,2048,256]{1,2,0:T(8,128)(2,1)} %copy.346) | copy-start | bytes 9437188
  590.6 194.7 %copy-start.52 = (f32[128,24]{0,1:T(8,128)S(1)}, f32[128,24]{0,1:T(8,128)}, u32[]{:S(2)}) copy-start(f32[128,24]{0,1:T(8,128)} %copy-done.51) | copy-start | bytes 36868
  590.6 194.7 %copy-start.54 = (f32[128,24]{0,1:T(8,128)S(1)}, f32[128,24]{0,1:T(8,128)}, u32[]{:S(2)}) copy-start(f32[128,24]{0,1:T(8,128)} %copy-done.53) | copy-start | bytes 36868
  590.6 194.7 %copy-start.1 = (bf16[128,2048]{0,1:T(8,128)(2,1)S(1)}, bf16[128,2048]{0,1:T(8,128)(2,1)}, u32[]{:S(2)}) copy-start(bf16[128,2048]{0,1:T(8,128)(2,1)} %copy-done) | copy-start | bytes 1572868
  590.6 194.7 %copy-start.8 = (bf16[128,2048]{0,1:T(8,128)(2,1)S(1)}, bf16[128,2048]{0,1:T(8,128)(2,1)}, u32[]{:S(2)}) copy-start(bf16[128,2048]{0,1:T(8,128)(2,1)} %copy-done.7) | copy-start | bytes 1572868
  590.6 194.7 %copy-start.34 = (bf16[2048,24]{1,0:T(8,128)(2,1)S(1)}, bf16[2048,24]{1,0:T(8,128)(2,1)}, u32[]{:S(2)}) copy-start(bf16[2048,24]{1,0:T(8,128)(2,1)} %copy-done.33) | copy-start | bytes 294916
  590.6 194.7 %copy-start.45 = (f32[2048]{0:T(1024)S(1)}, f32[2048]{0:T(1024)}, u32[]{:S(2)}) copy-start(f32[2048]{0:T(1024)} %copy-done.44) | copy-start | bytes 24580
  590.6 194.7 %copy-start.73 = (f32[128]{0:T(128)S(1)}, f32[128]{0:T(128)}, u32[]{:S(2)}) copy-start(f32[128]{0:T(128)} %copy-done.72) | copy-start | bytes 1540
  590.7 196.1 %copy-start.82 = (f32[128]{0:T(128)S(1)}, f32[128]{0:T(128)}, u32[]{:S(2)}) copy-start(f32[128]{0:T(128)} %copy-done.81) | copy-start | bytes 1540
  590.7 237.2 %all-gather.18.cloned.1.call-start = ((), (), s32[]{:S(2)}) async-start(), calls=%async_computation.20 | async-start | bytes 4718592 | tf_op jit(solution)/shard_map/all_gather | solution.py:360
  591.9 197.1 %copy-start.19 = (bf16[128,2048]{0,1:T(8,128)(2,1)}, bf16[128,2048]{0,1:T(8,128)(2,1)S(1)}, u32[]{:S(2)}) copy-start(bf16[128,2048]{0,1:T(8,128)(2,1)S(1)} %copy.288) | copy-start | bytes 1572868
  789.0 327.5 %reduce-scatter.24.cloned.1.call-start = ((), (), s32[]{:S(2)}) async-start(), calls=%async_computation.25 | async-start | bytes 17301504
  812.8 15.0 %copy-start.24 = (bf16[2,128,2048]{2,1,0:T(8,128)(2,1)S(1)}, bf16[2,128,2048]{2,1,0:T(8,128)(2,1)}, u32[]{:S(2)}) copy-start(bf16[2,128,2048]{2,1,0:T(8,128)(2,1)} %maximum_select_fusion) | copy-start | bytes 3145732
  812.8 18.6 %copy-start.39 = (bf16[1024,256]{0,1:T(8,128)(2,1)S(1)}, bf16[1024,256]{0,1:T(8,128)(2,1)}, u32[]{:S(2)}) copy-start(bf16[1024,256]{0,1:T(8,128)(2,1)} %slice.151) | copy-start | bytes 1572868
  812.8 18.6 %copy-start.65 = (f32[2,1024]{1,0:T(2,128)S(1)}, f32[2,1024]{1,0:T(2,128)}, u32[]{:S(2)}) copy-start(f32[2,1024]{1,0:T(2,128)} %copy-done.64) | copy-start | bytes 24580
  812.8 359.1 %reduce-scatter.16.cloned.1.call-start = ((), (), s32[]{:S(2)}) async-start(), calls=%async_computation.21 | async-start | bytes 3932160 | tf_op jit(solution)/shard_map/reduce_scatter | solution.py:364
  859.6 342.4 %reduce-scatter.18.cloned.1.call-start = ((), (), s32[]{:S(2)}) async-start(), calls=%async_computation.22 | async-start | bytes 1310720 | tf_op jit(solution)/shard_map/reduce_scatter | solution.py:364
  863.5 2.0 collective-permute-start.1
  897.5 90.9 %all-to-all-start.7 = ((bf16[4,3,512,256]{2,3,1,0:T(8,128)(2,1)}), bf16[4,3,512,256]{2,3,1,0:T(8,128)(2,1)}, u32[]{:S(2)}, u32[]{:S(2)}) async-start(bf16[4,3,512,256]{2,3,1,0:T(8,128)(2,1)} %copy.314), calls=%async_computation.10 | async-start | bytes 6291456 | tf_op jit(solution)/shard_map/all_to_all | solution.py:531
  902.2 353.1 %reduce-scatter.28.cloned.1.call-start = ((), (), s32[]{:S(2)}) async-start(), calls=%async_computation.27 | async-start | bytes 4718592
  988.3 118.0 %all-to-all-start.6 = ((bf16[4,3,512,256]{2,3,1,0:T(8,128)(2,1)}), bf16[4,3,512,256]{2,3,1,0:T(8,128)(2,1)S(1)}, u32[]{:S(2)}, u32[]{:S(2)}) async-start(bf16[4,3,512,256]{2,3,1,0:T(8,128)(2,1)} %copy.311), calls=%async_computation.9 | async-start | bytes 6291456 | tf_op jit(solution)/shard_map/all_to_all | solution.py:531
  1116.5 64.6 %copy-start.89 = (f32[128]{0:T(128)S(1)}, f32[128]{0:T(128)}, u32[]{:S(2)}) copy-start(f32[128]{0:T(128)} %get-tuple-element.87) | copy-start | bytes 1540
  1116.5 140.1 %copy-start.2 = (bf16[128,2048]{0,1:T(8,128)(2,1)S(1)}, bf16[128,2048]{0,1:T(8,128)(2,1)}, u32[]{:S(2)}) copy-start(bf16[128,2048]{0,1:T(8,128)(2,1)} %copy-done) | copy-start | bytes 1572868
  1117.9 143.6 %copy-start.70 = (f32[2048]{0:T(1024)S(1)}, f32[2048]{0:T(1024)}, u32[]{:S(2)}) copy-start(f32[2048]{0:T(1024)} %get-tuple-element.83) | copy-start | bytes 24580
  1117.9 143.6 %copy-start.79 = (f32[128]{0:T(128)S(1)}, f32[128]{0:T(128)}, u32[]{:S(2)}) copy-start(f32[128]{0:T(128)} %get-tuple-element.77) | copy-start | bytes 1540
  1117.9 143.6 %copy-start.80 = (f32[128]{0:T(128)S(1)}, f32[128]{0:T(128)}, u32[]{:S(2)}) copy-start(f32[128]{0:T(128)} %get-tuple-element.79) | copy-start | bytes 1540
  1174.4 98.3 %copy-start.9 = (bf16[128,2048]{0,1:T(8,128)(2,1)S(1)}, bf16[128,2048]{0,1:T(8,128)(2,1)}, u32[]{:S(2)}) copy-start(bf16[128,2048]{0,1:T(8,128)(2,1)} %copy-done.7) | copy-start | bytes 1572868
  1174.4 98.3 %copy-start.20 = (bf16[128,2048]{0,1:T(8,128)(2,1)S(1)}, bf16[128,2048]{0,1:T(8,128)(2,1)}, u32[]{:S(2)}) copy-start(bf16[128,2048]{0,1:T(8,128)(2,1)} %copy-done.19) | copy-start | bytes 1572868
  1174.5 98.3 %copy-start.46 = (f32[2048]{0:T(1024)S(1)}, f32[2048]{0:T(1024)}, u32[]{:S(2)}) copy-start(f32[2048]{0:T(1024)} %copy-done.44) | copy-start | bytes 24580
  1174.5 98.3 %copy-start.74 = (f32[128]{0:T(128)S(1)}, f32[128]{0:T(128)}, u32[]{:S(2)}) copy-start(f32[128]{0:T(128)} %copy-done.72) | copy-start | bytes 1540
  1174.5 98.3 %copy-start.78 = (f32[128]{0:T(128)S(1)}, f32[128]{0:T(128)}, u32[]{:S(2)}) copy-start(f32[128]{0:T(128)} %copy-done.77) | copy-start | bytes 1540
  1176.6 88.5 %copy-start.35 = (bf16[8,64,1,256]{3,2,1,0:T(2,128)(2,1)S(1)}, bf16[8,64,1,256]{3,2,1,0:T(2,128)(2,1)}, u32[]{:S(2)}) copy-start(bf16[8,64,1,256]{3,2,1,0:T(2,128)(2,1)} %get-tuple-element.110) | copy-start | bytes 786436
  1177.4 80.0 %all-to-all-start.5 = ((bf16[8,64,256]{2,1,0:T(8,128)(2,1)}), bf16[8,64,256]{2,1,0:T(8,128)(2,1)S(1)}, u32[]{:S(2)}, u32[]{:S(2)}) async-start(bf16[8,64,256]{2,1,0:T(8,128)(2,1)} %bitcast.142), calls=%async_computation.6 | async-start | bytes 524288 | tf_op jit(solution)/shard_map/all_to_all | solution.py:589
  1257.3 11.0 all-to-all-start.4
  1261.4 138.6 %reduce-scatter.20.cloned.1.call-start = ((), (), s32[]{:S(2)}) async-start(), calls=%async_computation.23 | async-start | bytes 270336 | tf_op jit(solution)/shard_map/reduce_scatter | solution.py:364
  1268.4 14.8 %all-to-all-start.3 = ((bf16[8,64,256]{2,1,0:T(8,128)(2,1)}), bf16[8,64,256]{2,1,0:T(8,128)(2,1)}, u32[]{:S(2)}, u32[]{:S(2)}) async-start(bf16[8,64,256]{2,1,0:T(8,128)(2,1)} %bitcast.171), calls=%async_computation.4 | async-start | bytes 524288 | tf_op jit(solution)/shard_map/all_to_all | solution.py:589
  (50 other events, 225.8 us)
Sparse Core Ops, SparseCore 0:
  9.6 30.6 all-gather.11
  42.2 36.6 all-gather.7
  81.0 63.4 all-gather.9
  176.2 49.9 reduce-scatter.21
  230.8 121.5 all-gather.13
  355.4 113.5 all-gather.15
  590.8 192.2 reduce-scatter.25
  789.1 38.6 all-gather.17
  830.2 202.3 reduce-scatter.23
  1034.8 137.0 reduce-scatter.15
  1174.9 27.1 reduce-scatter.17
  1205.3 49.9 reduce-scatter.27
  1265.2 134.7 reduce-scatter.19

commit v2 on v1

--- a/solution.py
+++ b/solution.py
@@ -3,6 +3,8 @@
 import jax
 import jax.numpy as jnp
 from jax import lax
+from jax.experimental import pallas as pl
+from jax.experimental.pallas import tpu as pltpu
 from jax.sharding import PartitionSpec as P
 
 HD = 128
@@ -356,6 +358,314 @@
     )
 
 
+MESH = pl.DeviceIdType.MESH
+
+
+def partners(e):
+    sib = e + 1 - 2 * (e % 2)
+    xn = e + 2 - 4 * ((e // 2) % 2)
+    yn = e + 4 - 8 * ((e // 4) % 2)
+    dg = xn + 4 - 8 * ((e // 4) % 2)
+    return sib, (xn, yn, dg)
+
+
+def greet(z, e, reps, across):
+    barrier = pltpu.get_barrier_semaphore()
+    sib, chips = partners(e)
+    for other in (sib, *chips):
+        pl.semaphore_signal(barrier, inc=1, device_id={"rep": z, "ep": other}, device_id_type=MESH)
+    if across:
+        @pl.when(z > 0)
+        def _():
+            pl.semaphore_signal(barrier, inc=1, device_id={"rep": z - 1, "ep": e}, device_id_type=MESH)
+        @pl.when(z < reps - 1)
+        def _():
+            pl.semaphore_signal(barrier, inc=1, device_id={"rep": z + 1, "ep": e}, device_id_type=MESH)
+    peers = 4
+    if across:
+        peers = peers + jnp.where(z > 0, 1, 0) + jnp.where(z < reps - 1, 1, 0)
+    pl.semaphore_wait(barrier, peers)
+
+
+def ag_kernel(reps, across, x_ref, out_ref, own_sem, zs, zr, ps, pr, cs, cr):
+    z = lax.axis_index("rep")
+    e = lax.axis_index("ep")
+    sib, chips = partners(e)
+    greet(z, e, reps, across)
+    own = z if across else 0
+    groups = reps if across else 1
+    half = x_ref.shape[0] // 2
+    local = pltpu.make_async_copy(x_ref, out_ref.at[own, e], own_sem)
+    local.start()
+
+    def zcopy(src, g, up):
+        d = 0 if up else 1
+        return pltpu.make_async_remote_copy(
+            src_ref=src, dst_ref=out_ref.at[g, e], send_sem=zs.at[d, g], recv_sem=zr.at[g],
+            device_id={"rep": z + 1 if up else z - 1, "ep": e}, device_id_type=MESH)
+
+    def pcopy(src, g, j):
+        return pltpu.make_async_remote_copy(
+            src_ref=src, dst_ref=out_ref.at[g, e], send_sem=ps.at[g, j], recv_sem=pr.at[g, j],
+            device_id={"rep": z, "ep": chips[j]}, device_id_type=MESH)
+
+    def relay(g, j):
+        rows = pl.ds(half * j, half)
+        part = out_ref.at[g, chips[j], rows]
+        return pltpu.make_async_remote_copy(
+            src_ref=part, dst_ref=part, send_sem=ps.at[g, 2 + j], recv_sem=pr.at[g, 2 + j],
+            device_id={"rep": z, "ep": chips[1 - j]}, device_id_type=MESH)
+
+    def relayed(g, j):
+        part = out_ref.at[g, chips[2], pl.ds(half * j, half)]
+        return pltpu.make_async_remote_copy(
+            src_ref=part, dst_ref=part, send_sem=ps.at[g, 2 + j], recv_sem=pr.at[g, 2 + j],
+            device_id={"rep": z, "ep": chips[1 - j]}, device_id_type=MESH)
+
+    def ccopy(src, g, j):
+        who = e if j == 0 else chips[j - 1]
+        return pltpu.make_async_remote_copy(
+            src_ref=src, dst_ref=out_ref.at[g, who], send_sem=cs.at[g, j], recv_sem=cr.at[g, j],
+            device_id={"rep": z, "ep": sib}, device_id_type=MESH)
+
+    def spread(src, g):
+        pcopy(src, g, 0).start()
+        pcopy(src, g, 1).start()
+        ccopy(src, g, 0).start()
+
+    def pass_on(g):
+        for j in range(2):
+            pcopy(x_ref, g, j).wait_recv()
+            relay(g, j).start()
+            ccopy(out_ref.at[g, chips[j]], g, j + 1).start()
+
+    def finish(g):
+        for j in range(2):
+            relayed(g, j).wait_recv()
+        ccopy(out_ref.at[g, chips[2]], g, 3).start()
+
+    def at(k, fn):
+        if k == 0:
+            fn(own)
+            return
+        @pl.when(z - k >= 0)
+        def _():
+            fn(z - k)
+        @pl.when(z + k < reps)
+        def _():
+            fn(z + k)
+
+    if across:
+        @pl.when(z < reps - 1)
+        def _():
+            zcopy(x_ref, z, True).start()
+        @pl.when(z > 0)
+        def _():
+            zcopy(x_ref, z, False).start()
+    spread(x_ref, own)
+    for k in range(1, groups):
+        @pl.when(z - k >= 0)
+        def _():
+            g = z - k
+            zcopy(x_ref, g, True).wait_recv()
+            @pl.when(z < reps - 1)
+            def _():
+                zcopy(out_ref.at[g, e], g, True).start()
+            spread(out_ref.at[g, e], g)
+        @pl.when(z + k < reps)
+        def _():
+            g = z + k
+            zcopy(x_ref, g, False).wait_recv()
+            @pl.when(z > 0)
+            def _():
+                zcopy(out_ref.at[g, e], g, False).start()
+            spread(out_ref.at[g, e], g)
+        at(k - 1, pass_on)
+        if k >= 2:
+            at(k - 2, finish)
+    at(groups - 1, pass_on)
+    if groups >= 2:
+        at(groups - 2, finish)
+    at(groups - 1, finish)
+    local.wait()
+    for g in range(groups):
+        for j in range(4):
+            ccopy(x_ref, g, j).wait()
+        for j in range(2):
+            pcopy(x_ref, g, j).wait_send()
+            relay(g, j).wait_send()
+        if across:
+            @pl.when((z < reps - 1) & (z >= g))
+            def _():
+                zcopy(x_ref, g, True).wait_send()
+            @pl.when((z > 0) & (z <= g))
+            def _():
+                zcopy(x_ref, g, False).wait_send()
+
+
+def all_gather(x, reps, eps, across, cid):
+    groups = reps if across else 1
+    D = pltpu.SemaphoreType.DMA
+    out = pl.pallas_call(
+        partial(ag_kernel, reps, across),
+        out_shape=jax.ShapeDtypeStruct((groups, eps, *x.shape), x.dtype),
+        in_specs=[pl.BlockSpec(memory_space=pl.ANY)],
+        out_specs=pl.BlockSpec(memory_space=pl.ANY),
+        scratch_shapes=[D, D((2, reps)), D((reps,)), D((groups, 4)), D((groups, 4)), D((groups, 4)), D((groups, 4))],
+        compiler_params=pltpu.CompilerParams(collective_id=cid, has_side_effects=True),
+    )(x)
+    return out
+
+
+def rs_kernel(reps, across, p_ref, out_ref, own, sib_in, chip_in, up_in, down_in, res,
+              own_sem, ss, sr, ps, pr, us, ur, ds, dr):
+    z = lax.axis_index("rep")
+    e = lax.axis_index("ep")
+    core = e % 2
+    chip = e // 2
+    sib, chips = partners(e)
+    groups = reps if across else 1
+    greet(z, e, reps, across)
+    rows, W = res.shape[1], res.shape[2]
+    half = reps // 2
+
+    def order(s):
+        if not across:
+            return 0
+        t = reps - 1 - s
+        down = jnp.where(t > z, t, t - 1)
+        upw = jnp.where(s < z, s, s + 1)
+        g = jnp.where(z < half, down, upw)
+        return z if s == reps - 1 else g
+
+    def sibcopy(g):
+        return pltpu.make_async_remote_copy(
+            src_ref=p_ref.at[g, :, 1 - core], dst_ref=sib_in.at[g], send_sem=ss.at[g], recv_sem=sr.at[g],
+            device_id={"rep": z, "ep": sib}, device_id_type=MESH)
+
+    def load(g):
+        return pltpu.make_async_copy(p_ref.at[g, :, core], own.at[g], own_sem.at[g])
+
+    def pcopy(g, j):
+        return pltpu.make_async_remote_copy(
+            src_ref=own.at[g, chips[j] // 2], dst_ref=chip_in.at[g, j], send_sem=ps.at[g, j], recv_sem=pr.at[g, j],
+            device_id={"rep": z, "ep": chips[j]}, device_id_type=MESH)
+
+    def zcopy(g, up):
+        if up:
+            return pltpu.make_async_remote_copy(
+                src_ref=res.at[g], dst_ref=up_in.at[g], send_sem=us.at[g], recv_sem=ur.at[g],
+                device_id={"rep": z + 1, "ep": e}, device_id_type=MESH)
+        return pltpu.make_async_remote_copy(
+            src_ref=res.at[g], dst_ref=down_in.at[g], send_sem=ds.at[g], recv_sem=dr.at[g],
+            device_id={"rep": z - 1, "ep": e}, device_id_type=MESH)
+
+    for s in range(groups):
+        g = order(s)
+        sibcopy(g).start()
+        load(g).start()
+    step = 16
+
+    def add_in(g, q):
+        @pl.loop(0, rows // step)
+        def _(i):
+            r = pl.ds(pl.multiple_of(i * step, step), step)
+            own[g, q, r, :] = (own[g, q, r, :].astype(jnp.float32) + sib_in[g, q, r, :].astype(jnp.float32)).astype(own.dtype)
+
+    def stage1(g):
+        load(g).wait()
+        sibcopy(g).wait_recv()
+        for j in (2, 0, 1):
+            add_in(g, chips[j] // 2)
+            pcopy(g, j).start()
+
+    def stage2(g):
+        for j in range(3):
+            pcopy(g, j).wait_recv()
+        @pl.loop(0, rows // step)
+        def _(i):
+            r = pl.ds(pl.multiple_of(i * step, step), step)
+            t = own[g, chip, r, :].astype(jnp.float32) + sib_in[g, chip, r, :].astype(jnp.float32)
+            for j in range(3):
+                t = t + chip_in[g, j, r, :].astype(jnp.float32)
+            res[g, r, :] = t.astype(res.dtype)
+
+    def plus(g, ref):
+        @pl.loop(0, rows // step)
+        def _(i):
+            r = pl.ds(pl.multiple_of(i * step, step), step)
+            res[g, r, :] = (res[g, r, :].astype(jnp.float32) + ref[g, r, :].astype(jnp.float32)).astype(res.dtype)
+
+    def stage3(g):
+        @pl.when(g > z)
+        def _():
+            @pl.when(z > 0)
+            def _():
+                zcopy(g, True).wait_recv()
+                plus(g, up_in)
+            zcopy(g, True).start()
+        @pl.when(g < z)
+        def _():
+            @pl.when(z < reps - 1)
+            def _():
+                zcopy(g, False).wait_recv()
+                plus(g, down_in)
+            zcopy(g, False).start()
+
+    stage1(order(0))
+    for s in range(1, groups):
+        stage1(order(s))
+        stage2(order(s - 1))
+        if s >= 2:
+            stage3(order(s - 2))
+    stage2(order(groups - 1))
+    if across:
+        stage3(order(groups - 2))
+        @pl.when(z > 0)
+        def _():
+            zcopy(z, True).wait_recv()
+            plus(z, up_in)
+        @pl.when(z < reps - 1)
+        def _():
+            zcopy(z, False).wait_recv()
+            plus(z, down_in)
+    fin = res.at[z if across else 0]
+    out = pltpu.make_async_copy(fin, out_ref, own_sem.at[0])
+    out.start()
+    out.wait()
+    for g in range(groups):
+        sibcopy(g).wait_send()
+        for j in range(3):
+            pcopy(g, j).wait_send()
+        if across:
+            @pl.when(g > z)
+            def _():
+                zcopy(g, True).wait_send()
+            @pl.when(g < z)
+            def _():
+                zcopy(g, False).wait_send()
+
+
+def reduce_scatter(p, reps, eps, across, cid):
+    groups = reps if across else 1
+    W = p.shape[1]
+    rows = p.shape[0] // groups // eps
+    p = p.reshape(groups, eps // 2, 2, rows, W)
+    D = pltpu.SemaphoreType.DMA
+    V = pltpu.VMEM
+    q = eps // 2
+    return pl.pallas_call(
+        partial(rs_kernel, reps, across),
+        out_shape=jax.ShapeDtypeStruct((rows, W), p.dtype),
+        in_specs=[pl.BlockSpec(memory_space=pl.ANY)],
+        out_specs=pl.BlockSpec(memory_space=pl.ANY),
+        scratch_shapes=[V((groups, q, rows, W), p.dtype), V((groups, q, rows, W), p.dtype), V((groups, 3, rows, W), p.dtype),
+                        V((groups, rows, W), p.dtype), V((groups, rows, W), p.dtype), V((groups, rows, W), p.dtype),
+                        D((groups,)), D((groups,)), D((groups,)), D((groups, 3)), D((groups, 3)),
+                        D((groups,)), D((groups,)), D((groups,)), D((groups,))],
+        compiler_params=pltpu.CompilerParams(collective_id=cid, has_side_effects=True, vmem_limit_bytes=56 * 2**20),
+    )(p)
+
 def gather_block(block, axes):
     return lax.all_gather(block, axes, axis=0, tiled=True)
 
@@ -440,8 +750,10 @@
         jnp.concatenate([out_other, out_own], axis=1),
     ).reshape(slice_width, width)
 
-    cot_all = gather_block(cotangent, every)
-    tokens_group = gather_block(tokens, "ep").astype(f32)
+    cot_all = all_gather(cotangent, rep_count, ep_count, True, 0).reshape(-1, width)
+    tokens_group = (
+        all_gather(tokens, rep_count, ep_count, False, 1).reshape(group_rows, width).astype(f32)
+    )
     normed_group = rms_scale(tokens_group, gain_in).astype(bf16)
     projected = jnp.dot(normed_group, qkv_slice, preferred_element_type=f32)
     query_pre = projected[:, :slice_width].reshape(group_rows, heads_dev, head_dim)
@@ -456,7 +768,7 @@
     mixed_low = mixed.reshape(group_rows, slice_width).astype(bf16)
     attn_part = jnp.dot(mixed_low, out_slice, preferred_element_type=f32).astype(bf16)
     residual = tokens.astype(f32)
-    after_attn = residual + scatter_sum(attn_part, "ep").astype(f32)
+    after_attn = residual + reduce_scatter(attn_part, rep_count, ep_count, False, 2).astype(f32)
     mid_low = rms_scale(after_attn, gain_mid).astype(bf16)
 
     logits = jnp.dot(mid_low, router_full, preferred_element_type=f32)
@@ -479,7 +791,9 @@
     side = jnp.concatenate(
         [weight_high, weight_low, jnp.zeros((tok_dev, 128 - 2 * experts_all), bf16)], axis=1
     )
-    sent = gather_block(jnp.concatenate([mid_low, side], axis=1), every)
+    sent = all_gather(
+        jnp.concatenate([mid_low, side], axis=1), rep_count, ep_count, True, 3
+    ).reshape(-1, width + 128)
     mid_all = sent[:, :width]
     side_all = sent[:, width:]
     weight_own = lax.dynamic_slice_in_dim(side_all, ep_index * exp_dev, exp_dev, axis=1).astype(
@@ -515,9 +829,11 @@
         ep_index * exp_dev,
         axis=1,
     )
-    row_sum = scatter_sum(jnp.concatenate([row_part, gate_cot_part], axis=1), every)
+    row_sum = reduce_scatter(
+        jnp.concatenate([row_part, gate_cot_part], axis=1), rep_count, ep_count, True, 4
+    )
     moe_part = jnp.dot(hidden_weighted, down_flat, preferred_element_type=f32).astype(bf16)
-    moe_out = scatter_sum(moe_part, every).astype(f32)
+    moe_out = reduce_scatter(moe_part, rep_count, ep_count, True, 5).astype(f32)
     block_out = (after_attn + moe_out).astype(bf16)
     gate_term = jnp.dot(mid_all.T, a_cot, preferred_element_type=f32)
     up_term = jnp.dot(mid_all.T, b_cot, preferred_element_type=f32)
@@ -545,7 +861,9 @@
     _, mid_pull = jax.vjp(rms_scale, after_attn, gain_mid)
     after_extra, gain_mid_cot = mid_pull(mid_cot)
     after_cot = out_grad + after_extra
-    attn_cot_group = gather_block(after_cot.astype(bf16), "ep")
+    attn_cot_group = all_gather(
+        after_cot.astype(bf16), rep_count, ep_count, False, 6
+    ).reshape(group_rows, width)
 
     mixed_cot = jnp.dot(attn_cot_group, out_slice.T, preferred_element_type=f32).astype(bf16)
     output_term = jnp.dot(mixed_low.T, attn_cot_group, preferred_element_type=f32)
@@ -577,7 +895,7 @@
         axis=1,
     )
     normed_part = jnp.dot(pre_cot, qkv_slice.T, preferred_element_type=f32).astype(bf16)
-    normed_cot = scatter_sum(normed_part, "ep").astype(f32)
+    normed_cot = reduce_scatter(normed_part, rep_count, ep_count, False, 7).astype(f32)
     _, input_pull = jax.vjp(rms_scale, residual, gain_in)
     input_extra, gain_in_cot = input_pull(normed_cot)
     input_grad = after_cot + input_extra

time: 1420 us -> 1100 us (0.77)
  waiting for transfers between devices: 823 us -> 8.57 us
  Pallas kernels: 0 us -> 528 us
  starting transfers between devices: 62.6 us -> 33.4 us
    pallas_call x0 -> x8, Pallas kernels: none -> 528 us  [the longest x4 306 us: reduce_scatter(): pl.pallas_call(partial(rs_kernel, reps, across), out_shape=jax.ShapeDtype...]
    unnamed x17 -> x5, waiting for transfers between devices: 291 us -> 0.75 us
    all_gather x6 -> x2, waiting for transfers between devices: 233 us -> 0.01 us  [gather_block(): return lax.all_gather(block, axes, axis=0, tiled=True)]
    reduce_scatter x3, waiting for transfers between devices: 186 us -> 0.02 us  [scatter_sum(): return lax.psum_scatter(partial_sums, axes, scatter_dimension=0, tiled=True)]
    all_to_all x2, waiting for transfers between devices: 98.9 us -> 0.01 us  [rows_of(): got = lax.all_to_all(parts, 'rep', split_axis=0, concat_axis=0, tiled=True)]
    unnamed x203 -> x159, local copies, waits for them, and re-layouts: 63.8 us -> 26 us
    all_to_all x2, starting transfers between devices: 40 us -> 9.45 us  [rows_of(): got = lax.all_to_all(parts, 'rep', split_axis=0, concat_axis=0, tiled=True)]
    concatenate x1 -> x2, local copies, waits for them, and re-layouts: 0.08 us -> 23.2 us  [the longest x1 22.2 us: on_device_split(): jnp.concatenate([row_part, gate_cot_part], axis=1)]
  transfers between devices with their start and end apart: 22 -> 15, of which waited for: 16 -> 3; matrix products, arithmetic and copies ran while one was open for 20% -> 20% of each run, Pallas kernels for 0% -> 25%
where the time goes in v2:
time: 1100 us; the launch traced here: 1090 us
  Pallas kernels  528 us (48%)
  matrix products  256 us (23%)
  local copies, waits for them, and re-layouts  120 us (11%)
  other arithmetic  76 us (7%)
  blocking collectives  51.9 us (5%)
  starting transfers between devices  33.4 us (3%)
  between operations  15.5 us (1%)
    pallas_call x4, Pallas kernels, reduce_scatter(): pl.pallas_call(partial(rs_kernel, reps, across), out_shape=jax.ShapeDtype...  306 us
    pallas_call x4, Pallas kernels, all_gather(): pl.pallas_call(partial(ag_kernel, reps, across), out_shape=jax.ShapeDtype...  222 us
    all_gather x2, blocking collectives, gather_block(): return lax.all_gather(block, axes, axis=0, tiled=True)  51.9 us
    dot_general x1, matrix products, on_device_split(): down_cot = jnp.dot(cot_all, down_flat.T, preferred_element_type=f32)  32.3 us
    dot_general x1, matrix products, on_device_split(): jnp.dot(b_cot, up_flat.T, preferred_element_type=f32)  26.6 us
    unnamed x159, local copies, waits for them, and re-layouts  26 us
    concatenate x1, local copies, waits for them, and re-layouts, on_device_split(): jnp.concatenate([row_part, gate_cot_part], axis=1)  22.2 us
  transfers between devices with their start and end apart: 15, of which 3 were waited for; matrix products, arithmetic and copies ran while one was open for 20% of the time, Pallas kernels for 25%

profile of v2, /device:TPU:0, one launch (start us, length us, event | category | flops | bytes accessed | tf_op | source)
XLA Modules:
  0.0 1089.2 jit_solution(9921249072447468247)
XLA Ops:
  10.1 5.2 all-to-all-start
  17.5 4.7 all-to-all-done
  22.2 3.4 all-to-all-start.1
  30.2 2.3 all-to-all-done.1
  32.5 3.4 all-to-all-start.2
  36.0 42.5 %all_gather.12 = bf16[512,128]{1,0:T(8,128)(2,1)S(1)} all-gather(bf16[16,128]{1,0:T(8,128)(2,1)S(1)} %bitcast.213), channel_id=1, replica_groups=mesh['rep'=4,'ep'=8] {'rep','ep'}, dimensions={0}, use_global_device_ids=true | all-gather | bytes 135168 | tf_op jit(solution)/shard_map/all_gather | solution.py:670
  81.7 2.1 constant_dynamic-slice_fusion.4
  83.8 3.0 copy.289
  86.8 2.2 constant_dynamic-slice_fusion.3
  89.0 3.1 copy.288
  92.1 24.4 %shard_map.230 = bf16[1,8,128,2048]{3,2,1,0:T(8,128)(2,1)} custom-call(bf16[128,2048]{1,0:T(8,128)(2,1)} %x_ref.2), custom_call_target="tpu_custom_call" | custom-call | tf_op jit(solution)/shard_map/pallas_call | solution.py:509
  116.6 93.9 %shard_map.234 = bf16[4,8,128,2048]{3,2,1,0:T(8,128)(2,1)} custom-call(bf16[128,2048]{1,0:T(8,128)(2,1)} %x_ref.3), custom_call_target="tpu_custom_call" | custom-call | tf_op jit(solution)/shard_map/pallas_call | solution.py:509
  210.6 9.4 all-gather
  220.3 3.1 multiply_reduce_fusion.1
  226.9 3.9 constant_dynamic-slice_fusion
  232.6 5.2 fusion.12
  239.0 6.5 fusion.72
  252.9 8.8 fusion.69
  261.8 4.2 fusion.29
  266.0 3.3 bitcast_convert_fusion
  269.3 31.5 %shard_map.231 = bf16[128,2048]{1,0:T(8,128)(2,1)} custom-call(bf16[1,4,2,128,2048]{4,3,2,1,0:T(8,128)(2,1)} %bitcast.167), custom_call_target="tpu_custom_call" | custom-call | tf_op jit(solution)/shard_map/pallas_call | solution.py:657
  306.0 80.7 %shard_map.232 = bf16[4,8,128,2176]{3,2,1,0:T(8,128)(2,1)} custom-call(bf16[128,2176]{1,0:T(8,128)(2,1)} %concatenate.45.x_ref), custom_call_target="tpu_custom_call" | custom-call | tf_op jit(solution)/shard_map/pallas_call | solution.py:509
  389.4 20.5 %fusion.7 = f32[4096,768]{0,1:T(8,128)} fusion(bf16[2048,768]{0,1:T(8,128)(2,1)} %bitcast.190, bf16[4096,2176]{1,0:T(8,128)(2,1)} %bitcast.171), kind=kOutput, calls=%fused_computation.17 | convolution fusion | flops 12884901888 | bytes 32505856 | tf_op jit(solution)/shard_map/dot_general | solution.py:811
  409.9 19.6 %fusion.9 = f32[4096,768]{0,1:T(8,128)} fusion(bf16[2048,768]{0,1:T(8,128)(2,1)S(1)} %bitcast.192, bf16[4096,2176]{1,0:T(8,128)(2,1)} %bitcast.172), kind=kOutput, calls=%fused_computation.19 | convolution fusion | flops 12884901888 | bytes 32505856 | tf_op jit(solution)/shard_map/dot_general | solution.py:810
  429.6 32.3 %convert_multiply_fusion = (f32[4096,768]{0,1:T(8,128)}, bf16[4096,768]{0,1:T(8,128)(2,1)}, bf16[4096,768]{0,1:T(8,128)(2,1)}, bf16[4096,768]{0,1:T(8,128)(2,1)}) fusion(f32[4096,768]{0,1:T(8,128)} %fusion.7, f32[4096,768]{0,1:T(8,128)} %fusion.9, f32[4096,3]{0,1:T(4,128)S(1)} %convert_add_fusion.1, bf16[768,2048]{1,0:T(8,128)(2,1)S(1)} %bitcast.177, ...), kind=kOutput, calls=%fused_computation.5 | convolution fusion | flops 12941524992 | bytes 76595200 | tf_op jit(solution)/shard_map/dot_general | solution.py:812
  461.9 20.1 %fusion.73 = f32[4096,2048]{0,1:T(8,128)} fusion(bf16[4096,768]{0,1:T(8,128)(2,1)} %get-tuple-element.83, bf16[2048,768]{0,1:T(8,128)(2,1)S(1)} %bitcast.193), kind=kOutput, calls=%fused_computation.180 | convolution fusion | flops 12884901888 | bytes 42991616 | tf_op jit(solution)/shard_map/dot_general | solution.py:822
  482.0 5.3 reduce_sum.216
  487.9 26.6 %add_convert_fusion = bf16[4096,2048]{0,1:T(8,128)(2,1)} fusion(f32[4096,2048]{0,1:T(8,128)} %fusion.73, bf16[4096,768]{0,1:T(8,128)(2,1)} %get-tuple-element.84, bf16[2048,768]{0,1:T(8,128)(2,1)} %bitcast.191), kind=kOutput, calls=%fused_computation.1 | convolution fusion | flops 12901679104 | bytes 59768832 | tf_op jit(solution)/shard_map/dot_general | solution.py:823
  514.5 14.2 %pad_maximum_fusion = bf16[4096,2176]{0,1:T(8,128)(2,1)} fusion(bf16[4096,128]{0,1:T(8,128)(2,1)S(1)} %dynamic_update_slice.3, bf16[4096,2048]{0,1:T(8,128)(2,1)} %add_convert_fusion), kind=kLoop, calls=%fused_computation.4 | loop fusion | flops 35651584 | bytes 35651584 | tf_op jit(solution)/shard_map/concatenate | solution.py:833
  528.7 22.2 %copy.239 = bf16[4096,2176]{1,0:T(8,128)(2,1)} copy(bf16[4096,2176]{0,1:T(8,128)(2,1)} %pad_maximum_fusion) | data formatting | bytes 35651584 | tf_op jit(solution)/shard_map/concatenate | solution.py:833
  551.0 119.2 %shard_map.235 = bf16[128,2176]{1,0:T(8,128)(2,1)} custom-call(bf16[4,4,2,128,2176]{4,3,2,1,0:T(8,128)(2,1)} %bitcast.163), custom_call_target="tpu_custom_call" | custom-call | tf_op jit(solution)/shard_map/pallas_call | solution.py:657
  675.3 22.5 %shard_map.236 = bf16[1,8,128,2048]{3,2,1,0:T(8,128)(2,1)} custom-call(bf16[128,2048]{1,0:T(8,128)(2,1)} %fusion.63.x_ref), custom_call_target="tpu_custom_call" | custom-call | tf_op jit(solution)/shard_map/pallas_call | solution.py:509
  697.8 3.6 convolution_convert_fusion.4
  701.5 5.8 fusion.32
  709.4 2.5 multiply_convert_fusion.3
  718.5 2.1 fusion.39
  721.0 7.5 convolution_convert_fusion.2
  728.6 19.8 %fusion.17 = bf16[2048,768]{1,0:T(8,128)(2,1)} fusion(bf16[4096,768]{0,1:T(8,128)(2,1)} %get-tuple-element.83, bf16[4096,2176]{1,0:T(8,128)(2,1)} %bitcast.173), kind=kOutput, calls=%fused_computation.36 | convolution fusion | flops 12886474752 | bytes 26214400 | tf_op jit(solution)/shard_map/dot_general | solution.py:838
  748.4 4.6 copy.259
  753.0 6.6 reshape.462
  759.6 4.3 copy.260
  763.9 4.7 all-to-all-start.6
  768.6 20.0 %fusion.20 = bf16[2048,768]{1,0:T(8,128)(2,1)} fusion(bf16[4096,768]{0,1:T(8,128)(2,1)} %get-tuple-element.84, bf16[4096,2176]{1,0:T(8,128)(2,1)} %bitcast.174), kind=kOutput, calls=%fused_computation.37 | convolution fusion | flops 12886474752 | bytes 26214400 | tf_op jit(solution)/shard_map/dot_general | solution.py:839
  788.7 4.6 copy.262
  793.3 6.2 reshape.463
  799.5 4.2 copy.263
  803.7 7.4 fusion.1
  812.8 3.6 convolution_convert_fusion.3
  817.7 5.2 convolution_convert_fusion.1
  822.8 32.3 %shard_map.237 = bf16[128,2048]{1,0:T(8,128)(2,1)} custom-call(bf16[1,4,2,128,2048]{4,3,2,1,0:T(8,128)(2,1)} %bitcast.185), custom_call_target="tpu_custom_call" | custom-call | tf_op jit(solution)/shard_map/pallas_call | solution.py:657
  857.8 4.7 all-to-all-start.7
  862.6 20.2 %fusion.74 = f32[3,256,2048]{2,1,0:T(8,128)} fusion(bf16[3,256,4096]{2,1,0:T(8,128)(2,1)} %bitcast.182, bf16[4096,2048,1]{1,0,2:T(8,128)(2,1)} %bitcast.165), kind=kOutput, calls=%fused_computation.181 | convolution fusion | flops 12884901888 | bytes 29360128 | tf_op jit(solution)/shard_map/dot_general | solution.py:840
  883.9 19.6 %convolution_convert_fusion = bf16[4096,2048]{1,0:T(8,128)(2,1)} fusion(bf16[4096,768]{0,1:T(8,128)(2,1)} %fusion.1, bf16[768,2048]{1,0:T(8,128)(2,1)} %bitcast.176), kind=kOutput, calls=%fused_computation.6 | convolution fusion | flops 12893290496 | bytes 26214400 | tf_op jit(solution)/shard_map/dot_general | solution.py:835
  903.6 123.2 %shard_map.233 = bf16[128,2048]{1,0:T(8,128)(2,1)} custom-call(bf16[4,4,2,128,2048]{4,3,2,1,0:T(8,128)(2,1)} %bitcast.175), custom_call_target="tpu_custom_call" | custom-call | tf_op jit(solution)/shard_map/pallas_call | solution.py:657
  1026.9 2.6 reshape.455
  1029.5 2.1 fusion.65
  1032.4 3.4 all-to-all-start.5
  1035.9 3.3 fusion.41
  1044.5 4.1 all-to-all-start.4
  1048.7 5.5 copy_convert_fusion
  1055.6 3.5 all-to-all-start.3
  1059.1 5.4 copy_convert_fusion.1
  1064.5 6.6 copy.267
  1071.1 6.6 copy.266
  (279 shorter events, 68.3 us)
Async XLA Ops:
  7.2 71.3 %copy-start.68 = (s32[1,3]{1,0:T(1,128)S(1)}, s32[1,3]{1,0:T(1,128)}, u32[]{:S(2)}) copy-start(s32[1,3]{1,0:T(1,128)} %param.26) | copy-start | bytes 40
  7.2 223.7 %all-gather.6.cloned.1.call-start = ((), (), s32[]{:S(2)}) async-start(), calls=%async_computation.12 | async-start | bytes 1310720 | tf_op jit(solution)/shard_map/all_gather | solution.py:670
  10.1 12.1 %all-to-all-start = ((bf16[8,64,256]{2,1,0:T(8,128)(2,1)}), bf16[8,64,256]{2,1,0:T(8,128)(2,1)S(1)}, u32[]{:S(2)}, u32[]{:S(2)}) async-start(bf16[8,64,256]{2,1,0:T(8,128)(2,1)} %reshape.426), calls=%async_computation | async-start | bytes 524288 | tf_op jit(solution)/shard_map/all_to_all | solution.py:734
  22.2 10.3 all-to-all-start.1
  32.5 48.1 %all-to-all-start.2 = ((bf16[8,64,256]{2,1,0:T(8,128)(2,1)}), bf16[8,64,256]{2,1,0:T(8,128)(2,1)S(1)}, u32[]{:S(2)}, u32[]{:S(2)}) async-start(bf16[8,64,256]{2,1,0:T(8,128)(2,1)} %reshape.430), calls=%async_computation.2 | async-start | bytes 524288 | tf_op jit(solution)/shard_map/all_to_all | solution.py:734
  35.9 203.1 %all-gather.4.cloned.1.call-start = ((), (), s32[]{:S(2)}) async-start(), calls=%async_computation.11 | async-start | bytes 3932160 | tf_op jit(solution)/shard_map/all_gather | solution.py:670
  81.6 945.2 %reduce-scatter.4.cloned.1.call-start = ((), (), s32[]{:S(2)}) async-start(), calls=%async_computation.13 | async-start | bytes 3932160 | tf_op jit(solution)/shard_map/reduce_scatter | solution.py:674
  116.6 94.0 %copy-start.53 = (s32[128,8]{0,1:T(8,128)S(1)}, s32[128,8]{0,1:T(8,128)}, u32[]{:S(2)}) copy-start(s32[128,8]{0,1:T(8,128)} %param.28) | copy-start | bytes 12292
  116.6 94.0 %copy-start.67 = (s32[128]{0:T(128)S(1)}, s32[128]{0:T(128)}, u32[]{:S(2)}) copy-start(s32[128]{0:T(128)} %param.27) | copy-start | bytes 1540
  116.6 94.0 %copy-start.69 = (s32[128]{0:T(128)S(1)}, s32[128]{0:T(128)}, u32[]{:S(2)}) copy-start(s32[128]{0:T(128)} %param.29) | copy-start | bytes 1540
  220.2 29.8 %copy-start.58 = (f32[128]{0:T(128)}, f32[128]{0:T(128)S(1)}, u32[]{:S(2)}) copy-start(f32[128]{0:T(128)S(1)} %get-tuple-element.115) | copy-start | bytes 1540
  220.3 30.2 %copy-start.56 = (f32[128]{0:T(128)}, f32[128]{0:T(128)S(1)}, u32[]{:S(2)}) copy-start(f32[128]{0:T(128)S(1)} %get-tuple-element.114) | copy-start | bytes 1540
  223.4 14.4 %copy-start.43 = (f32[2048]{0:T(1024)}, f32[2048]{0:T(1024)S(1)}, u32[]{:S(2)}) copy-start(f32[2048]{0:T(1024)S(1)} %get-tuple-element.113) | copy-start | bytes 24580
  223.4 78.8 %copy-start.40 = (f32[2048]{0:T(1024)}, f32[2048]{0:T(1024)S(1)}, u32[]{:S(2)}) copy-start(f32[2048]{0:T(1024)S(1)} %get-tuple-element.112) | copy-start | bytes 24580
  225.3 25.5 %copy-start.11 = (f32[1024,64]{1,0:T(8,128)}, f32[1024,64]{1,0:T(8,128)S(1)}, u32[]{:S(2)}) copy-start(f32[1024,64]{1,0:T(8,128)S(1)} %get-tuple-element.116) | copy-start | bytes 786436
  225.3 25.5 %copy-start.13 = (f32[1024,64]{1,0:T(8,128)}, f32[1024,64]{1,0:T(8,128)S(1)}, u32[]{:S(2)}) copy-start(f32[1024,64]{1,0:T(8,128)S(1)} %get-tuple-element.117) | copy-start | bytes 786436
  232.2 5.6 collective-permute-start
  247.7 5.1 copy-start.45
  247.8 5.1 copy-start.47
  250.1 11.7 %copy-start.4 = (f32[1024,2,128]{2,0,1:T(8,128)}, f32[1024,2,128]{2,0,1:T(8,128)S(1)}, u32[]{:S(2)}) copy-start(f32[1024,2,128]{2,0,1:T(8,128)S(1)} %copy.227) | copy-start | bytes 3145732
  252.9 8.9 copy-start.38
  266.0 34.9 %copy-start = (bf16[128,2048]{1,0:T(8,128)(2,1)S(1)}, bf16[128,2048]{1,0:T(8,128)(2,1)}, u32[]{:S(2)}) copy-start(bf16[128,2048]{1,0:T(8,128)(2,1)} %x_ref.2) | copy-start | bytes 1572868
  266.0 37.5 %copy-start.26 = (bf16[2048,24]{1,0:T(8,128)(2,1)S(1)}, bf16[2048,24]{1,0:T(8,128)(2,1)}, u32[]{:S(2)}) copy-start(bf16[2048,24]{1,0:T(8,128)(2,1)} %reshape.442) | copy-start | bytes 294916
  302.2 84.5 %copy-start.65 = (f32[128]{0:T(128)}, f32[128]{0:T(128)S(1)}, u32[]{:S(2)}) copy-start(f32[128]{0:T(128)S(1)} %multiply_reduce_fusion.8) | copy-start | bytes 1540
  302.2 84.5 %copy-start.60 = (f32[128]{0:T(128)}, f32[128]{0:T(128)S(1)}, u32[]{:S(2)}) copy-start(f32[128]{0:T(128)S(1)} %fusion.57) | copy-start | bytes 1540
  303.5 83.2 %copy-start.9 = (bf16[128,2048]{1,0:T(8,128)(2,1)}, bf16[128,2048]{1,0:T(8,128)(2,1)S(1)}, u32[]{:S(2)}) copy-start(bf16[128,2048]{1,0:T(8,128)(2,1)S(1)} %multiply_convert_fusion.4) | copy-start | bytes 1572868
  389.4 20.5 %copy-start.21 = (bf16[3,2048,256]{1,2,0:T(8,128)(2,1)S(1)}, bf16[3,2048,256]{1,2,0:T(8,128)(2,1)}, u32[]{:S(2)}) copy-start(bf16[3,2048,256]{1,2,0:T(8,128)(2,1)} %copy.289) | copy-start | bytes 9437188
  409.9 19.6 %copy-start.8 = (bf16[3,256,2048]{2,1,0:T(8,128)(2,1)S(1)}, bf16[3,256,2048]{2,1,0:T(8,128)(2,1)}, u32[]{:S(2)}) copy-start(bf16[3,256,2048]{2,1,0:T(8,128)(2,1)} %constant_dynamic-slice_fusion) | copy-start | bytes 9437188
  429.6 32.3 %copy-start.36 = (f32[4096,3]{0,1:T(4,128)}, f32[4096,3]{0,1:T(4,128)S(1)}, u32[]{:S(2)}) copy-start(f32[4096,3]{0,1:T(4,128)S(1)} %convert_add_fusion.1) | copy-start | bytes 147460
  550.9 119.3 %copy-start.33 = (f32[128,24]{1,0:T(8,128)S(1)}, f32[128,24]{1,0:T(8,128)}, u32[]{:S(2)}) copy-start(f32[128,24]{1,0:T(8,128)} %copy-done.32) | copy-start | bytes 36868
  550.9 119.3 %copy-start.35 = (f32[128,24]{1,0:T(8,128)S(1)}, f32[128,24]{1,0:T(8,128)}, u32[]{:S(2)}) copy-start(f32[128,24]{1,0:T(8,128)} %copy-done.34) | copy-start | bytes 36868
  550.9 120.3 %copy-start.1 = (bf16[128,2048]{1,0:T(8,128)(2,1)S(1)}, bf16[128,2048]{1,0:T(8,128)(2,1)}, u32[]{:S(2)}) copy-start(bf16[128,2048]{1,0:T(8,128)(2,1)} %x_ref.2) | copy-start | bytes 1572868
  550.9 120.3 %copy-start.6 = (bf16[128,2048]{1,0:T(8,128)(2,1)S(1)}, bf16[128,2048]{1,0:T(8,128)(2,1)}, u32[]{:S(2)}) copy-start(bf16[128,2048]{1,0:T(8,128)(2,1)} %shard_map.231) | copy-start | bytes 1572868
  550.9 120.3 %copy-start.27 = (bf16[2048,24]{1,0:T(8,128)(2,1)S(1)}, bf16[2048,24]{1,0:T(8,128)(2,1)}, u32[]{:S(2)}) copy-start(bf16[2048,24]{1,0:T(8,128)(2,1)} %reshape.442) | copy-start | bytes 294916
  550.9 120.3 %copy-start.41 = (f32[2048]{0:T(1024)S(1)}, f32[2048]{0:T(1024)}, u32[]{:S(2)}) copy-start(f32[2048]{0:T(1024)} %copy-done.40) | copy-start | bytes 24580
  550.9 120.3 %copy-start.61 = (f32[128]{0:T(128)S(1)}, f32[128]{0:T(128)}, u32[]{:S(2)}) copy-start(f32[128]{0:T(128)} %copy-done.60) | copy-start | bytes 1540
  551.0 122.0 %copy-start.66 = (f32[128]{0:T(128)S(1)}, f32[128]{0:T(128)}, u32[]{:S(2)}) copy-start(f32[128]{0:T(128)} %copy-done.65) | copy-start | bytes 1540
  551.0 123.0 %copy-start.16 = (bf16[128,2048]{1,0:T(8,128)(2,1)S(1)}, bf16[128,2048]{1,0:T(8,128)(2,1)}, u32[]{:S(2)}) copy-start(bf16[128,2048]{1,0:T(8,128)(2,1)} %x_ref.3) | copy-start | bytes 1572868
  670.2 27.6 %copy-start.20 = (bf16[2,128,2048]{2,1,0:T(8,128)(2,1)S(1)}, bf16[2,128,2048]{2,1,0:T(8,128)(2,1)}, u32[]{:S(2)}) copy-start(bf16[2,128,2048]{2,1,0:T(8,128)(2,1)} %maximum_select_fusion) | copy-start | bytes 3145732
  673.0 28.4 %copy-start.63 = (f32[128]{0:T(128)}, f32[128]{0:T(128)S(1)}, u32[]{:S(2)}) copy-start(f32[128]{0:T(128)S(1)} %multiply_multiply_fusion.5) | copy-start | bytes 1540
  675.3 26.2 %copy-start.55 = (f32[2,1024]{1,0:T(2,128)S(1)}, f32[2,1024]{1,0:T(2,128)}, u32[]{:S(2)}) copy-start(f32[2,1024]{1,0:T(2,128)} %copy-done.54) | copy-start | bytes 24580
  697.8 9.5 slice-start
  701.5 5.9 slice-start.1
  701.5 5.9 copy-start.39
  763.9 93.9 %all-to-all-start.6 = ((bf16[4,3,512,256]{2,3,1,0:T(8,128)(2,1)}), bf16[4,3,512,256]{2,3,1,0:T(8,128)(2,1)}, u32[]{:S(2)}, u32[]{:S(2)}) async-start(bf16[4,3,512,256]{2,3,1,0:T(8,128)(2,1)} %copy.260), calls=%async_computation.9 | async-start | bytes 6291456 | tf_op jit(solution)/shard_map/all_to_all | solution.py:847
  768.6 270.6 %reduce-scatter.8.cloned.1.call-start = ((), (), s32[]{:S(2)}) async-start(), calls=%async_computation.15 | async-start | bytes 270336 | tf_op jit(solution)/shard_map/reduce_scatter | solution.py:674
  793.3 10.4 copy-start.37
  803.7 7.4 copy-start.10
  803.7 9.1 copy-start.31
  817.3 37.8 %copy-start.44 = (f32[2048]{0:T(1024)S(1)}, f32[2048]{0:T(1024)}, u32[]{:S(2)}) copy-start(f32[2048]{0:T(1024)} %copy-done.43) | copy-start | bytes 24580
  817.3 65.4 %collective-permute-start.1 = (bf16[2,64,2048]{2,1,0:T(8,128)(2,1)}, bf16[2,64,2048]{2,1,0:T(8,128)(2,1)S(1)}, u32[]{:S(2)}, u32[]{:S(2)}) collective-permute-start(bf16[2,64,2048]{2,1,0:T(8,128)(2,1)} %get-tuple-element.96), channel_id=1, source_target_pairs={{0,1},{1,0},{2,3},{3,2},{4,5},{5,4},{6,7},{7,6},{8,9},{9,8},{10,11... | collective-permute-start | bytes 1572872 | tf_op jit(solution)/shard_map/ppermute | solution.py:914
  857.8 174.6 %all-to-all-start.7 = ((bf16[4,3,512,256]{2,3,1,0:T(8,128)(2,1)}), bf16[4,3,512,256]{2,3,1,0:T(8,128)(2,1)}, u32[]{:S(2)}, u32[]{:S(2)}) async-start(bf16[4,3,512,256]{2,3,1,0:T(8,128)(2,1)} %copy.263), calls=%async_computation.10 | async-start | bytes 6291456 | tf_op jit(solution)/shard_map/all_to_all | solution.py:847
  862.6 179.4 %reduce-scatter.6.cloned.1.call-start = ((), (), s32[]{:S(2)}) async-start(), calls=%async_computation.14 | async-start | bytes 1310720 | tf_op jit(solution)/shard_map/reduce_scatter | solution.py:674
  1026.8 9.1 copy-start.7
  1026.8 9.1 copy-start.15
  1026.8 9.1 copy-start.17
  1026.8 9.0 copy-start.42
  1026.8 9.0 copy-start.62
  1026.8 9.0 copy-start.64
  1031.6 12.2 %copy-start.29 = (bf16[8,64,1,256]{3,2,1,0:T(2,128)(2,1)S(1)}, bf16[8,64,1,256]{3,2,1,0:T(2,128)(2,1)}, u32[]{:S(2)}) copy-start(bf16[8,64,1,256]{3,2,1,0:T(2,128)(2,1)} %get-tuple-element.98) | copy-start | bytes 786436
  1032.4 12.2 %all-to-all-start.5 = ((bf16[8,64,256]{2,1,0:T(8,128)(2,1)}), bf16[8,64,256]{2,1,0:T(8,128)(2,1)S(1)}, u32[]{:S(2)}, u32[]{:S(2)}) async-start(bf16[8,64,256]{2,1,0:T(8,128)(2,1)} %bitcast.157), calls=%async_computation.6 | async-start | bytes 524288 | tf_op jit(solution)/shard_map/all_to_all | solution.py:907
  1039.2 14.9 %copy-start.28 = (bf16[8,64,1,256]{3,2,1,0:T(2,128)(2,1)S(1)}, bf16[8,64,1,256]{3,2,1,0:T(2,128)(2,1)}, u32[]{:S(2)}) copy-start(bf16[8,64,1,256]{3,2,1,0:T(2,128)(2,1)} %get-tuple-element.99) | copy-start | bytes 786436
  1044.5 11.1 %all-to-all-start.4 = ((bf16[8,64,256]{2,1,0:T(8,128)(2,1)}), bf16[8,64,256]{2,1,0:T(8,128)(2,1)S(1)}, u32[]{:S(2)}, u32[]{:S(2)}) async-start(bf16[8,64,256]{2,1,0:T(8,128)(2,1)} %bitcast.158), calls=%async_computation.5 | async-start | bytes 524288 | tf_op jit(solution)/shard_map/all_to_all | solution.py:907
  1055.6 25.3 %all-to-all-start.3 = ((bf16[8,64,256]{2,1,0:T(8,128)(2,1)}), bf16[8,64,256]{2,1,0:T(8,128)(2,1)S(1)}, u32[]{:S(2)}, u32[]{:S(2)}) async-start(bf16[8,64,256]{2,1,0:T(8,128)(2,1)} %bitcast.159), calls=%async_computation.4 | async-start | bytes 524288 | tf_op jit(solution)/shard_map/all_to_all | solution.py:907
  (25 other events, 62.6 us)
Sparse Core Ops, SparseCore 0:
  9.6 30.6 all-gather.5
  81.8 70.5 all-gather.3
  728.7 82.2 reduce-scatter.3
  857.9 137.9 reduce-scatter.7
  998.2 37.5 reduce-scatter.5

commit v3 on v2

--- a/solution.py
+++ b/solution.py
@@ -666,6 +666,489 @@
         compiler_params=pltpu.CompilerParams(collective_id=cid, has_side_effects=True, vmem_limit_bytes=56 * 2**20),
     )(p)
 
+NT = (((1,), (1,)), ((), ()))
+TN = (((0,), (0,)), ((), ()))
+
+
+def visit_order(reps):
+    return [sorted((g for g in range(reps) if g != z), key=lambda g: (abs(g - z), g)) + [z] for z in range(reps)]
+
+
+def moe_kernel(reps, side_lanes, experts_all, x_ref, cot_ref, eg_ref, eu_ref, ed_ref,
+               row_ref, moe_ref, gout_ref, uout_ref, dout_ref,
+               mid_ref, a_ref, b_ref, h_ref, xin_ref, yin_ref, zin_ref,
+               wgu, wd, xbuf, cbuf, abuf, pbuf, sib_in, relay_in, sendbuf, ownbuf, rbuf, tmp, colbuf, gst, dst,
+               own_sem, w_sem, x_sem, c_sem, ab_sem, t_sem, col_sem, g_sem, o_sem,
+               zs, zr, ps, pr, cs, cr, ss, sr, hs, hr, qs, qr, fs, fr):
+    f32, bf16 = jnp.float32, jnp.bfloat16
+    z = lax.axis_index("rep")
+    e = lax.axis_index("ep")
+    core = e % 2
+    chip = e // 2
+    sib, chips = partners(e)
+    rows = x_ref.shape[0]
+    half = rows // 2
+    width = cot_ref.shape[-1]
+    W1 = x_ref.shape[1]
+    WP = pbuf.shape[-1]
+    exp_dev = eg_ref.shape[0]
+    F = wgu.shape[2] // exp_dev
+    EF = exp_dev * F
+    steps = 4 * reps
+    table = visit_order(reps)
+
+    def group_of(s):
+        g = 0
+        for zi in range(reps):
+            for si in range(reps):
+                g = g + jnp.where((z == zi) & (s == si), table[zi][si], 0)
+        return g
+
+    def chip_of(k):
+        return jnp.where(k == 0, chips[2] // 2, jnp.where(k == 1, chip, jnp.where(k == 2, chips[0] // 2, chips[1] // 2)))
+
+    barrier = pltpu.get_barrier_semaphore()
+    for other in (sib, *chips):
+        pl.semaphore_signal(barrier, inc=1, device_id={"rep": z, "ep": other}, device_id_type=MESH)
+    for d in range(1, reps):
+        pl.semaphore_signal(barrier, inc=1, device_id={"rep": (z + d) % reps, "ep": e}, device_id_type=MESH)
+    weights = []
+    for j in range(exp_dev):
+        cut = pl.ds(pl.multiple_of(z * F, F), F)
+        weights.append(pltpu.make_async_copy(eg_ref.at[j, :, cut], wgu.at[0, :, pl.ds(j * F, F)], w_sem.at[j]))
+        weights.append(pltpu.make_async_copy(eu_ref.at[j, :, cut], wgu.at[1, :, pl.ds(j * F, F)], w_sem.at[exp_dev + j]))
+        weights.append(pltpu.make_async_copy(ed_ref.at[j, cut, :], wd.at[pl.ds(j * F, F), :], w_sem.at[2 * exp_dev + j]))
+    for w in weights:
+        w.start()
+    local = pltpu.make_async_copy(x_ref, mid_ref.at[z, e], own_sem)
+    local.start()
+    pl.semaphore_wait(barrier, 4 + reps - 1)
+
+    def zcopy(src, g, up):
+        d = 0 if up else 1
+        return pltpu.make_async_remote_copy(
+            src_ref=src, dst_ref=mid_ref.at[g, e], send_sem=zs.at[d, g], recv_sem=zr.at[g],
+            device_id={"rep": z + 1 if up else z - 1, "ep": e}, device_id_type=MESH)
+
+    def pcopy(src, g, j):
+        return pltpu.make_async_remote_copy(
+            src_ref=src, dst_ref=mid_ref.at[g, e], send_sem=ps.at[g, j], recv_sem=pr.at[g, j],
+            device_id={"rep": z, "ep": chips[j]}, device_id_type=MESH)
+
+    def relay(g, j, source):
+        part = mid_ref.at[g, source, pl.ds(half * j, half)]
+        return pltpu.make_async_remote_copy(
+            src_ref=part, dst_ref=part, send_sem=ps.at[g, 2 + j], recv_sem=pr.at[g, 2 + j],
+            device_id={"rep": z, "ep": chips[1 - j]}, device_id_type=MESH)
+
+    def ccopy(src, g, j):
+        who = e if j == 0 else chips[j - 1]
+        return pltpu.make_async_remote_copy(
+            src_ref=src, dst_ref=mid_ref.at[g, who], send_sem=cs.at[g, j], recv_sem=cr.at[g, j],
+            device_id={"rep": z, "ep": sib}, device_id_type=MESH)
+
+    def spread(src, g):
+        pcopy(src, g, 0).start()
+        pcopy(src, g, 1).start()
+        ccopy(src, g, 0).start()
+
+    def pass_on(g):
+        for j in range(2):
+            pcopy(x_ref, g, j).wait_recv()
+            relay(g, j, chips[j]).start()
+            ccopy(mid_ref.at[g, chips[j]], g, j + 1).start()
+
+    def finish_in(g):
+        for j in range(2):
+            relay(g, j, chips[2]).wait_recv()
+        ccopy(mid_ref.at[g, chips[2]], g, 3).start()
+
+    def at(k, fn):
+        if k == 0:
+            fn(z)
+            return
+        @pl.when(z - k >= 0)
+        def _():
+            fn(z - k)
+        @pl.when(z + k < reps)
+        def _():
+            fn(z + k)
+
+    def arrive(k):
+        @pl.when(z - k >= 0)
+        def _():
+            g = z - k
+            zcopy(x_ref, g, True).wait_recv()
+            @pl.when(z < reps - 1)
+            def _():
+                zcopy(mid_ref.at[g, e], g, True).start()
+            spread(mid_ref.at[g, e], g)
+        @pl.when(z + k < reps)
+        def _():
+            g = z + k
+            zcopy(x_ref, g, False).wait_recv()
+            @pl.when(z > 0)
+            def _():
+                zcopy(mid_ref.at[g, e], g, False).start()
+            spread(mid_ref.at[g, e], g)
+
+    def ready(g):
+        for j in range(4):
+            ccopy(x_ref, g, j).wait_recv()
+
+    def load_x(i):
+        g, q = group_of(i // 4), chip_of(i % 4)
+        return pltpu.make_async_copy(mid_ref.at[g, pl.ds(2 * q, 2)], xbuf.at[i % 2], x_sem.at[i % 2])
+
+    def load_c(i):
+        g, q = group_of(i // 4), chip_of(i % 4)
+        return pltpu.make_async_copy(cot_ref.at[g, pl.ds(2 * q, 2)], cbuf.at[i % 2], c_sem.at[i % 2])
+
+    def keep(i, m):
+        g, q = group_of(i // 4), chip_of(i % 4)
+        place = pl.ds(pl.multiple_of((g * 4 + q) * 2 * rows, 2 * rows), 2 * rows)
+        return pltpu.make_async_copy(abuf.at[i % 2, m], (a_ref, b_ref, h_ref)[m].at[place], ab_sem.at[i % 2, m])
+
+    def compute(i):
+        slot = i % 2
+        lane = lax.broadcasted_iota(jnp.int32, (2 * rows, side_lanes), 1)
+        side = xbuf[slot, :, :, pl.ds(width, side_lanes)].reshape(2 * rows, side_lanes).astype(f32)
+
+        def one(j, cots):
+            cols = pl.ds(pl.multiple_of(j * F, F), F)
+            x = xbuf[slot, :, :, pl.ds(0, width)].reshape(2 * rows, width)
+            c = cbuf[slot].reshape(2 * rows, width)
+            index = e * exp_dev + j
+            w = jnp.sum(jnp.where((lane == index) | (lane == index + experts_all), side, 0.0), axis=1, keepdims=True)
+            ga = jnp.dot(x, wgu[0, :, cols], preferred_element_type=f32)
+            up = jnp.dot(x, wgu[1, :, cols], preferred_element_type=f32)
+            hc = lax.dot_general(c, wd[cols, :], NT, preferred_element_type=f32)
+            sigma = 1.0 / (1.0 + jnp.exp(-ga))
+            silu = ga * sigma
+            hid = (silu * up).astype(bf16).astype(f32)
+            hcw = hc * w
+            abuf[slot, 0, :, cols] = (hcw * up * (sigma * (1.0 + ga * (1.0 - sigma)))).astype(bf16)
+            abuf[slot, 1, :, cols] = (hcw * silu).astype(bf16)
+            abuf[slot, 2, :, cols] = (hid * w).astype(bf16)
+            dots = jnp.sum(hid * hc, axis=1, keepdims=True)
+            return cots + jnp.where(lane == index, dots, 0.0)
+
+        cots = lax.fori_loop(0, exp_dev, one, jnp.zeros((2 * rows, side_lanes), f32))
+        pbuf[slot, :, :, pl.ds(width, side_lanes)] = cots.astype(bf16).reshape(2, rows, side_lanes)
+        block = min(512, width)
+
+        @pl.loop(0, width // block)
+        def _(n):
+            cut = pl.ds(pl.multiple_of(n * block, block), block)
+            t = lax.dot_general(abuf[slot, 0], wgu[0, cut, :], NT, preferred_element_type=f32)
+            t = t + lax.dot_general(abuf[slot, 1], wgu[1, cut, :], NT, preferred_element_type=f32)
+            pbuf[slot, :, :, cut] = t.astype(bf16).reshape(2, rows, block)
+            t = jnp.dot(abuf[slot, 2], wd[:, cut], preferred_element_type=f32)
+            cut = pl.ds(pl.multiple_of(W1 + n * block, 128), block)
+            pbuf[slot, :, :, cut] = t.astype(bf16).reshape(2, rows, block)
+
+    def sibcopy(i):
+        return pltpu.make_async_remote_copy(
+            src_ref=pbuf.at[i % 2, 1 - core], dst_ref=sib_in.at[i % 4], send_sem=ss.at[i], recv_sem=sr.at[i],
+            device_id={"rep": z, "ep": sib}, device_id_type=MESH)
+
+    def hcopy(s, j):
+        part = pl.ds(half * j, half)
+        return pltpu.make_async_remote_copy(
+            src_ref=sendbuf.at[0, part], dst_ref=relay_in.at[s, j], send_sem=hs.at[s, j], recv_sem=hr.at[s, j],
+            device_id={"rep": z, "ep": chips[j]}, device_id_type=MESH)
+
+    def qcopy(s, j):
+        return pltpu.make_async_remote_copy(
+            src_ref=sendbuf.at[1 + j], dst_ref=(xin_ref, yin_ref)[j].at[s], send_sem=qs.at[s, j], recv_sem=qr.at[s, j],
+            device_id={"rep": z, "ep": chips[j]}, device_id_type=MESH)
+
+    def fcopy(s, g):
+        return pltpu.make_async_remote_copy(
+            src_ref=rbuf.at[s % 2], dst_ref=zin_ref.at[z], send_sem=fs.at[s], recv_sem=fr.at[z],
+            device_id={"rep": g, "ep": e}, device_id_type=MESH)
+
+    step = 16
+
+    def add(out, terms, count=rows):
+        @pl.loop(0, count // step)
+        def _(i):
+            r = pl.ds(pl.multiple_of(i * step, step), step)
+            t = terms[0][r, :].astype(f32)
+            for other in terms[1:]:
+                t = t + other[r, :].astype(f32)
+            out[r, :] = t.astype(out.dtype)
+
+    def finish(i):
+        s, k = i // 4, i % 4
+        sibcopy(i).wait_recv()
+        mine, other = pbuf.at[i % 2, core], sib_in.at[i % 4]
+        lower, upper = pl.ds(0, half), pl.ds(half, half)
+        @pl.when(k == 1)
+        def _():
+            add(ownbuf.at[s % 2], (mine, other))
+        @pl.when(k == 0)
+        def _():
+            @pl.when(s > 0)
+            def _():
+                hcopy(s - 1, 0).wait_send()
+                hcopy(s - 1, 1).wait_send()
+            add(sendbuf.at[0], (mine, other))
+            hcopy(s, 0).start()
+            hcopy(s, 1).start()
+        @pl.when(k == 2)
+        def _():
+            @pl.when(s > 0)
+            def _():
+                qcopy(s - 1, 0).wait_send()
+            add(sendbuf.at[1, lower], (mine.at[lower], other.at[lower]), half)
+            hcopy(s, 1).wait_recv()
+            add(sendbuf.at[1, upper], (mine.at[upper], other.at[upper], relay_in.at[s, 1]), half)
+            qcopy(s, 0).start()
+        @pl.when(k == 3)
+        def _():
+            @pl.when(s > 0)
+            def _():
+                qcopy(s - 1, 1).wait_send()
+            add(sendbuf.at[2, upper], (mine.at[upper], other.at[upper]), half)
+            hcopy(s, 0).wait_recv()
+            add(sendbuf.at[2, lower], (mine.at[lower], other.at[lower], relay_in.at[s, 0]), half)
+            qcopy(s, 1).start()
+
+    def load_t(src, m):
+        return pltpu.make_async_copy(src, tmp.at[m], t_sem.at[m])
+
+    def total(s):
+        for j in range(2):
+            qcopy(s, j).wait_recv()
+            load_t((xin_ref, yin_ref)[j].at[s], j).start()
+        for j in range(2):
+            load_t((xin_ref, yin_ref)[j].at[s], j).wait()
+
+    def plane_sum(s):
+        total(s)
+        @pl.when(s >= 2)
+        def _():
+            fcopy(s - 2, group_of(s - 2)).wait_send()
+        add(rbuf.at[s % 2], (ownbuf.at[s % 2], tmp.at[0], tmp.at[1]))
+        fcopy(s, group_of(s)).start()
+
+    @pl.when(z < reps - 1)
+    def _():
+        zcopy(x_ref, z, True).start()
+    @pl.when(z > 0)
+    def _():
+        zcopy(x_ref, z, False).start()
+    spread(x_ref, z)
+    arrive(1)
+    pass_on(z)
+    arrive(2)
+    at(1, pass_on)
+    finish_in(z)
+    arrive(3)
+    at(2, pass_on)
+    at(1, finish_in)
+    for w in weights:
+        w.wait()
+    ready(group_of(0))
+    load_x(0).start()
+    load_c(0).start()
+
+    @pl.loop(0, steps)
+    def _(i):
+        load_x(i).wait()
+        load_c(i).wait()
+        @pl.when(i == 3)
+        def _():
+            at(3, pass_on)
+            at(2, finish_in)
+        @pl.when(i == 7)
+        def _():
+            at(3, finish_in)
+        @pl.when(i == steps - 5)
+        def _():
+            local.wait()
+        @pl.when(i < steps - 1)
+        def _():
+            @pl.when(i % 4 == 3)
+            def _():
+                ready(group_of(i // 4 + 1))
+            load_x(i + 1).start()
+            load_c(i + 1).start()
+        @pl.when(i >= 2)
+        def _():
+            sibcopy(i - 2).wait_send()
+            for m in range(3):
+                keep(i - 2, m).wait()
+        compute(i)
+        sibcopy(i).start()
+        for m in range(3):
+            keep(i, m).start()
+        @pl.when(i >= 1)
+        def _():
+            finish(i - 1)
+        @pl.when((i % 4 == 3) & (i >= 7) & (i < steps - 1))
+        def _():
+            plane_sum(i // 4 - 1)
+
+    for i in (steps - 2, steps - 1):
+        sibcopy(i).wait_send()
+        for m in range(3):
+            keep(i, m).wait()
+    finish(steps - 1)
+    plane_sum(reps - 2)
+
+    blocks = width // 256
+    halves = wgu.shape[1]
+
+    def resident(src, m):
+        return pltpu.make_async_copy(src.at[pl.ds(m * halves, halves)], wgu.at[m], w_sem.at[m])
+
+    def load_col(src, n):
+        return pltpu.make_async_copy(src.at[:, :, :, pl.ds(pl.multiple_of(n * 256, 256), 256)], colbuf.at[n % 2], col_sem.at[n % 2])
+
+    def product(n, m):
+        left = colbuf[n % 2, pl.ds(m * (reps // 2), reps // 2)].reshape(halves, 256)
+        return left, wgu[m]
+
+    def grad_rows(src, out):
+        def store(n, j):
+            per = width // reps
+            place = pl.ds(pl.multiple_of((n * 256) % per, 256), 256)
+            return pltpu.make_async_copy(gst.at[n % 2, j], out.at[(n * 256) // per, j, place], g_sem.at[n % 2, j])
+        for m in range(2):
+            resident(src, m).start()
+        load_col(mid_ref, 0).start()
+        for m in range(2):
+            resident(src, m).wait()
+        @pl.loop(0, blocks)
+        def _(n):
+            load_col(mid_ref, n).wait()
+            @pl.when(n < blocks - 1)
+            def _():
+                load_col(mid_ref, n + 1).start()
+            @pl.when(n >= 2)
+            def _():
+                for j in range(exp_dev):
+                    store(n - 2, j).wait()
+            t = jnp.zeros((256, EF), f32)
+            for m in range(2):
+                left, right = product(n, m)
+                t = t + lax.dot_general(left, right, TN, preferred_element_type=f32)
+            for j in range(exp_dev):
+                gst[n % 2, j] = t[:, j * F:(j + 1) * F].astype(bf16)
+                store(n, j).start()
+        for n in (blocks - 2, blocks - 1):
+            for j in range(exp_dev):
+                store(n, j).wait()
+
+    def grad_down():
+        def store(n):
+            return pltpu.make_async_copy(dst.at[n % 2], dout_ref.at[:, :, pl.ds(pl.multiple_of(n * 256, 256), 256)], g_sem.at[n % 2, 0])
+        for m in range(2):
+            resident(h_ref, m).start()
+        load_col(cot_ref, 0).start()
+        for m in range(2):
+            resident(h_ref, m).wait()
+        @pl.loop(0, blocks)
+        def _(n):
+            load_col(cot_ref, n).wait()
+            @pl.when(n < blocks - 1)
+            def _():
+                load_col(cot_ref, n + 1).start()
+            @pl.when(n >= 2)
+            def _():
+                store(n - 2).wait()
+            t = jnp.zeros((EF, 256), f32)
+            for m in range(2):
+                left, right = product(n, m)
+                t = t + lax.dot_general(right, left, TN, preferred_element_type=f32)
+            dst[n % 2] = t.reshape(exp_dev, F, 256)
+            store(n).start()
+        for n in (blocks - 2, blocks - 1):
+            store(n).wait()
+
+    grad_rows(a_ref, gout_ref)
+    grad_rows(b_ref, uout_ref)
+    grad_down()
+
+    last = reps - 1
+    total(last)
+    for d in range(1, reps):
+        src = (z + d) % reps
+        pltpu.make_async_remote_copy(
+            src_ref=rbuf.at[0], dst_ref=zin_ref.at[src], send_sem=fs.at[last], recv_sem=fr.at[src],
+            device_id={"rep": src, "ep": e}, device_id_type=MESH).wait_recv()
+        load_t(zin_ref.at[src], 1 + d).start()
+    for d in range(1, reps):
+        load_t(zin_ref.at[(z + d) % reps], 1 + d).wait()
+    fcopy(reps - 3, group_of(reps - 3)).wait_send()
+    add(rbuf.at[(reps - 3) % 2], (ownbuf.at[last % 2], *(tmp.at[m] for m in range(reps + 1))))
+    outs = (
+        pltpu.make_async_copy(rbuf.at[(reps - 3) % 2, :, pl.ds(0, W1)], row_ref, o_sem.at[0]),
+        pltpu.make_async_copy(rbuf.at[(reps - 3) % 2, :, pl.ds(W1, width)], moe_ref, o_sem.at[1]),
+    )
+    for o in outs:
+        o.start()
+    for o in outs:
+        o.wait()
+    fcopy(reps - 2, group_of(reps - 2)).wait_send()
+    for j in range(2):
+        hcopy(last, j).wait_send()
+        qcopy(last, j).wait_send()
+    for g in range(reps):
+        for j in range(4):
+            ccopy(x_ref, g, j).wait_send()
+        for j in range(2):
+            pcopy(x_ref, g, j).wait_send()
+            relay(g, j, chips[j]).wait_send()
+        @pl.when((z < reps - 1) & (z >= g))
+        def _():
+            zcopy(x_ref, g, True).wait_send()
+        @pl.when((z > 0) & (z <= g))
+        def _():
+            zcopy(x_ref, g, False).wait_send()
+
+
+def moe(x, cot_all, eg, eu, ed, experts_all, cid):
+    reps, eps, rows, width = cot_all.shape
+    W1 = x.shape[1]
+    side = W1 - width
+    WP = W1 + width
+    exp_dev, _, ff = eg.shape
+    F = ff // reps
+    EF = exp_dev * F
+    f32, bf16 = jnp.float32, jnp.bfloat16
+    D, V = pltpu.SemaphoreType.DMA, pltpu.VMEM
+    S = jax.ShapeDtypeStruct
+    tokens = reps * eps * rows
+    steps = 4 * reps
+    outs = (
+        S((rows, W1), bf16), S((rows, width), bf16),
+        S((reps, exp_dev, width // reps, F), bf16), S((reps, exp_dev, width // reps, F), bf16), S((exp_dev, F, width), f32),
+        S((reps, eps, rows, W1), bf16), S((tokens, EF), bf16), S((tokens, EF), bf16), S((tokens, EF), bf16),
+        S((reps, rows, WP), bf16), S((reps, rows, WP), bf16), S((reps, rows, WP), bf16),
+    )
+    return pl.pallas_call(
+        partial(moe_kernel, reps, side, experts_all),
+        out_shape=outs,
+        in_specs=[pl.BlockSpec(memory_space=pl.ANY)] * 5,
+        out_specs=[pl.BlockSpec(memory_space=pl.ANY)] * len(outs),
+        scratch_shapes=[
+            V((2, width, EF), bf16), V((EF, width), bf16),
+            V((2, 2, rows, W1), bf16), V((2, 2, rows, width), bf16),
+            V((2, 3, 2 * rows, EF), bf16), V((2, 2, rows, WP), bf16), V((4, rows, WP), bf16),
+            V((reps, 2, rows // 2, WP), bf16), V((3, rows, WP), bf16), V((2, rows, WP), bf16), V((2, rows, WP), bf16),
+            V((5, rows, WP), bf16), V((2, reps, eps, rows, 256), bf16),
+            V((2, exp_dev, 256, F), bf16), V((2, exp_dev, F, 256), f32),
+            D, D((3 * exp_dev,)), D((2,)), D((2,)), D((2, 3)), D((5,)), D((2,)), D((2, exp_dev)), D((2,)),
+            D((2, reps)), D((reps,)), D((reps, 4)), D((reps, 4)), D((reps, 4)), D((reps, 4)),
+            D((steps,)), D((steps,)), D((reps, 2)), D((reps, 2)), D((reps, 2)), D((reps, 2)), D((reps,)), D((reps,)),
+        ],
+        compiler_params=pltpu.CompilerParams(collective_id=cid, has_side_effects=True, vmem_limit_bytes=63 * 2**20),
+    )(x, cot_all, eg, eu, ed)[:5]
+
+
 def gather_block(block, axes):
     return lax.all_gather(block, axes, axis=0, tiled=True)
 
@@ -704,7 +1187,6 @@
     heads_dev = width // head_dim // ep_count
     slice_width = heads_dev * head_dim
     rows_dev = query_weight.shape[0]
-    ff_slice = ff_width // rep_count
     score_scale = head_dim ** (-0.5)
     core = ep_index % 2
     every = ("rep", "ep")
@@ -750,7 +1232,7 @@
         jnp.concatenate([out_other, out_own], axis=1),
     ).reshape(slice_width, width)
 
-    cot_all = all_gather(cotangent, rep_count, ep_count, True, 0).reshape(-1, width)
+    cot_all = all_gather(cotangent, rep_count, ep_count, True, 0)
     tokens_group = (
         all_gather(tokens, rep_count, ep_count, False, 1).reshape(group_rows, width).astype(f32)
     )
@@ -791,59 +1273,19 @@
     side = jnp.concatenate(
         [weight_high, weight_low, jnp.zeros((tok_dev, 128 - 2 * experts_all), bf16)], axis=1
     )
-    sent = all_gather(
-        jnp.concatenate([mid_low, side], axis=1), rep_count, ep_count, True, 3
-    ).reshape(-1, width + 128)
-    mid_all = sent[:, :width]
-    side_all = sent[:, width:]
-    weight_own = lax.dynamic_slice_in_dim(side_all, ep_index * exp_dev, exp_dev, axis=1).astype(
-        f32
-    ) + lax.dynamic_slice_in_dim(
-        side_all, experts_all + ep_index * exp_dev, exp_dev, axis=1
-    ).astype(f32)
-    gate_slice = lax.dynamic_slice_in_dim(expert_gate, rep_index * ff_slice, ff_slice, axis=2)
-    up_slice = lax.dynamic_slice_in_dim(expert_up, rep_index * ff_slice, ff_slice, axis=2)
-    down_slice = lax.dynamic_slice_in_dim(expert_down, rep_index * ff_slice, ff_slice, axis=1)
-    gate_flat = gate_slice.transpose(1, 0, 2).reshape(width, exp_dev * ff_slice)
-    up_flat = up_slice.transpose(1, 0, 2).reshape(width, exp_dev * ff_slice)
-    down_flat = down_slice.reshape(exp_dev * ff_slice, width)
-    gate_part = jnp.dot(mid_all, gate_flat, preferred_element_type=f32)
-    up_part = jnp.dot(mid_all, up_flat, preferred_element_type=f32)
-    down_cot = jnp.dot(cot_all, down_flat.T, preferred_element_type=f32)
-    weight_wide = jnp.repeat(weight_own, ff_slice, axis=1)
-    sigma = jax.nn.sigmoid(gate_part)
-    silu = gate_part * sigma
-    hidden = (silu * up_part).astype(bf16).astype(f32)
-    hidden_weighted = (hidden * weight_wide).astype(bf16)
-    hidden_cot = weight_wide * down_cot
-    a_cot = (hidden_cot * up_part * (sigma * (1 + gate_part * (1 - sigma)))).astype(bf16)
-    b_cot = (hidden_cot * silu).astype(bf16)
-    row_part = (
-        jnp.dot(a_cot, gate_flat.T, preferred_element_type=f32)
-        + jnp.dot(b_cot, up_flat.T, preferred_element_type=f32)
-    ).astype(bf16)
-    gate_cot_own = jnp.sum((hidden * down_cot).reshape(-1, exp_dev, ff_slice), axis=2)
-    gate_cot_part = lax.dynamic_update_slice_in_dim(
-        jnp.zeros((gate_cot_own.shape[0], 128), bf16),
-        gate_cot_own.astype(bf16),
-        ep_index * exp_dev,
-        axis=1,
-    )
-    row_sum = reduce_scatter(
-        jnp.concatenate([row_part, gate_cot_part], axis=1), rep_count, ep_count, True, 4
-    )
-    moe_part = jnp.dot(hidden_weighted, down_flat, preferred_element_type=f32).astype(bf16)
-    moe_out = reduce_scatter(moe_part, rep_count, ep_count, True, 5).astype(f32)
+    row_sum, moe_sum, gate_term, up_term, down_w_grad = moe(
+        jnp.concatenate([mid_low, side], axis=1),
+        cot_all,
+        expert_gate,
+        expert_up,
+        expert_down,
+        experts_all,
+        3,
+    )
+    moe_out = moe_sum.astype(f32)
     block_out = (after_attn + moe_out).astype(bf16)
-    gate_term = jnp.dot(mid_all.T, a_cot, preferred_element_type=f32)
-    up_term = jnp.dot(mid_all.T, b_cot, preferred_element_type=f32)
-    down_w_grad = jnp.dot(hidden_weighted.T, cot_all, preferred_element_type=f32).reshape(
-        exp_dev, ff_slice, width
-    )
-
-    def rows_of(term):
-        parts = term.astype(bf16).reshape(rep_count, width // rep_count, exp_dev, ff_slice)
-        parts = parts.transpose(0, 2, 1, 3)
+
+    def rows_of(parts):
         got = lax.all_to_all(parts, "rep", split_axis=0, concat_axis=0, tiled=True)
         return got.transpose(1, 2, 0, 3).reshape(exp_dev, width // rep_count, ff_width).astype(f32)
 

time: 1100 us -> 1040 us (0.945)
  waiting for transfers between devices: 8.57 us -> 260 us
  matrix products: 256 us -> 57.3 us
  Pallas kernels: 528 us -> 474 us
  local copies, waits for them, and re-layouts: 120 us -> 68.9 us
  other arithmetic: 76 us -> 53.8 us
    pallas_call x0 -> x1, Pallas kernels: none -> 287 us  [moe(): pl.pallas_call(partial(moe_kernel, reps, side, experts_all), out_shape=ou...]
    pallas_call x4 -> x2, Pallas kernels: 306 us -> 65 us  [reduce_scatter(): pl.pallas_call(partial(rs_kernel, reps, across), out_shape=jax.ShapeDtype...]
    dot_general x9 -> x0, matrix products: 199 us -> none  [the longest x1 32.3 us: on_device_split(): down_cot = jnp.dot(cot_all, down_flat.T, preferred_element_type=f32)]
    reduce_scatter x3, waiting for transfers between devices: 0.02 us -> 125 us  [scatter_sum(): return lax.psum_scatter(partial_sums, axes, scatter_dimension=0, tiled=True)]
    all_to_all x2, waiting for transfers between devices: 0.01 us -> 122 us  [rows_of(): got = lax.all_to_all(parts, 'rep', split_axis=0, concat_axis=0, tiled=True)]
    pallas_call x4 -> x3, Pallas kernels: 222 us -> 122 us  [all_gather(): pl.pallas_call(partial(ag_kernel, reps, across), out_shape=jax.ShapeDtype...]
    concatenate x1 -> x0, local copies, waits for them, and re-layouts: 22.2 us -> none  [on_device_split(): jnp.concatenate([row_part, gate_cot_part], axis=1)]
    concatenate x1 -> x0, other arithmetic: 14.2 us -> none  [on_device_split(): jnp.concatenate([row_part, gate_cot_part], axis=1)]
  transfers between devices with their start and end apart: 15 -> 14, of which waited for: 3 -> 8; matrix products, arithmetic and copies ran while one was open for 20% -> 11% of each run, Pallas kernels for 25% -> 13%
where the time goes in v3:
time: 1040 us; the launch traced here: 1030 us
  Pallas kernels  474 us (46%)
  waiting for transfers between devices  260 us (25%)
  local copies, waits for them, and re-layouts  68.9 us (7%)
  blocking collectives  59.8 us (6%)
  matrix products  57.3 us (6%)
  other arithmetic  53.8 us (5%)
  starting transfers between devices  37 us (4%)
  between operations  15.2 us (1%)
    pallas_call x1, Pallas kernels, moe(): pl.pallas_call(partial(moe_kernel, reps, side, experts_all), out_shape=ou...  287 us
    reduce_scatter x3, waiting for transfers between devices, scatter_sum(): return lax.psum_scatter(partial_sums, axes, scatter_dimension=0, tiled=True)  125 us
    all_to_all x2, waiting for transfers between devices, rows_of(): got = lax.all_to_all(parts, 'rep', split_axis=0, concat_axis=0, tiled=True)  122 us
    pallas_call x3, Pallas kernels, all_gather(): pl.pallas_call(partial(ag_kernel, reps, across), out_shape=jax.ShapeDtype...  122 us
    pallas_call x2, Pallas kernels, reduce_scatter(): pl.pallas_call(partial(rs_kernel, reps, across), out_shape=jax.ShapeDtype...  65 us
    all_gather x2, blocking collectives, gather_block(): return lax.all_gather(block, axes, axis=0, tiled=True)  50.5 us
    unnamed x88, local copies, waits for them, and re-layouts  25.4 us
  transfers between devices with their start and end apart: 14, of which 8 were waited for; matrix products, arithmetic and copies ran while one was open for 11% of the time, Pallas kernels for 13%

profile of v3, /device:TPU:0, one launch (start us, length us, event | category | flops | bytes accessed | tf_op | source)
XLA Modules:
  0.0 1026.0 jit_solution(3794518245994451724)
XLA Ops:
  10.1 5.2 all-to-all-start
  17.5 4.7 all-to-all-done
  22.3 3.4 all-to-all-start.1
  26.3 6.2 all-to-all-done.1
  32.5 9.3 all_to_all.40
  43.2 41.3 %all_gather.12 = bf16[512,128]{1,0:T(8,128)(2,1)S(1)} all-gather(bf16[16,128]{1,0:T(8,128)(2,1)S(1)} %bitcast.141), channel_id=1, replica_groups=mesh['rep'=4,'ep'=8] {'rep','ep'}, dimensions={0}, use_global_device_ids=true | all-gather | bytes 135168 | tf_op jit(solution)/shard_map/all_gather | solution.py:1153
  84.8 24.5 %shard_map.230 = bf16[1,8,128,2048]{3,2,1,0:T(8,128)(2,1)} custom-call(bf16[128,2048]{1,0:T(8,128)(2,1)} %x_ref.2), custom_call_target="tpu_custom_call" | custom-call | tf_op jit(solution)/shard_map/pallas_call | solution.py:509
  109.5 1.6 reshape.407
  111.2 74.7 %shard_map.232.cot_ref = bf16[4,8,128,2048]{3,2,1,0:T(8,128)(2,1)} custom-call(bf16[128,2048]{1,0:T(8,128)(2,1)} %x_ref.3), custom_call_target="tpu_custom_call" | custom-call | tf_op jit(solution)/shard_map/pallas_call | solution.py:509
  185.9 9.2 all-gather
  195.4 3.1 multiply_reduce_fusion.1
  198.5 1.9 multiply_cosine_fusion
  200.4 1.6 broadcast_compare_fusion
  202.0 1.3 dynamic-slice_bitcast_fusion.3
  203.7 5.2 fusion.2
  210.2 6.4 fusion.56
  219.2 1.9 copy.162
  221.9 2.0 subtract_convert_fusion.1
  223.9 8.8 fusion.53
  232.8 4.2 fusion.13
  237.0 3.3 bitcast_convert_fusion
  240.3 31.5 %shard_map.231 = bf16[128,2048]{1,0:T(8,128)(2,1)} custom-call(bf16[1,4,2,128,2048]{4,3,2,1,0:T(8,128)(2,1)} %bitcast.110), custom_call_target="tpu_custom_call" | custom-call | tf_op jit(solution)/shard_map/pallas_call | solution.py:657
  271.9 1.3 multiply_reduce_fusion.8
  273.2 1.3 multiply_convert_fusion.1
  276.3 287.2 %shard_map.233 = (bf16[128,2176]{1,0:T(8,128)(2,1)}, bf16[128,2048]{1,0:T(8,128)(2,1)}, bf16[4,3,512,256]{3,2,1,0:T(8,128)(2,1)}, bf16[4,3,512,256]{3,2,1,0:T(8,...) custom-call(bf16[128,2176]{1,0:T(8,128)(2,1)} %concatenate.42.x_ref,, ...), custom_call_target="tpu_custom_call" | custom-call | tf_op jit(solution)/shard_map/pallas_call | solution.py:1132
  564.4 2.1 multiply_reduce_fusion.4
  567.4 2.5 fusion.47.x_ref
  569.9 22.4 %shard_map.234 = bf16[1,8,128,2048]{3,2,1,0:T(8,128)(2,1)} custom-call(bf16[128,2048]{1,0:T(8,128)(2,1)} %fusion.47.x_ref), custom_call_target="tpu_custom_call" | custom-call | tf_op jit(solution)/shard_map/pallas_call | solution.py:509
  592.4 3.5 convolution_convert_fusion.3
  595.9 4.9 multiply_reduce_fusion
  601.8 2.6 multiply_convert_fusion
  604.4 1.3 fusion.11
  605.8 2.0 fusion.12
  607.8 2.3 fusion.16
  610.1 1.9 multiply_add_fusion.3
  614.0 12.1 %all-to-all-start.6 = ((bf16[4,3,512,256]{3,2,1,0:T(8,128)(2,1)}), bf16[4,3,512,256]{3,2,1,0:T(8,128)(2,1)}, u32[]{:S(2)}, u32[]{:S(2)}) async-start(bf16[4,3,512,256]{3,2,1,0:T(8,128)(2,1)} %get-tuple-element.18), calls=%async_computation.9 | async-start | bytes 6291456 | tf_op jit(solution)/shard_map/all_to_all | solution.py:1289
  626.1 2.4 multiply_reduce_fusion.3
  628.6 5.0 fusion.23
  633.5 1.2 copy.179
  634.8 1.2 copy.185
  636.1 7.7 convolution_convert_fusion.1
  643.8 105.0 %all-to-all-done.6 = bf16[4,3,512,256]{3,2,1,0:T(8,128)(2,1)} async-done(((bf16[4,3,512,256]{3,2,1,0:T(8,128)(2,1)}), bf16[4,3,512,256]{3,2,1,0:T(8,128)(2,1)}, u32[]{:S(2)}, u32[]{:S(2)}) %all-to-all-start.6) | async-done | bytes 3145760 | tf_op jit(solution)/shard_map/all_to_all | solution.py:1289
  748.8 4.6 all-to-all-start.7
  755.2 7.7 convolution_convert_fusion
  762.9 33.4 %shard_map.235 = bf16[128,2048]{1,0:T(8,128)(2,1)} custom-call(bf16[1,4,2,128,2048]{4,3,2,1,0:T(8,128)(2,1)} %bitcast.117), custom_call_target="tpu_custom_call" | custom-call | tf_op jit(solution)/shard_map/pallas_call | solution.py:657
  796.4 1.3 convolution_convert_fusion.2
  801.8 2.8 reshape.411
  804.6 2.2 fusion.49
  807.5 17.4 %all-to-all-done.7 = bf16[4,3,512,256]{3,2,1,0:T(8,128)(2,1)} async-done(((bf16[4,3,512,256]{3,2,1,0:T(8,128)(2,1)}), bf16[4,3,512,256]{3,2,1,0:T(8,128)(2,1)}, u32[]{:S(2)}, u32[]{:S(2)}) %all-to-all-start.7) | async-done | bytes 3145760 | tf_op jit(solution)/shard_map/all_to_all | solution.py:1289
  825.0 3.9 all-to-all-start.3
  828.8 3.5 fusion.25
  832.3 101.7 %reduce-scatter.8.cloned.1.call-done = f32[16,128]{1,0:T(8,128)} async-done(((f32[512,128]{1,0:T(8,128)}), f32[16,128]{1,0:T(8,128)}) %reduce-scatter.8.cloned.1.call-update) | async-done | bytes 8208 | tf_op jit(solution)/shard_map/reduce_scatter | solution.py:1157
  934.8 1.2 slice.113
  936.8 23.2 %reduce-scatter.6.cloned.1.call-done = bf16[64,2048]{1,0:T(8,128)(2,1)} async-done(((bf16[256,2048]{1,0:T(8,128)(2,1)}), bf16[64,2048]{1,0:T(8,128)(2,1)}) %reduce-scatter.6.cloned.1.call-update) | async-done | bytes 262160 | tf_op jit(solution)/shard_map/reduce_scatter | solution.py:1157
  959.9 1.8 convert_element_type.249
  962.5 3.7 all-to-all-start.4
  966.1 5.3 convert_bitcast_fusion.1
  973.1 3.4 all-to-all-start.5
  976.5 5.2 convert_bitcast_fusion
  981.7 6.6 copy.191
  988.2 6.6 copy.194
  994.8 6.6 copy.192
  1001.3 6.6 copy.195
  1012.7 6.3 copy.226
  (180 shorter events, 34.6 us)
Async XLA Ops:
  7.2 18.6 %copy-start.31 = (bf16[64,2048]{1,0:T(8,128)(2,1)S(1)}, bf16[64,2048]{1,0:T(8,128)(2,1)}, u32[]{:S(2)}) copy-start(bf16[64,2048]{1,0:T(8,128)(2,1)} %param.19) | copy-start | bytes 786436
  7.2 194.8 %all-gather.6.cloned.1.call-start = ((), (), s32[]{:S(2)}) async-start(), calls=%async_computation.12 | async-start | bytes 1310720 | tf_op jit(solution)/shard_map/all_gather | solution.py:1153
  9.0 33.8 %copy-start.33 = (bf16[64,24]{0,1:T(8,128)(2,1)S(1)}, bf16[64,24]{0,1:T(8,128)(2,1)}, u32[]{:S(2)}) copy-start(bf16[64,24]{0,1:T(8,128)(2,1)} %param.21) | copy-start | bytes 9220
  9.1 34.0 %copy-start.34 = (bf16[136]{0:T(256)(128)(2,1)S(1)}, bf16[136]{0:T(256)(128)(2,1)}, u32[]{:S(2)}) copy-start(bf16[136]{0:T(256)(128)(2,1)} %param.22) | copy-start | bytes 820
  10.1 12.1 %all-to-all-start = ((bf16[8,64,256]{2,1,0:T(8,128)(2,1)}), bf16[8,64,256]{2,1,0:T(8,128)(2,1)S(1)}, u32[]{:S(2)}, u32[]{:S(2)}) async-start(bf16[8,64,256]{2,1,0:T(8,128)(2,1)} %reshape.391), calls=%async_computation | async-start | bytes 524288 | tf_op jit(solution)/shard_map/all_to_all | solution.py:1216
  22.3 10.3 %all-to-all-start.1 = ((bf16[8,64,256]{2,1,0:T(8,128)(2,1)}), bf16[8,64,256]{2,1,0:T(8,128)(2,1)S(1)}, u32[]{:S(2)}, u32[]{:S(2)}) async-start(bf16[8,64,256]{2,1,0:T(8,128)(2,1)} %reshape.393), calls=%async_computation.1 | async-start | bytes 524288 | tf_op jit(solution)/shard_map/all_to_all | solution.py:1216
  25.7 184.5 %all-gather.4.cloned.1.call-start = ((), (), s32[]{:S(2)}) async-start(), calls=%async_computation.11 | async-start | bytes 3932160 | tf_op jit(solution)/shard_map/all_gather | solution.py:1153
  26.3 83.0 %copy-start.36 = (s32[1,3]{1,0:T(1,128)S(1)}, s32[1,3]{1,0:T(1,128)}, u32[]{:S(2)}) copy-start(s32[1,3]{1,0:T(1,128)} %param.26) | copy-start | bytes 40
  41.9 69.2 %copy-start.32 = (s32[128,8]{0,1:T(8,128)S(1)}, s32[128,8]{0,1:T(8,128)}, u32[]{:S(2)}) copy-start(s32[128,8]{0,1:T(8,128)} %param.28) | copy-start | bytes 12292
  111.2 74.7 %copy-start.35 = (s32[128]{0:T(128)S(1)}, s32[128]{0:T(128)}, u32[]{:S(2)}) copy-start(s32[128]{0:T(128)} %param.27) | copy-start | bytes 1540
  111.2 74.7 %copy-start.37 = (s32[128]{0:T(128)S(1)}, s32[128]{0:T(128)}, u32[]{:S(2)}) copy-start(s32[128]{0:T(128)} %param.29) | copy-start | bytes 1540
  200.4 21.5 %copy-start.10 = (f32[1024,64]{1,0:T(8,128)}, f32[1024,64]{1,0:T(8,128)S(1)}, u32[]{:S(2)}) copy-start(f32[1024,64]{1,0:T(8,128)S(1)} %get-tuple-element.109) | copy-start | bytes 786436
  200.4 21.5 %copy-start.12 = (f32[1024,64]{1,0:T(8,128)}, f32[1024,64]{1,0:T(8,128)S(1)}, u32[]{:S(2)}) copy-start(f32[1024,64]{1,0:T(8,128)S(1)} %get-tuple-element.110) | copy-start | bytes 786436
  203.3 5.6 collective-permute-start
  219.2 4.7 copy-start.1
  221.1 2.8 copy-start.3
  223.9 8.8 copy-start.28
  232.8 4.2 copy-start.17
  237.0 3.3 copy-start.26
  240.3 31.6 %copy-start = (bf16[128,2048]{1,0:T(8,128)(2,1)S(1)}, bf16[128,2048]{1,0:T(8,128)(2,1)}, u32[]{:S(2)}) copy-start(bf16[128,2048]{1,0:T(8,128)(2,1)} %x_ref.2) | copy-start | bytes 1572868
  240.3 34.1 %copy-start.23 = (bf16[2048,24]{1,0:T(8,128)(2,1)S(1)}, bf16[2048,24]{1,0:T(8,128)(2,1)}, u32[]{:S(2)}) copy-start(bf16[2048,24]{1,0:T(8,128)(2,1)} %reshape.407) | copy-start | bytes 294916
  274.5 0.9 copy-start.8
  566.5 0.9 copy-start.15
  566.5 25.9 %copy-start.18 = (bf16[2,128,2048]{2,1,0:T(8,128)(2,1)S(1)}, bf16[2,128,2048]{2,1,0:T(8,128)(2,1)}, u32[]{:S(2)}) copy-start(bf16[2,128,2048]{2,1,0:T(8,128)(2,1)} %maximum_select_fusion) | copy-start | bytes 3145732
  592.3 3.6 copy-start.29
  595.9 4.9 slice-start
  595.9 5.8 slice-start.1
  601.8 2.6 copy-start.21
  601.8 2.6 copy-start.22
  604.4 1.4 copy-start.19
  604.4 1.4 copy-start.20
  607.8 2.3 copy-start.11
  607.8 2.3 copy-start.13
  610.1 2.9 copy-start.2
  612.1 1.0 copy-start.6
  612.1 1.9 copy-start.7
  613.0 13.1 %copy-start.4 = (f32[1024,2,128]{2,0,1:T(8,128)S(1)}, f32[1024,2,128]{2,0,1:T(8,128)}, u32[]{:S(2)}) copy-start(f32[1024,2,128]{2,0,1:T(8,128)} %copy-done.3) | copy-start | bytes 3145732
  614.0 134.8 %all-to-all-start.6 = ((bf16[4,3,512,256]{3,2,1,0:T(8,128)(2,1)}), bf16[4,3,512,256]{3,2,1,0:T(8,128)(2,1)}, u32[]{:S(2)}, u32[]{:S(2)}) async-start(bf16[4,3,512,256]{3,2,1,0:T(8,128)(2,1)} %get-tuple-element.18), calls=%async_computation.9 | async-start | bytes 6291456 | tf_op jit(solution)/shard_map/all_to_all | solution.py:1289
  626.1 175.8 %reduce-scatter.4.cloned.1.call-start = ((), (), s32[]{:S(2)}) async-start(), calls=%async_computation.13 | async-start | bytes 3932160 | tf_op jit(solution)/shard_map/reduce_scatter | solution.py:1157
  636.0 7.8 copy-start.30
  643.8 109.7 %copy-start.9 = (bf16[128,2048]{1,0:T(8,128)(2,1)S(1)}, bf16[128,2048]{1,0:T(8,128)(2,1)}, u32[]{:S(2)}) copy-start(bf16[128,2048]{1,0:T(8,128)(2,1)} %copy-done.8) | copy-start | bytes 1572868
  748.8 76.1 %all-to-all-start.7 = ((bf16[4,3,512,256]{3,2,1,0:T(8,128)(2,1)}), bf16[4,3,512,256]{3,2,1,0:T(8,128)(2,1)}, u32[]{:S(2)}, u32[]{:S(2)}) async-start(bf16[4,3,512,256]{3,2,1,0:T(8,128)(2,1)} %get-tuple-element.19), calls=%async_computation.10 | async-start | bytes 6291456 | tf_op jit(solution)/shard_map/all_to_all | solution.py:1289
  753.5 180.5 %reduce-scatter.8.cloned.1.call-start = ((), (), s32[]{:S(2)}) async-start(), calls=%async_computation.15 | async-start | bytes 270336 | tf_op jit(solution)/shard_map/reduce_scatter | solution.py:1157
  762.9 33.4 %copy-start.16 = (bf16[1,8,128,2048]{3,2,1,0:T(8,128)(2,1)S(1)}, bf16[1,8,128,2048]{3,2,1,0:T(8,128)(2,1)}, u32[]{:S(2)}) copy-start(bf16[1,8,128,2048]{3,2,1,0:T(8,128)(2,1)} %shard_map.234) | copy-start | bytes 12582916
  762.9 33.4 %copy-start.27 = (bf16[2,128,1024]{2,1,0:T(8,128)(2,1)S(1)}, bf16[2,128,1024]{2,1,0:T(8,128)(2,1)}, u32[]{:S(2)}) copy-start(bf16[2,128,1024]{2,1,0:T(8,128)(2,1)} %copy-done.26) | copy-start | bytes 1572868
  796.3 2.4 copy-start.14
  798.5 2.1 collective-permute-start.1
  800.4 159.6 %reduce-scatter.6.cloned.1.call-start = ((), (), s32[]{:S(2)}) async-start(), calls=%async_computation.14 | async-start | bytes 1310720 | tf_op jit(solution)/shard_map/reduce_scatter | solution.py:1157
  801.8 27.1 %copy-start.5 = (bf16[128,2048]{1,0:T(8,128)(2,1)S(1)}, bf16[128,2048]{1,0:T(8,128)(2,1)}, u32[]{:S(2)}) copy-start(bf16[128,2048]{1,0:T(8,128)(2,1)} %shard_map.231) | copy-start | bytes 1572868
  806.8 154.9 %copy-start.25 = (bf16[8,64,1,256]{3,2,1,0:T(2,128)(2,1)S(1)}, bf16[8,64,1,256]{3,2,1,0:T(2,128)(2,1)}, u32[]{:S(2)}) copy-start(bf16[8,64,1,256]{3,2,1,0:T(2,128)(2,1)} %get-tuple-element.93) | copy-start | bytes 786436
  825.0 137.5 %all-to-all-start.3 = ((bf16[8,64,256]{2,1,0:T(8,128)(2,1)}), bf16[8,64,256]{2,1,0:T(8,128)(2,1)S(1)}, u32[]{:S(2)}, u32[]{:S(2)}) async-start(bf16[8,64,256]{2,1,0:T(8,128)(2,1)} %bitcast.106), calls=%async_computation.4 | async-start | bytes 524288 | tf_op jit(solution)/shard_map/all_to_all | solution.py:1349
  962.5 10.6 %all-to-all-start.4 = ((bf16[8,64,256]{2,1,0:T(8,128)(2,1)}), bf16[8,64,256]{2,1,0:T(8,128)(2,1)S(1)}, u32[]{:S(2)}, u32[]{:S(2)}) async-start(bf16[8,64,256]{2,1,0:T(8,128)(2,1)} %bitcast.105), calls=%async_computation.5 | async-start | bytes 524288 | tf_op jit(solution)/shard_map/all_to_all | solution.py:1349
  966.1 5.3 copy-start.24
  973.1 38.1 %all-to-all-start.5 = ((bf16[8,64,256]{2,1,0:T(8,128)(2,1)}), bf16[8,64,256]{2,1,0:T(8,128)(2,1)S(1)}, u32[]{:S(2)}, u32[]{:S(2)}) async-start(bf16[8,64,256]{2,1,0:T(8,128)(2,1)} %bitcast.104), calls=%async_computation.6 | async-start | bytes 524288 | tf_op jit(solution)/shard_map/all_to_all | solution.py:1349
Sparse Core Ops, SparseCore 0:
  9.6 30.6 all-gather.5
  43.0 63.2 all-gather.3
  643.9 100.8 reduce-scatter.3
  800.5 133.4 reduce-scatter.7
  936.8 23.0 reduce-scatter.5

commit v4 on v3

--- a/solution.py
+++ b/solution.py
@@ -1015,7 +1015,7 @@
         def store(n, j):
             per = width // reps
             place = pl.ds(pl.multiple_of((n * 256) % per, 256), 256)
-            return pltpu.make_async_copy(gst.at[n % 2, j], out.at[(n * 256) // per, j, place], g_sem.at[n % 2, j])
+            return pltpu.make_async_copy(gst.at[n % 2, j], out.at[((n * 256) // per + reps - z) % reps, j, place], g_sem.at[n % 2, j])
         for m in range(2):
             resident(src, m).start()
         load_col(mid_ref, 0).start()
@@ -1147,6 +1147,257 @@
         ],
         compiler_params=pltpu.CompilerParams(collective_id=cid, has_side_effects=True, vmem_limit_bytes=63 * 2**20),
     )(x, cot_all, eg, eu, ed)[:5]
+
+
+def last_kernel(reps, eps, part_ref, qkv_ref, out_ref, tok_ref, cot_ref, gain_ref, gains_ref, router_ref,
+                input_ref, q_ref, k_ref, v_ref, o_ref, gsum_ref, rsum_ref,
+                own, sib_in, relay_in, xin, yin, wo, qown, zq, zo, fin, gath, mats, omat, tok, cot, gain,
+                gown, gin, gz, gmid, rown, rin, rz, rmid,
+                l_sem, ss, sr, hs, hr, qs, qr, ws, wr, zs, zr, zos, zor, ps, pr, gs, gr, gzs, gzr, rs, rr, rzs, rzr):
+    f32, bf16 = jnp.float32, jnp.bfloat16
+    z = lax.axis_index("rep")
+    e = lax.axis_index("ep")
+    core = e % 2
+    chip = e // 2
+    sib, chips = partners(e)
+    rows, width = tok_ref.shape
+    half = rows // 2
+    rows_dev = o_ref.shape[0]
+    heads_dev = out_ref.shape[0]
+    head_dim = width // (heads_dev * eps)
+    slice_width = heads_dev * head_dim
+
+    barrier = pltpu.get_barrier_semaphore()
+    for d in range(1, eps):
+        pl.semaphore_signal(barrier, inc=1, device_id={"rep": z, "ep": (e + d) % eps}, device_id_type=MESH)
+    for d in range(1, reps):
+        pl.semaphore_signal(barrier, inc=1, device_id={"rep": (z + d) % reps, "ep": e}, device_id_type=MESH)
+    loads = [
+        pltpu.make_async_copy(part_ref.at[:, core], own, l_sem.at[0]),
+        pltpu.make_async_copy(qkv_ref.at[z], qown, l_sem.at[1]),
+        pltpu.make_async_copy(out_ref.at[:, core], wo.at[core], l_sem.at[2]),
+        pltpu.make_async_copy(tok_ref, tok, l_sem.at[3]),
+        pltpu.make_async_copy(cot_ref, cot, l_sem.at[4]),
+        pltpu.make_async_copy(gain_ref, gain, l_sem.at[5]),
+        pltpu.make_async_copy(gains_ref, gown, l_sem.at[6]),
+        pltpu.make_async_copy(router_ref, rown, l_sem.at[7]),
+    ]
+    for c in loads:
+        c.start()
+    pl.semaphore_wait(barrier, eps - 1 + reps - 1)
+
+    def to_sib(src, dst, send, recv):
+        return pltpu.make_async_remote_copy(src_ref=src, dst_ref=dst, send_sem=send, recv_sem=recv,
+                                            device_id={"rep": z, "ep": sib}, device_id_type=MESH)
+
+    def to_chip(src, dst, send, recv, j):
+        return pltpu.make_async_remote_copy(src_ref=src, dst_ref=dst, send_sem=send, recv_sem=recv,
+                                            device_id={"rep": z, "ep": chips[j]}, device_id_type=MESH)
+
+    def to_plane(src, dst, send, recv, d):
+        return pltpu.make_async_remote_copy(src_ref=src, dst_ref=dst, send_sem=send, recv_sem=recv,
+                                            device_id={"rep": z, "ep": (e + d) % eps}, device_id_type=MESH)
+
+    def to_rep(src, dst, send, recv, d):
+        return pltpu.make_async_remote_copy(src_ref=src, dst_ref=dst, send_sem=send, recv_sem=recv,
+                                            device_id={"rep": (z + d) % reps, "ep": e}, device_id_type=MESH)
+
+    zcopies = [to_rep(qkv_ref.at[(z + d) % reps], zq.at[d - 1], zs.at[d - 1], zr.at[d - 1], d) for d in range(1, reps)]
+    ocopies = [to_rep(wo.at[((z + d) % reps) // heads_dev, (z + d) % heads_dev], zo.at[d - 1], zos.at[d - 1], zor.at[d - 1], d)
+               for d in range(1, reps)]
+    wcopy = to_sib(out_ref.at[:, 1 - core], wo.at[core], ws, wr)
+    order = (chips[2] // 2, chips[0] // 2, chips[1] // 2, chip)
+    scopies = [to_sib(part_ref.at[q, 1 - core], sib_in.at[q], ss.at[n], sr.at[n]) for n, q in enumerate(order)]
+    for c in scopies:
+        c.start()
+    wcopy.start()
+    for c in zcopies:
+        c.start()
+    step = 16
+
+    def add(out, terms, count):
+        @pl.loop(0, count // step)
+        def _(i):
+            r = pl.ds(pl.multiple_of(i * step, step), step)
+            t = terms[0][r, :].astype(f32)
+            for other in terms[1:]:
+                t = t + other[r, :].astype(f32)
+            out[r, :] = t.astype(out.dtype)
+
+    lower, upper = pl.ds(0, half), pl.ds(half, half)
+    hcopies = [to_chip(own.at[order[0], (lower, upper)[j]], relay_in.at[j], hs.at[j], hr.at[j], j) for j in range(2)]
+    qcopies = [to_chip(own.at[order[1 + j]], (xin, yin)[j], qs.at[j], qr.at[j], j) for j in range(2)]
+    loads[0].wait()
+    scopies[0].wait_recv()
+    d = own.at[order[0]]
+    add(d, (d, sib_in.at[order[0]]), rows)
+    for c in hcopies:
+        c.start()
+    for j in range(2):
+        mine, other = own.at[order[1 + j]], sib_in.at[order[1 + j]]
+        scopies[1 + j].wait_recv()
+        direct, through = ((lower, upper), (upper, lower))[j]
+        add(mine.at[direct], (mine.at[direct], other.at[direct]), half)
+        hcopies[1 - j].wait_recv()
+        add(mine.at[through], (mine.at[through], other.at[through], relay_in.at[1 - j]), half)
+        qcopies[j].start()
+    loads[2].wait()
+    wcopy.wait_recv()
+    for c in ocopies:
+        c.start()
+    scopies[3].wait_recv()
+    for c in loads[3:]:
+        c.wait()
+    for c in qcopies:
+        c.wait_recv()
+
+    gown[0:1, :] = jnp.zeros((1, width), f32)
+
+    @pl.loop(0, rows // step)
+    def _(i):
+        r = pl.ds(pl.multiple_of(i * step, step), step)
+        nc = (own[chip, r, :].astype(f32) + sib_in[chip, r, :].astype(f32) + xin[r, :].astype(f32) + yin[r, :].astype(f32))
+        t = tok[r, :].astype(f32)
+        scale = lax.rsqrt(jnp.mean(t * t, axis=-1, keepdims=True) + 1e-6)
+        unit = t * scale
+        scaled = nc * gain[0:1, :]
+        cot[r, :] = cot[r, :] + scale * (scaled - unit * jnp.mean(scaled * unit, axis=-1, keepdims=True))
+        gown[0:1, :] += jnp.sum(nc * unit, axis=0, keepdims=True)
+
+    done = [pltpu.make_async_copy(cot, input_ref, l_sem.at[8])]
+    done[0].start()
+
+    gcopies = [to_plane(gown, gin.at[d - 1], gs.at[d - 1], gr.at[d - 1], d) for d in range(1, eps)]
+    rcopies = [to_plane(rown.at[:, (e + d) % eps], rin.at[d - 1], rs.at[d - 1], rr.at[d - 1], d) for d in range(1, eps)]
+    for c in (*gcopies, *rcopies):
+        c.start()
+    for c in (*gcopies, *rcopies):
+        c.wait_recv()
+    t = gown[...]
+    for d in range(1, eps):
+        t = t + gin[d - 1]
+    gmid[...] = t
+    t = rown[:, e]
+    for d in range(1, eps):
+        t = t + rin[d - 1]
+    rmid[...] = t
+    gzcopies = [to_rep(gmid, gz.at[d - 1], gzs.at[d - 1], gzr.at[d - 1], d) for d in range(1, reps)]
+    rzcopies = [to_rep(rmid.at[(z + d) % reps], rz.at[d - 1], rzs.at[d - 1], rzr.at[d - 1], d) for d in range(1, reps)]
+    for c in (*gzcopies, *rzcopies):
+        c.start()
+
+    loads[1].wait()
+    for c in zcopies:
+        c.wait_recv()
+    for n in range(eps):
+        @pl.loop(0, rows_dev // step)
+        def _(i):
+            r = pl.ds(pl.multiple_of(i * step, step), step)
+            a = pl.ds(pl.multiple_of(n * rows_dev + i * step, step), step)
+            t = qown[a, :].astype(f32)
+            for d in range(reps - 1):
+                t = t + zq[d, a, :].astype(f32)
+            fin[n, r, :] = t.astype(bf16)
+    pcopies = [to_plane(fin.at[(e + d) % eps], gath.at[e], ps.at[d - 1], pr.at[d - 1], d) for d in range(1, eps)]
+    for c in pcopies:
+        c.start()
+    mine = pltpu.make_async_copy(fin.at[e], gath.at[e], l_sem.at[9])
+    mine.start()
+    for c in (*gzcopies, *rzcopies, *ocopies):
+        c.wait_recv()
+    for c in gcopies:
+        c.wait_send()
+    t = gmid[...]
+    for d in range(reps - 1):
+        t = t + gz[d]
+    gown[...] = t
+    t = rmid[z]
+    for d in range(reps - 1):
+        t = t + rz[d]
+    rmid[z] = t
+    done.append(pltpu.make_async_copy(gown, gsum_ref, l_sem.at[10]))
+    done.append(pltpu.make_async_copy(rmid.at[z], rsum_ref, l_sem.at[11]))
+    wmine = wo.at[z // heads_dev, z % heads_dev]
+
+    @pl.loop(0, rows_dev // step)
+    def _(i):
+        r = pl.ds(pl.multiple_of(i * step, step), step)
+        t = wmine[r, :].astype(f32)
+        for d in range(reps - 1):
+            t = t + zo[d, r, :].astype(f32)
+        omat[r, :] = t
+    done.append(pltpu.make_async_copy(omat, o_ref, l_sem.at[12]))
+    for c in rzcopies:
+        c.wait_send()
+    for c in done[1:]:
+        c.start()
+    mine.wait()
+    for c in pcopies:
+        c.wait_recv()
+    for src in range(eps):
+        for m in range(3):
+            for i in range(heads_dev):
+                head = ((src % 2) * heads_dev + i) * (eps // 2) + src // 2
+                mats[m, :, head * head_dim:(head + 1) * head_dim] = gath[src, :, m * slice_width + i * head_dim:m * slice_width + (i + 1) * head_dim].astype(f32)
+    for m, ref in enumerate((q_ref, k_ref, v_ref)):
+        done.append(pltpu.make_async_copy(mats.at[m], ref, l_sem.at[13 + m]))
+        done[-1].start()
+    for c in done:
+        c.wait()
+    for c in (*scopies, wcopy, *zcopies, *ocopies, *hcopies, *qcopies, *pcopies, *rcopies, *gzcopies):
+        c.wait_send()
+
+
+def last_sums(part, qkv_term, out_term, tokens, after_cot, gain_in, gains, router, rows_dev, reps, eps, cid):
+    rows, width = tokens.shape
+    f32, bf16 = jnp.float32, jnp.bfloat16
+    heads_dev = out_term.shape[0]
+    slices = qkv_term.shape[2]
+    q = eps // 2
+    half = rows // 2
+    D, V = pltpu.SemaphoreType.DMA, pltpu.VMEM
+    S = jax.ShapeDtypeStruct
+    g8, rt = gains.shape, router.shape[2:]
+    outs = (S((rows, width), f32), *[S((rows_dev, width), f32)] * 4, S(g8, f32), S(rt, f32))
+    return pl.pallas_call(
+        partial(last_kernel, reps, eps),
+        out_shape=outs,
+        in_specs=[pl.BlockSpec(memory_space=pl.ANY)] * 8,
+        out_specs=[pl.BlockSpec(memory_space=pl.ANY)] * len(outs),
+        scratch_shapes=[
+            V((q, rows, width), bf16), V((q, rows, width), bf16), V((2, half, width), bf16), V((rows, width), bf16), V((rows, width), bf16),
+            V((2, heads_dev, rows_dev, width), bf16), V((rows_dev * eps, slices), bf16), V((reps - 1, rows_dev * eps, slices), bf16),
+            V((reps - 1, rows_dev, width), bf16), V((eps, rows_dev, slices), bf16), V((eps, rows_dev, slices), bf16),
+            V((3, rows_dev, width), f32), V((rows_dev, width), f32), V((rows, width), bf16), V((rows, width), f32), V((1, width), f32),
+            V(g8, f32), V((eps - 1, *g8), f32), V((reps - 1, *g8), f32), V(g8, f32),
+            V(router.shape, f32), V((eps - 1, reps, *rt), f32), V((reps - 1, *rt), f32), V((reps, *rt), f32),
+            D((16,)), D((4,)), D((4,)), D((2,)), D((2,)), D((2,)), D((2,)), D, D,
+            D((reps - 1,)), D((reps - 1,)), D((reps - 1,)), D((reps - 1,)), D((eps - 1,)), D((eps - 1,)),
+            D((eps - 1,)), D((eps - 1,)), D((reps - 1,)), D((reps - 1,)), D((eps - 1,)), D((eps - 1,)), D((reps - 1,)), D((reps - 1,)),
+        ],
+        compiler_params=pltpu.CompilerParams(collective_id=cid, has_side_effects=True, vmem_limit_bytes=56 * 2**20),
+    )(part, qkv_term, out_term, tokens, after_cot, gain_in, gains, router)
+
+
+def join_kernel(count, *refs):
+    ins, out = refs[:count], refs[count]
+    shift = (lax.axis_index("rep") + count - pl.program_id(1)) % count
+    for k in range(count):
+        @pl.when(shift == k)
+        def _():
+            out[...] = ins[k][...].astype(out.dtype)
+
+
+def join_columns(pieces):
+    count = len(pieces)
+    exp_dev, rows, cols = pieces[0].shape
+    return pl.pallas_call(
+        partial(join_kernel, count),
+        grid=(exp_dev, count),
+        out_shape=jax.ShapeDtypeStruct((exp_dev, rows, cols * count), jnp.float32),
+        in_specs=[pl.BlockSpec((1, rows, cols), lambda j, s: (j, 0, 0))] * count,
+        out_specs=pl.BlockSpec((1, rows, cols), lambda j, s: (j, 0, s)),
+    )(*pieces)
 
 
 def gather_block(block, axes):
@@ -1286,11 +1537,14 @@
     block_out = (after_attn + moe_out).astype(bf16)
 
     def rows_of(parts):
-        got = lax.all_to_all(parts, "rep", split_axis=0, concat_axis=0, tiled=True)
-        return got.transpose(1, 2, 0, 3).reshape(exp_dev, width // rep_count, ff_width).astype(f32)
-
-    gate_w_grad = rows_of(gate_term)
-    up_w_grad = rows_of(up_term)
+        pieces = [parts[0]]
+        for k in range(1, rep_count):
+            pieces.append(
+                lax.ppermute(parts[k], "rep", [(i, (i + k) % rep_count) for i in range(rep_count)])
+            )
+        return pieces
+
+    gate_pieces, up_pieces = rows_of(gate_term), rows_of(up_term)
 
     out_grad = cotangent.astype(f32)
     gate_cot = row_sum[:, width : width + experts_all].astype(f32) * kept_dense
@@ -1337,45 +1591,40 @@
         axis=1,
     )
     normed_part = jnp.dot(pre_cot, qkv_slice.T, preferred_element_type=f32).astype(bf16)
-    normed_cot = reduce_scatter(normed_part, rep_count, ep_count, False, 7).astype(f32)
-    _, input_pull = jax.vjp(rms_scale, residual, gain_in)
-    input_extra, gain_in_cot = input_pull(normed_cot)
-    input_grad = after_cot + input_extra
-    qkv_term = jnp.dot(normed_group.T, pre_cot, preferred_element_type=f32)
-
-    qkv_sum = scatter_sum(qkv_term.astype(bf16), "rep").reshape(ep_count, rows_dev, 3, slice_width)
-
-    def whole_rows(part):
-        got = lax.all_to_all(part, "ep", split_axis=0, concat_axis=0, tiled=True)
-        got = got.reshape(chips, 2, rows_dev, heads_dev, head_dim).transpose(2, 1, 3, 0, 4)
-        return got.reshape(rows_dev, width).astype(f32)
-
-    query_sum, key_sum, value_sum = (whole_rows(qkv_sum[:, :, i]) for i in range(3))
-    out_halves = output_term.astype(bf16).reshape(heads_dev, 2, rows_dev, width)
-    out_keep = lax.dynamic_index_in_dim(out_halves, core, 1, keepdims=False)
-    out_pass = lax.ppermute(
-        lax.dynamic_index_in_dim(out_halves, 1 - core, 1, keepdims=False),
-        "ep",
-        [(i, i + 1 - 2 * (i % 2)) for i in range(ep_count)],
-    )
-    out_parts = jnp.where(
-        core == 0, jnp.stack([out_keep, out_pass]), jnp.stack([out_pass, out_keep])
-    ).reshape(2 * heads_dev * rows_dev, width)
-    output_sum = scatter_sum(out_parts, "rep").astype(f32)
-    gains_term = jnp.concatenate([gain_in_cot, gain_mid_cot, gain_query_cot, gain_key_cot])
-    small_term = jnp.concatenate(
+    qkv_term = jnp.dot(normed_group.T, pre_cot, preferred_element_type=f32).astype(bf16)
+    gains_term = jnp.concatenate(
         [
-            gains_term.reshape(rep_count * ep_count, gains_dev),
-            router_term.reshape(rep_count * ep_count, router_weight.size),
-            jnp.zeros((rep_count * ep_count, 2048 - gains_dev - router_weight.size), f32),
-        ],
-        axis=1,
-    ).reshape(rep_count * ep_count * 16, 128)
-    small_sum = scatter_sum(small_term, every).reshape(-1)
-    gains_sum = small_sum[:gains_dev]
-    router_sum = small_sum[gains_dev : gains_dev + router_weight.size].reshape(
-        rows_dev, experts_all
-    )
+            jnp.zeros((width,), f32),
+            gain_mid_cot,
+            gain_query_cot,
+            gain_key_cot,
+            jnp.zeros((6 * width - 2 * head_dim,), f32),
+        ]
+    ).reshape(8, width)
+    router_rows = router_weight.size // 128
+    router_parts = jnp.pad(
+        router_term.reshape(rep_count, ep_count, router_rows, 128),
+        ((0, 0), (0, 0), (0, -router_rows % 8), (0, 0)),
+    )
+    input_grad, query_sum, key_sum, value_sum, output_sum, gains_all, router_own = last_sums(
+        normed_part.reshape(ep_count // 2, 2, tok_dev, width),
+        qkv_term.reshape(rep_count, ep_count * rows_dev, 3 * slice_width),
+        output_term.astype(bf16).reshape(heads_dev, 2, rows_dev, width),
+        tokens,
+        after_cot,
+        gain_in.reshape(1, width),
+        gains_term,
+        router_parts,
+        rows_dev,
+        rep_count,
+        ep_count,
+        4,
+    )
+    gains_sum = lax.dynamic_slice_in_dim(
+        gains_all.reshape(-1), (rep_index * ep_count + ep_index) * gains_dev, gains_dev
+    )
+    router_sum = router_own[:router_rows].reshape(rows_dev, experts_all)
+    gate_w_grad, up_w_grad = join_columns(gate_pieces), join_columns(up_pieces)
     return (
         block_out,
         input_grad,

time: 1040 us -> 902 us (0.87)
  waiting for transfers between devices: 260 us -> 11.7 us
  Pallas kernels: 474 us -> 650 us
  local copies, waits for them, and re-layouts: 68.9 us -> 34.8 us
  other arithmetic: 53.8 us -> 30.5 us
  starting transfers between devices: 37 us -> 26.4 us
    pallas_call x0 -> x3, Pallas kernels: none -> 209 us  [the longest x1 193 us: last_sums(): pl.pallas_call(partial(last_kernel, reps, eps), out_shape=outs, in_specs=...]
    reduce_scatter x3 -> x0, waiting for transfers between devices: 125 us -> none  [scatter_sum(): return lax.psum_scatter(partial_sums, axes, scatter_dimension=0, tiled=True)]
    all_to_all x5 -> x0, waiting for transfers between devices: 123 us -> none  [the longest x2 122 us: rows_of(): got = lax.all_to_all(parts, 'rep', split_axis=0, concat_axis=0, tiled=True)]
    pallas_call x2 -> x1, Pallas kernels: 65 us -> 31.5 us  [reduce_scatter(): pl.pallas_call(partial(rs_kernel, reps, across), out_shape=jax.ShapeDtype...]
    all_to_all x5 -> x0, starting transfers between devices: 27.7 us -> none  [the longest x2 16.7 us: rows_of(): got = lax.all_to_all(parts, 'rep', split_axis=0, concat_axis=0, tiled=True)]
    convert_element_type x11 -> x0, local copies, waits for them, and re-layouts: 17.9 us -> none  [the longest x2 13.1 us: rows_of(): got.transpose(1, 2, 0, 3).reshape(exp_dev, width // rep_count, ff_width)]
    ppermute x1 -> x6, starting transfers between devices: 0.23 us -> 17.3 us  [rows_of(): lax.ppermute(parts[k], 'rep', [(i, (i + k) % rep_count) for i in range(re...]
    convert_element_type x3 -> x0, other arithmetic: 12.2 us -> none  [the longest x2 10.4 us: rows_of(): got.transpose(1, 2, 0, 3).reshape(exp_dev, width // rep_count, ff_width)]
  transfers between devices with their start and end apart: 14 -> 11, of which waited for: 8 -> 2; matrix products, arithmetic and copies ran while one was open for 11% -> 6% of each run, Pallas kernels for 13% -> 34%
where the time goes in v4:
time: 902 us; the launch traced here: 887 us
  Pallas kernels  650 us (72%)
  blocking collectives  59.9 us (7%)
  matrix products  58.9 us (7%)
  local copies, waits for them, and re-layouts  34.8 us (4%)
  other arithmetic  30.5 us (3%)
  starting transfers between devices  26.4 us (3%)
  between operations  15.4 us (2%)
  waiting for transfers between devices  11.7 us (1%)
    pallas_call x1, Pallas kernels, moe(): pl.pallas_call(partial(moe_kernel, reps, side, experts_all), out_shape=ou...  287 us
    pallas_call x1, Pallas kernels, last_sums(): pl.pallas_call(partial(last_kernel, reps, eps), out_shape=outs, in_specs=...  193 us
    pallas_call x3, Pallas kernels, all_gather(): pl.pallas_call(partial(ag_kernel, reps, across), out_shape=jax.ShapeDtype...  121 us
    all_gather x2, blocking collectives, gather_block(): return lax.all_gather(block, axes, axis=0, tiled=True)  50.5 us
    pallas_call x1, Pallas kernels, reduce_scatter(): pl.pallas_call(partial(rs_kernel, reps, across), out_shape=jax.ShapeDtype...  31.5 us
  transfers between devices with their start and end apart: 11, of which 2 were waited for; matrix products, arithmetic and copies ran while one was open for 6% of the time, Pallas kernels for 34%

profile of v4, /device:TPU:0, one launch (start us, length us, event | category | flops | bytes accessed | tf_op | source)
XLA Modules:
  0.0 887.2 jit_solution(15070084311015128089)
XLA Ops:
  7.9 1.1 reshape.339
  9.3 0.9 reshape.340
  10.1 5.2 all-to-all-start
  15.3 1.1 reshape.341
  16.6 0.9 reshape.342
  17.5 4.7 all-to-all-done
  22.3 3.4 all-to-all-start.1
  26.3 6.2 all-to-all-done.1
  32.5 9.3 %all_to_all.15 = bf16[8,64,256]{2,1,0:T(8,128)(2,1)S(1)} all-to-all(bf16[8,64,256]{2,1,0:T(8,128)(2,1)S(1)} %reshape.344), channel_id=1, replica_groups=mesh['rep'=4,'ep'=8] {'ep'}, dimensions={0} | all-to-all | bytes 524288 | tf_op jit(solution)/shard_map/all_to_all | solution.py:1467
  41.9 0.9 pad_maximum_fusion.1
  43.2 41.3 %all_gather.12 = bf16[512,128]{1,0:T(8,128)(2,1)S(1)} all-gather(bf16[16,128]{1,0:T(8,128)(2,1)S(1)} %bitcast.134), channel_id=1, replica_groups=mesh['rep'=4,'ep'=8] {'rep','ep'}, dimensions={0}, use_global_device_ids=true | all-gather | bytes 135168 | tf_op jit(solution)/shard_map/all_gather | solution.py:1404
  84.8 24.5 %shard_map.230 = bf16[1,8,128,2048]{3,2,1,0:T(8,128)(2,1)} custom-call(bf16[128,2048]{1,0:T(8,128)(2,1)} %tok_ref.1), custom_call_target="tpu_custom_call" | custom-call | tf_op jit(solution)/shard_map/pallas_call | solution.py:509
  109.5 1.6 reshape.356
  111.2 74.7 %shard_map.232.cot_ref = bf16[4,8,128,2048]{3,2,1,0:T(8,128)(2,1)} custom-call(bf16[128,2048]{1,0:T(8,128)(2,1)} %x_ref.3), custom_call_target="tpu_custom_call" | custom-call | tf_op jit(solution)/shard_map/pallas_call | solution.py:509
  186.0 9.2 %all-gather = s32[8,10,128]{2,1,0:T(8,128)S(1)} all-gather(s32[1,10,128]{2,1,0:T(8,128)S(1)} %add_bitcast_fusion), channel_id=1, replica_groups=mesh['rep'=4,'ep'=8] {'ep'}, dimensions={0}, use_global_device_ids=true | all-gather | bytes 46080 | tf_op jit(solution)/shard_map/all_gather | solution.py:1404
  195.4 3.1 multiply_reduce_fusion.1
  198.5 1.9 multiply_cosine_fusion
  200.4 1.6 broadcast_compare_fusion
  202.1 1.3 dynamic-slice_bitcast_fusion.1
  203.8 5.2 fusion.2
  209.0 1.2 maximum_select_fusion
  210.2 6.7 fusion.50
  217.1 1.1 fusion.43
  219.5 1.9 copy.140
  222.1 2.0 subtract_convert_fusion.1
  224.2 8.8 fusion.47
  233.0 4.2 fusion.13
  237.2 3.3 bitcast_convert_fusion
  240.6 31.5 %shard_map.231 = bf16[128,2048]{1,0:T(8,128)(2,1)} custom-call(bf16[1,4,2,128,2048]{4,3,2,1,0:T(8,128)(2,1)} %bitcast.106), custom_call_target="tpu_custom_call" | custom-call | tf_op jit(solution)/shard_map/pallas_call | solution.py:657
  272.1 1.3 multiply_reduce_fusion.8
  273.4 1.3 multiply_convert_fusion.1
  275.6 1.0 concatenate.39.x_ref
  276.6 287.4 %shard_map.233 = (bf16[128,2176]{1,0:T(8,128)(2,1)}, bf16[128,2048]{1,0:T(8,128)(2,1)}, bf16[4,3,512,256]{3,2,1,0:T(8,128)(2,1)}, bf16[4,3,512,256]{3,2,1,0:T(8,...) custom-call(bf16[128,2176]{1,0:T(8,128)(2,1)} %concatenate.39.x_ref,, ...), custom_call_target="tpu_custom_call" | custom-call | tf_op jit(solution)/shard_map/pallas_call | solution.py:1132
  564.0 1.0 multiply_reduce_fusion.11
  565.0 1.4 fusion.49
  566.4 2.0 multiply_reduce_fusion.4
  568.5 1.8 fusion.41
  570.3 22.3 %shard_map.234 = bf16[1,8,128,2048]{3,2,1,0:T(8,128)(2,1)} custom-call(bf16[128,2048]{1,0:T(8,128)(2,1)} %get-tuple-element.100.x_ref), custom_call_target="tpu_custom_call" | custom-call | tf_op jit(solution)/shard_map/pallas_call | solution.py:509
  592.6 3.5 convolution_convert_fusion.3
  596.2 4.9 multiply_reduce_fusion
  601.0 0.9 slice-done.1
  602.0 2.6 multiply_convert_fusion
  604.7 1.3 fusion.11
  606.0 2.0 fusion.12
  608.1 2.3 fusion.16
  610.4 1.5 slice_bitcast_fusion
  611.9 9.9 %collective-permute-start.4 = (bf16[3,512,256]{2,1,0:T(8,128)(2,1)}, bf16[3,512,256]{2,1,0:T(8,128)(2,1)}, u32[]{:S(2)}, u32[]{:S(2)}) collective-permute-start(bf16[3,512,256]{2,1,0:T(8,128)(2,1)} %get-tuple-element.106), channel_id=1, source_target_pairs={{0,8},{8,16},{16,24},{24,0},{1,9},{9,17},{17,25},{25,1},{2,10},{10... | collective-permute-start | bytes 2359304 | tf_op jit(solution)/shard_map/ppermute | solution.py:1543
  622.6 2.9 collective-permute-start.6
  625.4 1.7 slice_bitcast_fusion.4
  627.1 1.4 collective-permute-start.2
  628.5 2.2 convolution_convert_fusion.2
  630.8 0.9 multiply_add_fusion.3
  632.0 0.9 multiply_reduce_fusion.2
  632.9 0.9 multiply_reduce_fusion.3
  633.9 2.2 fusion.21
  636.3 1.0 copy.163
  637.3 7.8 convolution_convert_fusion
  645.1 2.5 collective-permute-start.3
  649.5 7.7 convolution_convert_fusion.1
  657.2 193.2 %shard_map.235 = (f32[128,2048]{1,0:T(8,128)}, f32[64,2048]{1,0:T(8,128)}, f32[64,2048]{1,0:T(8,128)}, f32[64,2048]{1,0:T(8,128)}, f32[64,2048]{1,0:T(8,128)}, /*index=5*/f32[8,2048]{1,0:T(8,128)}, f32[16,128]{1,0:T(8,128)}) custom-call(bf16[4,2,128,2048]{3,2,1,0:T(8,128)(2,1)} %bitcast.111, bf16[4,512,768]{2,1,0:T(8,128)(2,1)} %bitcast.116, ...), custom_call_target="tpu_custom_call" | custom-call | tf_op jit(solution)/shard_map/pallas_call | solution.py:1362
  853.4 8.0 shard_map.237
  861.4 8.1 shard_map.236
  869.5 1.0 copy.198
  873.7 6.3 copy.203
  (161 shorter events, 15.7 us)
Async XLA Ops:
  7.2 18.6 %copy-start.33 = (bf16[64,2048]{1,0:T(8,128)(2,1)S(1)}, bf16[64,2048]{1,0:T(8,128)(2,1)}, u32[]{:S(2)}) copy-start(bf16[64,2048]{1,0:T(8,128)(2,1)} %param.19) | copy-start | bytes 786436
  7.2 194.9 %all-gather.6.cloned.1.call-start = ((), (), s32[]{:S(2)}) async-start(), calls=%async_computation.4 | async-start | bytes 1310720 | tf_op jit(solution)/shard_map/all_gather | solution.py:1404
  9.0 33.8 %copy-start.36 = (bf16[64,24]{0,1:T(8,128)(2,1)S(1)}, bf16[64,24]{0,1:T(8,128)(2,1)}, u32[]{:S(2)}) copy-start(bf16[64,24]{0,1:T(8,128)(2,1)} %param.21) | copy-start | bytes 9220
  9.1 34.0 %copy-start.37 = (bf16[136]{0:T(256)(128)(2,1)S(1)}, bf16[136]{0:T(256)(128)(2,1)}, u32[]{:S(2)}) copy-start(bf16[136]{0:T(256)(128)(2,1)} %param.22) | copy-start | bytes 820
  10.1 12.1 %all-to-all-start = ((bf16[8,64,256]{2,1,0:T(8,128)(2,1)}), bf16[8,64,256]{2,1,0:T(8,128)(2,1)S(1)}, u32[]{:S(2)}, u32[]{:S(2)}) async-start(bf16[8,64,256]{2,1,0:T(8,128)(2,1)} %reshape.340), calls=%async_computation | async-start | bytes 524288 | tf_op jit(solution)/shard_map/all_to_all | solution.py:1467
  22.3 10.3 %all-to-all-start.1 = ((bf16[8,64,256]{2,1,0:T(8,128)(2,1)}), bf16[8,64,256]{2,1,0:T(8,128)(2,1)S(1)}, u32[]{:S(2)}, u32[]{:S(2)}) async-start(bf16[8,64,256]{2,1,0:T(8,128)(2,1)} %reshape.342), calls=%async_computation.1 | async-start | bytes 524288 | tf_op jit(solution)/shard_map/all_to_all | solution.py:1467
  25.7 184.5 %all-gather.4.cloned.1.call-start = ((), (), s32[]{:S(2)}) async-start(), calls=%async_computation.3 | async-start | bytes 3932160 | tf_op jit(solution)/shard_map/all_gather | solution.py:1404
  26.3 83.0 %copy-start.39 = (s32[1,3]{1,0:T(1,128)S(1)}, s32[1,3]{1,0:T(1,128)}, u32[]{:S(2)}) copy-start(s32[1,3]{1,0:T(1,128)} %param.26) | copy-start | bytes 40
  41.9 69.2 %copy-start.35 = (s32[128,8]{0,1:T(8,128)S(1)}, s32[128,8]{0,1:T(8,128)}, u32[]{:S(2)}) copy-start(s32[128,8]{0,1:T(8,128)} %param.28) | copy-start | bytes 12292
  111.2 74.7 %copy-start.38 = (s32[128]{0:T(128)S(1)}, s32[128]{0:T(128)}, u32[]{:S(2)}) copy-start(s32[128]{0:T(128)} %param.27) | copy-start | bytes 1540
  111.2 74.7 %copy-start.40 = (s32[128]{0:T(128)S(1)}, s32[128]{0:T(128)}, u32[]{:S(2)}) copy-start(s32[128]{0:T(128)} %param.29) | copy-start | bytes 1540
  198.5 10.5 %copy-start.34 = (f32[2048]{0:T(1024)}, f32[2048]{0:T(1024)S(1)}, u32[]{:S(2)}) copy-start(f32[2048]{0:T(1024)S(1)} %get-tuple-element.132) | copy-start | bytes 24580
  200.4 21.7 %copy-start.7 = (f32[1024,64]{1,0:T(8,128)}, f32[1024,64]{1,0:T(8,128)S(1)}, u32[]{:S(2)}) copy-start(f32[1024,64]{1,0:T(8,128)S(1)} %get-tuple-element.135) | copy-start | bytes 786436
  200.4 21.7 %copy-start.9 = (f32[1024,64]{1,0:T(8,128)}, f32[1024,64]{1,0:T(8,128)S(1)}, u32[]{:S(2)}) copy-start(f32[1024,64]{1,0:T(8,128)S(1)} %get-tuple-element.136) | copy-start | bytes 786436
  203.4 5.6 collective-permute-start
  219.5 4.7 copy-start
  221.4 2.8 copy-start.2
  224.2 8.8 copy-start.27
  233.0 4.2 copy-start.12
  237.2 3.3 copy-start.22
  240.6 31.5 %copy-start.4 = (bf16[128,2048]{1,0:T(8,128)(2,1)S(1)}, bf16[128,2048]{1,0:T(8,128)(2,1)}, u32[]{:S(2)}) copy-start(bf16[128,2048]{1,0:T(8,128)(2,1)} %tok_ref.1) | copy-start | bytes 1572868
  240.6 34.1 %copy-start.21 = (bf16[2048,24]{1,0:T(8,128)(2,1)S(1)}, bf16[2048,24]{1,0:T(8,128)(2,1)}, u32[]{:S(2)}) copy-start(bf16[2048,24]{1,0:T(8,128)(2,1)} %reshape.356) | copy-start | bytes 294916
  274.7 0.9 copy-start.6
  564.0 4.5 copy-start.5
  564.0 4.5 copy-start.20
  564.0 4.5 copy-start.26
  568.5 24.1 %copy-start.13 = (bf16[2,128,2048]{2,1,0:T(8,128)(2,1)S(1)}, bf16[2,128,2048]{2,1,0:T(8,128)(2,1)}, u32[]{:S(2)}) copy-start(bf16[2,128,2048]{2,1,0:T(8,128)(2,1)} %maximum_select_fusion) | copy-start | bytes 3145732
  592.6 3.6 copy-start.28
  596.1 4.9 slice-start
  596.2 5.8 slice-start.1
  602.0 2.7 copy-start.18
  602.0 2.7 copy-start.19
  604.7 1.4 copy-start.16
  604.7 1.3 copy-start.17
  608.1 2.3 copy-start.15
  610.4 15.0 %copy-start.14 = (bf16[4,3,512,256]{3,2,1,0:T(8,128)(2,1)S(1)}, bf16[4,3,512,256]{3,2,1,0:T(8,128)(2,1)}, u32[]{:S(2)}) copy-start(bf16[4,3,512,256]{3,2,1,0:T(8,128)(2,1)} %get-tuple-element.32) | copy-start | bytes 9437188
  611.9 16.6 %copy-start.11 = (bf16[1,8,128,2048]{3,2,1,0:T(8,128)(2,1)S(1)}, bf16[1,8,128,2048]{3,2,1,0:T(8,128)(2,1)}, u32[]{:S(2)}) copy-start(bf16[1,8,128,2048]{3,2,1,0:T(8,128)(2,1)} %shard_map.234) | copy-start | bytes 12582916
  611.9 16.6 %copy-start.23 = (bf16[2,128,1024]{2,1,0:T(8,128)(2,1)S(1)}, bf16[2,128,1024]{2,1,0:T(8,128)(2,1)}, u32[]{:S(2)}) copy-start(bf16[2,128,1024]{2,1,0:T(8,128)(2,1)} %copy-done.22) | copy-start | bytes 1572868
  611.9 33.2 %collective-permute-start.4 = (bf16[3,512,256]{2,1,0:T(8,128)(2,1)}, bf16[3,512,256]{2,1,0:T(8,128)(2,1)}, u32[]{:S(2)}, u32[]{:S(2)}) collective-permute-start(bf16[3,512,256]{2,1,0:T(8,128)(2,1)} %get-tuple-element.106), channel_id=1, source_target_pairs={{0,8},{8,16},{16,24},{24,0},{1,9},{9,17},{17,25},{25,1},{2,10},{10... | collective-permute-start | bytes 2359304 | tf_op jit(solution)/shard_map/ppermute | solution.py:1543
  621.8 231.5 %collective-permute-start.5 = (bf16[3,512,256]{2,1,0:T(8,128)(2,1)}, bf16[3,512,256]{2,1,0:T(8,128)(2,1)}, u32[]{:S(2)}, u32[]{:S(2)}) collective-permute-start(bf16[3,512,256]{2,1,0:T(8,128)(2,1)} %get-tuple-element.105), channel_id=1, source_target_pairs={{0,16},{8,24},{16,0},{24,8},{1,17},{9,25},{17,1},{25,9},{2,18},{10... | collective-permute-start | bytes 2359304 | tf_op jit(solution)/shard_map/ppermute | solution.py:1543
  622.6 230.8 %collective-permute-start.6 = (bf16[3,512,256]{2,1,0:T(8,128)(2,1)S(1)}, bf16[3,512,256]{2,1,0:T(8,128)(2,1)}, u32[]{:S(2)}, u32[]{:S(2)}) collective-permute-start(bf16[3,512,256]{2,1,0:T(8,128)(2,1)S(1)} %get-tuple-element.104), channel_id=1, source_target_pairs={{0,24},{8,0},{16,8},{24,16},{1,25},{9,1},{17,9},{25,17},{2,26},{10... | collective-permute-start | bytes 2359304 | tf_op jit(solution)/shard_map/ppermute | solution.py:1543
  627.1 3.6 copy-start.8
  627.1 3.6 copy-start.10
  627.1 234.2 %collective-permute-start.1 = (bf16[3,512,256]{2,1,0:T(8,128)(2,1)}, bf16[3,512,256]{2,1,0:T(8,128)(2,1)}, u32[]{:S(2)}, u32[]{:S(2)}) collective-permute-start(bf16[3,512,256]{2,1,0:T(8,128)(2,1)} %get-tuple-element.110), channel_id=1, source_target_pairs={{0,8},{8,16},{16,24},{24,0},{1,9},{9,17},{17,25},{25,1},{2,10},{10... | collective-permute-start | bytes 2359304 | tf_op jit(solution)/shard_map/ppermute | solution.py:1543
  627.1 234.2 %collective-permute-start.2 = (bf16[3,512,256]{2,1,0:T(8,128)(2,1)}, bf16[3,512,256]{2,1,0:T(8,128)(2,1)}, u32[]{:S(2)}, u32[]{:S(2)}) collective-permute-start(bf16[3,512,256]{2,1,0:T(8,128)(2,1)} %get-tuple-element.109), channel_id=1, source_target_pairs={{0,16},{8,24},{16,0},{24,8},{1,17},{9,25},{17,1},{25,9},{2,18},{10... | collective-permute-start | bytes 2359304 | tf_op jit(solution)/shard_map/ppermute | solution.py:1543
  630.8 1.2 copy-start.1
  630.8 2.2 copy-start.3
  637.3 7.8 copy-start.25
  645.1 216.2 %collective-permute-start.3 = (bf16[3,512,256]{2,1,0:T(8,128)(2,1)S(1)}, bf16[3,512,256]{2,1,0:T(8,128)(2,1)}, u32[]{:S(2)}, u32[]{:S(2)}) collective-permute-start(bf16[3,512,256]{2,1,0:T(8,128)(2,1)S(1)} %copy-done.25), channel_id=1, source_target_pairs={{0,24},{8,0},{16,8},{24,16},{1,25},{9,1},{17,9},{25,17},{2,26},{10... | collective-permute-start | bytes 2359304 | tf_op jit(solution)/shard_map/ppermute | solution.py:1543
  861.4 8.1 copy-start.24
  861.4 9.1 %copy-start.32 = (f32[64,2048]{1,0:T(8,128)S(1)}, f32[64,2048]{1,0:T(8,128)}, u32[]{:S(2)}) copy-start(f32[64,2048]{1,0:T(8,128)} %get-tuple-element.160) | copy-start | bytes 1572868
  861.4 9.9 %copy-start.31 = (f32[64,2048]{1,0:T(8,128)S(1)}, f32[64,2048]{1,0:T(8,128)}, u32[]{:S(2)}) copy-start(f32[64,2048]{1,0:T(8,128)} %get-tuple-element.161) | copy-start | bytes 1572868
  869.5 2.6 copy-start.30
  869.5 3.4 copy-start.29
Sparse Core Ops, SparseCore 0:
  9.6 30.6 all-gather.5
  43.0 63.2 all-gather.3

commit v5 on v4

--- a/solution.py
+++ b/solution.py
@@ -87,6 +87,14 @@
     )
     value_grad = jnp.einsum("hts,thd->shd", prob_low, head_grad, preferred_element_type=jnp.float32)
     return (query_grad, key_grad, value_grad)
+
+
+def attend_again(parts, same_seq, score_scale):
+    head_query, head_key, head_value, head_grad = parts
+    _, top_score, total_sum = attend_forward(
+        (head_query, head_key, head_value), same_seq, score_scale
+    )
+    return attend_backward((*parts, top_score, total_sum), same_seq, score_scale)
 
 
 def on_device_general(
@@ -1400,12 +1408,420 @@
     )(*pieces)
 
 
-def gather_block(block, axes):
-    return lax.all_gather(block, axes, axis=0, tiled=True)
-
-
-def scatter_sum(partial_sums, axes):
-    return lax.psum_scatter(partial_sums, axes, scatter_dimension=0, tiled=True)
+def front_kernel(reps, eps, lengths_ref, tok_ref, cot_ref, wq_ref, wk_ref, wv_ref, wo_ref, gains_ref, router_ref, nums_ref, freq_ref,
+                 cots_ref, router_all_ref, nums_all_ref, gsum_ref, normed_ref, pre_ref, qkv_ref, mixed_ref, wqkv_ref, wout_ref, turn_ref, attn_ref,
+                 toks, normed, wraw, stage, wqkv, wz, wout, proj, qkv, mixed, turn, segs, part, sib_in, relay_in, xin, yin, acc,
+                 gown, gz, gmid, gin, gall, nums, freq,
+                 l_sem, o_sem, ws, wr, vs, vr, zs, zr, fs, fr, ts, tr, tcs, tcr, cps, cpr, ccs, ccr,
+                 gzs, gzr, gps, gpr, rzs, rzr, rps, rpr, ns, nr, ss, sr, hs, hr, qs, qr, os, orr):
+    f32, bf16 = jnp.float32, jnp.bfloat16
+    z = lax.axis_index("rep")
+    e = lax.axis_index("ep")
+    core = e % 2
+    chip = e // 2
+    sib, chips = partners(e)
+    rows, width = tok_ref.shape
+    half = rows // 2
+    rows_dev = wq_ref.shape[0]
+    slice_width = mixed.shape[1]
+    head_dim = turn.shape[2]
+    heads_dev = slice_width // head_dim
+    group_rows = eps * rows
+
+    barrier = pltpu.get_barrier_semaphore()
+    for d in range(1, eps):
+        pl.semaphore_signal(barrier, inc=1, device_id={"rep": z, "ep": (e + d) % eps}, device_id_type=MESH)
+    for d in range(1, reps):
+        pl.semaphore_signal(barrier, inc=1, device_id={"rep": (z + d) % reps, "ep": e}, device_id_type=MESH)
+
+    def local(src, dst, sem):
+        c = pltpu.make_async_copy(src, dst, sem)
+        c.start()
+        return c
+
+    raw = [local(r, wraw.at[m], l_sem.at[m]) for m, r in enumerate((wq_ref, wk_ref, wv_ref))]
+    tok_own = local(tok_ref, toks.at[e], l_sem.at[3])
+    wo_own = local(wo_ref, wz.at[z], l_sem.at[4])
+    cot_own = local(cot_ref, cots_ref.at[z, e], l_sem.at[5])
+    small = [
+        local(gains_ref, gown, l_sem.at[6]),
+        local(nums_ref, nums.at[e], l_sem.at[7]),
+        local(freq_ref, freq, l_sem.at[8]),
+        local(router_ref, router_all_ref.at[e, z], l_sem.at[9]),
+    ]
+    pl.semaphore_wait(barrier, eps - 1 + reps - 1)
+
+    def remote(src, dst, send, recv, rep, ep):
+        return pltpu.make_async_remote_copy(src_ref=src, dst_ref=dst, send_sem=send, recv_sem=recv,
+                                            device_id={"rep": rep, "ep": ep}, device_id_type=MESH)
+
+    def below(k, fn):
+        @pl.when(z - k >= 0)
+        def _():
+            fn(z - k)
+
+    def above(k, fn):
+        @pl.when(z + k < reps)
+        def _():
+            fn(z + k)
+
+    class Chain:
+        def __init__(self, slot, send, recv):
+            self.slot, self.send, self.recv = slot, send, recv
+
+        def copy(self, src, g, up):
+            d = 0 if up else 1
+            return remote(src, self.slot(g), self.send.at[d, g], self.recv.at[g], z + 1 if up else z - 1, e)
+
+        def begin(self, src):
+            @pl.when(z < reps - 1)
+            def _():
+                self.copy(src, z, True).start()
+            @pl.when(z > 0)
+            def _():
+                self.copy(src, z, False).start()
+
+        def take(self, k, then=None):
+            def from_below(g):
+                self.copy(self.slot(g), g, True).wait_recv()
+                if then is not None:
+                    then(g)
+            def from_above(g):
+                self.copy(self.slot(g), g, False).wait_recv()
+                if then is not None:
+                    then(g)
+            below(k, from_below)
+            above(k, from_above)
+
+        def forward(self, k):
+            @pl.when((z - k >= 0) & (z < reps - 1))
+            def _():
+                self.copy(self.slot(z - k), z - k, True).start()
+            @pl.when((z + k < reps) & (z > 0))
+            def _():
+                self.copy(self.slot(z + k), z + k, False).start()
+
+        def arrive(self, k):
+            self.take(k)
+            self.forward(k)
+
+        def sent(self):
+            for g in range(reps):
+                @pl.when((z < reps - 1) & (z >= g))
+                def _():
+                    self.copy(self.slot(g), g, True).wait_send()
+                @pl.when((z > 0) & (z <= g))
+                def _():
+                    self.copy(self.slot(g), g, False).wait_send()
+
+    class Spread:
+        def __init__(self, slot, send, recv, csend, crecv):
+            self.slot, self.send, self.recv, self.csend, self.crecv = slot, send, recv, csend, crecv
+
+        def near(self, src, j):
+            return remote(src, self.slot(e), self.send.at[j], self.recv.at[j], z, chips[j])
+
+        def relay(self, j, source):
+            p = self.slot(source).at[pl.ds(half * j, half)]
+            return remote(p, p, self.send.at[2 + j], self.recv.at[2 + j], z, chips[1 - j])
+
+        def core(self, src, j):
+            return remote(src, self.slot(e if j == 0 else chips[j - 1]), self.csend.at[j], self.crecv.at[j], z, sib)
+
+        def begin(self, src):
+            self.near(src, 0).start()
+            self.near(src, 1).start()
+            self.core(src, 0).start()
+
+        def pass_on(self):
+            for j in range(2):
+                self.near(self.slot(e), j).wait_recv()
+                self.relay(j, chips[j]).start()
+                self.core(self.slot(chips[j]), j + 1).start()
+
+        def finish(self):
+            for j in range(2):
+                self.relay(j, chips[2]).wait_recv()
+            self.core(self.slot(chips[2]), 3).start()
+
+        def arrived(self):
+            for j in range(4):
+                self.core(self.slot(e), j).wait_recv()
+
+        def sent(self):
+            for j in range(2):
+                self.near(self.slot(e), j).wait_send()
+                self.relay(j, chips[j]).wait_send()
+            for j in range(4):
+                self.core(self.slot(e), j).wait_send()
+
+    tok_spread = Spread(lambda who: toks.at[who], ts, tr, tcs, tcr)
+
+    def cot_spread(g):
+        return Spread(lambda who: cots_ref.at[g, who], cps.at[g], cpr.at[g], ccs.at[g], ccr.at[g])
+
+    wo_chain = Chain(lambda g: wz.at[g], ws, wr)
+    w_chain = Chain(lambda g: wqkv.at[g], vs, vr)
+    cot_chain = Chain(lambda g: cots_ref.at[g, e], zs, zr)
+
+    def cot_take(k):
+        cot_chain.take(k, lambda g: cot_spread(g).begin(cots_ref.at[g, e]))
+
+    def each(k, fn):
+        below(k, lambda g: fn(cot_spread(g)))
+        above(k, lambda g: fn(cot_spread(g)))
+
+    gzc = [remote(gains_ref, gz.at[d - 1], gzs.at[d - 1], gzr.at[d - 1], (z + d) % reps, e) for d in range(1, reps)]
+    rzc = [remote(router_ref, router_all_ref.at[e, z], rzs.at[d - 1], rzr.at[d - 1], (z + d) % reps, e) for d in range(1, reps)]
+    nc = [remote(nums_ref, nums.at[e], ns.at[d - 1], nr.at[d - 1], z, (e + d) % eps) for d in range(1, eps)]
+    for c in (*gzc, *rzc, *nc):
+        c.start()
+    wo_chain.begin(wo_ref)
+    for m in range(3):
+        raw[m].wait()
+        for who in range(eps):
+            for i in range(heads_dev):
+                head = ((who % 2) * heads_dev + i) * (eps // 2) + who // 2
+                at = m * slice_width + i * head_dim
+                stage[who, :, at:at + head_dim] = wraw[m, :, head * head_dim:(head + 1) * head_dim]
+    vc = [remote(stage.at[(e + d) % eps], wqkv.at[z, e], fs.at[d - 1], fr.at[d - 1], z, (e + d) % eps) for d in range(1, eps)]
+    for c in vc:
+        c.start()
+    v_own = local(stage.at[e], wqkv.at[z, e], l_sem.at[10])
+    tok_spread.begin(tok_ref)
+    cot_chain.begin(cot_ref)
+    cot_spread(z).begin(cot_ref)
+    v_own.wait()
+    for c in vc:
+        c.wait_recv()
+    w_chain.begin(wqkv.at[z])
+    wo_chain.arrive(1)
+
+    for c in gzc:
+        c.wait_recv()
+    small[0].wait()
+    t = gown[...].astype(f32)
+    for d in range(reps - 1):
+        t = t + gz[d].astype(f32)
+    gmid[...] = t.astype(bf16)
+    gpc = [remote(gmid, gin.at[d - 1], gps.at[d - 1], gpr.at[d - 1], z, (e + d) % eps) for d in range(1, eps)]
+    for c in gpc:
+        c.start()
+    small[3].wait()
+    for c in rzc:
+        c.wait_recv()
+    rpc = [remote(router_all_ref.at[e], router_all_ref.at[e], rps.at[d - 1], rpr.at[d - 1], z, (e + d) % eps) for d in range(1, eps)]
+    for c in rpc:
+        c.start()
+    tok_spread.pass_on()
+    tok_spread.finish()
+    wo_chain.arrive(2)
+    cot_take(1)
+    for c in gpc:
+        c.wait_recv()
+    t = gmid[...].astype(f32)
+    for d in range(eps - 1):
+        t = t + gin[d].astype(f32)
+    gall[...] = t
+    outs = [local(gall, gsum_ref, o_sem.at[0])]
+    w_chain.arrive(1)
+    wo_chain.arrive(3)
+    cot_chain.forward(1)
+
+    for c in small[1:3]:
+        c.wait()
+    for c in nc:
+        c.wait_recv()
+    outs.append(local(nums, nums_all_ref, o_sem.at[1]))
+    deal = nums[:, 0, :]
+    segment = jnp.zeros(deal.shape, jnp.int32)
+    start = jnp.zeros(deal.shape, jnp.int32)
+    end = 0
+    for n in range(lengths_ref.shape[1]):
+        end = end + lengths_ref[0, n]
+        after = (deal >= end).astype(jnp.int32)
+        segment = segment + after
+        start = start + after * lengths_ref[0, n]
+    position = (deal - start).astype(f32)
+    segs[...] = segment.astype(f32)
+    lane = lax.broadcasted_iota(jnp.int32, (rows, head_dim), 1)
+    sign = jnp.where(lane < head_dim // 2, -1.0, 1.0)
+    for n in range(eps):
+        spot = jnp.broadcast_to(position[n:n + 1, :], (rows, rows)).T
+        angle = spot * freq[0:1, :]
+        here = pl.ds(n * rows, rows)
+        turn[0, here, :] = jnp.cos(angle)
+        turn[1, here, :] = jnp.sin(angle) * sign
+    outs.append(local(turn, turn_ref, o_sem.at[2]))
+    cot_spread(z).pass_on()
+
+    tok_own.wait()
+    tok_spread.arrived()
+    gain_in = jnp.concatenate([gall[n:n + 1, :] for n in range(width // 128)], axis=1)
+    step = 16
+    for n in range(eps):
+        @pl.loop(0, rows // step)
+        def _(i):
+            r = pl.ds(pl.multiple_of(i * step, step), step)
+            t = toks[n, r, :].astype(f32)
+            scale = lax.rsqrt(jnp.mean(t * t, axis=-1, keepdims=True) + norm_eps)
+            normed[n, r, :] = (t * scale * gain_in).astype(bf16)
+    outs.append(local(normed, normed_ref, o_sem.at[3]))
+    w_chain.arrive(2)
+    cot_take(2)
+    cot_chain.forward(2)
+    cot_spread(z).finish()
+
+    wo_own.wait()
+    wc = [remote(wz.at[(1 - core) * heads_dev + i], wout.at[i, core], os.at[i], orr.at[i], z, sib) for i in range(heads_dev)]
+    wl = [local(wz.at[core * heads_dev + i], wout.at[i, core], l_sem.at[11 + i]) for i in range(heads_dev)]
+    for c in wc:
+        c.start()
+    w_chain.arrive(3)
+    each(1, lambda s: s.pass_on())
+
+
+    @pl.loop(0, eps)
+    def _(n):
+        here = pl.ds(pl.multiple_of(n * rows, rows), rows)
+        proj[here, :] = jnp.dot(normed[n], wqkv[...].reshape(width, 3 * slice_width), preferred_element_type=f32)
+        for h in range(2 * heads_dev):
+            cut = slice(h * head_dim, (h + 1) * head_dim)
+            t = proj[here, cut]
+            row = 2 * width // 128 + (0 if h < heads_dev else 1)
+            t = t * lax.rsqrt(jnp.mean(t * t, axis=-1, keepdims=True) + norm_eps) * gall[row:row + 1, :]
+            t = t * turn[0, here, :] + pltpu.roll(t, head_dim // 2, 1) * turn[1, here, :]
+            qkv[here, cut] = t.astype(bf16)
+        tail = slice(2 * slice_width, 3 * slice_width)
+        qkv[here, tail] = proj[here, tail].astype(bf16)
+
+    outs.append(local(proj.at[:, pl.ds(0, 2 * slice_width)], pre_ref, o_sem.at[4]))
+    outs.append(local(qkv, qkv_ref, o_sem.at[5]))
+    outs.append(local(wqkv, wqkv_ref, o_sem.at[6]))
+
+    seg_row = jnp.concatenate([segs[n:n + 1, :] for n in range(eps)], axis=1)
+    block = 2 * rows
+
+    def attend(h):
+        cut = slice(h * head_dim, (h + 1) * head_dim)
+        kcut = slice(slice_width + h * head_dim, slice_width + (h + 1) * head_dim)
+        vcut = slice(2 * slice_width + h * head_dim, 2 * slice_width + (h + 1) * head_dim)
+        for n in range(eps // 2):
+            here = pl.ds(n * block, block)
+            s = lax.dot_general(qkv[here, cut], qkv[:, kcut], NT, preferred_element_type=f32) * (head_dim ** -0.5)
+            seg_col = jnp.concatenate(
+                [jnp.broadcast_to(segs[2 * n + j:2 * n + j + 1, :], (rows, rows)).T[:, 0:1] for j in range(2)], axis=0)
+            s = jnp.where(seg_col == seg_row, s, masked_score)
+            p = jnp.exp(s - jnp.max(s, axis=-1, keepdims=True))
+            p = (p / jnp.sum(p, axis=-1, keepdims=True)).astype(bf16)
+            mixed[here, cut] = jnp.dot(p, qkv[:, vcut], preferred_element_type=f32).astype(bf16)
+
+    each(1, lambda s: s.finish())
+    attend(0)
+    each(2, lambda s: s.pass_on())
+    for h in range(1, heads_dev):
+        attend(h)
+    outs.append(local(mixed, mixed_ref, o_sem.at[7]))
+    for c in wl:
+        c.wait()
+    for c in wc:
+        c.wait_recv()
+    outs.append(local(wout, wout_ref, o_sem.at[8]))
+
+    order = (chips[2] // 2, chips[0] // 2, chips[1] // 2, chip)
+    scopies = [remote(part.at[q, 1 - core], sib_in.at[q], ss.at[n], sr.at[n], z, sib) for n, q in enumerate(order)]
+    for n in range(eps // 2):
+        q = order[n]
+        here = pl.ds(pl.multiple_of(q * block, block), block)
+        t = jnp.dot(mixed[here, :], wout[...].reshape(slice_width, width), preferred_element_type=f32)
+        part[q] = t.astype(bf16).reshape(2, rows, width)
+        scopies[n].start()
+
+    cot_take(3)
+
+    def add(out, terms, count):
+        @pl.loop(0, count // step)
+        def _(i):
+            r = pl.ds(pl.multiple_of(i * step, step), step)
+            t = terms[0][r, :].astype(f32)
+            for other in terms[1:]:
+                t = t + other[r, :].astype(f32)
+            out[r, :] = t.astype(out.dtype)
+
+    lower, upper = pl.ds(0, half), pl.ds(half, half)
+    first = part.at[order[0], core]
+    hcopies = [remote(first.at[(lower, upper)[j]], relay_in.at[j], hs.at[j], hr.at[j], z, chips[j]) for j in range(2)]
+    qcopies = [remote(part.at[order[1 + j], core], (xin, yin)[j], qs.at[j], qr.at[j], z, chips[j]) for j in range(2)]
+    scopies[0].wait_recv()
+    add(first, (first, sib_in.at[order[0]]), rows)
+    for c in hcopies:
+        c.start()
+    for j in range(2):
+        mine, other = part.at[order[1 + j], core], sib_in.at[order[1 + j]]
+        scopies[1 + j].wait_recv()
+        direct, through = ((lower, upper), (upper, lower))[j]
+        add(mine.at[direct], (mine.at[direct], other.at[direct]), half)
+        hcopies[1 - j].wait_recv()
+        add(mine.at[through], (mine.at[through], other.at[through], relay_in.at[1 - j]), half)
+        qcopies[j].start()
+    scopies[3].wait_recv()
+    each(3, lambda s: s.pass_on())
+    each(2, lambda s: s.finish())
+    for c in qcopies:
+        c.wait_recv()
+    add(acc, (part.at[chip, core], sib_in.at[chip], xin, yin, toks.at[e]), rows)
+    outs.append(local(acc, attn_ref, o_sem.at[9]))
+    each(3, lambda s: s.finish())
+    cot_own.wait()
+    for g in range(reps):
+        cot_spread(g).arrived()
+        cot_spread(g).sent()
+    for chain in (wo_chain, w_chain, cot_chain):
+        chain.sent()
+    tok_spread.sent()
+    for c in rpc:
+        c.wait_recv()
+    for c in (*gzc, *rzc, *nc, *vc, *gpc, *rpc, *wc, *scopies, *hcopies, *qcopies):
+        c.wait_send()
+    for c in outs:
+        c.wait()
+
+
+def front(lengths, tokens, cot, wq, wk, wv, wo, gains, router, nums, freq, heads_dev, reps, eps, cid):
+    rows, width = tokens.shape
+    rows_dev = wq.shape[0]
+    f32, bf16, i32 = jnp.float32, jnp.bfloat16, jnp.int32
+    head_dim = freq.shape[1]
+    sw = heads_dev * head_dim
+    gr = eps * rows
+    half = rows // 2
+    q = eps // 2
+    S, V, D = jax.ShapeDtypeStruct, pltpu.VMEM, pltpu.SemaphoreType.DMA
+    outs = (
+        S((reps, eps, rows, width), bf16), S((eps, reps, *router.shape), bf16), S((eps, *nums.shape), i32), S(gains.shape, f32),
+        S((eps, rows, width), bf16), S((gr, 2 * sw), f32), S((gr, 3 * sw), bf16), S((gr, sw), bf16),
+        S((reps, eps, rows_dev, 3 * sw), bf16), S((heads_dev, 2, rows_dev, width), bf16), S((2, gr, head_dim), f32), S((rows, width), f32),
+    )
+    return pl.pallas_call(
+        partial(front_kernel, reps, eps),
+        out_shape=outs,
+        in_specs=[pl.BlockSpec(memory_space=pltpu.SMEM)] + [pl.BlockSpec(memory_space=pl.ANY)] * 10,
+        out_specs=[pl.BlockSpec(memory_space=pl.ANY)] * len(outs),
+        scratch_shapes=[
+            V((eps, rows, width), bf16), V((eps, rows, width), bf16), V((3, rows_dev, width), bf16), V((eps, rows_dev, 3 * sw), bf16),
+            V((reps, eps, rows_dev, 3 * sw), bf16), V((reps, rows_dev, width), bf16), V((heads_dev, 2, rows_dev, width), bf16),
+            V((gr, 3 * sw), f32), V((gr, 3 * sw), bf16), V((gr, sw), bf16), V((2, gr, head_dim), f32), V((eps, rows), f32),
+            V((q, 2, rows, width), bf16), V((q, rows, width), bf16), V((2, half, width), bf16), V((rows, width), bf16), V((rows, width), bf16),
+            V((rows, width), f32),
+            V(gains.shape, bf16), V((reps - 1, *gains.shape), bf16), V(gains.shape, bf16), V((eps - 1, *gains.shape), bf16), V(gains.shape, f32),
+            V((eps, *nums.shape), i32), V(freq.shape, f32),
+            D((16,)), D((16,)), D((2, reps)), D((reps,)), D((2, reps)), D((reps,)), D((2, reps)), D((reps,)), D((eps - 1,)), D((eps - 1,)),
+            D((4,)), D((4,)), D((4,)), D((4,)), D((reps, 4)), D((reps, 4)), D((reps, 4)), D((reps, 4)),
+            D((reps - 1,)), D((reps - 1,)), D((eps - 1,)), D((eps - 1,)), D((reps - 1,)), D((reps - 1,)), D((eps - 1,)), D((eps - 1,)),
+            D((eps - 1,)), D((eps - 1,)), D((4,)), D((4,)), D((2,)), D((2,)), D((2,)), D((2,)), D((2,)), D((2,)),
+        ],
+        compiler_params=pltpu.CompilerParams(collective_id=cid, has_side_effects=True, vmem_limit_bytes=56 * 2**20),
+    )(lengths, tokens, cot, wq, wk, wv, wo, gains, router, nums, freq)
 
 
 def on_device_split(
@@ -1442,66 +1858,77 @@
     core = ep_index % 2
     every = ("rep", "ep")
 
+    chips = ep_count // 2
     gains_dev = gains.shape[0]
-    packed = jnp.concatenate(
-        [gains, router_weight.reshape(-1), jnp.zeros((2048 - gains_dev - router_weight.size,), bf16)]
-    ).reshape(16, 128)
-    packed_all = gather_block(packed, every).reshape(rep_count * ep_count, 2048)
-    gains_float = packed_all[:, :gains_dev].reshape(-1).astype(f32)
-    router_full = packed_all[:, gains_dev : gains_dev + router_weight.size].reshape(width, experts_all)
+    gain_rows = -(-gains_dev * rep_count * ep_count // 2048) * 16
+    gains_placed = lax.dynamic_update_slice_in_dim(
+        jnp.zeros((gain_rows * 128,), bf16),
+        gains,
+        (rep_index * ep_count + ep_index) * gains_dev,
+        axis=0,
+    ).reshape(gain_rows, 128)
+    router_rows = router_weight.size // 128
+    router_placed = jnp.pad(router_weight.reshape(router_rows, 128), ((0, -router_rows % 16), (0, 0)))
+    numbers = jnp.concatenate([deal[None], priority[None], routes.T])
+    numbers = jnp.pad(numbers, ((0, -numbers.shape[0] % 8), (0, 0)))
+    frequency = rope_base ** (
+        -2.0 * jnp.arange(head_dim // 2, dtype=jnp.float32) / head_dim
+    )
+    (
+        cot_all,
+        router_all,
+        numbers_all,
+        gains_all,
+        normed_group,
+        pre,
+        qkv_low,
+        mixed_low,
+        qkv_slice,
+        out_slice,
+        turn,
+        after_attn,
+    ) = front(
+        lengths,
+        tokens,
+        cotangent,
+        query_weight,
+        key_weight,
+        value_weight,
+        output_weight,
+        gains_placed,
+        router_placed,
+        numbers,
+        jnp.concatenate([frequency, frequency]).reshape(1, head_dim),
+        heads_dev,
+        rep_count,
+        ep_count,
+        0,
+    )
+    gains_float = gains_all.reshape(-1)
     gain_in = gains_float[:width]
     gain_mid = gains_float[width : 2 * width]
     gain_query = gains_float[2 * width : 2 * width + head_dim]
-    gain_key = gains_float[2 * width + head_dim :]
-    numbers = jnp.concatenate([deal, priority, routes.T.reshape(-1)]).reshape(-1, 128)
-    numbers_all = gather_block(numbers, "ep").reshape(ep_count, -1, tok_dev)
+    gain_key = gains_float[2 * width + head_dim : 2 * width + 2 * head_dim]
+    router_full = (
+        router_all[:, :, :router_rows].transpose(1, 0, 2, 3).reshape(width, experts_all)
+    )
     deal_all = numbers_all[:, 0].reshape(-1)
     priority_all = numbers_all[:, 1].reshape(-1)
-    routes_all = numbers_all[:, 2:].transpose(0, 2, 1).reshape(group_rows, top_count)
+    routes_all = numbers_all[:, 2 : 2 + top_count].transpose(0, 2, 1).reshape(group_rows, top_count)
     segment_all, position_all = placement(deal_all, lengths[0])
-
-    chips = ep_count // 2
-    def columns_of(weight):
-        parts = weight.reshape(rows_dev, 2, heads_dev, chips, head_dim).transpose(3, 1, 0, 2, 4)
-        parts = parts.reshape(ep_count, rows_dev, slice_width)
-        return lax.all_to_all(parts, "ep", split_axis=0, concat_axis=0, tiled=True)
-
-    qkv_rows = jnp.concatenate(
-        [columns_of(query_weight), columns_of(key_weight), columns_of(value_weight)], axis=2
-    ).reshape(ep_count * rows_dev, 3 * slice_width)
-    qkv_slice = gather_block(qkv_rows, "rep")
-    out_rows = gather_block(output_weight, "rep").reshape(2, heads_dev, rows_dev, width)
-    out_own = lax.dynamic_index_in_dim(out_rows, core, 0, keepdims=False)
-    out_other = lax.ppermute(
-        lax.dynamic_index_in_dim(out_rows, 1 - core, 0, keepdims=False),
-        "ep",
-        [(i, i + 1 - 2 * (i % 2)) for i in range(ep_count)],
-    )
-    out_slice = jnp.where(
-        core == 0,
-        jnp.concatenate([out_own, out_other], axis=1),
-        jnp.concatenate([out_other, out_own], axis=1),
-    ).reshape(slice_width, width)
-
-    cot_all = all_gather(cotangent, rep_count, ep_count, True, 0)
-    tokens_group = (
-        all_gather(tokens, rep_count, ep_count, False, 1).reshape(group_rows, width).astype(f32)
-    )
-    normed_group = rms_scale(tokens_group, gain_in).astype(bf16)
-    projected = jnp.dot(normed_group, qkv_slice, preferred_element_type=f32)
-    query_pre = projected[:, :slice_width].reshape(group_rows, heads_dev, head_dim)
-    key_pre = projected[:, slice_width : 2 * slice_width].reshape(group_rows, heads_dev, head_dim)
-    value_low = projected[:, 2 * slice_width :].astype(bf16).reshape(group_rows, heads_dev, head_dim)
-    query_low = rope_norm(query_pre, gain_query, position_all).astype(bf16)
-    key_low = rope_norm(key_pre, gain_key, position_all).astype(bf16)
     same_seq = segment_all[:, None] == segment_all[None, :]
-    mixed, top_score, total_sum = attend_forward(
-        (query_low, key_low, value_low), same_seq, score_scale
-    )
-    mixed_low = mixed.reshape(group_rows, slice_width).astype(bf16)
-    attn_part = jnp.dot(mixed_low, out_slice, preferred_element_type=f32).astype(bf16)
+    normed_group = normed_group.reshape(group_rows, width)
+    qkv_slice = qkv_slice.reshape(width, 3 * slice_width)
+    out_slice = out_slice.reshape(slice_width, width)
+    query_pre = pre[:, :slice_width].reshape(group_rows, heads_dev, head_dim)
+    key_pre = pre[:, slice_width:].reshape(group_rows, heads_dev, head_dim)
+    query_low, key_low, value_low = (
+        qkv_low[:, i * slice_width : (i + 1) * slice_width].reshape(
+            group_rows, heads_dev, head_dim
+        )
+        for i in range(3)
+    )
     residual = tokens.astype(f32)
-    after_attn = residual + reduce_scatter(attn_part, rep_count, ep_count, False, 2).astype(f32)
     mid_low = rms_scale(after_attn, gain_mid).astype(bf16)
 
     logits = jnp.dot(mid_low, router_full, preferred_element_type=f32)
@@ -1563,14 +1990,12 @@
 
     mixed_cot = jnp.dot(attn_cot_group, out_slice.T, preferred_element_type=f32).astype(bf16)
     output_term = jnp.dot(mixed_low.T, attn_cot_group, preferred_element_type=f32)
-    query_cot, key_cot, value_cot = attend_backward(
+    query_cot, key_cot, value_cot = attend_again(
         (
             query_low,
             key_low,
             value_low,
             mixed_cot.reshape(group_rows, heads_dev, head_dim),
-            top_score,
-            total_sum,
         ),
         same_seq,
         score_scale,
@@ -1601,7 +2026,6 @@
             jnp.zeros((6 * width - 2 * head_dim,), f32),
         ]
     ).reshape(8, width)
-    router_rows = router_weight.size // 128
     router_parts = jnp.pad(
         router_term.reshape(rep_count, ep_count, router_rows, 128),
         ((0, 0), (0, 0), (0, -router_rows % 8), (0, 0)),

time: 902 us -> 744 us (0.82)
  blocking collectives: 59.9 us -> 0 us
  Pallas kernels: 650 us -> 605 us
  matrix products: 58.9 us -> 43 us
  between operations: 15.4 us -> 1.29 us
  waiting for transfers between devices: 11.7 us -> 0.02 us
  other arithmetic: 30.5 us -> 21 us
  local copies, waits for them, and re-layouts: 34.8 us -> 44.2 us
    pallas_call x1, Pallas kernels: 31.5 us -> 162 us  [front(): pl.pallas_call(partial(front_kernel, reps, eps), out_shape=outs, in_specs...]
    pallas_call x3 -> x1, Pallas kernels: 121 us -> 22.4 us  [all_gather(): pl.pallas_call(partial(ag_kernel, reps, across), out_shape=jax.ShapeDtype...]
    pallas_call x1, Pallas kernels: 193 us -> 117 us  [last_sums(): pl.pallas_call(partial(last_kernel, reps, eps), out_shape=outs, in_specs=...]
    all_gather x2 -> x0, blocking collectives: 50.5 us -> none  [gather_block(): return lax.all_gather(block, axes, axis=0, tiled=True)]
    dot_general x3 -> x0, matrix products: 14.2 us -> none  [the longest x1 6.67 us: on_device_split(): projected = jnp.dot(normed_group, qkv_slice, preferred_element_type=f32)]
    all_to_all x2 -> x0, waiting for transfers between devices: 11 us -> none  [columns_of(): return lax.all_to_all(parts, 'ep', split_axis=0, concat_axis=0, tiled=True)]
    all_to_all x1 -> x0, blocking collectives: 9.33 us -> none  [columns_of(): return lax.all_to_all(parts, 'ep', split_axis=0, concat_axis=0, tiled=True)]
    unnamed x99 -> x74, local copies, waits for them, and re-layouts: 13.5 us -> 18.8 us
  transfers between devices with their start and end apart: 11 -> 6, of which waited for: 2 -> 0; matrix products, arithmetic and copies ran while one was open for 6% -> 10% of each run, Pallas kernels for 34% -> 20%
where the time goes in v5:
time: 744 us; the launch traced here: 733 us
  Pallas kernels  605 us (81%)
  local copies, waits for them, and re-layouts  44.2 us (6%)
  matrix products  43 us (6%)
  other arithmetic  21 us (3%)
  starting transfers between devices  18.5 us (2%)
    pallas_call x1, Pallas kernels, moe(): pl.pallas_call(partial(moe_kernel, reps, side, experts_all), out_shape=ou...  287 us
    pallas_call x1, Pallas kernels, front(): pl.pallas_call(partial(front_kernel, reps, eps), out_shape=outs, in_specs...  162 us
    pallas_call x1, Pallas kernels, last_sums(): pl.pallas_call(partial(last_kernel, reps, eps), out_shape=outs, in_specs=...  117 us
    pallas_call x1, Pallas kernels, all_gather(): pl.pallas_call(partial(ag_kernel, reps, across), out_shape=jax.ShapeDtype...  22.4 us
    unnamed x74, local copies, waits for them, and re-layouts  18.8 us
    ppermute x6, starting transfers between devices, rows_of(): lax.ppermute(parts[k], 'rep', [(i, (i + k) % rep_count) for i in range(re...  18.5 us
    pallas_call x2, Pallas kernels, join_columns(): pl.pallas_call(partial(join_kernel, count), grid=(exp_dev, count), out_sh...  16.1 us
  transfers between devices with their start and end apart: 6, of which 0 were waited for; matrix products, arithmetic and copies ran while one was open for 10% of the time, Pallas kernels for 20%

profile of v5, /device:TPU:0, one launch (start us, length us, event | category | flops | bytes accessed | tf_op | source)
XLA Modules:
  0.0 732.9 jit_solution(14292948589374733055)
XLA Ops:
  1.3 0.8 copy.156
  2.2 0.7 convert_reduce_fusion
  2.9 0.7 pad_add_fusion.2
  4.8 0.8 dynamic_update_slice.3
  6.2 162.3 %shard_map.230 = (bf16[4,8,128,2048]{3,2,1,0:T(8,128)(2,1)}, bf16[8,4,16,128]{3,2,1,0:T(8,128)(2,1)}, s32[8,16,128]{2,1,0:T(8,128)}, f32[48,128]{1,0:T(8,128)}, ...) custom-call(s32[1,3]{1,0:T(1,128)} %lengths_ref.1, ...), custom_call_target="tpu_custom_call" | custom-call | tf_op jit(solution)/shard_map/pallas_call | solution.py:1805
  168.5 0.8 fusion.39
  169.4 0.8 slice_bitcast_fusion.10
  170.2 1.4 multiply_reduce_fusion.9
  171.6 1.3 fusion.40
  172.9 0.9 slice_bitcast_fusion.9
  173.8 0.7 reshape.288
  174.7 1.4 multiply_convert_fusion.1
  177.0 1.0 concatenate.17.x_ref
  178.0 287.2 %shard_map.231 = (bf16[128,2176]{1,0:T(8,128)(2,1)}, bf16[128,2048]{1,0:T(8,128)(2,1)}, bf16[4,3,512,256]{3,2,1,0:T(8,128)(2,1)}, bf16[4,3,512,256]{3,2,1,0:T(8,...) custom-call(bf16[128,2176]{1,0:T(8,128)(2,1)} %concatenate.17.x_ref,, ...), custom_call_target="tpu_custom_call" | custom-call | tf_op jit(solution)/shard_map/pallas_call | solution.py:1140
  465.2 3.7 slice_bitcast_fusion
  469.0 11.9 %collective-permute-start.3 = (bf16[3,512,256]{2,1,0:T(8,128)(2,1)}, bf16[3,512,256]{2,1,0:T(8,128)(2,1)}, u32[]{:S(2)}, u32[]{:S(2)}) collective-permute-start(bf16[3,512,256]{2,1,0:T(8,128)(2,1)} %get-tuple-element.137), channel_id=1, source_target_pairs={{0,8},{8,16},{16,24},{24,0},{1,9},{9,17},{17,25},{25,1},{2,10},{10... | collective-permute-start | bytes 2359304 | tf_op jit(solution)/shard_map/ppermute | solution.py:1970
  480.9 2.7 collective-permute-start.5
  483.6 1.8 slice_bitcast_fusion.4
  485.4 2.2 collective-permute-start.1
  487.6 0.9 multiply_reduce_fusion.10
  488.5 2.2 fusion.43
  490.7 1.7 multiply_reduce_fusion.3
  492.4 1.8 fusion.36
  494.2 22.4 %shard_map.232 = bf16[1,8,128,2048]{3,2,1,0:T(8,128)(2,1)} custom-call(bf16[128,2048]{1,0:T(8,128)(2,1)} %get-tuple-element.131.x_ref), custom_call_target="tpu_custom_call" | custom-call | tf_op jit(solution)/shard_map/pallas_call | solution.py:517
  516.9 1.6 broadcast_compare_fusion
  518.5 0.9 slice_bitcast_fusion.8
  519.9 3.9 convolution_convert_fusion.3
  523.8 5.7 fusion.42
  529.5 4.8 multiply_reduce_fusion
  534.3 1.0 slice-done.1
  535.3 2.4 multiply_convert_fusion
  537.8 2.5 fusion.7
  540.3 0.7 fusion.8
  541.0 0.8 copy-done.7
  541.9 1.1 fusion.38
  543.5 2.0 multiply_reduce_fusion.7
  546.0 0.8 slice_bitcast_fusion.13
  546.8 1.7 reshape.298
  548.5 2.0 multiply_reduce_fusion.5
  550.5 1.3 copy.177
  551.8 5.9 fusion.9
  557.6 1.9 multiply_cosine_fusion
  559.6 1.2 copy.170
  560.8 1.2 copy.175
  562.1 1.7 multiply_add_fusion.3
  564.8 2.2 convolution_convert_fusion.2
  567.7 1.4 copy-done.24
  569.2 5.0 convolution_convert_fusion
  574.2 1.6 collective-permute-start.2
  577.0 0.7 pad.30.router_ref
  577.7 7.7 %convolution_convert_fusion.1 = bf16[2048,768]{1,0:T(8,128)(2,1)} fusion(bf16[1024,2048]{1,0:T(8,128)(2,1)} %bitcast.119, bf16[1024,256]{0,1:T(8,128)(2,1)} %bitcast.122, bf16[1024,256]{0,1:T(8,128)(2,1)} %bitcast.104, bf16[1024,256]{0,1:T(8,128)(2,1)S(1)} %bitcast.102), kind=kOutput, calls=%fused_computation.13 | convolution fusion | flops 3227516928 | bytes 8912896 | tf_op jit(solution)/shard_map/dot_general | solution.py:2019
  585.5 116.8 %shard_map.233 = (f32[128,2048]{1,0:T(8,128)}, f32[64,2048]{1,0:T(8,128)}, f32[64,2048]{1,0:T(8,128)}, f32[64,2048]{1,0:T(8,128)}, f32[64,2048]{1,0:T(8,128)}, /*index=5*/f32[8,2048]{1,0:T(8,128)}, f32[16,128]{1,0:T(8,128)}) custom-call(bf16[4,2,128,2048]{3,2,1,0:T(8,128)(2,1)} %bitcast.96, bf16[4,512,768]{2,1,0:T(8,128)(2,1)} %bitcast.97, ...), custom_call_target="tpu_custom_call" | custom-call | tf_op jit(solution)/shard_map/pallas_call | solution.py:1370
  702.3 0.9 copy.193
  703.1 0.8 reshape.307
  703.9 0.7 copy.182
  705.2 8.0 %shard_map.235 = f32[3,512,1024]{2,1,0:T(8,128)} custom-call(bf16[3,512,256]{2,1,0:T(8,128)(2,1)} %get-tuple-element.138.refs_0_, bf16[3,512,256]{2,1,0:T(8,128)(2,1)} %collective-permute-done.3.refs_1_, bf16[3,512,256]{2,1,0:T(8,128)(2,1)} %collective-permute-done.4.refs_2_, bf16[3,512,256]{2,1,0:T(8,128)(2,1)} %collective-permute-done.5.refs_3_), custom_call_target="tpu_custom_call" | custom-call | tf_op jit(solution)/shard_map/pallas_call | solution.py:1402
  713.2 0.9 copy-done.13
  714.1 8.1 %shard_map.234 = f32[3,512,1024]{2,1,0:T(8,128)} custom-call(bf16[3,512,256]{2,1,0:T(8,128)(2,1)} %get-tuple-element.142.refs_0_, bf16[3,512,256]{2,1,0:T(8,128)(2,1)} %collective-permute-done.refs_1_, bf16[3,512,256]{2,1,0:T(8,128)(2,1)} %collective-permute-done.1.refs_2_, bf16[3,512,256]{2,1,0:T(8,128)(2,1)} %copy-done.13), custom_call_target="tpu_custom_call" | custom-call | tf_op jit(solution)/shard_map/pallas_call | solution.py:1402
  722.2 1.0 copy.211
  723.2 0.8 copy.212
  724.0 0.8 copy.213
  724.8 0.8 copy.214
  725.6 0.8 copy.215
  726.4 6.3 copy.216
  (103 shorter events, 8.9 us)
Async XLA Ops:
  0.6 176.0 %copy-start.23 = (s32[128]{0:T(128)S(1)}, s32[128]{0:T(128)}, u32[]{:S(2)}) copy-start(s32[128]{0:T(128)} %param.29) | copy-start | bytes 1540
  5.6 0.6 copy-start.21
  174.5 1.6 copy-start.2
  465.2 18.4 %copy-start.6 = (bf16[4,3,512,256]{3,2,1,0:T(8,128)(2,1)S(1)}, bf16[4,3,512,256]{3,2,1,0:T(8,128)(2,1)}, u32[]{:S(2)}) copy-start(bf16[4,3,512,256]{3,2,1,0:T(8,128)(2,1)} %get-tuple-element.54) | copy-start | bytes 9437188
  468.9 21.7 %copy-start = (f32[128,2048]{1,0:T(8,128)S(1)}, f32[128,2048]{1,0:T(8,128)}, u32[]{:S(2)}) copy-start(f32[128,2048]{1,0:T(8,128)} %get-tuple-element.34) | copy-start | bytes 3145732
  469.0 21.7 %copy-start.3 = (bf16[2048,24]{1,0:T(8,128)(2,1)S(1)}, bf16[2048,24]{1,0:T(8,128)(2,1)}, u32[]{:S(2)}) copy-start(bf16[2048,24]{1,0:T(8,128)(2,1)} %copy-done.2) | copy-start | bytes 294916
  469.0 105.3 %collective-permute-start.3 = (bf16[3,512,256]{2,1,0:T(8,128)(2,1)}, bf16[3,512,256]{2,1,0:T(8,128)(2,1)}, u32[]{:S(2)}, u32[]{:S(2)}) collective-permute-start(bf16[3,512,256]{2,1,0:T(8,128)(2,1)} %get-tuple-element.137), channel_id=1, source_target_pairs={{0,8},{8,16},{16,24},{24,0},{1,9},{9,17},{17,25},{25,1},{2,10},{10... | collective-permute-start | bytes 2359304 | tf_op jit(solution)/shard_map/ppermute | solution.py:1970
  480.9 224.4 %collective-permute-start.4 = (bf16[3,512,256]{2,1,0:T(8,128)(2,1)}, bf16[3,512,256]{2,1,0:T(8,128)(2,1)}, u32[]{:S(2)}, u32[]{:S(2)}) collective-permute-start(bf16[3,512,256]{2,1,0:T(8,128)(2,1)} %get-tuple-element.136), channel_id=1, source_target_pairs={{0,16},{8,24},{16,0},{24,8},{1,17},{9,25},{17,1},{25,9},{2,18},{10... | collective-permute-start | bytes 2359304 | tf_op jit(solution)/shard_map/ppermute | solution.py:1970
  480.9 224.4 %collective-permute-start.5 = (bf16[3,512,256]{2,1,0:T(8,128)(2,1)}, bf16[3,512,256]{2,1,0:T(8,128)(2,1)}, u32[]{:S(2)}, u32[]{:S(2)}) collective-permute-start(bf16[3,512,256]{2,1,0:T(8,128)(2,1)} %get-tuple-element.135), channel_id=1, source_target_pairs={{0,24},{8,0},{16,8},{24,16},{1,25},{9,1},{17,9},{25,17},{2,26},{10... | collective-permute-start | bytes 2359304 | tf_op jit(solution)/shard_map/ppermute | solution.py:1970
  483.6 8.7 %copy-start.8 = (bf16[128,2048]{1,0:T(8,128)(2,1)S(1)}, bf16[128,2048]{1,0:T(8,128)(2,1)}, u32[]{:S(2)}) copy-start(bf16[128,2048]{1,0:T(8,128)(2,1)} %cot_ref.1) | copy-start | bytes 1572868
  483.6 8.8 %copy-start.14 = (bf16[128,2048]{1,0:T(8,128)(2,1)S(1)}, bf16[128,2048]{1,0:T(8,128)(2,1)}, u32[]{:S(2)}) copy-start(bf16[128,2048]{1,0:T(8,128)(2,1)} %get-tuple-element.39) | copy-start | bytes 1572868
  485.4 227.8 %collective-permute-start = (bf16[3,512,256]{2,1,0:T(8,128)(2,1)}, bf16[3,512,256]{2,1,0:T(8,128)(2,1)}, u32[]{:S(2)}, u32[]{:S(2)}) collective-permute-start(bf16[3,512,256]{2,1,0:T(8,128)(2,1)} %get-tuple-element.141), channel_id=1, source_target_pairs={{0,8},{8,16},{16,24},{24,0},{1,9},{9,17},{17,25},{25,1},{2,10},{10... | collective-permute-start | bytes 2359304 | tf_op jit(solution)/shard_map/ppermute | solution.py:1970
  485.4 227.8 %collective-permute-start.1 = (bf16[3,512,256]{2,1,0:T(8,128)(2,1)}, bf16[3,512,256]{2,1,0:T(8,128)(2,1)}, u32[]{:S(2)}, u32[]{:S(2)}) collective-permute-start(bf16[3,512,256]{2,1,0:T(8,128)(2,1)} %get-tuple-element.140), channel_id=1, source_target_pairs={{0,16},{8,24},{16,0},{24,8},{1,17},{9,25},{17,1},{25,9},{2,18},{10... | collective-permute-start | bytes 2359304 | tf_op jit(solution)/shard_map/ppermute | solution.py:1970
  492.4 24.2 %copy-start.22 = (s32[1,3]{1,0:T(1,128)S(1)}, s32[1,3]{1,0:T(1,128)}, u32[]{:S(2)}) copy-start(s32[1,3]{1,0:T(1,128)} %lengths_ref.1) | copy-start | bytes 40
  494.1 24.3 %copy-start.9 = (bf16[1024,768]{1,0:T(8,128)(2,1)S(1)}, bf16[1024,768]{1,0:T(8,128)(2,1)}, u32[]{:S(2)}) copy-start(bf16[1024,768]{1,0:T(8,128)(2,1)} %get-tuple-element.40) | copy-start | bytes 4718596
  519.6 4.1 copy-start.11
  523.7 5.7 copy-start.27
  523.8 5.7 copy-start.20
  529.5 4.8 slice-start
  529.5 5.8 slice-start.1
  540.3 1.6 copy-start.7
  557.6 6.2 copy-start.1
  562.1 2.6 copy-start.5
  562.1 2.7 copy-start.25
  567.0 2.1 copy-start.24
  567.0 2.2 copy-start.26
  567.6 6.6 copy-start.15
  569.2 5.0 copy-start.12
  569.2 6.7 copy-start.4
  574.2 139.0 %collective-permute-start.2 = (bf16[3,512,256]{2,1,0:T(8,128)(2,1)S(1)}, bf16[3,512,256]{2,1,0:T(8,128)(2,1)S(1)}, u32[]{:S(2)}, u32[]{:S(2)}) collective-permute-start(bf16[3,512,256]{2,1,0:T(8,128)(2,1)S(1)} %copy-done.12), channel_id=1, source_target_pairs={{0,24},{8,0},{16,8},{24,16},{1,25},{9,1},{17,9},{25,17},{2,26},{10... | collective-permute-start | bytes 2359304 | tf_op jit(solution)/shard_map/ppermute | solution.py:1970
  713.2 0.9 copy-start.13
  714.1 8.1 %copy-start.10 = (f32[128,2048]{1,0:T(8,128)S(1)}, f32[128,2048]{1,0:T(8,128)}, u32[]{:S(2)}) copy-start(f32[128,2048]{1,0:T(8,128)} %get-tuple-element.185) | copy-start | bytes 3145732
  714.1 9.1 %copy-start.19 = (f32[64,2048]{1,0:T(8,128)S(1)}, f32[64,2048]{1,0:T(8,128)}, u32[]{:S(2)}) copy-start(f32[64,2048]{1,0:T(8,128)} %get-tuple-element.186) | copy-start | bytes 1572868
  714.1 9.9 %copy-start.18 = (f32[64,2048]{1,0:T(8,128)S(1)}, f32[64,2048]{1,0:T(8,128)}, u32[]{:S(2)}) copy-start(f32[64,2048]{1,0:T(8,128)} %get-tuple-element.187) | copy-start | bytes 1572868
  722.2 2.6 copy-start.17
  722.2 3.4 copy-start.16

commit v6 on v5

--- a/solution.py
+++ b/solution.py
@@ -87,14 +87,6 @@
     )
     value_grad = jnp.einsum("hts,thd->shd", prob_low, head_grad, preferred_element_type=jnp.float32)
     return (query_grad, key_grad, value_grad)
-
-
-def attend_again(parts, same_seq, score_scale):
-    head_query, head_key, head_value, head_grad = parts
-    _, top_score, total_sum = attend_forward(
-        (head_query, head_key, head_value), same_seq, score_scale
-    )
-    return attend_backward((*parts, top_score, total_sum), same_seq, score_scale)
 
 
 def on_device_general(
@@ -377,303 +369,6 @@
     return sib, (xn, yn, dg)
 
 
-def greet(z, e, reps, across):
-    barrier = pltpu.get_barrier_semaphore()
-    sib, chips = partners(e)
-    for other in (sib, *chips):
-        pl.semaphore_signal(barrier, inc=1, device_id={"rep": z, "ep": other}, device_id_type=MESH)
-    if across:
-        @pl.when(z > 0)
-        def _():
-            pl.semaphore_signal(barrier, inc=1, device_id={"rep": z - 1, "ep": e}, device_id_type=MESH)
-        @pl.when(z < reps - 1)
-        def _():
-            pl.semaphore_signal(barrier, inc=1, device_id={"rep": z + 1, "ep": e}, device_id_type=MESH)
-    peers = 4
-    if across:
-        peers = peers + jnp.where(z > 0, 1, 0) + jnp.where(z < reps - 1, 1, 0)
-    pl.semaphore_wait(barrier, peers)
-
-
-def ag_kernel(reps, across, x_ref, out_ref, own_sem, zs, zr, ps, pr, cs, cr):
-    z = lax.axis_index("rep")
-    e = lax.axis_index("ep")
-    sib, chips = partners(e)
-    greet(z, e, reps, across)
-    own = z if across else 0
-    groups = reps if across else 1
-    half = x_ref.shape[0] // 2
-    local = pltpu.make_async_copy(x_ref, out_ref.at[own, e], own_sem)
-    local.start()
-
-    def zcopy(src, g, up):
-        d = 0 if up else 1
-        return pltpu.make_async_remote_copy(
-            src_ref=src, dst_ref=out_ref.at[g, e], send_sem=zs.at[d, g], recv_sem=zr.at[g],
-            device_id={"rep": z + 1 if up else z - 1, "ep": e}, device_id_type=MESH)
-
-    def pcopy(src, g, j):
-        return pltpu.make_async_remote_copy(
-            src_ref=src, dst_ref=out_ref.at[g, e], send_sem=ps.at[g, j], recv_sem=pr.at[g, j],
-            device_id={"rep": z, "ep": chips[j]}, device_id_type=MESH)
-
-    def relay(g, j):
-        rows = pl.ds(half * j, half)
-        part = out_ref.at[g, chips[j], rows]
-        return pltpu.make_async_remote_copy(
-            src_ref=part, dst_ref=part, send_sem=ps.at[g, 2 + j], recv_sem=pr.at[g, 2 + j],
-            device_id={"rep": z, "ep": chips[1 - j]}, device_id_type=MESH)
-
-    def relayed(g, j):
-        part = out_ref.at[g, chips[2], pl.ds(half * j, half)]
-        return pltpu.make_async_remote_copy(
-            src_ref=part, dst_ref=part, send_sem=ps.at[g, 2 + j], recv_sem=pr.at[g, 2 + j],
-            device_id={"rep": z, "ep": chips[1 - j]}, device_id_type=MESH)
-
-    def ccopy(src, g, j):
-        who = e if j == 0 else chips[j - 1]
-        return pltpu.make_async_remote_copy(
-            src_ref=src, dst_ref=out_ref.at[g, who], send_sem=cs.at[g, j], recv_sem=cr.at[g, j],
-            device_id={"rep": z, "ep": sib}, device_id_type=MESH)
-
-    def spread(src, g):
-        pcopy(src, g, 0).start()
-        pcopy(src, g, 1).start()
-        ccopy(src, g, 0).start()
-
-    def pass_on(g):
-        for j in range(2):
-            pcopy(x_ref, g, j).wait_recv()
-            relay(g, j).start()
-            ccopy(out_ref.at[g, chips[j]], g, j + 1).start()
-
-    def finish(g):
-        for j in range(2):
-            relayed(g, j).wait_recv()
-        ccopy(out_ref.at[g, chips[2]], g, 3).start()
-
-    def at(k, fn):
-        if k == 0:
-            fn(own)
-            return
-        @pl.when(z - k >= 0)
-        def _():
-            fn(z - k)
-        @pl.when(z + k < reps)
-        def _():
-            fn(z + k)
-
-    if across:
-        @pl.when(z < reps - 1)
-        def _():
-            zcopy(x_ref, z, True).start()
-        @pl.when(z > 0)
-        def _():
-            zcopy(x_ref, z, False).start()
-    spread(x_ref, own)
-    for k in range(1, groups):
-        @pl.when(z - k >= 0)
-        def _():
-            g = z - k
-            zcopy(x_ref, g, True).wait_recv()
-            @pl.when(z < reps - 1)
-            def _():
-                zcopy(out_ref.at[g, e], g, True).start()
-            spread(out_ref.at[g, e], g)
-        @pl.when(z + k < reps)
-        def _():
-            g = z + k
-            zcopy(x_ref, g, False).wait_recv()
-            @pl.when(z > 0)
-            def _():
-                zcopy(out_ref.at[g, e], g, False).start()
-            spread(out_ref.at[g, e], g)
-        at(k - 1, pass_on)
-        if k >= 2:
-            at(k - 2, finish)
-    at(groups - 1, pass_on)
-    if groups >= 2:
-        at(groups - 2, finish)
-    at(groups - 1, finish)
-    local.wait()
-    for g in range(groups):
-        for j in range(4):
-            ccopy(x_ref, g, j).wait()
-        for j in range(2):
-            pcopy(x_ref, g, j).wait_send()
-            relay(g, j).wait_send()
-        if across:
-            @pl.when((z < reps - 1) & (z >= g))
-            def _():
-                zcopy(x_ref, g, True).wait_send()
-            @pl.when((z > 0) & (z <= g))
-            def _():
-                zcopy(x_ref, g, False).wait_send()
-
-
-def all_gather(x, reps, eps, across, cid):
-    groups = reps if across else 1
-    D = pltpu.SemaphoreType.DMA
-    out = pl.pallas_call(
-        partial(ag_kernel, reps, across),
-        out_shape=jax.ShapeDtypeStruct((groups, eps, *x.shape), x.dtype),
-        in_specs=[pl.BlockSpec(memory_space=pl.ANY)],
-        out_specs=pl.BlockSpec(memory_space=pl.ANY),
-        scratch_shapes=[D, D((2, reps)), D((reps,)), D((groups, 4)), D((groups, 4)), D((groups, 4)), D((groups, 4))],
-        compiler_params=pltpu.CompilerParams(collective_id=cid, has_side_effects=True),
-    )(x)
-    return out
-
-
-def rs_kernel(reps, across, p_ref, out_ref, own, sib_in, chip_in, up_in, down_in, res,
-              own_sem, ss, sr, ps, pr, us, ur, ds, dr):
-    z = lax.axis_index("rep")
-    e = lax.axis_index("ep")
-    core = e % 2
-    chip = e // 2
-    sib, chips = partners(e)
-    groups = reps if across else 1
-    greet(z, e, reps, across)
-    rows, W = res.shape[1], res.shape[2]
-    half = reps // 2
-
-    def order(s):
-        if not across:
-            return 0
-        t = reps - 1 - s
-        down = jnp.where(t > z, t, t - 1)
-        upw = jnp.where(s < z, s, s + 1)
-        g = jnp.where(z < half, down, upw)
-        return z if s == reps - 1 else g
-
-    def sibcopy(g):
-        return pltpu.make_async_remote_copy(
-            src_ref=p_ref.at[g, :, 1 - core], dst_ref=sib_in.at[g], send_sem=ss.at[g], recv_sem=sr.at[g],
-            device_id={"rep": z, "ep": sib}, device_id_type=MESH)
-
-    def load(g):
-        return pltpu.make_async_copy(p_ref.at[g, :, core], own.at[g], own_sem.at[g])
-
-    def pcopy(g, j):
-        return pltpu.make_async_remote_copy(
-            src_ref=own.at[g, chips[j] // 2], dst_ref=chip_in.at[g, j], send_sem=ps.at[g, j], recv_sem=pr.at[g, j],
-            device_id={"rep": z, "ep": chips[j]}, device_id_type=MESH)
-
-    def zcopy(g, up):
-        if up:
-            return pltpu.make_async_remote_copy(
-                src_ref=res.at[g], dst_ref=up_in.at[g], send_sem=us.at[g], recv_sem=ur.at[g],
-                device_id={"rep": z + 1, "ep": e}, device_id_type=MESH)
-        return pltpu.make_async_remote_copy(
-            src_ref=res.at[g], dst_ref=down_in.at[g], send_sem=ds.at[g], recv_sem=dr.at[g],
-            device_id={"rep": z - 1, "ep": e}, device_id_type=MESH)
-
-    for s in range(groups):
-        g = order(s)
-        sibcopy(g).start()
-        load(g).start()
-    step = 16
-
-    def add_in(g, q):
-        @pl.loop(0, rows // step)
-        def _(i):
-            r = pl.ds(pl.multiple_of(i * step, step), step)
-            own[g, q, r, :] = (own[g, q, r, :].astype(jnp.float32) + sib_in[g, q, r, :].astype(jnp.float32)).astype(own.dtype)
-
-    def stage1(g):
-        load(g).wait()
-        sibcopy(g).wait_recv()
-        for j in (2, 0, 1):
-            add_in(g, chips[j] // 2)
-            pcopy(g, j).start()
-
-    def stage2(g):
-        for j in range(3):
-            pcopy(g, j).wait_recv()
-        @pl.loop(0, rows // step)
-        def _(i):
-            r = pl.ds(pl.multiple_of(i * step, step), step)
-            t = own[g, chip, r, :].astype(jnp.float32) + sib_in[g, chip, r, :].astype(jnp.float32)
-            for j in range(3):
-                t = t + chip_in[g, j, r, :].astype(jnp.float32)
-            res[g, r, :] = t.astype(res.dtype)
-
-    def plus(g, ref):
-        @pl.loop(0, rows // step)
-        def _(i):
-            r = pl.ds(pl.multiple_of(i * step, step), step)
-            res[g, r, :] = (res[g, r, :].astype(jnp.float32) + ref[g, r, :].astype(jnp.float32)).astype(res.dtype)
-
-    def stage3(g):
-        @pl.when(g > z)
-        def _():
-            @pl.when(z > 0)
-            def _():
-                zcopy(g, True).wait_recv()
-                plus(g, up_in)
-            zcopy(g, True).start()
-        @pl.when(g < z)
-        def _():
-            @pl.when(z < reps - 1)
-            def _():
-                zcopy(g, False).wait_recv()
-                plus(g, down_in)
-            zcopy(g, False).start()
-
-    stage1(order(0))
-    for s in range(1, groups):
-        stage1(order(s))
-        stage2(order(s - 1))
-        if s >= 2:
-            stage3(order(s - 2))
-    stage2(order(groups - 1))
-    if across:
-        stage3(order(groups - 2))
-        @pl.when(z > 0)
-        def _():
-            zcopy(z, True).wait_recv()
-            plus(z, up_in)
-        @pl.when(z < reps - 1)
-        def _():
-            zcopy(z, False).wait_recv()
-            plus(z, down_in)
-    fin = res.at[z if across else 0]
-    out = pltpu.make_async_copy(fin, out_ref, own_sem.at[0])
-    out.start()
-    out.wait()
-    for g in range(groups):
-        sibcopy(g).wait_send()
-        for j in range(3):
-            pcopy(g, j).wait_send()
-        if across:
-            @pl.when(g > z)
-            def _():
-                zcopy(g, True).wait_send()
-            @pl.when(g < z)
-            def _():
-                zcopy(g, False).wait_send()
-
-
-def reduce_scatter(p, reps, eps, across, cid):
-    groups = reps if across else 1
-    W = p.shape[1]
-    rows = p.shape[0] // groups // eps
-    p = p.reshape(groups, eps // 2, 2, rows, W)
-    D = pltpu.SemaphoreType.DMA
-    V = pltpu.VMEM
-    q = eps // 2
-    return pl.pallas_call(
-        partial(rs_kernel, reps, across),
-        out_shape=jax.ShapeDtypeStruct((rows, W), p.dtype),
-        in_specs=[pl.BlockSpec(memory_space=pl.ANY)],
-        out_specs=pl.BlockSpec(memory_space=pl.ANY),
-        scratch_shapes=[V((groups, q, rows, W), p.dtype), V((groups, q, rows, W), p.dtype), V((groups, 3, rows, W), p.dtype),
-                        V((groups, rows, W), p.dtype), V((groups, rows, W), p.dtype), V((groups, rows, W), p.dtype),
-                        D((groups,)), D((groups,)), D((groups,)), D((groups, 3)), D((groups, 3)),
-                        D((groups,)), D((groups,)), D((groups,)), D((groups,))],
-        compiler_params=pltpu.CompilerParams(collective_id=cid, has_side_effects=True, vmem_limit_bytes=56 * 2**20),
-    )(p)
-
 NT = (((1,), (1,)), ((), ()))
 TN = (((0,), (0,)), ((), ()))
 
@@ -841,19 +536,13 @@
             dots = jnp.sum(hid * hc, axis=1, keepdims=True)
             return cots + jnp.where(lane == index, dots, 0.0)
 
-        cots = lax.fori_loop(0, exp_dev, one, jnp.zeros((2 * rows, side_lanes), f32))
+        cots = lax.fori_loop(0, exp_dev, one, jnp.zeros((2 * rows, side_lanes), f32), unroll=True)
         pbuf[slot, :, :, pl.ds(width, side_lanes)] = cots.astype(bf16).reshape(2, rows, side_lanes)
-        block = min(512, width)
-
-        @pl.loop(0, width // block)
-        def _(n):
-            cut = pl.ds(pl.multiple_of(n * block, block), block)
-            t = lax.dot_general(abuf[slot, 0], wgu[0, cut, :], NT, preferred_element_type=f32)
-            t = t + lax.dot_general(abuf[slot, 1], wgu[1, cut, :], NT, preferred_element_type=f32)
-            pbuf[slot, :, :, cut] = t.astype(bf16).reshape(2, rows, block)
-            t = jnp.dot(abuf[slot, 2], wd[:, cut], preferred_element_type=f32)
-            cut = pl.ds(pl.multiple_of(W1 + n * block, 128), block)
-            pbuf[slot, :, :, cut] = t.astype(bf16).reshape(2, rows, block)
+        t = lax.dot_general(abuf[slot, 0], wgu[0], NT, preferred_element_type=f32)
+        t = t + lax.dot_general(abuf[slot, 1], wgu[1], NT, preferred_element_type=f32)
+        pbuf[slot, :, :, pl.ds(0, width)] = t.astype(bf16).reshape(2, rows, width)
+        t = jnp.dot(abuf[slot, 2], wd[...], preferred_element_type=f32)
+        pbuf[slot, :, :, pl.ds(W1, width)] = t.astype(bf16).reshape(2, rows, width)
 
     def sibcopy(i):
         return pltpu.make_async_remote_copy(
@@ -1157,11 +846,177 @@
     )(x, cot_all, eg, eu, ed)[:5]
 
 
+def back_kernel(heads_dev, cot_ref, wout_ref, mixed_ref, qkv_ref, pre_ref, turn_ref, segs_ref, gains_ref, normed_ref, wqkv_ref,
+                part_ref, qkv_out, out_out, gain_out,
+                cots, wout, mixed, qkv, pre, turn, segs, gains, normed, wqkv, probs, dsc, dmix, dkey, pcot, part, term, oterm, gsum,
+                l_sem, o_sem, ts, tr, tcs, tcr):
+    f32, bf16 = jnp.float32, jnp.bfloat16
+    z = lax.axis_index("rep")
+    e = lax.axis_index("ep")
+    sib, chips = partners(e)
+    eps, rows, width = cots.shape
+    half = rows // 2
+    group_rows = eps * rows
+    slice_width = mixed.shape[1]
+    head_dim = slice_width // heads_dev
+    scale = head_dim ** -0.5
+
+    barrier = pltpu.get_barrier_semaphore()
+    for other in (sib, *chips):
+        pl.semaphore_signal(barrier, inc=1, device_id={"rep": z, "ep": other}, device_id_type=MESH)
+    pairs = ((qkv_ref, qkv), (segs_ref, segs), (wout_ref, wout), (mixed_ref, mixed), (pre_ref, pre), (turn_ref, turn),
+             (gains_ref, gains), (normed_ref, normed), (wqkv_ref, wqkv), (cot_ref, cots.at[e]))
+    loads = [pltpu.make_async_copy(a, b, l_sem.at[n]) for n, (a, b) in enumerate(pairs)]
+    for c in loads:
+        c.start()
+    pl.semaphore_wait(barrier, 4)
+
+    def remote(src, dst, send, recv, ep):
+        return pltpu.make_async_remote_copy(src_ref=src, dst_ref=dst, send_sem=send, recv_sem=recv,
+                                            device_id={"rep": z, "ep": ep}, device_id_type=MESH)
+
+    def near(j):
+        return remote(cot_ref, cots.at[e], ts.at[j], tr.at[j], chips[j])
+
+    def relay(j, source):
+        p = cots.at[source, pl.ds(half * j, half)]
+        return remote(p, p, ts.at[2 + j], tr.at[2 + j], chips[1 - j])
+
+    def other_core(j):
+        if j == 0:
+            return remote(cot_ref, cots.at[e], tcs.at[0], tcr.at[0], sib)
+        p = cots.at[chips[j - 1]]
+        return remote(p, p, tcs.at[j], tcr.at[j], sib)
+
+    near(0).start()
+    near(1).start()
+    other_core(0).start()
+
+    block = 2 * rows
+    blocks = group_rows // block
+    loads[0].wait()
+    loads[1].wait()
+    seg_row = jnp.concatenate([segs[n:n + 1, :] for n in range(eps)], axis=1)
+
+    def softmax(h, n):
+        here = pl.ds(n * block, block)
+        cut = slice(h * head_dim, (h + 1) * head_dim)
+        kcut = slice(slice_width + h * head_dim, slice_width + (h + 1) * head_dim)
+        s = lax.dot_general(qkv[here, cut], qkv[:, kcut], NT, preferred_element_type=f32) * scale
+        seg_col = jnp.concatenate(
+            [jnp.broadcast_to(segs[2 * n + j:2 * n + j + 1, :], (rows, rows)).T[:, 0:1] for j in range(2)], axis=0)
+        s = jnp.where(seg_col == seg_row, s, masked_score)
+        p = jnp.exp(s - jnp.max(s, axis=-1, keepdims=True))
+        probs[h, here, :] = p / jnp.sum(p, axis=-1, keepdims=True)
+
+    for n in range(blocks):
+        softmax(0, n)
+    for j in range(2):
+        near(j).wait_recv()
+        relay(j, chips[j]).start()
+        other_core(j + 1).start()
+    for h in range(1, heads_dev):
+        for n in range(blocks):
+            softmax(h, n)
+    for j in range(2):
+        relay(j, chips[2]).wait_recv()
+    other_core(3).start()
+    for c in loads[2:]:
+        c.wait()
+    for j in range(4):
+        other_core(j).wait_recv()
+
+    flat = cots[...].reshape(group_rows, width)
+    weight = wout[...].reshape(slice_width, width)
+    for n in range(blocks):
+        here = pl.ds(n * block, block)
+        left = cots[pl.ds(2 * n, 2)].reshape(block, width)
+        dmix[here, :] = lax.dot_general(left, weight, NT, preferred_element_type=f32).astype(bf16)
+    oterm[...] = lax.dot_general(mixed[...], flat, TN, preferred_element_type=f32).astype(bf16).reshape(oterm.shape)
+    outs = [pltpu.make_async_copy(oterm, out_out, o_sem.at[0])]
+    outs[0].start()
+
+    def through_norm(index, dy, here, gain_row):
+        cut = slice(index * head_dim, (index + 1) * head_dim)
+        x = pre[here, cut]
+        dn = dy * turn[0, here, :] + pltpu.roll(dy * turn[1, here, :], head_dim // 2, 1)
+        r = lax.rsqrt(jnp.mean(x * x, axis=-1, keepdims=True) + norm_eps)
+        unit = x * r
+        gsum[gain_row:gain_row + 1, :] += jnp.sum(dn * unit, axis=0, keepdims=True)
+        base = 2 * width // 128 + gain_row
+        w = dn * gains[base:base + 1, :]
+        pcot[here, cut] = (r * (w - unit * jnp.mean(w * unit, axis=-1, keepdims=True))).astype(bf16)
+
+    gsum[...] = jnp.zeros_like(gsum)
+    for h in range(heads_dev):
+        cut = slice(h * head_dim, (h + 1) * head_dim)
+        kcut = slice(slice_width + h * head_dim, slice_width + (h + 1) * head_dim)
+        vcut = slice(2 * slice_width + h * head_dim, 2 * slice_width + (h + 1) * head_dim)
+        for n in range(blocks):
+            here = pl.ds(n * block, block)
+            p = probs[h, here, :]
+            dp = lax.dot_general(dmix[here, cut], qkv[:, vcut], NT, preferred_element_type=f32)
+            ds = (p * (dp - jnp.sum(p * dp, axis=-1, keepdims=True))).astype(bf16)
+            dsc[0, here, :] = ds
+            dsc[1, here, :] = p.astype(bf16)
+            through_norm(h, jnp.dot(ds, qkv[:, kcut], preferred_element_type=f32) * scale, here, 0)
+        dkey[...] = lax.dot_general(dsc[0], qkv[:, cut], TN, preferred_element_type=f32) * scale
+        for n in range(blocks):
+            here = pl.ds(n * block, block)
+            through_norm(heads_dev + h, dkey[here, :], here, 1)
+        pcot[:, vcut] = lax.dot_general(dsc[1], dmix[:, cut], TN, preferred_element_type=f32).astype(bf16)
+    outs.append(pltpu.make_async_copy(gsum, gain_out, o_sem.at[1]))
+    outs[-1].start()
+
+    for n in range(blocks):
+        here = pl.ds(n * block, block)
+        t = lax.dot_general(pcot[here, :], wqkv[...], NT, preferred_element_type=f32)
+        part[n] = t.astype(bf16).reshape(2, rows, width)
+        outs.append(pltpu.make_async_copy(part.at[n], part_ref.at[n], o_sem.at[2 + n]))
+        outs[-1].start()
+    piece = width // term.shape[0]
+    for n in range(term.shape[0]):
+        left = normed[:, n * piece:(n + 1) * piece]
+        term[n] = lax.dot_general(left, pcot[...], TN, preferred_element_type=f32).astype(bf16)
+        outs.append(pltpu.make_async_copy(term.at[n], qkv_out.at[n], o_sem.at[2 + blocks + n]))
+        outs[-1].start()
+    for c in outs:
+        c.wait()
+    for j in range(2):
+        near(j).wait_send()
+        relay(j, chips[j]).wait_send()
+    for j in range(4):
+        other_core(j).wait_send()
+
+
+def attention_back(cot, wout, mixed, qkv, pre, turn, segs, gains, normed, wqkv, reps, eps, cid):
+    rows, width = cot.shape
+    heads_dev = wout.shape[0]
+    gr, sw = mixed.shape
+    f32, bf16 = jnp.float32, jnp.bfloat16
+    S, V, D = jax.ShapeDtypeStruct, pltpu.VMEM, pltpu.SemaphoreType.DMA
+    hd = sw // heads_dev
+    outs = (S((eps // 2, 2, rows, width), bf16), S((reps, width // reps, 3 * sw), bf16), S(wout.shape, bf16), S((8, hd), f32))
+    return pl.pallas_call(
+        partial(back_kernel, heads_dev),
+        out_shape=outs,
+        in_specs=[pl.BlockSpec(memory_space=pl.ANY)] * 10,
+        out_specs=[pl.BlockSpec(memory_space=pl.ANY)] * len(outs),
+        scratch_shapes=[
+            V((eps, rows, width), bf16), *[V(a.shape, a.dtype) for a in (wout, mixed, qkv, pre, turn, segs, gains, normed, wqkv)],
+            V((heads_dev, gr, gr), f32), V((2, gr, gr), bf16), V((gr, sw), bf16), V((gr, hd), f32), V((gr, 3 * sw), bf16),
+            V(outs[0].shape, bf16), V(outs[1].shape, bf16), V(wout.shape, bf16), V((8, hd), f32),
+            D((10,)), D((2 + eps // 2 + reps,)), D((4,)), D((4,)), D((4,)), D((4,)),
+        ],
+        compiler_params=pltpu.CompilerParams(collective_id=cid, has_side_effects=True, vmem_limit_bytes=58 * 2**20),
+    )(cot, wout, mixed, qkv, pre, turn, segs, gains, normed, wqkv)
+
+
 def last_kernel(reps, eps, part_ref, qkv_ref, out_ref, tok_ref, cot_ref, gain_ref, gains_ref, router_ref,
                 input_ref, q_ref, k_ref, v_ref, o_ref, gsum_ref, rsum_ref,
-                own, sib_in, relay_in, xin, yin, wo, qown, zq, zo, fin, gath, mats, omat, tok, cot, gain,
+                own, sib_in, relay_in, xin, yin, wo, qall, qup, qdown, wup, wdown, fin, gath, mats, omat, tok, cot, gain,
                 gown, gin, gz, gmid, rown, rin, rz, rmid,
-                l_sem, ss, sr, hs, hr, qs, qr, ws, wr, zs, zr, zos, zor, ps, pr, gs, gr, gzs, gzr, rs, rr, rzs, rzr):
+                l_sem, ss, sr, hs, hr, qs, qr, ws, wr, us, ur, ds, dr, wus, wur, wds, wdr, ps, pr, gs, gr, gzs, gzr, rs, rr, rzs, rzr):
     f32, bf16 = jnp.float32, jnp.bfloat16
     z = lax.axis_index("rep")
     e = lax.axis_index("ep")
@@ -1182,7 +1037,7 @@
         pl.semaphore_signal(barrier, inc=1, device_id={"rep": (z + d) % reps, "ep": e}, device_id_type=MESH)
     loads = [
         pltpu.make_async_copy(part_ref.at[:, core], own, l_sem.at[0]),
-        pltpu.make_async_copy(qkv_ref.at[z], qown, l_sem.at[1]),
+        pltpu.make_async_copy(qkv_ref, qall, l_sem.at[1]),
         pltpu.make_async_copy(out_ref.at[:, core], wo.at[core], l_sem.at[2]),
         pltpu.make_async_copy(tok_ref, tok, l_sem.at[3]),
         pltpu.make_async_copy(cot_ref, cot, l_sem.at[4]),
@@ -1210,17 +1065,66 @@
         return pltpu.make_async_remote_copy(src_ref=src, dst_ref=dst, send_sem=send, recv_sem=recv,
                                             device_id={"rep": (z + d) % reps, "ep": e}, device_id_type=MESH)
 
-    zcopies = [to_rep(qkv_ref.at[(z + d) % reps], zq.at[d - 1], zs.at[d - 1], zr.at[d - 1], d) for d in range(1, reps)]
-    ocopies = [to_rep(wo.at[((z + d) % reps) // heads_dev, (z + d) % heads_dev], zo.at[d - 1], zos.at[d - 1], zor.at[d - 1], d)
-               for d in range(1, reps)]
-    wcopy = to_sib(out_ref.at[:, 1 - core], wo.at[core], ws, wr)
-    order = (chips[2] // 2, chips[0] // 2, chips[1] // 2, chip)
-    scopies = [to_sib(part_ref.at[q, 1 - core], sib_in.at[q], ss.at[n], sr.at[n]) for n, q in enumerate(order)]
-    for c in scopies:
-        c.start()
-    wcopy.start()
-    for c in zcopies:
-        c.start()
+    def along(src, slot, send, recv, up):
+        return pltpu.make_async_remote_copy(src_ref=src, dst_ref=slot, send_sem=send, recv_sem=recv,
+                                            device_id={"rep": z + 1 if up else z - 1, "ep": e}, device_id_type=MESH)
+
+    class Sum:
+        def __init__(self, mine, up, down, usend, urecv, dsend, drecv, count):
+            self.mine, self.up, self.down, self.count = mine, up, down, count
+            self.usend, self.urecv, self.dsend, self.drecv = usend, urecv, dsend, drecv
+
+        def hop(self, src, g, up):
+            if up:
+                return along(src, self.up.at[g], self.usend.at[g], self.urecv.at[g], True)
+            return along(src, self.down.at[g], self.dsend.at[g], self.drecv.at[g], False)
+
+        def begin(self):
+            @pl.when(z == 0)
+            def _():
+                for g in range(reps - 1, 0, -1):
+                    self.hop(self.mine(g), g, True).start()
+            @pl.when(z == reps - 1)
+            def _():
+                for g in range(reps - 1):
+                    self.hop(self.mine(g), g, False).start()
+
+        def forward(self, n):
+            g = reps - 1 - n
+            @pl.when((z > 0) & (z < g))
+            def _():
+                self.hop(self.mine(g), g, True).wait_recv()
+                add(self.up.at[g], (self.up.at[g], self.mine(g)), self.count)
+                self.hop(self.up.at[g], g, True).start()
+            @pl.when((z < reps - 1) & (z > n))
+            def _():
+                self.hop(self.mine(n), n, False).wait_recv()
+                add(self.down.at[n], (self.down.at[n], self.mine(n)), self.count)
+                self.hop(self.down.at[n], n, False).start()
+
+        def arrived(self):
+            @pl.when(z > 0)
+            def _():
+                self.hop(self.mine(0), z, True).wait_recv()
+            @pl.when(z == 0)
+            def _():
+                self.up[z] = jnp.zeros(self.up.shape[1:], bf16)
+            @pl.when(z < reps - 1)
+            def _():
+                self.hop(self.mine(0), z, False).wait_recv()
+            @pl.when(z == reps - 1)
+            def _():
+                self.down[z] = jnp.zeros(self.down.shape[1:], bf16)
+
+        def sent(self):
+            for g in range(reps):
+                @pl.when(z < g)
+                def _():
+                    self.hop(self.mine(g), g, True).wait_send()
+                @pl.when(z > g)
+                def _():
+                    self.hop(self.mine(g), g, False).wait_send()
+
     step = 16
 
     def add(out, terms, count):
@@ -1233,6 +1137,17 @@
             out[r, :] = t.astype(out.dtype)
 
     lower, upper = pl.ds(0, half), pl.ds(half, half)
+    qkv_sum = Sum(lambda g: qall.at[g], qup, qdown, us, ur, ds, dr, rows_dev * eps)
+    out_sum = Sum(lambda g: wo.at[g // heads_dev, g % heads_dev], wup, wdown, wus, wur, wds, wdr, rows_dev)
+    wcopy = to_sib(out_ref.at[:, 1 - core], wo.at[core], ws, wr)
+    order = (chips[2] // 2, chips[0] // 2, chips[1] // 2, chip)
+    scopies = [to_sib(part_ref.at[q, 1 - core], sib_in.at[q], ss.at[n], sr.at[n]) for n, q in enumerate(order)]
+    for c in scopies:
+        c.start()
+    wcopy.start()
+
+    loads[1].wait()
+    qkv_sum.begin()
     hcopies = [to_chip(own.at[order[0], (lower, upper)[j]], relay_in.at[j], hs.at[j], hr.at[j], j) for j in range(2)]
     qcopies = [to_chip(own.at[order[1 + j]], (xin, yin)[j], qs.at[j], qr.at[j], j) for j in range(2)]
     loads[0].wait()
@@ -1251,10 +1166,10 @@
         qcopies[j].start()
     loads[2].wait()
     wcopy.wait_recv()
-    for c in ocopies:
-        c.start()
+    out_sum.begin()
+    qkv_sum.forward(0)
     scopies[3].wait_recv()
-    for c in loads[3:]:
+    for c in loads[3:8]:
         c.wait()
     for c in qcopies:
         c.wait_recv()
@@ -1279,6 +1194,12 @@
     rcopies = [to_plane(rown.at[:, (e + d) % eps], rin.at[d - 1], rs.at[d - 1], rr.at[d - 1], d) for d in range(1, eps)]
     for c in (*gcopies, *rcopies):
         c.start()
+    qkv_sum.forward(1)
+    out_sum.forward(0)
+    for n in range(2, reps - 1):
+        qkv_sum.forward(n)
+    for n in range(1, reps - 1):
+        out_sum.forward(n)
     for c in (*gcopies, *rcopies):
         c.wait_recv()
     t = gown[...]
@@ -1294,24 +1215,21 @@
     for c in (*gzcopies, *rzcopies):
         c.start()
 
-    loads[1].wait()
-    for c in zcopies:
-        c.wait_recv()
+    qkv_sum.arrived()
     for n in range(eps):
         @pl.loop(0, rows_dev // step)
         def _(i):
             r = pl.ds(pl.multiple_of(i * step, step), step)
             a = pl.ds(pl.multiple_of(n * rows_dev + i * step, step), step)
-            t = qown[a, :].astype(f32)
-            for d in range(reps - 1):
-                t = t + zq[d, a, :].astype(f32)
+            t = qall[z, a, :].astype(f32) + qup[z, a, :].astype(f32) + qdown[z, a, :].astype(f32)
             fin[n, r, :] = t.astype(bf16)
     pcopies = [to_plane(fin.at[(e + d) % eps], gath.at[e], ps.at[d - 1], pr.at[d - 1], d) for d in range(1, eps)]
     for c in pcopies:
         c.start()
     mine = pltpu.make_async_copy(fin.at[e], gath.at[e], l_sem.at[9])
     mine.start()
-    for c in (*gzcopies, *rzcopies, *ocopies):
+    out_sum.arrived()
+    for c in (*gzcopies, *rzcopies):
         c.wait_recv()
     for c in gcopies:
         c.wait_send()
@@ -1330,9 +1248,7 @@
     @pl.loop(0, rows_dev // step)
     def _(i):
         r = pl.ds(pl.multiple_of(i * step, step), step)
-        t = wmine[r, :].astype(f32)
-        for d in range(reps - 1):
-            t = t + zo[d, r, :].astype(f32)
+        t = wmine[r, :].astype(f32) + wup[z, r, :].astype(f32) + wdown[z, r, :].astype(f32)
         omat[r, :] = t
     done.append(pltpu.make_async_copy(omat, o_ref, l_sem.at[12]))
     for c in rzcopies:
@@ -1352,7 +1268,9 @@
         done[-1].start()
     for c in done:
         c.wait()
-    for c in (*scopies, wcopy, *zcopies, *ocopies, *hcopies, *qcopies, *pcopies, *rcopies, *gzcopies):
+    qkv_sum.sent()
+    out_sum.sent()
+    for c in (*scopies, wcopy, *hcopies, *qcopies, *pcopies, *rcopies, *gzcopies):
         c.wait_send()
 
 
@@ -1374,38 +1292,41 @@
         out_specs=[pl.BlockSpec(memory_space=pl.ANY)] * len(outs),
         scratch_shapes=[
             V((q, rows, width), bf16), V((q, rows, width), bf16), V((2, half, width), bf16), V((rows, width), bf16), V((rows, width), bf16),
-            V((2, heads_dev, rows_dev, width), bf16), V((rows_dev * eps, slices), bf16), V((reps - 1, rows_dev * eps, slices), bf16),
-            V((reps - 1, rows_dev, width), bf16), V((eps, rows_dev, slices), bf16), V((eps, rows_dev, slices), bf16),
+            V((2, heads_dev, rows_dev, width), bf16), *[V((reps, rows_dev * eps, slices), bf16)] * 3, *[V((reps, rows_dev, width), bf16)] * 2,
+            V((eps, rows_dev, slices), bf16), V((eps, rows_dev, slices), bf16),
             V((3, rows_dev, width), f32), V((rows_dev, width), f32), V((rows, width), bf16), V((rows, width), f32), V((1, width), f32),
             V(g8, f32), V((eps - 1, *g8), f32), V((reps - 1, *g8), f32), V(g8, f32),
             V(router.shape, f32), V((eps - 1, reps, *rt), f32), V((reps - 1, *rt), f32), V((reps, *rt), f32),
-            D((16,)), D((4,)), D((4,)), D((2,)), D((2,)), D((2,)), D((2,)), D, D,
-            D((reps - 1,)), D((reps - 1,)), D((reps - 1,)), D((reps - 1,)), D((eps - 1,)), D((eps - 1,)),
+            D((17,)), D((4,)), D((4,)), D((2,)), D((2,)), D((2,)), D((2,)), D, D,
+            *[D((reps,))] * 8, D((eps - 1,)), D((eps - 1,)),
             D((eps - 1,)), D((eps - 1,)), D((reps - 1,)), D((reps - 1,)), D((eps - 1,)), D((eps - 1,)), D((reps - 1,)), D((reps - 1,)),
         ],
-        compiler_params=pltpu.CompilerParams(collective_id=cid, has_side_effects=True, vmem_limit_bytes=56 * 2**20),
+        compiler_params=pltpu.CompilerParams(collective_id=cid, has_side_effects=True, vmem_limit_bytes=60 * 2**20),
     )(part, qkv_term, out_term, tokens, after_cot, gain_in, gains, router)
 
 
 def join_kernel(count, *refs):
-    ins, out = refs[:count], refs[count]
-    shift = (lax.axis_index("rep") + count - pl.program_id(1)) % count
-    for k in range(count):
-        @pl.when(shift == k)
-        def _():
-            out[...] = ins[k][...].astype(out.dtype)
-
-
-def join_columns(pieces):
-    count = len(pieces)
-    exp_dev, rows, cols = pieces[0].shape
+    z = lax.axis_index("rep")
+    cols = refs[0].shape[2]
+    for n in range(2):
+        ins, out = refs[n * count:(n + 1) * count], refs[2 * count + n]
+        for k in range(count):
+            place = pl.multiple_of((z + count - k) % count * cols, cols)
+            out[:, :, pl.ds(place, cols)] = ins[k][...].astype(out.dtype)
+
+
+def join_columns(first, second):
+    count = len(first)
+    exp_dev, rows, cols = first[0].shape
+    whole = jax.ShapeDtypeStruct((exp_dev, rows, cols * count), jnp.float32)
+    piece = pl.BlockSpec((1, rows // 2, cols), lambda j, i: (j, i, 0))
     return pl.pallas_call(
         partial(join_kernel, count),
-        grid=(exp_dev, count),
-        out_shape=jax.ShapeDtypeStruct((exp_dev, rows, cols * count), jnp.float32),
-        in_specs=[pl.BlockSpec((1, rows, cols), lambda j, s: (j, 0, 0))] * count,
-        out_specs=pl.BlockSpec((1, rows, cols), lambda j, s: (j, 0, s)),
-    )(*pieces)
+        grid=(exp_dev, 2),
+        out_shape=(whole, whole),
+        in_specs=[piece] * (2 * count),
+        out_specs=[pl.BlockSpec((1, rows // 2, cols * count), lambda j, i: (j, i, 0))] * 2,
+    )(*first, *second)
 
 
 def front_kernel(reps, eps, lengths_ref, tok_ref, cot_ref, wq_ref, wk_ref, wv_ref, wo_ref, gains_ref, router_ref, nums_ref, freq_ref,
@@ -1854,11 +1775,7 @@
     heads_dev = width // head_dim // ep_count
     slice_width = heads_dev * head_dim
     rows_dev = query_weight.shape[0]
-    score_scale = head_dim ** (-0.5)
-    core = ep_index % 2
-    every = ("rep", "ep")
-
-    chips = ep_count // 2
+
     gains_dev = gains.shape[0]
     gain_rows = -(-gains_dev * rep_count * ep_count // 2048) * 16
     gains_placed = lax.dynamic_update_slice_in_dim(
@@ -1907,28 +1824,15 @@
     gains_float = gains_all.reshape(-1)
     gain_in = gains_float[:width]
     gain_mid = gains_float[width : 2 * width]
-    gain_query = gains_float[2 * width : 2 * width + head_dim]
-    gain_key = gains_float[2 * width + head_dim : 2 * width + 2 * head_dim]
     router_full = (
         router_all[:, :, :router_rows].transpose(1, 0, 2, 3).reshape(width, experts_all)
     )
     deal_all = numbers_all[:, 0].reshape(-1)
     priority_all = numbers_all[:, 1].reshape(-1)
     routes_all = numbers_all[:, 2 : 2 + top_count].transpose(0, 2, 1).reshape(group_rows, top_count)
-    segment_all, position_all = placement(deal_all, lengths[0])
-    same_seq = segment_all[:, None] == segment_all[None, :]
+    segment_all, _ = placement(deal_all, lengths[0])
     normed_group = normed_group.reshape(group_rows, width)
     qkv_slice = qkv_slice.reshape(width, 3 * slice_width)
-    out_slice = out_slice.reshape(slice_width, width)
-    query_pre = pre[:, :slice_width].reshape(group_rows, heads_dev, head_dim)
-    key_pre = pre[:, slice_width:].reshape(group_rows, heads_dev, head_dim)
-    query_low, key_low, value_low = (
-        qkv_low[:, i * slice_width : (i + 1) * slice_width].reshape(
-            group_rows, heads_dev, head_dim
-        )
-        for i in range(3)
-    )
-    residual = tokens.astype(f32)
     mid_low = rms_scale(after_attn, gain_mid).astype(bf16)
 
     logits = jnp.dot(mid_low, router_full, preferred_element_type=f32)
@@ -1984,45 +1888,26 @@
     _, mid_pull = jax.vjp(rms_scale, after_attn, gain_mid)
     after_extra, gain_mid_cot = mid_pull(mid_cot)
     after_cot = out_grad + after_extra
-    attn_cot_group = all_gather(
-        after_cot.astype(bf16), rep_count, ep_count, False, 6
-    ).reshape(group_rows, width)
-
-    mixed_cot = jnp.dot(attn_cot_group, out_slice.T, preferred_element_type=f32).astype(bf16)
-    output_term = jnp.dot(mixed_low.T, attn_cot_group, preferred_element_type=f32)
-    query_cot, key_cot, value_cot = attend_again(
-        (
-            query_low,
-            key_low,
-            value_low,
-            mixed_cot.reshape(group_rows, heads_dev, head_dim),
-        ),
-        same_seq,
-        score_scale,
-    )
-    _, query_pull = jax.vjp(
-        lambda pre, gain_vec: rope_norm(pre, gain_vec, position_all), query_pre, gain_query
-    )
-    query_pre_cot, gain_query_cot = query_pull(query_cot)
-    _, key_pull = jax.vjp(
-        lambda pre, gain_vec: rope_norm(pre, gain_vec, position_all), key_pre, gain_key
-    )
-    key_pre_cot, gain_key_cot = key_pull(key_cot)
-    pre_cot = jnp.concatenate(
-        [
-            part.reshape(group_rows, slice_width).astype(bf16)
-            for part in (query_pre_cot, key_pre_cot, value_cot)
-        ],
-        axis=1,
-    )
-    normed_part = jnp.dot(pre_cot, qkv_slice.T, preferred_element_type=f32).astype(bf16)
-    qkv_term = jnp.dot(normed_group.T, pre_cot, preferred_element_type=f32).astype(bf16)
+    normed_part, qkv_term, output_term, head_gains = attention_back(
+        after_cot.astype(bf16),
+        out_slice,
+        mixed_low,
+        qkv_low,
+        pre,
+        turn,
+        segment_all.astype(f32).reshape(ep_count, tok_dev),
+        gains_all,
+        normed_group,
+        qkv_slice,
+        rep_count,
+        ep_count,
+        1,
+    )
     gains_term = jnp.concatenate(
         [
             jnp.zeros((width,), f32),
             gain_mid_cot,
-            gain_query_cot,
-            gain_key_cot,
+            head_gains[:2].reshape(-1),
             jnp.zeros((6 * width - 2 * head_dim,), f32),
         ]
     ).reshape(8, width)
@@ -2031,9 +1916,9 @@
         ((0, 0), (0, 0), (0, -router_rows % 8), (0, 0)),
     )
     input_grad, query_sum, key_sum, value_sum, output_sum, gains_all, router_own = last_sums(
-        normed_part.reshape(ep_count // 2, 2, tok_dev, width),
-        qkv_term.reshape(rep_count, ep_count * rows_dev, 3 * slice_width),
-        output_term.astype(bf16).reshape(heads_dev, 2, rows_dev, width),
+        normed_part,
+        qkv_term,
+        output_term,
         tokens,
         after_cot,
         gain_in.reshape(1, width),
@@ -2048,7 +1933,7 @@
         gains_all.reshape(-1), (rep_index * ep_count + ep_index) * gains_dev, gains_dev
     )
     router_sum = router_own[:router_rows].reshape(rows_dev, experts_all)
-    gate_w_grad, up_w_grad = join_columns(gate_pieces), join_columns(up_pieces)
+    gate_w_grad, up_w_grad = join_columns(gate_pieces, up_pieces)
     return (
         block_out,
         input_grad,

time: 744 us -> 701 us (0.942)
  matrix products: 43 us -> 4.38 us
  Pallas kernels: 605 us -> 618 us
  other arithmetic: 21 us -> 9.73 us
  local copies, waits for them, and re-layouts: 44.2 us -> 34 us
    dot_general x8 -> x0, matrix products: 32.8 us -> none  [the longest x1 7.72 us: on_device_split(): jnp.dot(normed_group.T, pre_cot, preferred_element_type=f32).astype(bf16)]
    pallas_call x1, Pallas kernels: 117 us -> 137 us  [last_sums(): pl.pallas_call(partial(last_kernel, reps, eps), out_shape=outs, in_specs=...]
    pallas_call x3 -> x2, Pallas kernels: 38.5 us -> 47.5 us  [the longest x1 39.4 us: attention_back(): pl.pallas_call(partial(back_kernel, heads_dev), out_shape=outs, in_specs=...]
    pallas_call x1, Pallas kernels: 287 us -> 278 us  [moe(): pl.pallas_call(partial(moe_kernel, reps, side, experts_all), out_shape=ou...]
    pallas_call x1, Pallas kernels: 162 us -> 155 us  [front(): pl.pallas_call(partial(front_kernel, reps, eps), out_shape=outs, in_specs...]
    unnamed x74 -> x35, local copies, waits for them, and re-layouts: 18.8 us -> 15.4 us
  transfers between devices with their start and end apart: 6 -> 6, of which waited for: 0 -> 1; matrix products, arithmetic and copies ran while one was open for 10% -> 2% of each run, Pallas kernels for 20% -> 26%
where the time goes in v6:
time: 701 us; the launch traced here: 692 us
  Pallas kernels  618 us (88%)
  local copies, waits for them, and re-layouts  34 us (5%)
  starting transfers between devices  23.6 us (3%)
  other arithmetic  9.73 us (1%)
    pallas_call x1, Pallas kernels, moe(): pl.pallas_call(partial(moe_kernel, reps, side, experts_all), out_shape=ou...  278 us
    pallas_call x1, Pallas kernels, front(): pl.pallas_call(partial(front_kernel, reps, eps), out_shape=outs, in_specs...  155 us
    pallas_call x1, Pallas kernels, last_sums(): pl.pallas_call(partial(last_kernel, reps, eps), out_shape=outs, in_specs=...  137 us
    pallas_call x1, Pallas kernels, attention_back(): pl.pallas_call(partial(back_kernel, heads_dev), out_shape=outs, in_specs=...  39.4 us
    ppermute x6, starting transfers between devices, rows_of(): lax.ppermute(parts[k], 'rep', [(i, (i + k) % rep_count) for i in range(re...  23.6 us
    unnamed x35, local copies, waits for them, and re-layouts  15.4 us
  transfers between devices with their start and end apart: 6, of which 1 were waited for; matrix products, arithmetic and copies ran while one was open for 2% of the time, Pallas kernels for 26%

profile of v6, /device:TPU:0, one launch (start us, length us, event | category | flops | bytes accessed | tf_op | source)
XLA Modules:
  0.0 692.0 jit_solution(991771546451001200)
XLA Ops:
  0.6 0.0 copy-start.11
  0.7 0.8 copy.49
  1.5 0.1 reshape.119
  1.6 0.7 convert_reduce_fusion
  2.3 0.7 pad_add_fusion
  3.0 0.6 pad.13.nums_ref
  3.6 0.6 maximum_bitcast_fusion.freq_ref
  4.2 0.6 pad.12.router_ref
  4.8 0.8 dynamic_update_slice.3
  5.6 0.6 copy-done.10
  6.2 154.7 %shard_map.230 = (bf16[4,8,128,2048]{3,2,1,0:T(8,128)(2,1)}, bf16[8,4,16,128]{3,2,1,0:T(8,128)(2,1)}, s32[8,16,128]{2,1,0:T(8,128)}, f32[48,128]{1,0:T(8,128)}, ...) custom-call(s32[1,3]{1,0:T(1,128)} %lengths_ref.1, ...), custom_call_target="tpu_custom_call" | custom-call | tf_op jit(solution)/shard_map/pallas_call | solution.py:1726
  160.9 0.8 fusion.11
  161.8 0.8 slice_bitcast_fusion.9
  162.6 1.4 multiply_reduce_fusion.2
  164.0 1.3 fusion.12
  165.3 0.9 slice_bitcast_fusion.8
  166.2 0.7 reshape.121
  166.9 0.0 copy-start.1
  166.9 0.1 copy.50
  167.0 0.1 fusion.4
  167.1 1.4 multiply_convert_fusion
  168.5 0.4 fusion.13
  168.9 0.2 fusion.7
  169.1 0.3 subtract_convert_fusion
  169.4 1.0 concatenate.14.x_ref
  170.4 278.2 %shard_map.231 = (bf16[128,2176]{1,0:T(8,128)(2,1)}, bf16[128,2048]{1,0:T(8,128)(2,1)}, bf16[4,3,512,256]{3,2,1,0:T(8,128)(2,1)}, bf16[4,3,512,256]{3,2,1,0:T(8,...) custom-call(bf16[128,2176]{1,0:T(8,128)(2,1)} %concatenate.14.x_ref,, ...), custom_call_target="tpu_custom_call" | custom-call | tf_op jit(solution)/shard_map/pallas_call | solution.py:829
  448.6 3.8 slice_bitcast_fusion.4
  452.4 13.0 %collective-permute-start = (bf16[3,512,256]{2,1,0:T(8,128)(2,1)}, bf16[3,512,256]{2,1,0:T(8,128)(2,1)}, u32[]{:S(2)}, u32[]{:S(2)}) collective-permute-start(bf16[3,512,256]{2,1,0:T(8,128)(2,1)} %get-tuple-element.127), channel_id=1, source_target_pairs={{0,8},{8,16},{16,24},{24,0},{1,9},{9,17},{17,25},{25,1},{2,10},{10... | collective-permute-start | bytes 2359304 | tf_op jit(solution)/shard_map/ppermute | solution.py:1874
  465.4 0.0 collective-permute-start.1
  465.4 2.8 collective-permute-start.2
  468.3 1.7 slice_bitcast_fusion
  470.0 0.0 collective-permute-start.3
  470.0 2.1 collective-permute-start.4
  472.1 0.9 multiply_reduce_fusion.3
  472.9 2.1 fusion.14
  475.0 1.6 multiply_reduce_fusion
  476.7 1.8 reshape.129
  478.5 0.2 reduce-window.8
  478.6 0.7 pad.14.router_ref
  479.4 2.9 fusion.9
  482.3 1.4 collective-permute-done.refs_1_
  483.7 5.6 collective-permute-start.5
  489.4 0.1 convert_reduce_fusion.1
  489.4 0.6 convert_bitcast_fusion.segs_ref
  490.0 39.4 %shard_map.232 = (bf16[4,2,128,2048]{3,2,1,0:T(8,128)(2,1)}, bf16[4,512,768]{2,1,0:T(8,128)(2,1)}, bf16[2,2,64,2048]{3,2,1,0:T(8,128)(2,1)}, f32[8,128]{1,0:T(8,128)}) custom-call(bf16[128,2048]{1,0:T(8,128)(2,1)} %get-tuple-element.117.cot_ref, bf16[2,2,64,2048]{3,2,1,0:T(8,128)(2,1)} %get-tuple-element.48.wout_ref, ...), custom_call_target="tpu_custom_call" | custom-call | tf_op jit(solution)/shard_map/pallas_call | solution.py:1000
  529.4 0.7 slice_bitcast_fusion.11
  530.1 0.6 reshape.128.gains_ref
  530.7 137.3 %shard_map.233 = (f32[128,2048]{1,0:T(8,128)}, f32[64,2048]{1,0:T(8,128)}, f32[64,2048]{1,0:T(8,128)}, f32[64,2048]{1,0:T(8,128)}, f32[64,2048]{1,0:T(8,128)}, /*index=5*/f32[8,2048]{1,0:T(8,128)}, f32[16,128]{1,0:T(8,128)}) custom-call(bf16[4,2,128,2048]{3,2,1,0:T(8,128)(2,1)} %get-tuple-element.55.part_ref, ...), custom_call_target="tpu_custom_call" | custom-call | tf_op jit(solution)/shard_map/pallas_call | solution.py:1288
  668.1 0.9 copy.62
  669.0 0.8 reshape.130
  669.8 0.7 copy.58
  670.5 0.6 dynamic_slice.3
  671.1 0.0 collective-permute-done.1.refs_2_
  671.2 0.0 collective-permute-done.4.refs_6_
  671.2 0.0 collective-permute-done.5.refs_7_
  671.2 0.0 copy-start.6
  671.2 0.9 copy-done.6
  672.1 8.2 %shard_map.234 = (f32[3,512,1024]{2,1,0:T(8,128)}, f32[3,512,1024]{2,1,0:T(8,128)}) custom-call(bf16[3,512,256]{2,1,0:T(8,128)(2,1)} %get-tuple-element.128.refs_0_, bf16[3,512,256]{2,1,0:T(8,128)(2,1)} %collective-permute-done.refs_1_, bf16[3,512,256]{2,1,0:T(8,128)(2,1)} %collective-permute-done.1.refs_2_, ...), custom_call_target="tpu_custom_call" | custom-call | tf_op jit(solution)/shard_map/pallas_call | solution.py:1323
  680.2 1.0 copy.70
  681.2 1.9 copy.71
  683.1 0.8 copy.72
  683.9 0.8 copy.73
  684.7 0.8 copy.74
  685.5 6.3 copy.75
  (33 shorter events, 0.1 us)
Async XLA Ops:
  0.6 168.4 %copy-start.11 = (s32[128]{0:T(128)S(1)}, s32[128]{0:T(128)}, u32[]{:S(2)}) copy-start(s32[128]{0:T(128)} %param.29) | copy-start | bytes 1540
  5.6 0.6 copy-start.10
  166.9 1.6 copy-start.1
  448.6 19.7 %copy-start.3 = (bf16[4,3,512,256]{3,2,1,0:T(8,128)(2,1)S(1)}, bf16[4,3,512,256]{3,2,1,0:T(8,128)(2,1)}, u32[]{:S(2)}) copy-start(bf16[4,3,512,256]{3,2,1,0:T(8,128)(2,1)} %get-tuple-element.67) | copy-start | bytes 9437188
  452.4 22.6 %copy-start = (f32[128,2048]{1,0:T(8,128)S(1)}, f32[128,2048]{1,0:T(8,128)}, u32[]{:S(2)}) copy-start(f32[128,2048]{1,0:T(8,128)} %get-tuple-element.41) | copy-start | bytes 3145732
  452.4 22.6 %copy-start.2 = (bf16[2048,24]{1,0:T(8,128)(2,1)S(1)}, bf16[2048,24]{1,0:T(8,128)(2,1)}, u32[]{:S(2)}) copy-start(bf16[2048,24]{1,0:T(8,128)(2,1)} %copy-done.1) | copy-start | bytes 294916
  452.4 31.3 %collective-permute-start = (bf16[3,512,256]{2,1,0:T(8,128)(2,1)}, bf16[3,512,256]{2,1,0:T(8,128)(2,1)}, u32[]{:S(2)}, u32[]{:S(2)}) collective-permute-start(bf16[3,512,256]{2,1,0:T(8,128)(2,1)} %get-tuple-element.127), channel_id=1, source_target_pairs={{0,8},{8,16},{16,24},{24,0},{1,9},{9,17},{17,25},{25,1},{2,10},{10... | collective-permute-start | bytes 2359304 | tf_op jit(solution)/shard_map/ppermute | solution.py:1874
  465.4 205.7 %collective-permute-start.1 = (bf16[3,512,256]{2,1,0:T(8,128)(2,1)}, bf16[3,512,256]{2,1,0:T(8,128)(2,1)}, u32[]{:S(2)}, u32[]{:S(2)}) collective-permute-start(bf16[3,512,256]{2,1,0:T(8,128)(2,1)} %get-tuple-element.126), channel_id=1, source_target_pairs={{0,16},{8,24},{16,0},{24,8},{1,17},{9,25},{17,1},{25,9},{2,18},{10... | collective-permute-start | bytes 2359304 | tf_op jit(solution)/shard_map/ppermute | solution.py:1874
  465.4 205.7 %collective-permute-start.2 = (bf16[3,512,256]{2,1,0:T(8,128)(2,1)}, bf16[3,512,256]{2,1,0:T(8,128)(2,1)}, u32[]{:S(2)}, u32[]{:S(2)}) collective-permute-start(bf16[3,512,256]{2,1,0:T(8,128)(2,1)} %get-tuple-element.125), channel_id=1, source_target_pairs={{0,24},{8,0},{16,8},{24,16},{1,25},{9,1},{17,9},{25,17},{2,26},{10... | collective-permute-start | bytes 2359304 | tf_op jit(solution)/shard_map/ppermute | solution.py:1874
  470.0 8.5 %copy-start.12 = (s32[1,3]{1,0:T(1,128)S(1)}, s32[1,3]{1,0:T(1,128)}, u32[]{:S(2)}) copy-start(s32[1,3]{1,0:T(1,128)} %lengths_ref.1) | copy-start | bytes 40
  470.0 201.2 %collective-permute-start.3 = (bf16[3,512,256]{2,1,0:T(8,128)(2,1)}, bf16[3,512,256]{2,1,0:T(8,128)(2,1)}, u32[]{:S(2)}, u32[]{:S(2)}) collective-permute-start(bf16[3,512,256]{2,1,0:T(8,128)(2,1)} %get-tuple-element.123), channel_id=1, source_target_pairs={{0,8},{8,16},{16,24},{24,0},{1,9},{9,17},{17,25},{25,1},{2,10},{10... | collective-permute-start | bytes 2359304 | tf_op jit(solution)/shard_map/ppermute | solution.py:1874
  470.0 201.2 %collective-permute-start.4 = (bf16[3,512,256]{2,1,0:T(8,128)(2,1)}, bf16[3,512,256]{2,1,0:T(8,128)(2,1)}, u32[]{:S(2)}, u32[]{:S(2)}) collective-permute-start(bf16[3,512,256]{2,1,0:T(8,128)(2,1)} %get-tuple-element.122), channel_id=1, source_target_pairs={{0,16},{8,24},{16,0},{24,8},{1,17},{9,25},{17,1},{25,9},{2,18},{10... | collective-permute-start | bytes 2359304 | tf_op jit(solution)/shard_map/ppermute | solution.py:1874
  476.7 7.1 %copy-start.5 = (bf16[3,512,256]{2,1,0:T(8,128)(2,1)S(1)}, bf16[3,512,256]{2,1,0:T(8,128)(2,1)}, u32[]{:S(2)}) copy-start(bf16[3,512,256]{2,1,0:T(8,128)(2,1)} %get-tuple-element.121) | copy-start | bytes 2359300
  483.7 187.4 %collective-permute-start.5 = (bf16[3,512,256]{2,1,0:T(8,128)(2,1)S(1)}, bf16[3,512,256]{2,1,0:T(8,128)(2,1)S(1)}, u32[]{:S(2)}, u32[]{:S(2)}) collective-permute-start(bf16[3,512,256]{2,1,0:T(8,128)(2,1)S(1)} %copy-done.5), channel_id=1, source_target_pairs={{0,24},{8,0},{16,8},{24,16},{1,25},{9,1},{17,9},{25,17},{2,26},{10... | collective-permute-start | bytes 2359304 | tf_op jit(solution)/shard_map/ppermute | solution.py:1874
  668.1 12.1 %copy-start.4 = (f32[128,2048]{1,0:T(8,128)S(1)}, f32[128,2048]{1,0:T(8,128)}, u32[]{:S(2)}) copy-start(f32[128,2048]{1,0:T(8,128)} %get-tuple-element.150) | copy-start | bytes 3145732
  671.2 0.9 copy-start.6
  672.1 11.0 %copy-start.9 = (f32[64,2048]{1,0:T(8,128)S(1)}, f32[64,2048]{1,0:T(8,128)}, u32[]{:S(2)}) copy-start(f32[64,2048]{1,0:T(8,128)} %get-tuple-element.152) | copy-start | bytes 1572868
  672.1 11.8 %copy-start.8 = (f32[64,2048]{1,0:T(8,128)S(1)}, f32[64,2048]{1,0:T(8,128)}, u32[]{:S(2)}) copy-start(f32[64,2048]{1,0:T(8,128)} %get-tuple-element.153) | copy-start | bytes 1572868
  672.1 12.6 %copy-start.7 = (f32[64,2048]{1,0:T(8,128)S(1)}, f32[64,2048]{1,0:T(8,128)}, u32[]{:S(2)}) copy-start(f32[64,2048]{1,0:T(8,128)} %get-tuple-element.154) | copy-start | bytes 1572868

commit v7 on v6

--- a/solution.py
+++ b/solution.py
@@ -374,15 +374,17 @@
 
 
 def visit_order(reps):
-    return [sorted((g for g in range(reps) if g != z), key=lambda g: (abs(g - z), g)) + [z] for z in range(reps)]
+    if reps != 4:
+        return [sorted((g for g in range(reps) if g != z), key=lambda g: (abs(g - z), g)) + [z] for z in range(reps)]
+    return [[2, 3, 1, 0], [2, 3, 0, 1], [1, 0, 3, 2], [1, 0, 2, 3]]
 
 
 def moe_kernel(reps, side_lanes, experts_all, x_ref, cot_ref, eg_ref, eu_ref, ed_ref,
-               row_ref, moe_ref, gout_ref, uout_ref, dout_ref,
+               row_ref, moe_ref, gout_ref, uout_ref, dout_ref, gin_ref,
                mid_ref, a_ref, b_ref, h_ref, xin_ref, yin_ref, zin_ref,
                wgu, wd, xbuf, cbuf, abuf, pbuf, sib_in, relay_in, sendbuf, ownbuf, rbuf, tmp, colbuf, gst, dst,
                own_sem, w_sem, x_sem, c_sem, ab_sem, t_sem, col_sem, g_sem, o_sem,
-               zs, zr, ps, pr, cs, cr, ss, sr, hs, hr, qs, qr, fs, fr):
+               zs, zr, ps, pr, cs, cr, ss, sr, hs, hr, qs, qr, fs, fr, xs, xr):
     f32, bf16 = jnp.float32, jnp.bfloat16
     z = lax.axis_index("rep")
     e = lax.axis_index("ep")
@@ -645,6 +647,11 @@
     arrive(3)
     at(2, pass_on)
     at(1, finish_in)
+    end = (z == 0) | (z == reps - 1)
+
+    @pl.when(end)
+    def _():
+        at(2, finish_in)
     for w in weights:
         w.wait()
     ready(group_of(0))
@@ -655,13 +662,16 @@
     def _(i):
         load_x(i).wait()
         load_c(i).wait()
+        @pl.when(i == 1)
+        def _():
+            at(3, pass_on)
         @pl.when(i == 3)
         def _():
-            at(3, pass_on)
-            at(2, finish_in)
-        @pl.when(i == 7)
-        def _():
             at(3, finish_in)
+
+            @pl.when(jnp.logical_not(end))
+            def _():
+                at(2, finish_in)
         @pl.when(i == steps - 5)
         def _():
             local.wait()
@@ -708,7 +718,20 @@
         left = colbuf[n % 2, pl.ds(m * (reps // 2), reps // 2)].reshape(halves, 256)
         return left, wgu[m]
 
-    def grad_rows(src, out):
+    def hand_over(k):
+        return pltpu.make_async_remote_copy(
+            src_ref=gout_ref.at[k], dst_ref=gin_ref.at[k], send_sem=xs.at[k], recv_sem=xr.at[k],
+            device_id={"rep": (z + k) % reps, "ep": e}, device_id_type=MESH)
+
+    per_piece = width // reps // 256
+
+    def piece_done(n):
+        k = (n // per_piece + reps - z) % reps
+        @pl.when((n % per_piece == per_piece - 1) & (k > 0))
+        def _():
+            hand_over(k).start()
+
+    def grad_rows(src, out, send):
         def store(n, j):
             per = width // reps
             place = pl.ds(pl.multiple_of((n * 256) % per, 256), 256)
@@ -728,6 +751,8 @@
             def _():
                 for j in range(exp_dev):
                     store(n - 2, j).wait()
+                if send:
+                    piece_done(n - 2)
             t = jnp.zeros((256, EF), f32)
             for m in range(2):
                 left, right = product(n, m)
@@ -738,6 +763,8 @@
         for n in (blocks - 2, blocks - 1):
             for j in range(exp_dev):
                 store(n, j).wait()
+            if send:
+                piece_done(n)
 
     def grad_down():
         def store(n):
@@ -760,13 +787,13 @@
             for m in range(2):
                 left, right = product(n, m)
                 t = t + lax.dot_general(right, left, TN, preferred_element_type=f32)
-            dst[n % 2] = t.reshape(exp_dev, F, 256)
+            dst[n % 2] = t.reshape(exp_dev, F, 256).astype(bf16)
             store(n).start()
         for n in (blocks - 2, blocks - 1):
             store(n).wait()
 
-    grad_rows(a_ref, gout_ref)
-    grad_rows(b_ref, uout_ref)
+    grad_rows(a_ref, gout_ref, True)
+    grad_rows(b_ref, uout_ref, False)
     grad_down()
 
     last = reps - 1
@@ -790,6 +817,8 @@
     for o in outs:
         o.wait()
     fcopy(reps - 2, group_of(reps - 2)).wait_send()
+    for k in range(1, reps):
+        hand_over(k).wait()
     for j in range(2):
         hcopy(last, j).wait_send()
         qcopy(last, j).wait_send()
@@ -822,7 +851,8 @@
     steps = 4 * reps
     outs = (
         S((rows, W1), bf16), S((rows, width), bf16),
-        S((reps, exp_dev, width // reps, F), bf16), S((reps, exp_dev, width // reps, F), bf16), S((exp_dev, F, width), f32),
+        S((reps, exp_dev, width // reps, F), bf16), S((reps, exp_dev, width // reps, F), bf16), S((exp_dev, F, width), bf16),
+        S((reps, exp_dev, width // reps, F), bf16),
         S((reps, eps, rows, W1), bf16), S((tokens, EF), bf16), S((tokens, EF), bf16), S((tokens, EF), bf16),
         S((reps, rows, WP), bf16), S((reps, rows, WP), bf16), S((reps, rows, WP), bf16),
     )
@@ -837,13 +867,13 @@
             V((2, 3, 2 * rows, EF), bf16), V((2, 2, rows, WP), bf16), V((4, rows, WP), bf16),
             V((reps, 2, rows // 2, WP), bf16), V((3, rows, WP), bf16), V((2, rows, WP), bf16), V((2, rows, WP), bf16),
             V((5, rows, WP), bf16), V((2, reps, eps, rows, 256), bf16),
-            V((2, exp_dev, 256, F), bf16), V((2, exp_dev, F, 256), f32),
+            V((2, exp_dev, 256, F), bf16), V((2, exp_dev, F, 256), bf16),
             D, D((3 * exp_dev,)), D((2,)), D((2,)), D((2, 3)), D((5,)), D((2,)), D((2, exp_dev)), D((2,)),
             D((2, reps)), D((reps,)), D((reps, 4)), D((reps, 4)), D((reps, 4)), D((reps, 4)),
-            D((steps,)), D((steps,)), D((reps, 2)), D((reps, 2)), D((reps, 2)), D((reps, 2)), D((reps,)), D((reps,)),
+            D((steps,)), D((steps,)), D((reps, 2)), D((reps, 2)), D((reps, 2)), D((reps, 2)), D((reps,)), D((reps,)), D((reps,)), D((reps,)),
         ],
         compiler_params=pltpu.CompilerParams(collective_id=cid, has_side_effects=True, vmem_limit_bytes=63 * 2**20),
-    )(x, cot_all, eg, eu, ed)[:5]
+    )(x, cot_all, eg, eu, ed)[:6]
 
 
 def back_kernel(heads_dev, cot_ref, wout_ref, mixed_ref, qkv_ref, pre_ref, turn_ref, segs_ref, gains_ref, normed_ref, wqkv_ref,
@@ -1308,25 +1338,31 @@
 def join_kernel(count, *refs):
     z = lax.axis_index("rep")
     cols = refs[0].shape[2]
+    down, outs = refs[2 * count], refs[2 * count + 1:]
+    outs[2][...] = down[...].astype(outs[2].dtype)
     for n in range(2):
-        ins, out = refs[n * count:(n + 1) * count], refs[2 * count + n]
+        ins, out = refs[n * count:(n + 1) * count], outs[n]
         for k in range(count):
             place = pl.multiple_of((z + count - k) % count * cols, cols)
             out[:, :, pl.ds(place, cols)] = ins[k][...].astype(out.dtype)
 
 
-def join_columns(first, second):
-    count = len(first)
-    exp_dev, rows, cols = first[0].shape
+def join_columns(first, first_got, second, second_got, down):
+    count, exp_dev, rows, cols = first.shape
     whole = jax.ShapeDtypeStruct((exp_dev, rows, cols * count), jnp.float32)
+
+    def part(k):
+        return pl.BlockSpec((None, 1, rows // 2, cols), lambda j, i: (k, j, i, 0))
+
     piece = pl.BlockSpec((1, rows // 2, cols), lambda j, i: (j, i, 0))
+    tall = pl.BlockSpec((1, down.shape[1] // 2, down.shape[2]), lambda j, i: (j, i, 0))
     return pl.pallas_call(
         partial(join_kernel, count),
         grid=(exp_dev, 2),
-        out_shape=(whole, whole),
-        in_specs=[piece] * (2 * count),
-        out_specs=[pl.BlockSpec((1, rows // 2, cols * count), lambda j, i: (j, i, 0))] * 2,
-    )(*first, *second)
+        out_shape=(whole, whole, jax.ShapeDtypeStruct(down.shape, jnp.float32)),
+        in_specs=[part(0)] + [part(k) for k in range(1, count)] + [part(0)] + [piece] * (count - 1) + [tall],
+        out_specs=[pl.BlockSpec((1, rows // 2, cols * count), lambda j, i: (j, i, 0))] * 2 + [tall],
+    )(first, *[first_got] * (count - 1), second, *second_got, down)
 
 
 def front_kernel(reps, eps, lengths_ref, tok_ref, cot_ref, wq_ref, wk_ref, wv_ref, wo_ref, gains_ref, router_ref, nums_ref, freq_ref,
@@ -1855,7 +1891,7 @@
     side = jnp.concatenate(
         [weight_high, weight_low, jnp.zeros((tok_dev, 128 - 2 * experts_all), bf16)], axis=1
     )
-    row_sum, moe_sum, gate_term, up_term, down_w_grad = moe(
+    row_sum, moe_sum, gate_term, up_term, down_term, gate_got = moe(
         jnp.concatenate([mid_low, side], axis=1),
         cot_all,
         expert_gate,
@@ -1868,14 +1904,14 @@
     block_out = (after_attn + moe_out).astype(bf16)
 
     def rows_of(parts):
-        pieces = [parts[0]]
+        pieces = []
         for k in range(1, rep_count):
             pieces.append(
                 lax.ppermute(parts[k], "rep", [(i, (i + k) % rep_count) for i in range(rep_count)])
             )
         return pieces
 
-    gate_pieces, up_pieces = rows_of(gate_term), rows_of(up_term)
+    up_pieces = rows_of(up_term)
 
     out_grad = cotangent.astype(f32)
     gate_cot = row_sum[:, width : width + experts_all].astype(f32) * kept_dense
@@ -1933,7 +1969,9 @@
         gains_all.reshape(-1), (rep_index * ep_count + ep_index) * gains_dev, gains_dev
     )
     router_sum = router_own[:router_rows].reshape(rows_dev, experts_all)
-    gate_w_grad, up_w_grad = join_columns(gate_pieces, up_pieces)
+    gate_w_grad, up_w_grad, down_w_grad = join_columns(
+        gate_term, gate_got, up_term, up_pieces, down_term
+    )
     return (
         block_out,
         input_grad,

time: 701 us -> 681 us (0.971)
  starting transfers between devices: 23.6 us -> 4.85 us
  local copies, waits for them, and re-layouts: 34 us -> 23.3 us
  Pallas kernels: 618 us -> 628 us
    pallas_call x1, Pallas kernels: 278 us -> 313 us  [moe(): pl.pallas_call(partial(moe_kernel, reps, side, experts_all), out_shape=ou...]
    pallas_call x1, Pallas kernels: 137 us -> 112 us  [last_sums(): pl.pallas_call(partial(last_kernel, reps, eps), out_shape=outs, in_specs=...]
    ppermute x6 -> x3, starting transfers between devices: 23.6 us -> 4.85 us  [rows_of(): lax.ppermute(parts[k], 'rep', [(i, (i + k) % rep_count) for i in range(re...]
    unnamed x35 -> x30, local copies, waits for them, and re-layouts: 15.4 us -> 7.11 us
  transfers between devices with their start and end apart: 6 -> 3, of which waited for: 1 -> 0; matrix products, arithmetic and copies ran while one was open for 2% -> 2% of each run, Pallas kernels for 26% -> 22%
where the time goes in v7:
time: 681 us; the launch traced here: 672 us
  Pallas kernels  628 us (92%)
  local copies, waits for them, and re-layouts  23.3 us (3%)
  other arithmetic  9.73 us (1%)
    pallas_call x1, Pallas kernels, moe(): pl.pallas_call(partial(moe_kernel, reps, side, experts_all), out_shape=ou...  313 us
    pallas_call x1, Pallas kernels, front(): pl.pallas_call(partial(front_kernel, reps, eps), out_shape=outs, in_specs...  155 us
    pallas_call x1, Pallas kernels, last_sums(): pl.pallas_call(partial(last_kernel, reps, eps), out_shape=outs, in_specs=...  112 us
    pallas_call x1, Pallas kernels, attention_back(): pl.pallas_call(partial(back_kernel, heads_dev), out_shape=outs, in_specs=...  38.4 us
  transfers between devices with their start and end apart: 3, of which 0 were waited for; matrix products, arithmetic and copies ran while one was open for 2% of the time, Pallas kernels for 22%

profile of v7, /device:TPU:0, one launch (start us, length us, event | category | flops | bytes accessed | tf_op | source)
XLA Modules:
  0.0 671.8 jit_solution(8156531747350848937)
XLA Ops:
  0.6 0.0 copy-start.9
  0.7 0.8 copy.49
  1.5 0.1 reshape.119
  1.6 0.7 convert_reduce_fusion
  2.3 0.7 pad_add_fusion
  3.0 0.6 pad.13.nums_ref
  3.6 0.6 maximum_bitcast_fusion.freq_ref
  4.2 0.6 pad.12.router_ref
  4.8 0.8 dynamic_update_slice.3
  5.6 0.6 copy-done.8
  6.2 154.7 %shard_map.230 = (bf16[4,8,128,2048]{3,2,1,0:T(8,128)(2,1)}, bf16[8,4,16,128]{3,2,1,0:T(8,128)(2,1)}, s32[8,16,128]{2,1,0:T(8,128)}, f32[48,128]{1,0:T(8,128)}, ...) custom-call(s32[1,3]{1,0:T(1,128)} %lengths_ref.1, ...), custom_call_target="tpu_custom_call" | custom-call | tf_op jit(solution)/shard_map/pallas_call | solution.py:1762
  160.9 0.8 fusion.11
  161.8 0.8 slice_bitcast_fusion.4
  162.6 1.4 multiply_reduce_fusion.2
  164.0 1.3 fusion.12
  165.3 0.9 slice_bitcast_fusion.3
  166.2 0.7 reshape.121
  166.9 0.0 copy-start.1
  166.9 0.1 copy.50
  167.0 0.1 fusion.4
  167.1 1.4 multiply_convert_fusion
  168.5 0.4 fusion.13
  168.9 0.2 fusion.7
  169.1 0.3 subtract_convert_fusion
  169.4 1.0 concatenate.14.x_ref
  170.4 312.5 %shard_map.231 = (bf16[128,2176]{1,0:T(8,128)(2,1)}, bf16[128,2048]{1,0:T(8,128)(2,1)}, bf16[4,3,512,256]{3,2,1,0:T(8,128)(2,1)}, bf16[4,3,512,256]{3,2,1,0:T(8,...) custom-call(bf16[128,2176]{1,0:T(8,128)(2,1)} %concatenate.14.x_ref,, ...), custom_call_target="tpu_custom_call" | custom-call | tf_op jit(solution)/shard_map/pallas_call | solution.py:859
  482.9 0.0 copy-start
  482.9 0.0 copy-start.2
  483.0 0.0 copy-start.10
  483.0 3.2 slice_bitcast_fusion
  486.1 1.3 collective-permute-start
  487.5 3.4 collective-permute-start.1
  490.8 0.2 collective-permute-start.2
  491.0 0.9 multiply_reduce_fusion.3
  491.9 2.1 fusion.14
  494.0 0.0 copy-done.2
  494.0 1.6 multiply_reduce_fusion
  495.6 1.7 reshape.129
  497.3 0.0 copy-done.10
  497.4 0.2 reduce-window.8
  497.5 0.7 pad.14.router_ref
  498.3 2.9 fusion.9
  501.2 0.1 convert_reduce_fusion.1
  501.3 0.6 convert_bitcast_fusion.segs_ref
  501.9 38.4 %shard_map.232 = (bf16[4,2,128,2048]{3,2,1,0:T(8,128)(2,1)}, bf16[4,512,768]{2,1,0:T(8,128)(2,1)}, bf16[2,2,64,2048]{3,2,1,0:T(8,128)(2,1)}, f32[8,128]{1,0:T(8,128)}) custom-call(bf16[128,2048]{1,0:T(8,128)(2,1)} %get-tuple-element.121.cot_ref, bf16[2,2,64,2048]{3,2,1,0:T(8,128)(2,1)} %get-tuple-element.50.wout_ref, ...), custom_call_target="tpu_custom_call" | custom-call | tf_op jit(solution)/shard_map/pallas_call | solution.py:1030
  540.2 0.7 slice_bitcast_fusion.6
  540.9 0.6 reshape.128.gains_ref
  541.6 111.8 %shard_map.233 = (f32[128,2048]{1,0:T(8,128)}, f32[64,2048]{1,0:T(8,128)}, f32[64,2048]{1,0:T(8,128)}, f32[64,2048]{1,0:T(8,128)}, f32[64,2048]{1,0:T(8,128)}, /*index=5*/f32[8,2048]{1,0:T(8,128)}, f32[16,128]{1,0:T(8,128)}) custom-call(bf16[4,2,128,2048]{3,2,1,0:T(8,128)(2,1)} %get-tuple-element.57.part_ref, ...), custom_call_target="tpu_custom_call" | custom-call | tf_op jit(solution)/shard_map/pallas_call | solution.py:1318
  653.4 0.9 copy.62
  654.2 0.8 reshape.130
  655.0 0.7 copy.58
  655.7 0.6 dynamic_slice.3
  656.3 0.0 collective-permute-done.refs_5_
  656.3 0.0 collective-permute-done.1.refs_6_
  656.3 0.0 collective-permute-done.2.refs_7_
  656.4 11.0 %shard_map.234 = (f32[3,512,1024]{2,1,0:T(8,128)}, f32[3,512,1024]{2,1,0:T(8,128)}, f32[3,256,2048]{2,1,0:T(8,128)}) custom-call(bf16[4,3,512,256]{3,2,1,0:T(8,128)(2,1)} %get-tuple-element.68.refs_0_, bf16[4,3,512,256]{3,2,1,0:T(8,128)(2,1)} %get-tuple-element.69.refs_1_.refs_2_.refs_3_, bf16[4,3,512,256]{3,2,1,0:T(8,128)(2,1)} %get-tuple-element.69.refs_1_.refs_2_.refs_3_, ...), custom_call_target="tpu_custom_call" | custom-call | tf_op jit(solution)/shard_map/pallas_call | solution.py:1359
  667.4 0.0 copy-start.5
  667.4 0.0 copy-start.4
  667.4 0.0 copy-done.3
  667.4 1.0 copy.69
  668.4 0.8 copy.70
  669.2 0.8 copy.71
  670.0 0.8 copy.72
  670.8 0.8 copy.73
  (21 shorter events, 0.1 us)
Async XLA Ops:
  0.6 168.4 %copy-start.9 = (s32[128]{0:T(128)S(1)}, s32[128]{0:T(128)}, u32[]{:S(2)}) copy-start(s32[128]{0:T(128)} %param.29) | copy-start | bytes 1540
  5.6 0.6 copy-start.8
  166.9 1.6 copy-start.1
  482.9 11.0 %copy-start = (f32[128,2048]{1,0:T(8,128)S(1)}, f32[128,2048]{1,0:T(8,128)}, u32[]{:S(2)}) copy-start(f32[128,2048]{1,0:T(8,128)} %get-tuple-element.43) | copy-start | bytes 3145732
  482.9 11.0 %copy-start.2 = (bf16[2048,24]{1,0:T(8,128)(2,1)S(1)}, bf16[2048,24]{1,0:T(8,128)(2,1)}, u32[]{:S(2)}) copy-start(bf16[2048,24]{1,0:T(8,128)(2,1)} %copy-done.1) | copy-start | bytes 294916
  483.0 14.4 %copy-start.10 = (s32[1,3]{1,0:T(1,128)S(1)}, s32[1,3]{1,0:T(1,128)}, u32[]{:S(2)}) copy-start(s32[1,3]{1,0:T(1,128)} %lengths_ref.1) | copy-start | bytes 40
  486.1 170.2 %collective-permute-start = (bf16[3,512,256]{2,1,0:T(8,128)(2,1)}, bf16[3,512,256]{2,1,0:T(8,128)(2,1)}, u32[]{:S(2)}, u32[]{:S(2)}) collective-permute-start(bf16[3,512,256]{2,1,0:T(8,128)(2,1)} %get-tuple-element.127), channel_id=1, source_target_pairs={{0,8},{8,16},{16,24},{24,0},{1,9},{9,17},{17,25},{25,1},{2,10},{10... | collective-permute-start | bytes 2359304 | tf_op jit(solution)/shard_map/ppermute | solution.py:1910
  487.5 168.9 %collective-permute-start.1 = (bf16[3,512,256]{2,1,0:T(8,128)(2,1)}, bf16[3,512,256]{2,1,0:T(8,128)(2,1)}, u32[]{:S(2)}, u32[]{:S(2)}) collective-permute-start(bf16[3,512,256]{2,1,0:T(8,128)(2,1)} %get-tuple-element.126), channel_id=1, source_target_pairs={{0,16},{8,24},{16,0},{24,8},{1,17},{9,25},{17,1},{25,9},{2,18},{10... | collective-permute-start | bytes 2359304 | tf_op jit(solution)/shard_map/ppermute | solution.py:1910
  490.8 165.5 %collective-permute-start.2 = (bf16[3,512,256]{2,1,0:T(8,128)(2,1)}, bf16[3,512,256]{2,1,0:T(8,128)(2,1)}, u32[]{:S(2)}, u32[]{:S(2)}) collective-permute-start(bf16[3,512,256]{2,1,0:T(8,128)(2,1)} %get-tuple-element.125), channel_id=1, source_target_pairs={{0,24},{8,0},{16,8},{24,16},{1,25},{9,1},{17,9},{25,17},{2,26},{10... | collective-permute-start | bytes 2359304 | tf_op jit(solution)/shard_map/ppermute | solution.py:1910
  656.3 11.1 %copy-start.3 = (f32[128,2048]{1,0:T(8,128)S(1)}, f32[128,2048]{1,0:T(8,128)}, u32[]{:S(2)}) copy-start(f32[128,2048]{1,0:T(8,128)} %get-tuple-element.149) | copy-start | bytes 3145732
  656.3 12.1 %copy-start.7 = (f32[64,2048]{1,0:T(8,128)S(1)}, f32[64,2048]{1,0:T(8,128)}, u32[]{:S(2)}) copy-start(f32[64,2048]{1,0:T(8,128)} %get-tuple-element.150) | copy-start | bytes 1572868
  656.3 12.9 %copy-start.6 = (f32[64,2048]{1,0:T(8,128)S(1)}, f32[64,2048]{1,0:T(8,128)}, u32[]{:S(2)}) copy-start(f32[64,2048]{1,0:T(8,128)} %get-tuple-element.151) | copy-start | bytes 1572868
  667.4 2.6 copy-start.5
  667.4 3.4 copy-start.4

commit v8 on v7

--- a/solution.py
+++ b/solution.py
@@ -727,7 +727,7 @@
 
     def piece_done(n):
         k = (n // per_piece + reps - z) % reps
-        @pl.when((n % per_piece == per_piece - 1) & (k > 0))
+        @pl.when((n % per_piece == per_piece - 1) & (k % 2 == 1))
         def _():
             hand_over(k).start()
 
@@ -817,7 +817,7 @@
     for o in outs:
         o.wait()
     fcopy(reps - 2, group_of(reps - 2)).wait_send()
-    for k in range(1, reps):
+    for k in range(1, reps, 2):
         hand_over(k).wait()
     for j in range(2):
         hcopy(last, j).wait_send()
@@ -1347,7 +1347,7 @@
             out[:, :, pl.ds(place, cols)] = ins[k][...].astype(out.dtype)
 
 
-def join_columns(first, first_got, second, second_got, down):
+def join_columns(first, first_got, first_even, second, second_got, down):
     count, exp_dev, rows, cols = first.shape
     whole = jax.ShapeDtypeStruct((exp_dev, rows, cols * count), jnp.float32)
 
@@ -1360,9 +1360,9 @@
         partial(join_kernel, count),
         grid=(exp_dev, 2),
         out_shape=(whole, whole, jax.ShapeDtypeStruct(down.shape, jnp.float32)),
-        in_specs=[part(0)] + [part(k) for k in range(1, count)] + [part(0)] + [piece] * (count - 1) + [tall],
+        in_specs=[part(0)] + [part(k) if k % 2 else piece for k in range(1, count)] + [part(0)] + [piece] * (count - 1) + [tall],
         out_specs=[pl.BlockSpec((1, rows // 2, cols * count), lambda j, i: (j, i, 0))] * 2 + [tall],
-    )(first, *[first_got] * (count - 1), second, *second_got, down)
+    )(first, *[first_got if k % 2 else first_even[k // 2 - 1] for k in range(1, count)], second, *second_got, down)
 
 
 def front_kernel(reps, eps, lengths_ref, tok_ref, cot_ref, wq_ref, wk_ref, wv_ref, wo_ref, gains_ref, router_ref, nums_ref, freq_ref,
@@ -1903,15 +1903,11 @@
     moe_out = moe_sum.astype(f32)
     block_out = (after_attn + moe_out).astype(bf16)
 
-    def rows_of(parts):
-        pieces = []
-        for k in range(1, rep_count):
-            pieces.append(
-                lax.ppermute(parts[k], "rep", [(i, (i + k) % rep_count) for i in range(rep_count)])
-            )
-        return pieces
-
-    up_pieces = rows_of(up_term)
+    def from_below(part, k):
+        return lax.ppermute(part, "rep", [(i, (i + k) % rep_count) for i in range(rep_count)])
+
+    gate_pieces = [from_below(gate_term[k], k) for k in range(2, rep_count, 2)]
+    up_pieces = [from_below(up_term[k], k) for k in range(1, rep_count)]
 
     out_grad = cotangent.astype(f32)
     gate_cot = row_sum[:, width : width + experts_all].astype(f32) * kept_dense
@@ -1970,7 +1966,7 @@
     )
     router_sum = router_own[:router_rows].reshape(rows_dev, experts_all)
     gate_w_grad, up_w_grad, down_w_grad = join_columns(
-        gate_term, gate_got, up_term, up_pieces, down_term
+        gate_term, gate_got, gate_pieces, up_term, up_pieces, down_term
     )
     return (
         block_out,

time: 681 us -> 677 us (level)
    pallas_call x1, Pallas kernels: 313 us -> 296 us  [moe(): pl.pallas_call(partial(moe_kernel, reps, side, experts_all), out_shape=ou...]
    pallas_call x1, Pallas kernels: 112 us -> 122 us  [last_sums(): pl.pallas_call(partial(last_kernel, reps, eps), out_shape=outs, in_specs=...]
  transfers between devices with their start and end apart: 3 -> 4, of which waited for: 0 -> 0; matrix products, arithmetic and copies ran while one was open for 2% -> 3% of each run, Pallas kernels for 22% -> 24%
where the time goes in v8:
time: 677 us; the launch traced here: 668 us
  Pallas kernels  622 us (92%)
  local copies, waits for them, and re-layouts  25.4 us (4%)
  other arithmetic  9.73 us (1%)
    pallas_call x1, Pallas kernels, moe(): pl.pallas_call(partial(moe_kernel, reps, side, experts_all), out_shape=ou...  296 us
    pallas_call x1, Pallas kernels, front(): pl.pallas_call(partial(front_kernel, reps, eps), out_shape=outs, in_specs...  155 us
    pallas_call x1, Pallas kernels, last_sums(): pl.pallas_call(partial(last_kernel, reps, eps), out_shape=outs, in_specs=...  122 us
    pallas_call x1, Pallas kernels, attention_back(): pl.pallas_call(partial(back_kernel, heads_dev), out_shape=outs, in_specs=...  38.2 us
  transfers between devices with their start and end apart: 4, of which 0 were waited for; matrix products, arithmetic and copies ran while one was open for 3% of the time, Pallas kernels for 24%

profile of v8, /device:TPU:0, one launch (start us, length us, event | category | flops | bytes accessed | tf_op | source)
XLA Modules:
  0.0 668.3 jit_solution(10328863784099725459)
XLA Ops:
  0.6 0.0 copy-start.9
  0.7 0.8 copy.49
  1.5 0.1 reshape.119
  1.6 0.7 convert_reduce_fusion
  2.3 0.7 pad_add_fusion
  3.0 0.6 pad.13.nums_ref
  3.6 0.6 maximum_bitcast_fusion.freq_ref
  4.2 0.6 pad.12.router_ref
  4.8 0.8 dynamic_update_slice.3
  5.6 0.6 copy-done.8
  6.2 154.7 %shard_map.230 = (bf16[4,8,128,2048]{3,2,1,0:T(8,128)(2,1)}, bf16[8,4,16,128]{3,2,1,0:T(8,128)(2,1)}, s32[8,16,128]{2,1,0:T(8,128)}, f32[48,128]{1,0:T(8,128)}, ...) custom-call(s32[1,3]{1,0:T(1,128)} %lengths_ref.1, ...), custom_call_target="tpu_custom_call" | custom-call | tf_op jit(solution)/shard_map/pallas_call | solution.py:1762
  160.9 0.8 fusion.11
  161.8 0.8 slice_bitcast_fusion.5
  162.6 1.4 multiply_reduce_fusion.2
  164.0 1.3 fusion.12
  165.3 0.9 slice_bitcast_fusion.4
  166.2 0.7 reshape.121
  166.9 0.0 copy-start.1
  166.9 0.1 copy.50
  167.0 0.1 fusion.4
  167.1 1.4 multiply_convert_fusion
  168.5 0.0 copy-done.1
  168.5 0.4 fusion.13
  168.9 0.2 fusion.7
  169.1 0.0 copy-done.9
  169.1 0.3 subtract_convert_fusion
  169.4 1.0 concatenate.14.x_ref
  170.4 295.7 %shard_map.231 = (bf16[128,2176]{1,0:T(8,128)(2,1)}, bf16[128,2048]{1,0:T(8,128)(2,1)}, bf16[4,3,512,256]{3,2,1,0:T(8,128)(2,1)}, bf16[4,3,512,256]{3,2,1,0:T(8,...) custom-call(bf16[128,2176]{1,0:T(8,128)(2,1)} %concatenate.14.x_ref,, ...), custom_call_target="tpu_custom_call" | custom-call | tf_op jit(solution)/shard_map/pallas_call | solution.py:859
  466.1 0.0 copy-start.2
  466.1 3.2 slice_bitcast_fusion
  469.3 0.3 collective-permute-start.1
  469.6 3.2 collective-permute-start.2
  472.8 0.6 collective-permute-start.3
  473.4 2.1 slice_bitcast_fusion.3
  475.5 1.9 collective-permute-start
  477.4 0.9 multiply_reduce_fusion.3
  478.2 2.1 fusion.14
  480.4 1.6 multiply_reduce_fusion
  482.0 1.7 reshape.129
  483.7 0.2 reduce-window.8
  483.9 0.7 pad.14.router_ref
  484.6 2.9 fusion.9
  487.6 0.1 convert_reduce_fusion.1
  487.6 0.6 convert_bitcast_fusion.segs_ref
  488.2 38.2 %shard_map.232 = (bf16[4,2,128,2048]{3,2,1,0:T(8,128)(2,1)}, bf16[4,512,768]{2,1,0:T(8,128)(2,1)}, bf16[2,2,64,2048]{3,2,1,0:T(8,128)(2,1)}, f32[8,128]{1,0:T(8,128)}) custom-call(bf16[128,2048]{1,0:T(8,128)(2,1)} %get-tuple-element.121.cot_ref, bf16[2,2,64,2048]{3,2,1,0:T(8,128)(2,1)} %get-tuple-element.50.wout_ref, ...), custom_call_target="tpu_custom_call" | custom-call | tf_op jit(solution)/shard_map/pallas_call | solution.py:1030
  526.5 0.7 slice_bitcast_fusion.7
  527.2 0.6 reshape.128.gains_ref
  527.9 122.0 %shard_map.233 = (f32[128,2048]{1,0:T(8,128)}, f32[64,2048]{1,0:T(8,128)}, f32[64,2048]{1,0:T(8,128)}, f32[64,2048]{1,0:T(8,128)}, f32[64,2048]{1,0:T(8,128)}, /*index=5*/f32[8,2048]{1,0:T(8,128)}, f32[16,128]{1,0:T(8,128)}) custom-call(bf16[4,2,128,2048]{3,2,1,0:T(8,128)(2,1)} %get-tuple-element.57.part_ref, ...), custom_call_target="tpu_custom_call" | custom-call | tf_op jit(solution)/shard_map/pallas_call | solution.py:1318
  649.9 0.9 copy.62
  650.7 0.8 reshape.130
  651.5 0.7 copy.58
  652.2 0.6 dynamic_slice.3
  652.8 0.0 collective-permute-done.1.refs_5_
  652.8 0.0 collective-permute-done.2.refs_6_
  652.8 0.0 collective-permute-done.3.refs_7_
  652.8 0.0 collective-permute-done.refs_2_
  652.9 11.0 %shard_map.234 = (f32[3,512,1024]{2,1,0:T(8,128)}, f32[3,512,1024]{2,1,0:T(8,128)}, f32[3,256,2048]{2,1,0:T(8,128)}) custom-call(bf16[4,3,512,256]{3,2,1,0:T(8,128)(2,1)} %get-tuple-element.68.refs_0_, bf16[4,3,512,256]{3,2,1,0:T(8,128)(2,1)} %get-tuple-element.69.refs_1_.refs_3_, bf16[3,512,256]{2,1,0:T(8,128)(2,1)} %collective-permute-done.refs_2_, ...), custom_call_target="tpu_custom_call" | custom-call | tf_op jit(solution)/shard_map/pallas_call | solution.py:1359
  664.0 1.0 copy.69
  664.9 0.8 copy.70
  665.7 0.8 copy.71
  666.5 0.0 copy-done.5
  666.5 0.8 copy.72
  667.3 0.0 copy-done.4
  667.3 0.8 copy.73
  (24 shorter events, 0.1 us)
Async XLA Ops:
  0.6 168.4 %copy-start.9 = (s32[128]{0:T(128)S(1)}, s32[128]{0:T(128)}, u32[]{:S(2)}) copy-start(s32[128]{0:T(128)} %param.29) | copy-start | bytes 1540
  5.6 0.6 copy-start.8
  166.9 1.6 copy-start.1
  466.1 14.3 %copy-start = (f32[128,2048]{1,0:T(8,128)S(1)}, f32[128,2048]{1,0:T(8,128)}, u32[]{:S(2)}) copy-start(f32[128,2048]{1,0:T(8,128)} %get-tuple-element.43) | copy-start | bytes 3145732
  466.1 14.3 %copy-start.2 = (bf16[2048,24]{1,0:T(8,128)(2,1)S(1)}, bf16[2048,24]{1,0:T(8,128)(2,1)}, u32[]{:S(2)}) copy-start(bf16[2048,24]{1,0:T(8,128)(2,1)} %copy-done.1) | copy-start | bytes 294916
  469.3 14.4 %copy-start.10 = (s32[1,3]{1,0:T(1,128)S(1)}, s32[1,3]{1,0:T(1,128)}, u32[]{:S(2)}) copy-start(s32[1,3]{1,0:T(1,128)} %lengths_ref.1) | copy-start | bytes 40
  469.3 183.5 %collective-permute-start.1 = (bf16[3,512,256]{2,1,0:T(8,128)(2,1)}, bf16[3,512,256]{2,1,0:T(8,128)(2,1)}, u32[]{:S(2)}, u32[]{:S(2)}) collective-permute-start(bf16[3,512,256]{2,1,0:T(8,128)(2,1)} %get-tuple-element.127), channel_id=1, source_target_pairs={{0,8},{8,16},{16,24},{24,0},{1,9},{9,17},{17,25},{25,1},{2,10},{10... | collective-permute-start | bytes 2359304 | tf_op jit(solution)/shard_map/ppermute | solution.py:1907
  469.6 183.2 %collective-permute-start.2 = (bf16[3,512,256]{2,1,0:T(8,128)(2,1)}, bf16[3,512,256]{2,1,0:T(8,128)(2,1)}, u32[]{:S(2)}, u32[]{:S(2)}) collective-permute-start(bf16[3,512,256]{2,1,0:T(8,128)(2,1)} %get-tuple-element.126), channel_id=1, source_target_pairs={{0,16},{8,24},{16,0},{24,8},{1,17},{9,25},{17,1},{25,9},{2,18},{10... | collective-permute-start | bytes 2359304 | tf_op jit(solution)/shard_map/ppermute | solution.py:1907
  472.8 180.0 %collective-permute-start.3 = (bf16[3,512,256]{2,1,0:T(8,128)(2,1)}, bf16[3,512,256]{2,1,0:T(8,128)(2,1)}, u32[]{:S(2)}, u32[]{:S(2)}) collective-permute-start(bf16[3,512,256]{2,1,0:T(8,128)(2,1)} %get-tuple-element.125), channel_id=1, source_target_pairs={{0,24},{8,0},{16,8},{24,16},{1,25},{9,1},{17,9},{25,17},{2,26},{10... | collective-permute-start | bytes 2359304 | tf_op jit(solution)/shard_map/ppermute | solution.py:1907
  475.5 177.4 %collective-permute-start = (bf16[3,512,256]{2,1,0:T(8,128)(2,1)}, bf16[3,512,256]{2,1,0:T(8,128)(2,1)}, u32[]{:S(2)}, u32[]{:S(2)}) collective-permute-start(bf16[3,512,256]{2,1,0:T(8,128)(2,1)} %slice_bitcast_fusion.3), channel_id=1, source_target_pairs={{0,16},{8,24},{16,0},{24,8},{1,17},{9,25},{17,1},{25,9},{2,18},{10... | collective-permute-start | bytes 2359304 | tf_op jit(solution)/shard_map/ppermute | solution.py:1907
  652.9 11.1 %copy-start.3 = (f32[128,2048]{1,0:T(8,128)S(1)}, f32[128,2048]{1,0:T(8,128)}, u32[]{:S(2)}) copy-start(f32[128,2048]{1,0:T(8,128)} %get-tuple-element.149) | copy-start | bytes 3145732
  652.9 12.1 %copy-start.7 = (f32[64,2048]{1,0:T(8,128)S(1)}, f32[64,2048]{1,0:T(8,128)}, u32[]{:S(2)}) copy-start(f32[64,2048]{1,0:T(8,128)} %get-tuple-element.150) | copy-start | bytes 1572868
  652.9 12.9 %copy-start.6 = (f32[64,2048]{1,0:T(8,128)S(1)}, f32[64,2048]{1,0:T(8,128)}, u32[]{:S(2)}) copy-start(f32[64,2048]{1,0:T(8,128)} %get-tuple-element.151) | copy-start | bytes 1572868
  663.9 2.6 copy-start.5
  663.9 3.4 copy-start.4

commit v9 on v8

--- a/solution.py
+++ b/solution.py
@@ -381,9 +381,9 @@
 
 def moe_kernel(reps, side_lanes, experts_all, x_ref, cot_ref, eg_ref, eu_ref, ed_ref,
                row_ref, moe_ref, gout_ref, uout_ref, dout_ref, gin_ref,
-               mid_ref, a_ref, b_ref, h_ref, xin_ref, yin_ref, zin_ref,
-               wgu, wd, xbuf, cbuf, abuf, pbuf, sib_in, relay_in, sendbuf, ownbuf, rbuf, tmp, colbuf, gst, dst,
-               own_sem, w_sem, x_sem, c_sem, ab_sem, t_sem, col_sem, g_sem, o_sem,
+               mid_ref, a_ref, b_ref, h_ref,
+               wgu, wd, xbuf, cbuf, abuf, pbuf, sib_in, relay_in, sendbuf, ownbuf, rbuf, xin, yin, zin, colbuf, gst, dst,
+               own_sem, w_sem, x_sem, c_sem, ab_sem, col_sem, g_sem, o_sem,
                zs, zr, ps, pr, cs, cr, ss, sr, hs, hr, qs, qr, fs, fr, xs, xr):
     f32, bf16 = jnp.float32, jnp.bfloat16
     z = lax.axis_index("rep")
@@ -559,12 +559,12 @@
 
     def qcopy(s, j):
         return pltpu.make_async_remote_copy(
-            src_ref=sendbuf.at[1 + j], dst_ref=(xin_ref, yin_ref)[j].at[s], send_sem=qs.at[s, j], recv_sem=qr.at[s, j],
+            src_ref=sendbuf.at[1 + j], dst_ref=(xin, yin)[j].at[s], send_sem=qs.at[s, j], recv_sem=qr.at[s, j],
             device_id={"rep": z, "ep": chips[j]}, device_id_type=MESH)
 
     def fcopy(s, g):
         return pltpu.make_async_remote_copy(
-            src_ref=rbuf.at[s % 2], dst_ref=zin_ref.at[z], send_sem=fs.at[s], recv_sem=fr.at[z],
+            src_ref=rbuf.at[s % 2], dst_ref=zin.at[z], send_sem=fs.at[s], recv_sem=fr.at[z],
             device_id={"rep": g, "ep": e}, device_id_type=MESH)
 
     step = 16
@@ -614,22 +614,16 @@
             add(sendbuf.at[2, lower], (mine.at[lower], other.at[lower], relay_in.at[s, 0]), half)
             qcopy(s, 1).start()
 
-    def load_t(src, m):
-        return pltpu.make_async_copy(src, tmp.at[m], t_sem.at[m])
-
     def total(s):
         for j in range(2):
             qcopy(s, j).wait_recv()
-            load_t((xin_ref, yin_ref)[j].at[s], j).start()
-        for j in range(2):
-            load_t((xin_ref, yin_ref)[j].at[s], j).wait()
 
     def plane_sum(s):
         total(s)
         @pl.when(s >= 2)
         def _():
             fcopy(s - 2, group_of(s - 2)).wait_send()
-        add(rbuf.at[s % 2], (ownbuf.at[s % 2], tmp.at[0], tmp.at[1]))
+        add(rbuf.at[s % 2], (ownbuf.at[s % 2], xin.at[s], yin.at[s]))
         fcopy(s, group_of(s)).start()
 
     @pl.when(z < reps - 1)
@@ -801,13 +795,10 @@
     for d in range(1, reps):
         src = (z + d) % reps
         pltpu.make_async_remote_copy(
-            src_ref=rbuf.at[0], dst_ref=zin_ref.at[src], send_sem=fs.at[last], recv_sem=fr.at[src],
+            src_ref=rbuf.at[0], dst_ref=zin.at[src], send_sem=fs.at[last], recv_sem=fr.at[src],
             device_id={"rep": src, "ep": e}, device_id_type=MESH).wait_recv()
-        load_t(zin_ref.at[src], 1 + d).start()
-    for d in range(1, reps):
-        load_t(zin_ref.at[(z + d) % reps], 1 + d).wait()
     fcopy(reps - 3, group_of(reps - 3)).wait_send()
-    add(rbuf.at[(reps - 3) % 2], (ownbuf.at[last % 2], *(tmp.at[m] for m in range(reps + 1))))
+    add(rbuf.at[(reps - 3) % 2], (ownbuf.at[last % 2], xin.at[last], yin.at[last], *(zin.at[(z + d) % reps] for d in range(1, reps))))
     outs = (
         pltpu.make_async_copy(rbuf.at[(reps - 3) % 2, :, pl.ds(0, W1)], row_ref, o_sem.at[0]),
         pltpu.make_async_copy(rbuf.at[(reps - 3) % 2, :, pl.ds(W1, width)], moe_ref, o_sem.at[1]),
@@ -854,7 +845,6 @@
         S((reps, exp_dev, width // reps, F), bf16), S((reps, exp_dev, width // reps, F), bf16), S((exp_dev, F, width), bf16),
         S((reps, exp_dev, width // reps, F), bf16),
         S((reps, eps, rows, W1), bf16), S((tokens, EF), bf16), S((tokens, EF), bf16), S((tokens, EF), bf16),
-        S((reps, rows, WP), bf16), S((reps, rows, WP), bf16), S((reps, rows, WP), bf16),
     )
     return pl.pallas_call(
         partial(moe_kernel, reps, side, experts_all),
@@ -866,9 +856,9 @@
             V((2, 2, rows, W1), bf16), V((2, 2, rows, width), bf16),
             V((2, 3, 2 * rows, EF), bf16), V((2, 2, rows, WP), bf16), V((4, rows, WP), bf16),
             V((reps, 2, rows // 2, WP), bf16), V((3, rows, WP), bf16), V((2, rows, WP), bf16), V((2, rows, WP), bf16),
-            V((5, rows, WP), bf16), V((2, reps, eps, rows, 256), bf16),
+            *[V((reps, rows, WP), bf16)] * 3, V((2, reps, eps, rows, 256), bf16),
             V((2, exp_dev, 256, F), bf16), V((2, exp_dev, F, 256), bf16),
-            D, D((3 * exp_dev,)), D((2,)), D((2,)), D((2, 3)), D((5,)), D((2,)), D((2, exp_dev)), D((2,)),
+            D, D((3 * exp_dev,)), D((2,)), D((2,)), D((2, 3)), D((2,)), D((2, exp_dev)), D((2,)),
             D((2, reps)), D((reps,)), D((reps, 4)), D((reps, 4)), D((reps, 4)), D((reps, 4)),
             D((steps,)), D((steps,)), D((reps, 2)), D((reps, 2)), D((reps, 2)), D((reps, 2)), D((reps,)), D((reps,)), D((reps,)), D((reps,)),
         ],
@@ -1109,15 +1099,15 @@
                 return along(src, self.up.at[g], self.usend.at[g], self.urecv.at[g], True)
             return along(src, self.down.at[g], self.dsend.at[g], self.drecv.at[g], False)
 
-        def begin(self):
+        def begin(self, source):
             @pl.when(z == 0)
             def _():
                 for g in range(reps - 1, 0, -1):
-                    self.hop(self.mine(g), g, True).start()
+                    self.hop(source(g), g, True).start()
             @pl.when(z == reps - 1)
             def _():
                 for g in range(reps - 1):
-                    self.hop(self.mine(g), g, False).start()
+                    self.hop(source(g), g, False).start()
 
         def forward(self, n):
             g = reps - 1 - n
@@ -1172,12 +1162,11 @@
     wcopy = to_sib(out_ref.at[:, 1 - core], wo.at[core], ws, wr)
     order = (chips[2] // 2, chips[0] // 2, chips[1] // 2, chip)
     scopies = [to_sib(part_ref.at[q, 1 - core], sib_in.at[q], ss.at[n], sr.at[n]) for n, q in enumerate(order)]
+    qkv_sum.begin(lambda g: qkv_ref.at[g])
     for c in scopies:
         c.start()
     wcopy.start()
 
-    loads[1].wait()
-    qkv_sum.begin()
     hcopies = [to_chip(own.at[order[0], (lower, upper)[j]], relay_in.at[j], hs.at[j], hr.at[j], j) for j in range(2)]
     qcopies = [to_chip(own.at[order[1 + j]], (xin, yin)[j], qs.at[j], qr.at[j], j) for j in range(2)]
     loads[0].wait()
@@ -1196,7 +1185,8 @@
         qcopies[j].start()
     loads[2].wait()
     wcopy.wait_recv()
-    out_sum.begin()
+    out_sum.begin(out_sum.mine)
+    loads[1].wait()
     qkv_sum.forward(0)
     scopies[3].wait_recv()
     for c in loads[3:8]:
@@ -1572,7 +1562,6 @@
         c.start()
     tok_spread.pass_on()
     tok_spread.finish()
-    wo_chain.arrive(2)
     cot_take(1)
     for c in gpc:
         c.wait_recv()
@@ -1582,7 +1571,7 @@
     gall[...] = t
     outs = [local(gall, gsum_ref, o_sem.at[0])]
     w_chain.arrive(1)
-    wo_chain.arrive(3)
+    wo_chain.arrive(2)
     cot_chain.forward(1)
 
     for c in small[1:3]:
@@ -1625,6 +1614,7 @@
             normed[n, r, :] = (t * scale * gain_in).astype(bf16)
     outs.append(local(normed, normed_ref, o_sem.at[3]))
     w_chain.arrive(2)
+    wo_chain.arrive(3)
     cot_take(2)
     cot_chain.forward(2)
     cot_spread(z).finish()

time: 677 us -> 675 us (level)
  no operation moved by 1% of the time
where the time goes in v9:
time: 675 us; the launch traced here: 666 us
  Pallas kernels  619 us (92%)
  local copies, waits for them, and re-layouts  25.4 us (4%)
  other arithmetic  9.73 us (1%)
    pallas_call x1, Pallas kernels, moe(): pl.pallas_call(partial(moe_kernel, reps, side, experts_all), out_shape=ou...  295 us
    pallas_call x1, Pallas kernels, front(): pl.pallas_call(partial(front_kernel, reps, eps), out_shape=outs, in_specs...  153 us
    pallas_call x1, Pallas kernels, last_sums(): pl.pallas_call(partial(last_kernel, reps, eps), out_shape=outs, in_specs=...  121 us
    pallas_call x1, Pallas kernels, attention_back(): pl.pallas_call(partial(back_kernel, heads_dev), out_shape=outs, in_specs=...  38.7 us
  transfers between devices with their start and end apart: 4, of which 0 were waited for; matrix products, arithmetic and copies ran while one was open for 3% of the time, Pallas kernels for 24%

profile of v9, /device:TPU:0, one launch (start us, length us, event | category | flops | bytes accessed | tf_op | source)
XLA Modules:
  0.0 666.0 jit_solution(3323130546533730321)
XLA Ops:
  0.6 0.0 copy-start.9
  0.7 0.8 copy.49
  1.5 0.1 reshape.119
  1.6 0.7 convert_reduce_fusion
  2.3 0.7 pad_add_fusion
  3.0 0.6 pad.13.nums_ref
  3.6 0.6 maximum_bitcast_fusion.freq_ref
  4.2 0.6 pad.12.router_ref
  4.8 0.8 dynamic_update_slice.3
  5.6 0.6 copy-done.8
  6.2 153.1 %shard_map.230 = (bf16[4,8,128,2048]{3,2,1,0:T(8,128)(2,1)}, bf16[8,4,16,128]{3,2,1,0:T(8,128)(2,1)}, s32[8,16,128]{2,1,0:T(8,128)}, f32[48,128]{1,0:T(8,128)}, ...) custom-call(s32[1,3]{1,0:T(1,128)} %lengths_ref.1, ...), custom_call_target="tpu_custom_call" | custom-call | tf_op jit(solution)/shard_map/pallas_call | solution.py:1752
  159.4 0.8 fusion.11
  160.2 0.8 slice_bitcast_fusion.5
  161.1 1.4 multiply_reduce_fusion.2
  162.5 1.3 fusion.12
  163.8 0.9 slice_bitcast_fusion.4
  164.7 0.7 reshape.121
  165.4 0.0 copy-start.1
  165.4 0.1 copy.50
  165.5 0.1 fusion.4
  165.6 1.4 multiply_convert_fusion
  167.0 0.4 fusion.13
  167.4 0.2 fusion.7
  167.6 0.3 subtract_convert_fusion
  167.9 1.0 concatenate.14.x_ref
  168.8 295.2 %shard_map.231 = (bf16[128,2176]{1,0:T(8,128)(2,1)}, bf16[128,2048]{1,0:T(8,128)(2,1)}, bf16[4,3,512,256]{3,2,1,0:T(8,128)(2,1)}, bf16[4,3,512,256]{3,2,1,0:T(8,...) custom-call(bf16[128,2176]{1,0:T(8,128)(2,1)} %concatenate.14.x_ref,, ...), custom_call_target="tpu_custom_call" | custom-call | tf_op jit(solution)/shard_map/pallas_call | solution.py:849
  464.0 0.0 copy-start.2
  464.0 3.2 slice_bitcast_fusion
  467.3 0.0 collective-permute-start.1
  467.3 3.9 collective-permute-start.2
  471.1 0.6 collective-permute-start.3
  471.7 2.1 slice_bitcast_fusion.3
  473.8 1.5 collective-permute-start
  475.3 0.9 multiply_reduce_fusion.3
  476.2 2.1 fusion.14
  478.3 0.0 copy-done
  478.3 1.6 multiply_reduce_fusion
  479.9 1.7 reshape.129
  481.7 0.2 reduce-window.8
  481.8 0.7 pad.14.router_ref
  482.6 2.9 fusion.9
  485.5 0.1 convert_reduce_fusion.1
  485.6 0.6 convert_bitcast_fusion.segs_ref
  486.2 38.7 %shard_map.232 = (bf16[4,2,128,2048]{3,2,1,0:T(8,128)(2,1)}, bf16[4,512,768]{2,1,0:T(8,128)(2,1)}, bf16[2,2,64,2048]{3,2,1,0:T(8,128)(2,1)}, f32[8,128]{1,0:T(8,128)}) custom-call(bf16[128,2048]{1,0:T(8,128)(2,1)} %get-tuple-element.121.cot_ref, bf16[2,2,64,2048]{3,2,1,0:T(8,128)(2,1)} %get-tuple-element.50.wout_ref, ...), custom_call_target="tpu_custom_call" | custom-call | tf_op jit(solution)/shard_map/pallas_call | solution.py:1020
  524.9 0.7 slice_bitcast_fusion.7
  525.6 0.6 reshape.128.gains_ref
  526.2 121.3 %shard_map.233 = (f32[128,2048]{1,0:T(8,128)}, f32[64,2048]{1,0:T(8,128)}, f32[64,2048]{1,0:T(8,128)}, f32[64,2048]{1,0:T(8,128)}, f32[64,2048]{1,0:T(8,128)}, /*index=5*/f32[8,2048]{1,0:T(8,128)}, f32[16,128]{1,0:T(8,128)}) custom-call(bf16[4,2,128,2048]{3,2,1,0:T(8,128)(2,1)} %get-tuple-element.57.part_ref, ...), custom_call_target="tpu_custom_call" | custom-call | tf_op jit(solution)/shard_map/pallas_call | solution.py:1308
  647.6 0.9 copy.62
  648.4 0.8 reshape.130
  649.2 0.7 copy.58
  649.9 0.6 dynamic_slice.3
  650.5 0.0 collective-permute-done.1.refs_5_
  650.5 0.0 collective-permute-done.2.refs_6_
  650.5 0.0 collective-permute-done.3.refs_7_
  650.5 0.0 collective-permute-done.refs_2_
  650.6 11.0 %shard_map.234 = (f32[3,512,1024]{2,1,0:T(8,128)}, f32[3,512,1024]{2,1,0:T(8,128)}, f32[3,256,2048]{2,1,0:T(8,128)}) custom-call(bf16[4,3,512,256]{3,2,1,0:T(8,128)(2,1)} %get-tuple-element.68.refs_0_, bf16[4,3,512,256]{3,2,1,0:T(8,128)(2,1)} %get-tuple-element.69.refs_1_.refs_3_, bf16[3,512,256]{2,1,0:T(8,128)(2,1)} %collective-permute-done.refs_2_, ...), custom_call_target="tpu_custom_call" | custom-call | tf_op jit(solution)/shard_map/pallas_call | solution.py:1349
  661.6 0.0 copy-start.5
  661.6 0.0 copy-start.4
  661.6 0.0 copy-done.3
  661.6 1.0 copy.69
  662.6 0.8 copy.70
  663.4 0.8 copy.71
  664.2 0.8 copy.72
  665.0 0.8 copy.73
  (24 shorter events, 0.1 us)
Async XLA Ops:
  0.6 166.9 %copy-start.9 = (s32[128]{0:T(128)S(1)}, s32[128]{0:T(128)}, u32[]{:S(2)}) copy-start(s32[128]{0:T(128)} %param.29) | copy-start | bytes 1540
  5.6 0.6 copy-start.8
  165.4 1.6 copy-start.1
  464.0 14.3 %copy-start = (f32[128,2048]{1,0:T(8,128)S(1)}, f32[128,2048]{1,0:T(8,128)}, u32[]{:S(2)}) copy-start(f32[128,2048]{1,0:T(8,128)} %get-tuple-element.43) | copy-start | bytes 3145732
  464.0 14.3 %copy-start.2 = (bf16[2048,24]{1,0:T(8,128)(2,1)S(1)}, bf16[2048,24]{1,0:T(8,128)(2,1)}, u32[]{:S(2)}) copy-start(bf16[2048,24]{1,0:T(8,128)(2,1)} %copy-done.1) | copy-start | bytes 294916
  467.2 14.4 %copy-start.10 = (s32[1,3]{1,0:T(1,128)S(1)}, s32[1,3]{1,0:T(1,128)}, u32[]{:S(2)}) copy-start(s32[1,3]{1,0:T(1,128)} %lengths_ref.1) | copy-start | bytes 40
  467.3 183.3 %collective-permute-start.1 = (bf16[3,512,256]{2,1,0:T(8,128)(2,1)}, bf16[3,512,256]{2,1,0:T(8,128)(2,1)}, u32[]{:S(2)}, u32[]{:S(2)}) collective-permute-start(bf16[3,512,256]{2,1,0:T(8,128)(2,1)} %get-tuple-element.127), channel_id=1, source_target_pairs={{0,8},{8,16},{16,24},{24,0},{1,9},{9,17},{17,25},{25,1},{2,10},{10... | collective-permute-start | bytes 2359304 | tf_op jit(solution)/shard_map/ppermute | solution.py:1897
  467.3 183.3 %collective-permute-start.2 = (bf16[3,512,256]{2,1,0:T(8,128)(2,1)}, bf16[3,512,256]{2,1,0:T(8,128)(2,1)}, u32[]{:S(2)}, u32[]{:S(2)}) collective-permute-start(bf16[3,512,256]{2,1,0:T(8,128)(2,1)} %get-tuple-element.126), channel_id=1, source_target_pairs={{0,16},{8,24},{16,0},{24,8},{1,17},{9,25},{17,1},{25,9},{2,18},{10... | collective-permute-start | bytes 2359304 | tf_op jit(solution)/shard_map/ppermute | solution.py:1897
  471.1 179.4 %collective-permute-start.3 = (bf16[3,512,256]{2,1,0:T(8,128)(2,1)}, bf16[3,512,256]{2,1,0:T(8,128)(2,1)}, u32[]{:S(2)}, u32[]{:S(2)}) collective-permute-start(bf16[3,512,256]{2,1,0:T(8,128)(2,1)} %get-tuple-element.125), channel_id=1, source_target_pairs={{0,24},{8,0},{16,8},{24,16},{1,25},{9,1},{17,9},{25,17},{2,26},{10... | collective-permute-start | bytes 2359304 | tf_op jit(solution)/shard_map/ppermute | solution.py:1897
  473.8 176.7 %collective-permute-start = (bf16[3,512,256]{2,1,0:T(8,128)(2,1)}, bf16[3,512,256]{2,1,0:T(8,128)(2,1)}, u32[]{:S(2)}, u32[]{:S(2)}) collective-permute-start(bf16[3,512,256]{2,1,0:T(8,128)(2,1)} %slice_bitcast_fusion.3), channel_id=1, source_target_pairs={{0,16},{8,24},{16,0},{24,8},{1,17},{9,25},{17,1},{25,9},{2,18},{10... | collective-permute-start | bytes 2359304 | tf_op jit(solution)/shard_map/ppermute | solution.py:1897
  650.5 11.1 %copy-start.3 = (f32[128,2048]{1,0:T(8,128)S(1)}, f32[128,2048]{1,0:T(8,128)}, u32[]{:S(2)}) copy-start(f32[128,2048]{1,0:T(8,128)} %get-tuple-element.149) | copy-start | bytes 3145732
  650.5 12.1 %copy-start.7 = (f32[64,2048]{1,0:T(8,128)S(1)}, f32[64,2048]{1,0:T(8,128)}, u32[]{:S(2)}) copy-start(f32[64,2048]{1,0:T(8,128)} %get-tuple-element.150) | copy-start | bytes 1572868
  650.5 12.9 %copy-start.6 = (f32[64,2048]{1,0:T(8,128)S(1)}, f32[64,2048]{1,0:T(8,128)}, u32[]{:S(2)}) copy-start(f32[64,2048]{1,0:T(8,128)} %get-tuple-element.151) | copy-start | bytes 1572868
  661.6 2.6 copy-start.5
  661.6 3.4 copy-start.4
